TPU v7x, 32 devices: a whole 2x2x4 slice. The times are simulated.
32 devices in a mesh: col: 4 (over x, core), dp: 8 (over z, y).
Axes of the slice: x: 2, y: 2, z: 4, core: 2. Of those that a mesh axis runs over, the one named last changes fastest.
Arguments:
- layer_input: bfloat16 [1024, 8192], P('dp', 'col'), may hold values from -6 to 6
- query_cotangent: bfloat16 [1024, 4096], P('dp'), may hold values from -0.1875 to 0.1875
- key_cotangent: bfloat16 [1024, 1024], P('dp'), may hold values from -0.1875 to 0.1875
- up_cotangent: bfloat16 [1024, 14336], P('dp'), may hold values from -0.1875 to 0.1875
- query_weight: bfloat16 [4096, 8192], P('dp', 'col'), may hold values from -24 to 24
- key_weight: bfloat16 [1024, 8192], P('dp', 'col'), may hold values from -24 to 24
- up_weight: bfloat16 [14336, 8192], P('dp', 'col'), may hold values from -24 to 24
- moment_query: bfloat16 [4096, 8192], P('dp', 'col'), may hold values from -3 to 3
- moment_key: bfloat16 [1024, 8192], P('dp', 'col'), may hold values from -3 to 3
- moment_up: bfloat16 [14336, 8192], P('dp', 'col'), may hold values from -3 to 3
- second_query: bfloat16 [4096, 8192], P('dp', 'col'), may hold values from 0.25 to 4
- second_key: bfloat16 [1024, 8192], P('dp', 'col'), may hold values from 0.25 to 4
- second_up: bfloat16 [14336, 8192], P('dp', 'col'), may hold values from 0.25 to 4
Outputs:
- updated_query: bfloat16 [4096, 8192], P('dp', 'col')
- updated_key: bfloat16 [1024, 8192], P('dp', 'col')
- updated_up: bfloat16 [14336, 8192], P('dp', 'col')
- mean_query: bfloat16 [4096, 8192], P('dp', 'col')
- mean_key: bfloat16 [1024, 8192], P('dp', 'col')
- mean_up: bfloat16 [14336, 8192], P('dp', 'col')
- square_query: bfloat16 [4096, 8192], P('dp', 'col')
- square_key: bfloat16 [1024, 8192], P('dp', 'col')
- square_up: bfloat16 [14336, 8192], P('dp', 'col')
All inputs are finite; a program needn't handle non-finite values.
Results may differ from a plain program's by a relative error of at most 0.001.
Values may be sent and summed in bfloat16 or wider, within the bound.
No kernel may reach another device: no remote copies, remote signals or barrier semaphores. Data moves between devices by JAX's collectives and lax.ppermute only.
A program may use at most 192 MiB of HBM per device.

v0:
```python
import jax
import jax.numpy as jnp
from jax import lax
from jax.sharding import PartitionSpec as P

beta_one = 0.9
beta_two = 0.95
rate = 0.1
eps_adam = 1e-08
eps_norm = 1e-06


def contract_tokens(cotangent_rows, inputs):
    return lax.dot_general(
        cotangent_rows, inputs, (((0,), (0,)), ((), ())), preferred_element_type=jnp.float32
    )


def optimizer_pass(gradient, weight, moment, second):
    first = beta_one * moment.astype(jnp.float32) + (1.0 - beta_one) * gradient
    square = beta_two * second.astype(jnp.float32) + (1.0 - beta_two) * gradient * gradient
    step = weight.astype(jnp.float32) - rate * first / (jnp.sqrt(square) + eps_adam)
    partial_power = jnp.sum(step * step, axis=1)
    return (step, first.astype(jnp.bfloat16), square.astype(jnp.bfloat16), partial_power)


def finish_rows(step, total_power, width):
    scale = jnp.sqrt(total_power / width + eps_norm)
    return (step / scale[:, None]).astype(jnp.bfloat16)


def per_device(
    layer_input,
    query_cotangent,
    key_cotangent,
    up_cotangent,
    query_weight,
    key_weight,
    up_weight,
    moment_query,
    moment_key,
    moment_up,
    second_query,
    second_key,
    second_up,
):
    groups = lax.axis_size("dp")
    tok_local = layer_input.shape[0]
    query_rows = query_weight.shape[0]
    key_rows = key_weight.shape[0]
    up_rows = up_weight.shape[0]
    all_rows = query_rows + key_rows + up_rows
    width = layer_input.shape[1] * lax.axis_size("col")
    joined = jnp.concatenate(
        [
            query_cotangent.reshape(tok_local, groups, query_rows),
            key_cotangent.reshape(tok_local, groups, key_rows),
            up_cotangent.reshape(tok_local, groups, up_rows),
        ],
        axis=2,
    )
    owned = lax.all_to_all(joined, "dp", split_axis=1, concat_axis=0, tiled=True).reshape(
        -1, all_rows
    )
    gathered = lax.all_gather(layer_input, "dp", axis=0, tiled=True)
    gradient = contract_tokens(owned, gathered)
    grad_query = gradient[:query_rows]
    grad_key = gradient[query_rows : query_rows + key_rows]
    grad_up = gradient[query_rows + key_rows :]
    step_query, first_query, sq_query, power_query = optimizer_pass(
        grad_query, query_weight, moment_query, second_query
    )
    step_key, first_key, sq_key, power_key = optimizer_pass(
        grad_key, key_weight, moment_key, second_key
    )
    step_up, first_up, sq_up, power_up = optimizer_pass(grad_up, up_weight, moment_up, second_up)
    total_query, total_key, total_up = lax.psum((power_query, power_key, power_up), "col")
    new_query = finish_rows(step_query, total_query, width)
    new_key = finish_rows(step_key, total_key, width)
    new_up = finish_rows(step_up, total_up, width)
    return (new_query, new_key, new_up, first_query, first_key, first_up, sq_query, sq_key, sq_up)


def solution(mesh):
    placed = (
        P("dp", "col"),
        P("dp", None),
        P("dp", None),
        P("dp", None),
        P("dp", "col"),
        P("dp", "col"),
        P("dp", "col"),
        P("dp", "col"),
        P("dp", "col"),
        P("dp", "col"),
        P("dp", "col"),
        P("dp", "col"),
        P("dp", "col"),
    )
    return jax.shard_map(
        per_device,
        mesh=mesh,
        in_specs=placed,
        out_specs=(
            P("dp", "col"),
            P("dp", "col"),
            P("dp", "col"),
            P("dp", "col"),
            P("dp", "col"),
            P("dp", "col"),
            P("dp", "col"),
            P("dp", "col"),
            P("dp", "col"),
        ),
        check_vma=False,
    )
```

profile of v0, /device:TPU:0, one launch (start us, length us, event | category | flops | bytes accessed | tf_op | source)
XLA Modules:
  0.0 323.3 jit_solution(13304169438476023738)
XLA Ops:
  7.2 0.0 copy-start.10
  7.2 0.0 copy-start.13
  7.2 6.1 %copy.62 = bf16[128,14336]{0,1:T(8,128)(2,1)} copy(bf16[128,14336]{1,0:T(8,128)(2,1)} %param.16) | data formatting | bytes 7340032 | tf_op args[3]
  13.3 0.0 copy-done.10
  13.3 0.7 copy.60
  14.0 0.2 copy.61
  14.2 4.7 %pad_maximum_fusion = bf16[128,8,2432]{0,2,1:T(8,128)(2,1)} fusion(bf16[128,8,1792]{0,2,1:T(8,128)(2,1)} %bitcast.11, bf16[128,8,128]{0,2,1:T(8,128)(2,1)S(1)} %bitcast.14, bf16[128,8,512]{0,2,1:T(8,128)(2,1)S(1)} %bitcast.13), kind=kLoop, calls=%fused_computation.9 | loop fusion | flops 14942208 | bytes 9961472 | tf_op jit(solution)/shard_map/concatenate | solution.py:54
  18.8 7.3 %all-to-all-start = ((bf16[128,8,2432]{0,2,1:T(8,128)(2,1)}), bf16[128,8,2432]{0,2,1:T(8,128)(2,1)}, u32[]{:S(2)}, u32[]{:S(2)}) async-start(bf16[128,8,2432]{0,2,1:T(8,128)(2,1)} %pad_maximum_fusion), calls=%async_computation | async-start | bytes 9961472 | tf_op jit(solution)/shard_map/all_to_all | solution.py:62
  26.1 0.0 all-gather.2.cloned.1.call-start
  26.2 0.7 all-gather.2.cloned.1.call-update
  26.9 9.9 %copy.68 = bf16[1792,2048]{0,1:T(8,128)(2,1)} copy(bf16[1792,2048]{1,0:T(8,128)(2,1)} %param.19) | data formatting | bytes 14680064 | tf_op args[6]
  36.8 10.0 %copy.69 = bf16[1792,2048]{0,1:T(8,128)(2,1)} copy(bf16[1792,2048]{1,0:T(8,128)(2,1)} %param.22) | data formatting | bytes 14680064 | tf_op args[9]
  46.8 10.1 %copy.70 = bf16[1792,2048]{0,1:T(8,128)(2,1)} copy(bf16[1792,2048]{1,0:T(8,128)(2,1)} %param.25) | data formatting | bytes 14680064 | tf_op args[12]
  56.9 2.5 copy.58
  59.4 4.1 %copy.59 = bf16[512,2048]{0,1:T(8,128)(2,1)} copy(bf16[512,2048]{1,0:T(8,128)(2,1)} %param.20) | data formatting | bytes 4194304 | tf_op args[7]
  63.5 2.5 copy.64
  66.0 1.0 copy.65
  67.0 1.0 copy.66
  68.0 2.0 copy.67
  70.0 116.9 %all-to-all-done = bf16[128,8,2432]{0,2,1:T(8,128)(2,1)} async-done(((bf16[128,8,2432]{0,2,1:T(8,128)(2,1)}), bf16[128,8,2432]{0,2,1:T(8,128)(2,1)}, u32[]{:S(2)}, u32[]{:S(2)}) %all-to-all-start) | async-done | bytes 4980768 | tf_op jit(solution)/shard_map/all_to_all | solution.py:62
  186.9 7.7 %copy.63 = bf16[8,128,1,2432]{3,1,0,2:T(8,128)(2,1)} copy(bf16[8,128,1,2432]{1,3,0,2:T(8,128)(2,1)} %bitcast.4) | data formatting | bytes 9961472 | tf_op jit(solution)/shard_map/all_to_all | solution.py:62
  194.7 18.2 %fusion.9 = f32[2432,2048]{0,1:T(8,128)} fusion(bf16[1024,2432]{1,0:T(8,128)(2,1)} %bitcast.12, bf16[1024,2048]{1,0:T(8,128)(2,1)} %all-gather.2.cloned.1.call-done), kind=kOutput, calls=%fused_computation.28 | convolution fusion | flops 10200547328 | bytes 29097984 | tf_op jit(solution)/shard_map/dot_general | solution.py:14
  212.9 0.0 slice-done
  212.9 0.0 copy-start
  212.9 0.0 copy-start.1
  212.9 0.0 copy-start.2
  212.9 23.1 %multiply_reduce_fusion = (f32[1792]{0:T(1024)S(1)}, f32[1792,2048]{0,1:T(8,128)}, bf16[1792,2048]{0,1:T(8,128)(2,1)}, bf16[1792,2048]{0,1:T(8,128)(2,1)}) fusion(bf16[1792,2048]{0,1:T(8,128)(2,1)} %copy.70, f32[2432,2048]{0,1:T(8,128)} %fusion.9, bf16[1792,2048]{0,1:T(8,128)(2,1)} %copy.69, bf16[1792,2048]{0,1:T(8,128)(2,1)S(1)} %bitcast.10), kind=kLoop, calls=%fused_computation.3 | loop fusion | flops 66058496 | bytes 66067456 | tf_op jit(solution)/shard_map/reduce_sum | solution.py:23
  236.0 0.0 copy-done.1
  236.0 0.0 copy-start.5
  236.0 0.0 copy-start.6
  236.0 0.0 copy-start.7
  236.1 7.2 %multiply_reduce_fusion.1 = (f32[512]{0:T(512)S(1)}, f32[512,2048]{0,1:T(8,128)}, bf16[512,2048]{0,1:T(8,128)(2,1)S(1)}, bf16[512,2048]{0,1:T(8,128)(2,1)}) fusion(bf16[512,2048]{0,1:T(8,128)(2,1)S(1)} %copy-done.2, f32[2432,2048]{0,1:T(8,128)} %fusion.9, bf16[512,2048]{0,1:T(8,128)(2,1)S(1)} %copy-done.1, bf16[512,2048]{0,1:T(8,128)(2,1)S(1)} %copy-done), kind=kLoop, calls=%fused_computation.12 | loop fusion | flops 18873856 | bytes 18876416 | tf_op jit(solution)/shard_map/reduce_sum | solution.py:23
  243.3 0.0 copy-done.6
  243.3 3.1 multiply_reduce_fusion.2
  246.4 10.1 %all-reduce = (f32[512]{0:T(512)S(1)}, f32[128]{0:T(128)S(1)}, f32[1792]{0:T(1024)S(1)}) all-reduce(f32[512]{0:T(512)S(1)} %get-tuple-element.43, f32[128]{0:T(128)S(1)} %get-tuple-element.41, f32[1792]{0:T(1024)S(1)} %get-tuple-element.39), channel_id=1, replica_groups=mesh['col'=4,'dp'=8] {'col'}, use_global_device_ids=true, to_apply=%region_1.0 | all-reduce | flops 2432 | bytes 19456 | tf_op jit(solution)/shard_map/psum | solution.py:77
  256.5 9.4 %divide_convert_fusion = bf16[1792,2048]{0,1:T(8,128)(2,1)} fusion(f32[1792,2048]{0,1:T(8,128)} %get-tuple-element.40, f32[1792]{0:T(1024)S(1)} %add_sqrt_fusion), kind=kLoop, calls=%fused_computation.2 | loop fusion | flops 7340032 | bytes 22027264 | tf_op jit(solution)/shard_map/convert_element_type | solution.py:29
  265.9 10.4 %copy.73 = bf16[1792,2048]{1,0:T(8,128)(2,1)} copy(bf16[1792,2048]{0,1:T(8,128)(2,1)} %divide_convert_fusion) | data formatting | bytes 14680064
  276.3 0.9 divide_convert_fusion.2
  277.2 2.0 copy.72
  279.3 4.1 %divide_convert_fusion.1 = bf16[512,2048]{0,1:T(8,128)(2,1)} fusion(f32[512,2048]{0,1:T(8,128)} %get-tuple-element.44, f32[512]{0:T(512)S(1)} %add_sqrt_fusion.1), kind=kLoop, calls=%fused_computation.11 | loop fusion | flops 2097152 | bytes 6293504 | tf_op jit(solution)/shard_map/convert_element_type | solution.py:29
  283.3 3.9 %copy.71 = bf16[512,2048]{1,0:T(8,128)(2,1)} copy(bf16[512,2048]{0,1:T(8,128)(2,1)} %divide_convert_fusion.1) | data formatting | bytes 4194304
  287.3 10.4 %copy.76 = bf16[1792,2048]{1,0:T(8,128)(2,1)} copy(bf16[1792,2048]{0,1:T(8,128)(2,1)} %get-tuple-element.46) | data formatting | bytes 14680064
  297.7 10.4 %copy.79 = bf16[1792,2048]{1,0:T(8,128)(2,1)} copy(bf16[1792,2048]{0,1:T(8,128)(2,1)} %get-tuple-element.45) | data formatting | bytes 14680064
  308.1 4.0 %copy.74 = bf16[512,2048]{1,0:T(8,128)(2,1)} copy(bf16[512,2048]{0,1:T(8,128)(2,1)} %get-tuple-element.48) | data formatting | bytes 4194304
  312.1 2.4 copy.77
  314.5 0.0 copy-done.4
  314.5 1.0 copy.75
  315.5 1.0 copy.78
  (24 shorter events, 0.1 us)
Async XLA Ops:
  7.2 6.2 %copy-start.10 = (bf16[128,4096]{1,0:T(8,128)(2,1)S(1)}, bf16[128,4096]{1,0:T(8,128)(2,1)}, u32[]{:S(2)}) copy-start(bf16[128,4096]{1,0:T(8,128)(2,1)} %param.14) | copy-start | bytes 3145732
  7.2 6.8 %copy-start.13 = (bf16[128,1024]{1,0:T(8,128)(2,1)S(1)}, bf16[128,1024]{1,0:T(8,128)(2,1)}, u32[]{:S(2)}) copy-start(bf16[128,1024]{1,0:T(8,128)(2,1)} %param.15) | copy-start | bytes 786436
  18.8 168.1 %all-to-all-start = ((bf16[128,8,2432]{0,2,1:T(8,128)(2,1)}), bf16[128,8,2432]{0,2,1:T(8,128)(2,1)}, u32[]{:S(2)}, u32[]{:S(2)}) async-start(bf16[128,8,2432]{0,2,1:T(8,128)(2,1)} %pad_maximum_fusion), calls=%async_computation | async-start | bytes 9961472 | tf_op jit(solution)/shard_map/all_to_all | solution.py:62
  26.1 168.5 %all-gather.2.cloned.1.call-start = ((), (), s32[]{:S(2)}) async-start(), calls=%async_computation.1 | async-start | bytes 4718592 | tf_op jit(solution)/shard_map/all_gather | solution.py:65
  46.8 10.1 %copy-start.8 = (bf16[512,2048]{1,0:T(8,128)(2,1)S(1)}, bf16[512,2048]{1,0:T(8,128)(2,1)}, u32[]{:S(2)}) copy-start(bf16[512,2048]{1,0:T(8,128)(2,1)} %param.17) | copy-start | bytes 6291460
  59.4 4.1 %copy-start.9 = (bf16[512,2048]{1,0:T(8,128)(2,1)S(1)}, bf16[512,2048]{1,0:T(8,128)(2,1)}, u32[]{:S(2)}) copy-start(bf16[512,2048]{1,0:T(8,128)(2,1)} %param.23) | copy-start | bytes 6291460
  59.4 6.6 %copy-start.11 = (bf16[128,2048]{1,0:T(8,128)(2,1)S(1)}, bf16[128,2048]{1,0:T(8,128)(2,1)}, u32[]{:S(2)}) copy-start(bf16[128,2048]{1,0:T(8,128)(2,1)} %param.18) | copy-start | bytes 1572868
  59.4 7.6 %copy-start.12 = (bf16[128,2048]{1,0:T(8,128)(2,1)S(1)}, bf16[128,2048]{1,0:T(8,128)(2,1)}, u32[]{:S(2)}) copy-start(bf16[128,2048]{1,0:T(8,128)(2,1)} %param.21) | copy-start | bytes 1572868
  186.9 26.0 %slice-start = ((s8[7340032]{0:T(1024)(128)(4,1)}), s8[3145728]{0:T(1024)(128)(4,1)S(1)}, s32[]{:S(2)}) async-start(s8[7340032]{0:T(1024)(128)(4,1)} %bitcast.9), calls=%async_computation.2 | async-start | bytes 6291456
  194.7 18.2 %slice-start.1 = ((s8[7340032]{0:T(1024)(128)(4,1)}), s8[4194304]{0:T(1024)(128)(4,1)S(1)}, s32[]{:S(2)}) async-start(s8[7340032]{0:T(1024)(128)(4,1)} %bitcast.9), calls=%async_computation.3 | async-start | bytes 8388608
  212.9 23.1 %copy-start = (bf16[512,2048]{0,1:T(8,128)(2,1)S(1)}, bf16[512,2048]{0,1:T(8,128)(2,1)}, u32[]{:S(2)}) copy-start(bf16[512,2048]{0,1:T(8,128)(2,1)} %copy.58) | copy-start | bytes 6291460
  212.9 23.1 %copy-start.1 = (bf16[512,2048]{0,1:T(8,128)(2,1)S(1)}, bf16[512,2048]{0,1:T(8,128)(2,1)}, u32[]{:S(2)}) copy-start(bf16[512,2048]{0,1:T(8,128)(2,1)} %copy.59) | copy-start | bytes 6291460
  212.9 23.1 %copy-start.2 = (bf16[512,2048]{0,1:T(8,128)(2,1)S(1)}, bf16[512,2048]{0,1:T(8,128)(2,1)}, u32[]{:S(2)}) copy-start(bf16[512,2048]{0,1:T(8,128)(2,1)} %copy.64) | copy-start | bytes 6291460
  236.0 7.3 %copy-start.5 = (bf16[128,2048]{0,1:T(8,128)(2,1)S(1)}, bf16[128,2048]{0,1:T(8,128)(2,1)}, u32[]{:S(2)}) copy-start(bf16[128,2048]{0,1:T(8,128)(2,1)} %copy.65) | copy-start | bytes 1572868
  236.0 7.3 %copy-start.6 = (bf16[128,2048]{0,1:T(8,128)(2,1)S(1)}, bf16[128,2048]{0,1:T(8,128)(2,1)}, u32[]{:S(2)}) copy-start(bf16[128,2048]{0,1:T(8,128)(2,1)} %copy.66) | copy-start | bytes 1572868
  236.0 7.3 %copy-start.7 = (bf16[128,2048]{0,1:T(8,128)(2,1)S(1)}, bf16[128,2048]{0,1:T(8,128)(2,1)}, u32[]{:S(2)}) copy-start(bf16[128,2048]{0,1:T(8,128)(2,1)} %copy.67) | copy-start | bytes 1572868
  308.1 6.4 %copy-start.4 = (bf16[128,2048]{0,1:T(8,128)(2,1)S(1)}, bf16[128,2048]{0,1:T(8,128)(2,1)}, u32[]{:S(2)}) copy-start(bf16[128,2048]{0,1:T(8,128)(2,1)} %get-tuple-element.50) | copy-start | bytes 1572868
  308.1 7.4 %copy-start.3 = (bf16[128,2048]{0,1:T(8,128)(2,1)S(1)}, bf16[128,2048]{0,1:T(8,128)(2,1)}, u32[]{:S(2)}) copy-start(bf16[128,2048]{0,1:T(8,128)(2,1)} %get-tuple-element.49) | copy-start | bytes 1572868
Sparse Core Ops, SparseCore 0:
  29.1 149.4 all-gather.1
where the time goes:
time: 326 us; the launch traced here: 323 us
  waiting for transfers between devices  118 us (36%)
  local copies, waits for them, and re-layouts  104 us (32%)
  other arithmetic  52.4 us (16%)
  matrix products  18.2 us (6%)
  between operations  14.2 us (4%)
  blocking collectives  10.1 us (3%)
  starting transfers between devices  7.32 us (2%)
    all_to_all x1, waiting for transfers between devices, per_device(): lax.all_to_all(joined, 'dp', split_axis=1, concat_axis=0, tiled=True)  117 us
    unnamed x53, local copies, waits for them, and re-layouts  95.8 us
    reduce_sum x3, other arithmetic, optimizer_pass(): partial_power = jnp.sum(step * step, axis=1)  33.3 us
    dot_general x1, matrix products, contract_tokens(): lax.dot_general(cotangent_rows, inputs, (((0,), (0,)), ((), ())), preferr...  18.2 us
    convert_element_type x3, other arithmetic, finish_rows(): return (step / scale[:, None]).astype(jnp.bfloat16)  14.4 us
    psum x1, blocking collectives, per_device(): lax.psum((power_query, power_key, power_up), 'col')  10.1 us
    all_to_all x1, local copies, waits for them, and re-layouts, per_device(): lax.all_to_all(joined, 'dp', split_axis=1, concat_axis=0, tiled=True)  7.75 us
    all_to_all x1, starting transfers between devices, per_device(): lax.all_to_all(joined, 'dp', split_axis=1, concat_axis=0, tiled=True)  7.28 us
  transfers between devices with their start and end apart: 2, of which 1 were waited for; matrix products, arithmetic and copies ran while one was open for 16% of the time, Pallas kernels for 0%

commit v1 on v0

v1 whole, which is shorter than its diff:
```python
import functools

import jax
import jax.numpy as jnp
from jax import lax
from jax.experimental import pallas as pl
from jax.experimental.pallas import tpu as pltpu
from jax.sharding import PartitionSpec as P

beta_one = 0.9
beta_two = 0.95
rate = 0.1
eps_adam = 1e-08
eps_norm = 1e-06

params = pltpu.CompilerParams(vmem_limit_bytes=56 * 1024 * 1024)


def row_block(rows, largest=256):
    for block in range(largest, 0, -128):
        if rows % block == 0:
            return block
    return rows


def row_chunks(rows, count):
    block = row_block(rows)
    blocks = rows // block
    count = min(count, blocks)
    edges = [block * (-(-blocks * at // count)) for at in range(count + 1)]
    return list(zip(edges, edges[1:]))


def strip_of(width, largest=512):
    for strip in range(min(largest, width), 0, -128):
        if width % strip == 0:
            return strip
    return width


def pack_kernel(plan, groups, at_ref, *refs):
    inputs, outputs = refs[: -len(plan)], refs[-len(plan) :]
    for (source, rows, low, high), out_ref in zip(plan, outputs):
        for group in range(groups):
            out_ref[group] = inputs[source][:, group * rows + low : group * rows + high]


def pack(cotangents, plan, groups, part, place):
    return pl.pallas_call(
        functools.partial(pack_kernel, plan, groups),
        grid_spec=pltpu.PrefetchScalarGridSpec(
            num_scalar_prefetch=1,
            grid=(1,),
            in_specs=[
                pl.BlockSpec((part, array.shape[1]), lambda i, at: (at[0], 0))
                for array in cotangents
            ],
            out_specs=[
                pl.BlockSpec((groups, part, high - low), lambda i, at: (0, 0, 0))
                for _, _, low, high in plan
            ],
        ),
        out_shape=[
            jax.ShapeDtypeStruct((groups, part, high - low), jnp.bfloat16)
            for _, _, low, high in plan
        ],
        compiler_params=params,
        cost_estimate=pl.CostEstimate(
            flops=0,
            bytes_accessed=sum(4 * part * array.shape[1] for array in cotangents),
            transcendentals=0,
        ),
        name="pack",
    )(place, *cotangents)


def adam_kernel(strip, c_ref, x_ref, w_ref, m_ref, v_ref, *refs):
    step_ref, power_ref, first_ref, square_ref = refs[-4:]
    cols, groups, part, rows = c_ref.shape
    width = x_ref.shape[1]
    lhs = jnp.concatenate(
        [c_ref[at, group] for group in range(groups) for at in range(cols)], axis=0
    ).T
    power = jnp.zeros((rows, 128), jnp.float32)
    for start in range(0, width, strip):
        at = slice(start, start + strip)
        grad = jnp.dot(lhs, x_ref[:, at], preferred_element_type=jnp.float32)
        first = beta_one * m_ref[:, at].astype(jnp.float32) + (1.0 - beta_one) * grad
        square = beta_two * v_ref[:, at].astype(jnp.float32) + (1.0 - beta_two) * grad * grad
        step = w_ref[:, at].astype(jnp.float32) - rate * first / (jnp.sqrt(square) + eps_adam)
        first_ref[:, at] = first.astype(jnp.bfloat16)
        square_ref[:, at] = square.astype(jnp.bfloat16)
        step_ref[:, at] = step
        for lane in range(0, strip, 128):
            piece = step[:, lane : lane + 128]
            power += piece * piece
    power_ref[...] = jnp.sum(power.T, axis=0, keepdims=True)


def adam_pass(cotangent, inputs, state, low, high, made):
    cols, groups, part, rows = cotangent.shape
    tokens, width = inputs.shape
    total = state[0].shape[0]
    block = row_block(total)
    shift = low // block
    tile = pl.BlockSpec((block, width), lambda i: (i + shift, 0))
    return pl.pallas_call(
        functools.partial(adam_kernel, strip_of(width)),
        grid=(rows // block,),
        in_specs=[
            pl.BlockSpec((cols, groups, part, block), lambda i: (0, 0, 0, i)),
            pl.BlockSpec((tokens, width), lambda i: (0, 0), pipeline_mode=pl.Buffered(1)),
            tile,
            tile,
            tile,
        ]
        + [pl.BlockSpec(memory_space=pl.ANY)] * len(made),
        out_specs=[
            pl.BlockSpec((block, width), lambda i: (i, 0)),
            pl.BlockSpec((1, block), lambda i: (0, i)),
            tile,
            tile,
        ],
        out_shape=[
            jax.ShapeDtypeStruct((rows, width), jnp.float32),
            jax.ShapeDtypeStruct((1, rows), jnp.float32),
            jax.ShapeDtypeStruct((total, width), jnp.bfloat16),
            jax.ShapeDtypeStruct((total, width), jnp.bfloat16),
        ],
        input_output_aliases={5 + at: 2 + at for at in range(len(made))},
        compiler_params=params,
        cost_estimate=pl.CostEstimate(
            flops=2 * tokens * rows * width,
            bytes_accessed=14 * rows * width + 2 * tokens * (rows + width),
            transcendentals=0,
        ),
        name="adam",
    )(cotangent, inputs, *state, *made)


def finish_kernel(count, whole_width, step_ref, *refs):
    out_ref = refs[-1]
    power = refs[0][...]
    for other in refs[1:count]:
        power = power + other[...]
    scale = 1.0 / jnp.sqrt(power / whole_width + eps_norm)
    scale = jnp.broadcast_to(scale, (128, scale.shape[1])).T
    for lane in range(0, step_ref.shape[1], 128):
        at = slice(lane, lane + 128)
        out_ref[:, at] = (step_ref[:, at] * scale).astype(jnp.bfloat16)


def finish_rows(step, powers, whole_width, total, low, made):
    rows, width = step.shape
    block = row_block(total)
    shift = low // block
    return pl.pallas_call(
        functools.partial(finish_kernel, len(powers), whole_width),
        grid=(rows // block,),
        in_specs=[pl.BlockSpec((block, width), lambda i: (i, 0))]
        + [pl.BlockSpec((1, block), lambda i: (0, i))] * len(powers)
        + [pl.BlockSpec(memory_space=pl.ANY)] * len(made),
        out_specs=[pl.BlockSpec((block, width), lambda i: (i + shift, 0))],
        out_shape=[jax.ShapeDtypeStruct((total, width), jnp.bfloat16)],
        input_output_aliases={1 + len(powers) + at: at for at in range(len(made))},
        compiler_params=params,
        cost_estimate=pl.CostEstimate(
            flops=rows * width, bytes_accessed=6 * rows * width, transcendentals=0
        ),
        name="finish",
    )(step, *powers, *made)


def from_others(array, axis):
    size = lax.axis_size(axis)
    return [
        lax.ppermute(array, axis, [(at, (at + turn) % size) for at in range(size)])
        for turn in range(1, size)
    ]


def per_device(
    layer_input,
    query_cotangent,
    key_cotangent,
    up_cotangent,
    query_weight,
    key_weight,
    up_weight,
    moment_query,
    moment_key,
    moment_up,
    second_query,
    second_key,
    second_up,
):
    groups = lax.axis_size("dp")
    cols = lax.axis_size("col")
    part = layer_input.shape[0] // cols
    whole_width = layer_input.shape[1] * cols
    states = (
        (query_weight, moment_query, second_query),
        (key_weight, moment_key, second_key),
        (up_weight, moment_up, second_up),
    )
    plan = [
        (at, state[0].shape[0], low, high)
        for at, state, count in zip(range(3), states, (1, 1, 2))
        for low, high in row_chunks(state[0].shape[0], count)
    ]
    place = lax.axis_index("col").astype(jnp.int32).reshape(1)
    packed = pack((query_cotangent, key_cotangent, up_cotangent), plan, groups, part, place)
    gathered = lax.all_gather(layer_input, "dp", axis=0, tiled=True)
    owned = [
        lax.all_to_all(array, "dp", split_axis=0, concat_axis=0, tiled=True) for array in packed
    ]
    every = [lax.all_gather(array, "col", axis=0) for array in owned]
    moments = [[], [], []]
    updated = [[], [], []]
    for (at, total, low, high), cotangent in zip(plan, every):
        step, power, *moments[at] = adam_pass(
            cotangent, gathered, states[at], low, high, moments[at]
        )
        powers = [power, *from_others(power, "col")]
        updated[at] = finish_rows(step, powers, whole_width, total, low, updated[at])
    return (
        *(made[0] for made in updated),
        *(made[0] for made in moments),
        *(made[1] for made in moments),
    )


def solution(mesh):
    tokens_split = P("dp", None)
    split = P("dp", "col")
    return jax.shard_map(
        per_device,
        mesh=mesh,
        in_specs=(split, *(tokens_split,) * 3, *(split,) * 9),
        out_specs=(split,) * 9,
        check_vma=False,
    )
```

time: 326 us -> 211 us (0.65)
  local copies, waits for them, and re-layouts: 104 us -> 1.17 us
  waiting for transfers between devices: 118 us -> 27 us
  blocking collectives: 10.1 us -> 89.2 us
  Pallas kernels: 0 us -> 69.2 us
  other arithmetic: 52.4 us -> 0 us
  matrix products: 18.2 us -> 0 us
    all_to_all x1 -> x0, waiting for transfers between devices: 117 us -> none  [per_device(): lax.all_to_all(joined, 'dp', split_axis=1, concat_axis=0, tiled=True)]
    unnamed x53 -> x26, local copies, waits for them, and re-layouts: 95.8 us -> 1.17 us
    all_to_all x0 -> x4, blocking collectives: none -> 83 us  [per_device(): lax.all_to_all(array, 'dp', split_axis=0, concat_axis=0, tiled=True)]
    pallas_call x0 -> x9, Pallas kernels: none -> 69.2 us  [the longest x4 49.4 us: adam_pass(): pl.pallas_call(functools.partial(adam_kernel, strip_of(width)), grid=(row...]
    reduce_sum x3 -> x0, other arithmetic: 33.3 us -> none  [optimizer_pass(): partial_power = jnp.sum(step * step, axis=1)]
    all_gather x0 -> x3, waiting for transfers between devices: none -> 21.6 us  [per_device(): every = [lax.all_gather(array, 'col', axis=0) for array in owned]]
    dot_general x1 -> x0, matrix products: 18.2 us -> none  [contract_tokens(): lax.dot_general(cotangent_rows, inputs, (((0,), (0,)), ((), ())), preferr...]
    convert_element_type x3 -> x0, other arithmetic: 14.4 us -> none  [finish_rows(): return (step / scale[:, None]).astype(jnp.bfloat16)]
  transfers between devices with their start and end apart: 2 -> 16, of which waited for: 1 -> 3; matrix products, arithmetic and copies ran while one was open for 16% -> 0% of each run, Pallas kernels for 0% -> 30%
where the time goes in v1:
time: 211 us; the launch traced here: 210 us
  blocking collectives  89.2 us (42%)
  Pallas kernels  69.2 us (33%)
  waiting for transfers between devices  27 us (13%)
  between operations  13.9 us (7%)
  starting transfers between devices  10 us (5%)
    all_to_all x4, blocking collectives, per_device(): lax.all_to_all(array, 'dp', split_axis=0, concat_axis=0, tiled=True)  83 us
    pallas_call x4, Pallas kernels, adam_pass(): pl.pallas_call(functools.partial(adam_kernel, strip_of(width)), grid=(row...  49.4 us
    all_gather x3, waiting for transfers between devices, per_device(): every = [lax.all_gather(array, 'col', axis=0) for array in owned]  21.6 us
    pallas_call x4, Pallas kernels, finish_rows(): pl.pallas_call(functools.partial(finish_kernel, len(powers), whole_width)...  17.4 us
    ppermute x12, starting transfers between devices, from_others(): lax.ppermute(array, axis, [(at, (at + turn) % size) for at in range(size)])  9.84 us
    all_gather x1, blocking collectives, per_device(): every = [lax.all_gather(array, 'col', axis=0) for array in owned]  6.22 us
    all_gather x1, waiting for transfers between devices, per_device(): gathered = lax.all_gather(layer_input, 'dp', axis=0, tiled=True)  4.59 us
  transfers between devices with their start and end apart: 16, of which 3 were waited for; matrix products, arithmetic and copies ran while one was open for 0% of the time, Pallas kernels for 30%

profile of v1, /device:TPU:0, one launch (start us, length us, event | category | flops | bytes accessed | tf_op | source)
XLA Modules:
  0.0 210.5 jit_solution(8076733074628018279)
XLA Ops:
  7.2 0.0 all-gather.9.cloned.1.call-start
  7.2 0.7 all-gather.9.cloned.1.call-update
  7.9 0.0 all-gather.11.cloned.1.call-start
  8.0 2.3 %pack.1 = (bf16[8,32,512]{2,1,0:T(8,128)(2,1)}, bf16[8,32,128]{2,1,0:T(8,128)(2,1)}, bf16[8,32,1024]{2,1,0:T(8,128)(2,1)}, bf16[8,32,768]{2,1,0:T(8,128)(2,1)}) custom-call(s32[1]{0:T(128)} %bitcast.at_ref, bf16[128,4096]{1,0:T(8,128)(2,1)} %refs_0_.1, bf16[128,1024]{1,0:T(8,128)(2,1)} %refs_1_.1, bf16[128,14336]{1,0:T(8,128)(2,1)} %refs_2_.1), custom_call_target="tpu_custom_call" | custom-call | bytes 2490368 | tf_op jit(solution)/shard_map/pack/pallas_call | solution.py:49
  10.3 19.4 %all_to_all.20 = bf16[8,32,512]{2,1,0:T(8,128)(2,1)} all-to-all(bf16[8,32,512]{2,1,0:T(8,128)(2,1)} %get-tuple-element.29), channel_id=1, replica_groups=mesh['col'=4,'dp'=8] {'dp'}, dimensions={0} | all-to-all | bytes 524288 | tf_op jit(solution)/shard_map/all_to_all | solution.py:215
  29.7 0.0 all-gather.11.cloned.1.call-update
  29.7 0.0 all-gather.15.cloned.1.call-start
  29.7 24.9 %all_to_all.21 = bf16[8,32,1024]{2,1,0:T(8,128)(2,1)} all-to-all(bf16[8,32,1024]{2,1,0:T(8,128)(2,1)} %get-tuple-element.36), channel_id=1, replica_groups=mesh['col'=4,'dp'=8] {'dp'}, dimensions={0} | all-to-all | bytes 1048576 | tf_op jit(solution)/shard_map/all_to_all | solution.py:215
  54.7 0.0 all-gather.15.cloned.1.call-update
  54.7 0.0 all-gather.13.cloned.1.call-start
  54.8 26.7 %all_to_all.22 = bf16[8,32,768]{2,1,0:T(8,128)(2,1)} all-to-all(bf16[8,32,768]{2,1,0:T(8,128)(2,1)} %get-tuple-element.35), channel_id=1, replica_groups=mesh['col'=4,'dp'=8] {'dp'}, dimensions={0} | all-to-all | bytes 786432 | tf_op jit(solution)/shard_map/all_to_all | solution.py:215
  81.4 0.0 all-gather.13.cloned.1.call-update
  81.5 12.0 %all_to_all.23 = bf16[8,32,128]{2,1,0:T(8,128)(2,1)S(1)} all-to-all(bf16[8,32,128]{2,1,0:T(8,128)(2,1)} %get-tuple-element.32), channel_id=1, replica_groups=mesh['col'=4,'dp'=8] {'dp'}, dimensions={0} | all-to-all | bytes 131072 | tf_op jit(solution)/shard_map/all_to_all | solution.py:215
  93.5 6.2 %all-gather.1 = bf16[32,32,128]{2,1,0:T(8,128)(2,1)} all-gather(bf16[8,32,128]{2,1,0:T(8,128)(2,1)S(1)} %all_to_all.23), channel_id=3, replica_groups=mesh['col'=4,'dp'=8] {'col'}, dimensions={0}, use_global_device_ids=true | all-gather | bytes 327680 | tf_op jit(solution)/shard_map/all_gather | solution.py:217
  99.7 4.6 %all-gather.9.cloned.1.call-done.x_ref = bf16[1024,2048]{1,0:T(8,128)(2,1)} async-done(((bf16[128,2048]{1,0:T(8,128)(2,1)}), bf16[1024,2048]{1,0:T(8,128)(2,1)}) %all-gather.9.cloned.1.call-update) | async-done | bytes 4194320 | tf_op jit(solution)/shard_map/all_gather | solution.py:213
  104.3 5.4 %adam.5 = (f32[128,2048]{1,0:T(8,128)}, f32[1,128]{1,0:T(1,128)}, bf16[128,2048]{1,0:T(8,128)(2,1)}, bf16[128,2048]{1,0:T(8,128)(2,1)}) custom-call(bf16[4,8,32,128]{3,2,1,0:T(8,128)(2,1)} %bitcast.7, bf16[1024,2048]{1,0:T(8,128)(2,1)} %all-gather.9.cloned.1.call-done.x_ref, bf16[128,2048]{1,0:T(8,128)(2,1)} %w_ref.5, bf16[128,2048]{1,0:T(8,128)(2,1)} %m_ref.5, ...), custom_call_target="tpu_custom_call" | custom-call | flops 536870912 | bytes 8126464 | tf_op jit(solution)/shard_map/adam/pallas_call | solution.py:107
  109.6 0.0 collective-permute-start.3
  109.6 1.5 collective-permute-start.4
  111.1 1.4 collective-permute-start.5
  112.6 9.0 %all-gather.11.cloned.1.call-done = bf16[32,32,512]{2,1,0:T(8,128)(2,1)} async-done(((bf16[8,32,512]{2,1,0:T(8,128)(2,1)}), bf16[32,32,512]{2,1,0:T(8,128)(2,1)}) %all-gather.11.cloned.1.call-update) | async-done | bytes 1048592 | tf_op jit(solution)/shard_map/all_gather | solution.py:217
  121.6 11.4 %adam.4 = (f32[512,2048]{1,0:T(8,128)}, f32[1,512]{1,0:T(1,128)}, bf16[512,2048]{1,0:T(8,128)(2,1)}, bf16[512,2048]{1,0:T(8,128)(2,1)}) custom-call(bf16[4,8,32,512]{3,2,1,0:T(8,128)(2,1)} %bitcast.8, bf16[1024,2048]{1,0:T(8,128)(2,1)} %all-gather.9.cloned.1.call-done.x_ref, bf16[512,2048]{1,0:T(8,128)(2,1)} %w_ref.4, bf16[512,2048]{1,0:T(8,128)(2,1)} %m_ref.4, ...), custom_call_target="tpu_custom_call" | custom-call | flops 2147483648 | bytes 19922944 | tf_op jit(solution)/shard_map/adam/pallas_call | solution.py:107
  133.0 0.2 collective-permute-start
  133.2 12.6 %all-gather.15.cloned.1.call-done = bf16[32,32,1024]{2,1,0:T(8,128)(2,1)} async-done(((bf16[8,32,1024]{2,1,0:T(8,128)(2,1)}), bf16[32,32,1024]{2,1,0:T(8,128)(2,1)}) %all-gather.15.cloned.1.call-update) | async-done | bytes 2097168 | tf_op jit(solution)/shard_map/all_gather | solution.py:217
  145.8 18.0 %adam.6 = (f32[1024,2048]{1,0:T(8,128)}, f32[1,1024]{1,0:T(1,128)}, bf16[1792,2048]{1,0:T(8,128)(2,1)}, bf16[1792,2048]{1,0:T(8,128)(2,1)}) custom-call(bf16[4,8,32,1024]{3,2,1,0:T(8,128)(2,1)} %bitcast.5, bf16[1024,2048]{1,0:T(8,128)(2,1)} %all-gather.9.cloned.1.call-done.x_ref, bf16[1792,2048]{1,0:T(8,128)(2,1)} %w_ref.7, bf16[1792,2048]{1,0:T(8,128)(2,1)} %m_ref.7, ...), custom_call_target="tpu_custom_call" | custom-call | flops 4294967296 | bytes 35651584 | tf_op jit(solution)/shard_map/adam/pallas_call | solution.py:107
  163.8 0.3 collective-permute-start.10
  164.1 0.0 collective-permute-done.3.refs_1_
  164.1 1.4 collective-permute-start.11
  165.5 0.0 collective-permute-done.5.refs_3_
  165.5 0.9 collective-permute-start.1
  166.4 1.0 collective-permute-start.2
  167.4 14.7 %adam.7 = (f32[768,2048]{1,0:T(8,128)}, f32[1,768]{1,0:T(1,128)}, bf16[1792,2048]{1,0:T(8,128)(2,1)}, bf16[1792,2048]{1,0:T(8,128)(2,1)}) custom-call(bf16[4,8,32,768]{3,2,1,0:T(8,128)(2,1)} %bitcast.6, bf16[1024,2048]{1,0:T(8,128)(2,1)} %all-gather.9.cloned.1.call-done.x_ref, ...), custom_call_target="tpu_custom_call", output_to_operand_aliasing={{2}: (5, {}), {3}: (6, {})} | custom-call | flops 3221225472 | bytes 27787264 | tf_op jit(solution)/shard_map/adam/pallas_call | solution.py:107
  182.2 0.0 collective-permute-done.1.refs_2_
  182.2 0.1 collective-permute-start.6
  182.3 0.0 collective-permute-done.2.refs_3_
  182.3 1.7 collective-permute-start.7
  183.9 0.0 collective-permute-done.10.refs_2_
  183.9 1.4 collective-permute-start.8
  185.3 2.2 %finish.5 = bf16[128,2048]{1,0:T(8,128)(2,1)} custom-call(f32[128,2048]{1,0:T(8,128)} %get-tuple-element.33.step_ref, f32[1,128]{1,0:T(1,128)} %get-tuple-element.34.refs_0_, f32[1,128]{1,0:T(1,128)} %copy-done.10, f32[1,128]{1,0:T(1,128)} %copy-done.11, f32[1,128]{1,0:T(1,128)} %copy-done.12), custom_call_target="tpu_custom_call" | custom-call | flops 262144 | bytes 1572864 | tf_op jit(solution)/shard_map/finish/pallas_call | solution.py:157
  187.5 3.5 %finish.4 = bf16[512,2048]{1,0:T(8,128)(2,1)} custom-call(f32[512,2048]{1,0:T(8,128)} %get-tuple-element.30.step_ref, f32[1,512]{1,0:T(1,128)} %get-tuple-element.31.refs_0_, f32[1,512]{1,0:T(1,128)} %copy-done.7, f32[1,512]{1,0:T(1,128)} %copy-done.8, f32[1,512]{1,0:T(1,128)} %copy-done.9), custom_call_target="tpu_custom_call" | custom-call | flops 1048576 | bytes 6291456 | tf_op jit(solution)/shard_map/finish/pallas_call | solution.py:157
  191.0 0.0 collective-permute-done.9.refs_1_
  191.1 0.5 copy-done.1
  191.6 0.0 copy-done.2
  191.6 6.1 %finish.6.refs_4_ = bf16[1792,2048]{1,0:T(8,128)(2,1)} custom-call(f32[1024,2048]{1,0:T(8,128)} %get-tuple-element.41.step_ref, f32[1,1024]{1,0:T(1,128)} %get-tuple-element.42.refs_0_, f32[1,1024]{1,0:T(1,128)} %copy-done.2, f32[1,1024]{1,0:T(1,128)} %copy-done, f32[1,1024]{1,0:T(1,128)} %copy-done.1), custom_call_target="tpu_custom_call" | custom-call | flops 2097152 | bytes 12582912 | tf_op jit(solution)/shard_map/finish/pallas_call | solution.py:157
  197.8 0.0 collective-permute-done.6.refs_1_
  197.8 0.5 copy-done.3
  198.4 0.0 copy-done.4
  198.4 0.0 copy-done.5
  198.4 5.6 %finish.7 = bf16[1792,2048]{1,0:T(8,128)(2,1)} custom-call(f32[768,2048]{1,0:T(8,128)} %get-tuple-element.39.step_ref, f32[1,768]{1,0:T(1,128)} %get-tuple-element.40.refs_0_, f32[1,768]{1,0:T(1,128)} %copy-done.3, f32[1,768]{1,0:T(1,128)} %copy-done.4, f32[1,768]{1,0:T(1,128)} %copy-done.5, ...), custom_call_target="tpu_custom_call", output_to_operand_aliasing={{}: (5, {})} | custom-call | flops 1572864 | bytes 9437184 | tf_op jit(solution)/shard_map/finish/pallas_call | solution.py:157
  (28 shorter events, 0.1 us)
Async XLA Ops:
  7.2 97.1 %all-gather.9.cloned.1.call-start = ((), (), s32[]{:S(2)}) async-start(), calls=%async_computation.4 | async-start | bytes 4718592 | tf_op jit(solution)/shard_map/all_gather | solution.py:213
  7.9 113.7 %all-gather.11.cloned.1.call-start = ((), (), s32[]{:S(2)}) async-start(), calls=%async_computation.5 | async-start | bytes 1310720 | tf_op jit(solution)/shard_map/all_gather | solution.py:217
  29.7 116.1 %all-gather.15.cloned.1.call-start = ((), (), s32[]{:S(2)}) async-start(), calls=%async_computation.7 | async-start | bytes 2621440 | tf_op jit(solution)/shard_map/all_gather | solution.py:217
  54.7 112.7 %all-gather.13.cloned.1.call-start = ((), (), s32[]{:S(2)}) async-start(), calls=%async_computation.6 | async-start | bytes 1966080 | tf_op jit(solution)/shard_map/all_gather | solution.py:217
  109.6 54.4 %collective-permute-start.3 = (f32[1,128]{1,0:T(1,128)}, f32[1,128]{1,0:T(1,128)S(1)}, u32[]{:S(2)}, u32[]{:S(2)}) collective-permute-start(f32[1,128]{1,0:T(1,128)} %get-tuple-element.34.refs_0_), channel_id=1, source_target_pairs={{0,8},{8,16},{16,24},{24,0},{1,9},{9,17},{17,25},{25,1},{2,10},{10... | collective-permute-start | bytes 1544 | tf_op jit(solution)/shard_map/ppermute | solution.py:177
  109.6 55.8 %collective-permute-start.4 = (f32[1,128]{1,0:T(1,128)}, f32[1,128]{1,0:T(1,128)S(1)}, u32[]{:S(2)}, u32[]{:S(2)}) collective-permute-start(f32[1,128]{1,0:T(1,128)} %get-tuple-element.34.refs_0_), channel_id=1, source_target_pairs={{0,16},{8,24},{16,0},{24,8},{1,17},{9,25},{17,1},{25,9},{2,18},{10... | collective-permute-start | bytes 1544 | tf_op jit(solution)/shard_map/ppermute | solution.py:177
  111.1 54.3 %collective-permute-start.5 = (f32[1,128]{1,0:T(1,128)}, f32[1,128]{1,0:T(1,128)S(1)}, u32[]{:S(2)}, u32[]{:S(2)}) collective-permute-start(f32[1,128]{1,0:T(1,128)} %get-tuple-element.34.refs_0_), channel_id=1, source_target_pairs={{0,24},{8,0},{16,8},{24,16},{1,25},{9,1},{17,9},{25,17},{2,26},{10... | collective-permute-start | bytes 1544 | tf_op jit(solution)/shard_map/ppermute | solution.py:177
  133.0 33.4 %collective-permute-start = (f32[1,512]{1,0:T(1,128)}, f32[1,512]{1,0:T(1,128)S(1)}, u32[]{:S(2)}, u32[]{:S(2)}) collective-permute-start(f32[1,512]{1,0:T(1,128)} %get-tuple-element.31.refs_0_), channel_id=1, source_target_pairs={{0,8},{8,16},{16,24},{24,0},{1,9},{9,17},{17,25},{25,1},{2,10},{10... | collective-permute-start | bytes 6152 | tf_op jit(solution)/shard_map/ppermute | solution.py:177
  145.8 19.7 %copy-start.6 = (f32[1,512]{1,0:T(1,128)S(1)}, f32[1,512]{1,0:T(1,128)}, u32[]{:S(2)}) copy-start(f32[1,512]{1,0:T(1,128)} %get-tuple-element.31.refs_0_) | copy-start | bytes 6148
  163.8 20.2 %collective-permute-start.10 = (f32[1,1024]{1,0:T(1,128)}, f32[1,1024]{1,0:T(1,128)S(1)}, u32[]{:S(2)}, u32[]{:S(2)}) collective-permute-start(f32[1,1024]{1,0:T(1,128)} %get-tuple-element.42.refs_0_), channel_id=1, source_target_pairs={{0,16},{8,24},{16,0},{24,8},{1,17},{9,25},{17,1},{25,9},{2,18},{10... | collective-permute-start | bytes 12296 | tf_op jit(solution)/shard_map/ppermute | solution.py:177
  164.1 18.1 %copy-start.10 = (f32[1,128]{1,0:T(1,128)}, f32[1,128]{1,0:T(1,128)S(1)}, u32[]{:S(2)}) copy-start(f32[1,128]{1,0:T(1,128)S(1)} %collective-permute-done.3.refs_1_) | copy-start | bytes 1540
  164.1 27.0 %collective-permute-start.11 = (f32[1,1024]{1,0:T(1,128)}, f32[1,1024]{1,0:T(1,128)S(1)}, u32[]{:S(2)}, u32[]{:S(2)}) collective-permute-start(f32[1,1024]{1,0:T(1,128)} %get-tuple-element.42.refs_0_), channel_id=1, source_target_pairs={{0,24},{8,0},{16,8},{24,16},{1,25},{9,1},{17,9},{25,17},{2,26},{10... | collective-permute-start | bytes 12296 | tf_op jit(solution)/shard_map/ppermute | solution.py:177
  165.5 16.7 %copy-start.11 = (f32[1,128]{1,0:T(1,128)}, f32[1,128]{1,0:T(1,128)S(1)}, u32[]{:S(2)}) copy-start(f32[1,128]{1,0:T(1,128)S(1)} %collective-permute-done.4.refs_2_) | copy-start | bytes 1540
  165.5 25.6 %collective-permute-start.9 = (f32[1,1024]{1,0:T(1,128)}, f32[1,1024]{1,0:T(1,128)S(1)}, u32[]{:S(2)}, u32[]{:S(2)}) collective-permute-start(f32[1,1024]{1,0:T(1,128)} %get-tuple-element.42.refs_0_), channel_id=1, source_target_pairs={{0,8},{8,16},{16,24},{24,0},{1,9},{9,17},{17,25},{25,1},{2,10},{10... | collective-permute-start | bytes 12296 | tf_op jit(solution)/shard_map/ppermute | solution.py:177
  165.5 16.7 %copy-start.12 = (f32[1,128]{1,0:T(1,128)}, f32[1,128]{1,0:T(1,128)S(1)}, u32[]{:S(2)}) copy-start(f32[1,128]{1,0:T(1,128)S(1)} %collective-permute-done.5.refs_3_) | copy-start | bytes 1540
  165.5 16.7 %collective-permute-start.1 = (f32[1,512]{1,0:T(1,128)S(1)}, f32[1,512]{1,0:T(1,128)S(1)}, u32[]{:S(2)}, u32[]{:S(2)}) collective-permute-start(f32[1,512]{1,0:T(1,128)S(1)} %copy-done.6), channel_id=1, source_target_pairs={{0,16},{8,24},{16,0},{24,8},{1,17},{9,25},{17,1},{25,9},{2,18},{10... | collective-permute-start | bytes 6152 | tf_op jit(solution)/shard_map/ppermute | solution.py:177
  166.4 15.8 %copy-start.7 = (f32[1,512]{1,0:T(1,128)}, f32[1,512]{1,0:T(1,128)S(1)}, u32[]{:S(2)}) copy-start(f32[1,512]{1,0:T(1,128)S(1)} %collective-permute-done.refs_1_) | copy-start | bytes 6148
  166.4 15.9 %collective-permute-start.2 = (f32[1,512]{1,0:T(1,128)S(1)}, f32[1,512]{1,0:T(1,128)S(1)}, u32[]{:S(2)}, u32[]{:S(2)}) collective-permute-start(f32[1,512]{1,0:T(1,128)S(1)} %copy-done.6), channel_id=1, source_target_pairs={{0,24},{8,0},{16,8},{24,16},{1,25},{9,1},{17,9},{25,17},{2,26},{10... | collective-permute-start | bytes 6152 | tf_op jit(solution)/shard_map/ppermute | solution.py:177
  182.2 5.3 %copy-start.8 = (f32[1,512]{1,0:T(1,128)}, f32[1,512]{1,0:T(1,128)S(1)}, u32[]{:S(2)}) copy-start(f32[1,512]{1,0:T(1,128)S(1)} %collective-permute-done.1.refs_2_) | copy-start | bytes 6148
  182.2 15.6 %collective-permute-start.6 = (f32[1,768]{1,0:T(1,128)}, f32[1,768]{1,0:T(1,128)S(1)}, u32[]{:S(2)}, u32[]{:S(2)}) collective-permute-start(f32[1,768]{1,0:T(1,128)} %get-tuple-element.40.refs_0_), channel_id=1, source_target_pairs={{0,8},{8,16},{16,24},{24,0},{1,9},{9,17},{17,25},{25,1},{2,10},{10... | collective-permute-start | bytes 9224 | tf_op jit(solution)/shard_map/ppermute | solution.py:177
  182.3 5.3 %copy-start.9 = (f32[1,512]{1,0:T(1,128)}, f32[1,512]{1,0:T(1,128)S(1)}, u32[]{:S(2)}) copy-start(f32[1,512]{1,0:T(1,128)S(1)} %collective-permute-done.2.refs_3_) | copy-start | bytes 6148
  182.3 15.5 %collective-permute-start.7 = (f32[1,768]{1,0:T(1,128)}, f32[1,768]{1,0:T(1,128)S(1)}, u32[]{:S(2)}, u32[]{:S(2)}) collective-permute-start(f32[1,768]{1,0:T(1,128)} %get-tuple-element.40.refs_0_), channel_id=1, source_target_pairs={{0,16},{8,24},{16,0},{24,8},{1,17},{9,25},{17,1},{25,9},{2,18},{10... | collective-permute-start | bytes 9224 | tf_op jit(solution)/shard_map/ppermute | solution.py:177
  183.9 7.1 %copy-start = (f32[1,1024]{1,0:T(1,128)}, f32[1,1024]{1,0:T(1,128)S(1)}, u32[]{:S(2)}) copy-start(f32[1,1024]{1,0:T(1,128)S(1)} %collective-permute-done.10.refs_2_) | copy-start | bytes 12292
  183.9 13.9 %collective-permute-start.8 = (f32[1,768]{1,0:T(1,128)}, f32[1,768]{1,0:T(1,128)S(1)}, u32[]{:S(2)}, u32[]{:S(2)}) collective-permute-start(f32[1,768]{1,0:T(1,128)} %get-tuple-element.40.refs_0_), channel_id=1, source_target_pairs={{0,24},{8,0},{16,8},{24,16},{1,25},{9,1},{17,9},{25,17},{2,26},{10... | collective-permute-start | bytes 9224 | tf_op jit(solution)/shard_map/ppermute | solution.py:177
  191.0 0.6 copy-start.1
  191.0 0.6 copy-start.2
  197.8 0.6 copy-start.3
  197.8 0.6 copy-start.4
  197.8 0.6 copy-start.5
Sparse Core Ops, SparseCore 0:
  10.1 94.0 all-gather.8
  105.8 15.7 all-gather.10
  123.2 22.5 all-gather.14
  147.2 19.6 all-gather.12

commit v2 on v1

v2 whole, which is shorter than its diff:
```python
import functools

import jax
import jax.numpy as jnp
from jax import lax
from jax.experimental import pallas as pl
from jax.experimental.pallas import tpu as pltpu
from jax.sharding import PartitionSpec as P

beta_one = 0.9
beta_two = 0.95
rate = 0.1
eps_adam = 1e-08
eps_norm = 1e-06


def with_vmem(mebibytes):
    return pltpu.CompilerParams(vmem_limit_bytes=mebibytes * 1024 * 1024)


def row_block(rows, largest=256):
    for block in range(largest, 0, -128):
        if rows % block == 0:
            return block
    return rows


def column_chunk(width, count):
    while width % (count * 128):
        count -= 1
    return width // count


def strip_of(width, largest=512):
    for strip in range(min(largest, width), 0, -128):
        if width % strip == 0:
            return strip
    return width


def pack_kernel(groups, *refs):
    out_ref = refs[-1]
    low = 0
    for ref in refs[1:-1]:
        rows = ref.shape[1] // groups
        for group in range(groups):
            out_ref[group, :, low : low + rows] = ref[:, group * rows : (group + 1) * rows]
        low += rows


def pack(cotangents, groups, part, place):
    rows = sum(array.shape[1] for array in cotangents) // groups
    return pl.pallas_call(
        functools.partial(pack_kernel, groups),
        grid_spec=pltpu.PrefetchScalarGridSpec(
            num_scalar_prefetch=1,
            grid=(1,),
            in_specs=[
                pl.BlockSpec((part, array.shape[1]), lambda i, at: (at[0], 0))
                for array in cotangents
            ],
            out_specs=pl.BlockSpec((groups, part, rows), lambda i, at: (0, 0, 0)),
        ),
        out_shape=jax.ShapeDtypeStruct((groups, part, rows), jnp.bfloat16),
        compiler_params=with_vmem(12),
        cost_estimate=pl.CostEstimate(
            flops=0, bytes_accessed=4 * groups * part * rows, transcendentals=0
        ),
        name="pack",
    )(place, *cotangents)


def unpack_kernel(count, at_ref, *refs):
    pieces, outputs, order = refs[:count], refs[count:-1], refs[-1]
    groups, part, _ = pieces[0].shape
    for turn, piece in enumerate(pieces):
        for group in range(groups):
            order[group * count + (at_ref[0] ^ turn)] = piece[group]
    low = 0
    for out_ref in outputs:
        rows = out_ref.shape[0]
        for start in range(0, rows, 128):
            high = min(start + 128, rows)
            tokens = order[:, :, low + start : low + high].reshape(-1, high - start)
            out_ref[start:high] = tokens.T
        low += rows


def unpack(pieces, row_counts, place):
    groups, part, rows = pieces[0].shape
    tokens = groups * part * len(pieces)
    vmem = pl.BlockSpec(memory_space=pltpu.VMEM)
    return pl.pallas_call(
        functools.partial(unpack_kernel, len(pieces)),
        in_specs=[pl.BlockSpec(memory_space=pltpu.SMEM)] + [vmem] * len(pieces),
        out_specs=[vmem] * len(row_counts),
        out_shape=[jax.ShapeDtypeStruct((count, tokens), jnp.bfloat16) for count in row_counts],
        scratch_shapes=[pltpu.VMEM((groups * len(pieces), part, rows), jnp.bfloat16)],
        compiler_params=with_vmem(28),
        cost_estimate=pl.CostEstimate(
            flops=0, bytes_accessed=4 * tokens * rows, transcendentals=0
        ),
        name="unpack",
    )(place, *pieces)


def adam_kernel(strip, c_ref, x_ref, w_ref, m_ref, v_ref, *refs):
    power_ref, step_ref, first_ref, square_ref = refs[-4:]
    rows = c_ref.shape[0]
    width = x_ref.shape[1]
    lhs = c_ref[...]
    power = jnp.zeros((rows, 128), jnp.float32)
    for start in range(0, width, strip):
        at = slice(start, start + strip)
        grad = jnp.dot(lhs, x_ref[:, at], preferred_element_type=jnp.float32)
        first = beta_one * m_ref[:, at].astype(jnp.float32) + (1.0 - beta_one) * grad
        square = beta_two * v_ref[:, at].astype(jnp.float32) + (1.0 - beta_two) * grad * grad
        root = square * lax.rsqrt(square) + eps_adam
        inverse = pl.reciprocal(root, approx=True)
        inverse = inverse * (2.0 - root * inverse)
        step = w_ref[:, at].astype(jnp.float32) - rate * first * inverse
        first_ref[:, at] = first.astype(jnp.bfloat16)
        square_ref[:, at] = square.astype(jnp.bfloat16)
        step_ref[:, at] = step
        for lane in range(0, strip, 128):
            piece = step[:, lane : lane + 128]
            power += piece * piece
    power = jnp.sum(power.T, axis=0, keepdims=True)
    if len(refs) > 4:
        power += refs[0][...]
    power_ref[...] = power


def adam_pass(cotangent, inputs, state, chunk, made):
    rows, tokens = cotangent.shape
    width = inputs.shape[1]
    whole = state[0].shape[1]
    block = row_block(rows)
    tile = pl.BlockSpec((block, width), lambda i: (i, chunk))
    power = pl.BlockSpec((1, block), lambda i: (0, i))
    return pl.pallas_call(
        functools.partial(adam_kernel, strip_of(width)),
        grid=(rows // block,),
        in_specs=[
            pl.BlockSpec((block, tokens), lambda i: (i, 0)),
            pl.BlockSpec((tokens, width), lambda i: (0, 0), pipeline_mode=pl.Buffered(1)),
            tile,
            tile,
            tile,
        ]
        + ([power] + [pl.BlockSpec(memory_space=pl.ANY)] * 3 if made else []),
        out_specs=[power, tile, tile, tile],
        out_shape=[
            jax.ShapeDtypeStruct((1, rows), jnp.float32),
            jax.ShapeDtypeStruct((rows, whole), jnp.float32),
            jax.ShapeDtypeStruct((rows, whole), jnp.bfloat16),
            jax.ShapeDtypeStruct((rows, whole), jnp.bfloat16),
        ],
        input_output_aliases={5 + at: at for at in range(len(made))},
        compiler_params=with_vmem(48),
        cost_estimate=pl.CostEstimate(
            flops=2 * tokens * rows * width,
            bytes_accessed=14 * rows * width + 2 * tokens * (rows + width),
            transcendentals=0,
        ),
        name="adam",
    )(cotangent, inputs, *state, *made)


def finish_kernel(count, whole_width, step_ref, *refs):
    out_ref = refs[-1]
    power = refs[0][...]
    for other in refs[1:count]:
        power = power + other[...]
    scale = 1.0 / jnp.sqrt(power / whole_width + eps_norm)
    scale = jnp.broadcast_to(scale, (128, scale.shape[1])).T
    for lane in range(0, step_ref.shape[1], 128):
        at = slice(lane, lane + 128)
        out_ref[:, at] = (step_ref[:, at] * scale).astype(jnp.bfloat16)


def finish_rows(step, powers, whole_width):
    rows, width = step.shape
    block = row_block(rows)
    tile = pl.BlockSpec((block, width), lambda i: (i, 0))
    return pl.pallas_call(
        functools.partial(finish_kernel, len(powers), whole_width),
        grid=(rows // block,),
        in_specs=[tile] + [pl.BlockSpec((1, block), lambda i: (0, i))] * len(powers),
        out_specs=tile,
        out_shape=jax.ShapeDtypeStruct((rows, width), jnp.bfloat16),
        compiler_params=with_vmem(24),
        cost_estimate=pl.CostEstimate(
            flops=rows * width, bytes_accessed=6 * rows * width, transcendentals=0
        ),
        name="finish",
    )(step, *powers)


def from_others(array, axis):
    size = lax.axis_size(axis)
    bit = size // 2
    got = {0: array}
    while bit:
        for turn in list(got):
            got[turn ^ bit] = lax.ppermute(got[turn], axis, [(at, at ^ bit) for at in range(size)])
        bit //= 2
    return [got[turn] for turn in range(size)]


def per_device(
    layer_input,
    query_cotangent,
    key_cotangent,
    up_cotangent,
    query_weight,
    key_weight,
    up_weight,
    moment_query,
    moment_key,
    moment_up,
    second_query,
    second_key,
    second_up,
):
    groups = lax.axis_size("dp")
    cols = lax.axis_size("col")
    part = layer_input.shape[0] // cols
    whole_width = layer_input.shape[1] * cols
    states = (
        (query_weight, moment_query, second_query),
        (key_weight, moment_key, second_key),
        (up_weight, moment_up, second_up),
    )
    counts = [state[0].shape[0] for state in states]
    place = lax.axis_index("col").astype(jnp.int32).reshape(1)
    packed = pack((query_cotangent, key_cotangent, up_cotangent), groups, part, place)
    owned = lax.all_to_all(packed, "dp", split_axis=0, concat_axis=0, tiled=True)
    layer_input, owned = lax.optimization_barrier((layer_input, owned))
    chunk = column_chunk(layer_input.shape[1], 2)
    gathered = [
        lax.all_gather(layer_input[:, low : low + chunk], "dp", axis=0, tiled=True)
        for low in range(0, layer_input.shape[1], chunk)
    ]
    every = unpack(from_others(owned, "col"), counts, place)
    made = [(), (), ()]
    for at, inputs in enumerate(gathered):
        for which in (2, 0, 1):
            made[which] = adam_pass(every[which], inputs, states[which], at, made[which])
    updated = [None] * 3
    for which in (2, 0, 1):
        updated[which] = finish_rows(
            made[which][1], from_others(made[which][0], "col"), whole_width
        )
    return (*updated, *(done[2] for done in made), *(done[3] for done in made))


def solution(mesh):
    tokens_split = P("dp", None)
    split = P("dp", "col")
    return jax.shard_map(
        per_device,
        mesh=mesh,
        in_specs=(split, *(tokens_split,) * 3, *(split,) * 9),
        out_specs=(split,) * 9,
        check_vma=False,
    )
```

time: 211 us -> 211 us (level)
  waiting for transfers between devices: 27 us -> 81.8 us
  blocking collectives: 89.2 us -> 37.3 us
  local copies, waits for them, and re-layouts: 1.17 us -> 19.3 us
  Pallas kernels: 69.2 us -> 52.3 us
  starting transfers between devices: 10 us -> 5.19 us
    all_to_all x4 -> x1, blocking collectives: 83 us -> 37.3 us  [per_device(): lax.all_to_all(packed, 'dp', split_axis=0, concat_axis=0, tiled=True)]
    ppermute x12, waiting for transfers between devices: 0.03 us -> 35.3 us  [from_others(): lax.ppermute(got[turn], axis, [(at, at ^ bit) for at in range(size)])]
    all_gather x4 -> x2, waiting for transfers between devices: 26.2 us -> 45.7 us  [per_device(): lax.all_gather(layer_input[:, low:low + chunk], 'dp', axis=0, tiled=True)]
    unnamed x26 -> x34, local copies, waits for them, and re-layouts: 1.17 us -> 18.5 us
    pallas_call x4 -> x3, Pallas kernels: 17.4 us -> 7.47 us  [finish_rows(): pl.pallas_call(functools.partial(finish_kernel, len(powers), whole_width)...]
    pallas_call x4 -> x6, Pallas kernels: 49.4 us -> 43.1 us  [adam_pass(): pl.pallas_call(functools.partial(adam_kernel, strip_of(width)), grid=(row...]
    all_gather x1 -> x0, blocking collectives: 6.22 us -> none  [per_device(): every = [lax.all_gather(array, 'col', axis=0) for array in owned]]
    ppermute x12, starting transfers between devices: 9.84 us -> 5.11 us  [from_others(): lax.ppermute(got[turn], axis, [(at, at ^ bit) for at in range(size)])]
  transfers between devices with their start and end apart: 16 -> 14, of which waited for: 3 -> 8; matrix products, arithmetic and copies ran while one was open for 0% -> 0% of each run, Pallas kernels for 30% -> 16%
where the time goes in v2:
time: 211 us; the launch traced here: 210 us
  waiting for transfers between devices  81.8 us (39%)
  Pallas kernels  52.3 us (25%)
  blocking collectives  37.3 us (18%)
  local copies, waits for them, and re-layouts  19.3 us (9%)
  between operations  14.2 us (7%)
  starting transfers between devices  5.19 us (2%)
    all_gather x2, waiting for transfers between devices, per_device(): lax.all_gather(layer_input[:, low:low + chunk], 'dp', axis=0, tiled=True)  45.7 us
    pallas_call x6, Pallas kernels, adam_pass(): pl.pallas_call(functools.partial(adam_kernel, strip_of(width)), grid=(row...  43.1 us
    all_to_all x1, blocking collectives, per_device(): lax.all_to_all(packed, 'dp', split_axis=0, concat_axis=0, tiled=True)  37.3 us
    ppermute x12, waiting for transfers between devices, from_others(): lax.ppermute(got[turn], axis, [(at, at ^ bit) for at in range(size)])  35.3 us
    unnamed x34, local copies, waits for them, and re-layouts  18.5 us
    pallas_call x3, Pallas kernels, finish_rows(): pl.pallas_call(functools.partial(finish_kernel, len(powers), whole_width)...  7.47 us
    ppermute x12, starting transfers between devices, from_others(): lax.ppermute(got[turn], axis, [(at, at ^ bit) for at in range(size)])  5.11 us
  transfers between devices with their start and end apart: 14, of which 8 were waited for; matrix products, arithmetic and copies ran while one was open for 0% of the time, Pallas kernels for 16%

profile of v2, /device:TPU:0, one launch (start us, length us, event | category | flops | bytes accessed | tf_op | source)
XLA Modules:
  0.0 210.1 jit_solution(4435339829598005736)
XLA Ops:
  7.2 0.0 all-gather.5.cloned.1.call-start
  7.2 2.0 copy-done.10
  9.3 1.2 copy-done.14
  10.5 0.9 copy-done.15
  11.4 0.1 pack.1
  11.5 0.0 copy-start.16
  11.5 37.3 %all_to_all.5.refs_0_ = bf16[8,32,2432]{2,1,0:T(8,128)(2,1)S(1)} all-to-all(bf16[8,32,2432]{2,1,0:T(8,128)(2,1)S(1)} %pack.1), channel_id=1, replica_groups=mesh['col'=4,'dp'=8] {'dp'}, dimensions={0} | all-to-all | bytes 2490368 | tf_op jit(solution)/shard_map/all_to_all | solution.py:238
  48.8 0.8 fusion
  49.7 0.0 all-gather.5.cloned.1.call-update
  49.7 0.0 all-gather.3.cloned.1.call-start
  49.7 0.7 all-gather.3.cloned.1.call-update
  50.5 1.6 collective-permute-start.1
  52.0 26.1 %collective-permute-done.1.refs_2_ = bf16[8,32,2432]{2,1,0:T(8,128)(2,1)S(1)} collective-permute-done((bf16[8,32,2432]{2,1,0:T(8,128)(2,1)S(1)}, bf16[8,32,2432]{2,1,0:T(8,128)(2,1)S(1)}, u32[]{:S(2)}, u32[]{:S(2)}) %collective-permute-start.1) | collective-permute-done | bytes 1245216 | tf_op jit(solution)/shard_map/ppermute | solution.py:206
  78.1 2.9 %collective-permute-done.2.refs_3_ = bf16[8,32,2432]{2,1,0:T(8,128)(2,1)S(1)} collective-permute-done((bf16[8,32,2432]{2,1,0:T(8,128)(2,1)S(1)}, bf16[8,32,2432]{2,1,0:T(8,128)(2,1)S(1)}, u32[]{:S(2)}, u32[]{:S(2)}) %collective-permute-start.2) | collective-permute-done | bytes 1245216 | tf_op jit(solution)/shard_map/ppermute | solution.py:206
  81.0 1.7 unpack.1
  82.7 0.0 copy-start.6
  82.7 1.8 copy-done.6
  84.6 13.5 %all-gather.5.cloned.1.call-done.x_ref = bf16[1024,1024]{1,0:T(8,128)(2,1)} async-done(((bf16[128,1024]{1,0:T(8,128)(2,1)}), bf16[1024,1024]{1,0:T(8,128)(2,1)}) %all-gather.5.cloned.1.call-update) | async-done | bytes 2097168 | tf_op jit(solution)/shard_map/all_gather | solution.py:242
  98.0 1.6 copy-done.3
  99.6 2.0 copy-done.7
  101.7 14.6 %adam.10 = (f32[1,1792]{1,0:T(1,128)S(1)}, f32[1792,2048]{1,0:T(8,128)}, bf16[1792,2048]{1,0:T(8,128)(2,1)}, bf16[1792,2048]{1,0:T(8,128)(2,1)}) custom-call(bf16[1792,1024]{1,0:T(8,128)(2,1)S(1)} %copy-done.7, bf16[1024,1024]{1,0:T(8,128)(2,1)S(1)} %copy-done.3, bf16[1792,2048]{1,0:T(8,128)(2,1)} %w_ref.11, bf16[1792,2048]{1,0:T(8,128)(2,1)} %m_ref.11, ...), custom_call_target="tpu_custom_call" | custom-call | flops 3758096384 | bytes 31457280 | tf_op jit(solution)/shard_map/adam/pallas_call | solution.py:141
  116.3 32.3 %all-gather.3.cloned.1.call-done.x_ref = bf16[1024,1024]{1,0:T(8,128)(2,1)} async-done(((bf16[128,1024]{1,0:T(8,128)(2,1)}), bf16[1024,1024]{1,0:T(8,128)(2,1)}) %all-gather.3.cloned.1.call-update) | async-done | bytes 2097168 | tf_op jit(solution)/shard_map/all_gather | solution.py:242
  148.5 1.6 copy-done.1
  150.1 2.0 copy-done.8
  152.2 14.5 %adam.11 = (f32[1,1792]{1,0:T(1,128)S(1)}, f32[1792,2048]{1,0:T(8,128)}, bf16[1792,2048]{1,0:T(8,128)(2,1)}, bf16[1792,2048]{1,0:T(8,128)(2,1)}) custom-call(bf16[1792,1024]{1,0:T(8,128)(2,1)S(1)} %copy-done.8, bf16[1024,1024]{1,0:T(8,128)(2,1)S(1)} %copy-done.1, ...), custom_call_target="tpu_custom_call", output_to_operand_aliasing={{0}: (5, {}), {1}: (6, {}), {2}: (7, {}), {3}: (8, {})} | custom-call | flops 3758096384 | bytes 31457280 | tf_op jit(solution)/shard_map/adam/pallas_call | solution.py:141
  166.7 1.4 collective-permute-start.10
  168.1 0.0 collective-permute-start.9
  168.1 5.6 %adam.6 = (f32[1,512]{1,0:T(1,128)S(1)}, f32[512,2048]{1,0:T(8,128)}, bf16[512,2048]{1,0:T(8,128)(2,1)}, bf16[512,2048]{1,0:T(8,128)(2,1)}) custom-call(bf16[512,1024]{1,0:T(8,128)(2,1)S(1)} %get-tuple-element.39.c_ref, bf16[1024,1024]{1,0:T(8,128)(2,1)S(1)} %copy-done.4, bf16[512,2048]{1,0:T(8,128)(2,1)S(1)} %copy-done.9, bf16[512,2048]{1,0:T(8,128)(2,1)} %m_ref.7, ...), custom_call_target="tpu_custom_call" | custom-call | flops 1073741824 | bytes 10485760 | tf_op jit(solution)/shard_map/adam/pallas_call | solution.py:141
  173.7 0.0 copy-start.11
  173.7 0.0 copy-start.12
  173.7 0.0 copy-start.13
  173.7 5.5 %adam.7 = (f32[1,512]{1,0:T(1,128)S(1)}, f32[512,2048]{1,0:T(8,128)}, bf16[512,2048]{1,0:T(8,128)(2,1)}, bf16[512,2048]{1,0:T(8,128)(2,1)}) custom-call(bf16[512,1024]{1,0:T(8,128)(2,1)S(1)} %get-tuple-element.39.c_ref, bf16[1024,1024]{1,0:T(8,128)(2,1)S(1)} %copy-done.2, ...), custom_call_target="tpu_custom_call", output_to_operand_aliasing={{0}: (5, {}), {1}: (6, {}), {2}: (7, {}), {3}: (8, {})} | custom-call | flops 1073741824 | bytes 10485760 | tf_op jit(solution)/shard_map/adam/pallas_call | solution.py:141
  179.3 0.6 collective-permute-start.4
  179.8 0.2 collective-permute-start.3
  180.1 1.5 adam.8
  181.5 1.3 collective-permute-done.4.refs_2_
  182.8 0.0 collective-permute-done.10.refs_2_
  182.8 0.5 collective-permute-start.11
  183.4 1.5 adam.9
  184.8 0.6 collective-permute-start.7
  185.4 3.0 %collective-permute-done.7.refs_2_ = f32[1,128]{1,0:T(1,128)S(1)} collective-permute-done((f32[1,128]{1,0:T(1,128)S(1)}, f32[1,128]{1,0:T(1,128)S(1)}, u32[]{:S(2)}, u32[]{:S(2)}) %collective-permute-start.7) | collective-permute-done | bytes 544 | tf_op jit(solution)/shard_map/ppermute | solution.py:206
  188.4 1.1 collective-permute-done.6.refs_1_
  189.5 0.2 collective-permute-start.8
  189.7 0.9 collective-permute-done.8.refs_3_
  190.6 1.0 finish.4
  191.6 1.6 finish.3
  193.2 5.2 %copy-done = f32[1792,2048]{1,0:T(8,128)S(1)} copy-done((f32[1792,2048]{1,0:T(8,128)S(1)}, f32[1792,2048]{1,0:T(8,128)}, u32[]{:S(2)}) %copy-start) | copy-done | bytes 14680088
  198.4 4.9 %finish.5 = bf16[1792,2048]{1,0:T(8,128)(2,1)} custom-call(f32[1792,2048]{1,0:T(8,128)S(1)} %copy-done, f32[1,1792]{1,0:T(1,128)S(1)} %get-tuple-element.60.refs_0_, f32[1,1792]{1,0:T(1,128)S(1)} %collective-permute-done.9.refs_1_, f32[1,1792]{1,0:T(1,128)S(1)} %collective-permute-done.10.refs_2_, f32[1,1792]{1,0:T(1,128)S(1)} %collective-permute-done.11.refs_3_), custom_call_target="tpu_custom_call" | custom-call | flops 3670016 | bytes 22020096 | tf_op jit(solution)/shard_map/finish/pallas_call | solution.py:186
  (29 shorter events, 0.1 us)
Async XLA Ops:
  7.2 90.9 %all-gather.5.cloned.1.call-start = ((), (), s32[]{:S(2)}) async-start(), calls=%async_computation.2 | async-start | bytes 2359296 | tf_op jit(solution)/shard_map/all_gather | solution.py:242
  7.2 2.0 copy-start.10
  9.3 1.2 copy-start.14
  10.5 0.9 copy-start.15
  11.5 37.3 %copy-start.16 = (bf16[128,2048]{1,0:T(8,128)(2,1)S(1)}, bf16[128,2048]{1,0:T(8,128)(2,1)}, u32[]{:S(2)}) copy-start(bf16[128,2048]{1,0:T(8,128)(2,1)} %param.13) | copy-start | bytes 1572868
  49.7 98.8 %all-gather.3.cloned.1.call-start = ((), (), s32[]{:S(2)}) async-start(), calls=%async_computation.1 | async-start | bytes 2359296 | tf_op jit(solution)/shard_map/all_gather | solution.py:242
  50.5 27.6 %collective-permute-start.1 = (bf16[8,32,2432]{2,1,0:T(8,128)(2,1)S(1)}, bf16[8,32,2432]{2,1,0:T(8,128)(2,1)S(1)}, u32[]{:S(2)}, u32[]{:S(2)}) collective-permute-start(bf16[8,32,2432]{2,1,0:T(8,128)(2,1)S(1)} %all_to_all.5.refs_0_), channel_id=1, source_target_pairs={{0,16},{8,24},{16,0},{24,8},{1,17},{9,25},{17,1},{25,9},{2,18},{10... | collective-permute-start | bytes 3735560 | tf_op jit(solution)/shard_map/ppermute | solution.py:206
  52.0 26.1 %collective-permute-start = (bf16[8,32,2432]{2,1,0:T(8,128)(2,1)S(1)}, bf16[8,32,2432]{2,1,0:T(8,128)(2,1)S(1)}, u32[]{:S(2)}, u32[]{:S(2)}) collective-permute-start(bf16[8,32,2432]{2,1,0:T(8,128)(2,1)S(1)} %all_to_all.5.refs_0_), channel_id=1, source_target_pairs={{0,8},{8,0},{16,24},{24,16},{1,9},{9,1},{17,25},{25,17},{2,10},{10... | collective-permute-start | bytes 3735560 | tf_op jit(solution)/shard_map/ppermute | solution.py:206
  78.1 2.9 %collective-permute-start.2 = (bf16[8,32,2432]{2,1,0:T(8,128)(2,1)S(1)}, bf16[8,32,2432]{2,1,0:T(8,128)(2,1)S(1)}, u32[]{:S(2)}, u32[]{:S(2)}) collective-permute-start(bf16[8,32,2432]{2,1,0:T(8,128)(2,1)S(1)} %collective-permute-done.1.refs_2_), channel_id=1, source_target_pairs={{0,8},{8,0},{16,24},{24,16},{1,9},{9,1},{17,25},{25,17},{2,10},{10... | collective-permute-start | bytes 3735560 | tf_op jit(solution)/shard_map/ppermute | solution.py:206
  82.7 1.8 copy-start.6
  98.0 1.6 copy-start.3
  99.6 2.0 copy-start.7
  148.5 1.6 copy-start.1
  150.1 2.0 copy-start.8
  152.2 16.0 %copy-start.4 = (bf16[1024,1024]{1,0:T(8,128)(2,1)S(1)}, bf16[1024,1024]{1,0:T(8,128)(2,1)}, u32[]{:S(2)}) copy-start(bf16[1024,1024]{1,0:T(8,128)(2,1)} %all-gather.5.cloned.1.call-done.x_ref) | copy-start | bytes 6291460
  152.2 16.0 %copy-start.9 = (bf16[512,2048]{1,0:T(8,128)(2,1)S(1)}, bf16[512,2048]{1,0:T(8,128)(2,1)}, u32[]{:S(2)}) copy-start(bf16[512,2048]{1,0:T(8,128)(2,1)} %w_ref.7) | copy-start | bytes 6291460
  166.7 16.2 %collective-permute-start.10 = (f32[1,1792]{1,0:T(1,128)S(1)}, f32[1,1792]{1,0:T(1,128)S(1)}, u32[]{:S(2)}, u32[]{:S(2)}) collective-permute-start(f32[1,1792]{1,0:T(1,128)S(1)} %get-tuple-element.60.refs_0_), channel_id=1, source_target_pairs={{0,16},{8,24},{16,0},{24,8},{1,17},{9,25},{17,1},{25,9},{2,18},{10... | collective-permute-start | bytes 21512 | tf_op jit(solution)/shard_map/ppermute | solution.py:206
  168.1 25.1 %collective-permute-start.9 = (f32[1,1792]{1,0:T(1,128)S(1)}, f32[1,1792]{1,0:T(1,128)S(1)}, u32[]{:S(2)}, u32[]{:S(2)}) collective-permute-start(f32[1,1792]{1,0:T(1,128)S(1)} %get-tuple-element.60.refs_0_), channel_id=1, source_target_pairs={{0,8},{8,0},{16,24},{24,16},{1,9},{9,1},{17,25},{25,17},{2,10},{10... | collective-permute-start | bytes 21512 | tf_op jit(solution)/shard_map/ppermute | solution.py:206
  168.1 5.6 %copy-start.2 = (bf16[1024,1024]{1,0:T(8,128)(2,1)S(1)}, bf16[1024,1024]{1,0:T(8,128)(2,1)}, u32[]{:S(2)}) copy-start(bf16[1024,1024]{1,0:T(8,128)(2,1)} %all-gather.3.cloned.1.call-done.x_ref) | copy-start | bytes 6291460
  173.7 6.4 %copy-start.11 = (bf16[128,2048]{1,0:T(8,128)(2,1)S(1)}, bf16[128,2048]{1,0:T(8,128)(2,1)}, u32[]{:S(2)}) copy-start(bf16[128,2048]{1,0:T(8,128)(2,1)} %w_ref.9) | copy-start | bytes 1572868
  173.7 6.4 %copy-start.12 = (bf16[128,2048]{1,0:T(8,128)(2,1)S(1)}, bf16[128,2048]{1,0:T(8,128)(2,1)}, u32[]{:S(2)}) copy-start(bf16[128,2048]{1,0:T(8,128)(2,1)} %m_ref.9) | copy-start | bytes 1572868
  173.7 6.4 %copy-start.13 = (bf16[128,2048]{1,0:T(8,128)(2,1)S(1)}, bf16[128,2048]{1,0:T(8,128)(2,1)}, u32[]{:S(2)}) copy-start(bf16[128,2048]{1,0:T(8,128)(2,1)} %v_ref.9) | copy-start | bytes 1572868
  179.3 3.6 %collective-permute-start.4 = (f32[1,512]{1,0:T(1,128)S(1)}, f32[1,512]{1,0:T(1,128)S(1)}, u32[]{:S(2)}, u32[]{:S(2)}) collective-permute-start(f32[1,512]{1,0:T(1,128)S(1)} %get-tuple-element.46.refs_0_), channel_id=1, source_target_pairs={{0,16},{8,24},{16,0},{24,8},{1,17},{9,25},{17,1},{25,9},{2,18},{10... | collective-permute-start | bytes 6152 | tf_op jit(solution)/shard_map/ppermute | solution.py:206
  179.8 11.7 %collective-permute-start.3 = (f32[1,512]{1,0:T(1,128)S(1)}, f32[1,512]{1,0:T(1,128)S(1)}, u32[]{:S(2)}, u32[]{:S(2)}) collective-permute-start(f32[1,512]{1,0:T(1,128)S(1)} %get-tuple-element.46.refs_0_), channel_id=1, source_target_pairs={{0,8},{8,0},{16,24},{24,16},{1,9},{9,1},{17,25},{25,17},{2,10},{10... | collective-permute-start | bytes 6152 | tf_op jit(solution)/shard_map/ppermute | solution.py:206
  182.8 8.7 %collective-permute-start.5 = (f32[1,512]{1,0:T(1,128)S(1)}, f32[1,512]{1,0:T(1,128)S(1)}, u32[]{:S(2)}, u32[]{:S(2)}) collective-permute-start(f32[1,512]{1,0:T(1,128)S(1)} %collective-permute-done.4.refs_2_), channel_id=1, source_target_pairs={{0,8},{8,0},{16,24},{24,16},{1,9},{9,1},{17,25},{25,17},{2,10},{10... | collective-permute-start | bytes 6152 | tf_op jit(solution)/shard_map/ppermute | solution.py:206
  182.8 10.3 %collective-permute-start.11 = (f32[1,1792]{1,0:T(1,128)S(1)}, f32[1,1792]{1,0:T(1,128)S(1)}, u32[]{:S(2)}, u32[]{:S(2)}) collective-permute-start(f32[1,1792]{1,0:T(1,128)S(1)} %collective-permute-done.10.refs_2_), channel_id=1, source_target_pairs={{0,8},{8,0},{16,24},{24,16},{1,9},{9,1},{17,25},{25,17},{2,10},{10... | collective-permute-start | bytes 21512 | tf_op jit(solution)/shard_map/ppermute | solution.py:206
  183.4 8.2 %copy-start.5 = (f32[512,2048]{1,0:T(8,128)S(1)}, f32[512,2048]{1,0:T(8,128)}, u32[]{:S(2)}) copy-start(f32[512,2048]{1,0:T(8,128)} %get-tuple-element.45.step_ref) | copy-start | bytes 12582916
  184.8 3.5 %collective-permute-start.7 = (f32[1,128]{1,0:T(1,128)S(1)}, f32[1,128]{1,0:T(1,128)S(1)}, u32[]{:S(2)}, u32[]{:S(2)}) collective-permute-start(f32[1,128]{1,0:T(1,128)S(1)} %get-tuple-element.53.refs_0_), channel_id=1, source_target_pairs={{0,16},{8,24},{16,0},{24,8},{1,17},{9,25},{17,1},{25,9},{2,18},{10... | collective-permute-start | bytes 1544 | tf_op jit(solution)/shard_map/ppermute | solution.py:206
  188.4 1.1 collective-permute-start.6
  189.5 1.1 collective-permute-start.8
  193.2 5.2 %copy-start = (f32[1792,2048]{1,0:T(8,128)S(1)}, f32[1792,2048]{1,0:T(8,128)}, u32[]{:S(2)}) copy-start(f32[1792,2048]{1,0:T(8,128)} %get-tuple-element.59.step_ref) | copy-start | bytes 44040196
Sparse Core Ops, SparseCore 0:
  49.8 48.1 all-gather.4
  100.7 47.7 all-gather.2

commit v3 on v2

--- a/solution.py
+++ b/solution.py
@@ -25,6 +25,15 @@
     return rows
 
 
+def chunk_plan(totals):
+    first = [(which, 0, total) for which, total in enumerate(totals[:-1])]
+    up = len(totals) - 1
+    block = row_block(totals[up])
+    blocks = totals[up] // block
+    edges = sorted({0, block * (-(-blocks // 2)), totals[up]})
+    return [first] + [[(up, low, high)] for low, high in zip(edges, edges[1:])]
+
+
 def column_chunk(width, count):
     while width % (count * 128):
         count -= 1
@@ -38,20 +47,45 @@
     return width
 
 
-def pack_kernel(groups, *refs):
-    out_ref = refs[-1]
-    low = 0
-    for ref in refs[1:-1]:
+def ring_order(groups):
+    return [*range(0, groups, 2), *range(groups - 1 - groups % 2, 0, -2)]
+
+
+def ring_place(at, groups):
+    return jnp.where(at % 2 == 0, at // 2, groups - 1 - at // 2)
+
+
+def pack_kernel(plan, groups, at_ref, *refs):
+    count = len(plan) * groups
+    inputs, outputs, whole = refs[: -count - 1], refs[-count - 1 : -1], refs[-1]
+    edges = [0]
+    for ref in inputs:
         rows = ref.shape[1] // groups
+        low = edges[-1]
         for group in range(groups):
-            out_ref[group, :, low : low + rows] = ref[:, group * rows : (group + 1) * rows]
-        low += rows
-
-
-def pack(cotangents, groups, part, place):
+            whole[group, :, low : low + rows] = ref[:, group * rows : (group + 1) * rows]
+        edges.append(low + rows)
+    for chunk, pieces in enumerate(plan):
+        for turn in range(groups):
+            to = (at_ref[1] + turn) % groups
+            out_ref = outputs[chunk * groups + turn]
+            start = 0
+            for which, low, high in pieces:
+                out_ref[:, start : start + high - low] = whole[
+                    to, :, edges[which] + low : edges[which] + high
+                ]
+                start += high - low
+
+
+def pack(cotangents, plan, groups, part, place):
     rows = sum(array.shape[1] for array in cotangents) // groups
-    return pl.pallas_call(
-        functools.partial(pack_kernel, groups),
+    outs = [
+        jax.ShapeDtypeStruct((part, sum(high - low for _, low, high in pieces)), jnp.bfloat16)
+        for pieces in plan
+        for _ in range(groups)
+    ]
+    return pl.pallas_call(
+        functools.partial(pack_kernel, plan, groups),
         grid_spec=pltpu.PrefetchScalarGridSpec(
             num_scalar_prefetch=1,
             grid=(1,),
@@ -59,15 +93,86 @@
                 pl.BlockSpec((part, array.shape[1]), lambda i, at: (at[0], 0))
                 for array in cotangents
             ],
-            out_specs=pl.BlockSpec((groups, part, rows), lambda i, at: (0, 0, 0)),
-        ),
-        out_shape=jax.ShapeDtypeStruct((groups, part, rows), jnp.bfloat16),
-        compiler_params=with_vmem(12),
+            out_specs=[pl.BlockSpec(out.shape, lambda i, at: (0, 0)) for out in outs],
+            scratch_shapes=[pltpu.VMEM((groups, part, rows), jnp.bfloat16)],
+        ),
+        out_shape=outs,
+        compiler_params=with_vmem(56),
         cost_estimate=pl.CostEstimate(
             flops=0, bytes_accessed=4 * groups * part * rows, transcendentals=0
         ),
         name="pack",
     )(place, *cotangents)
+
+
+def bundle_kernel(at_ref, *refs):
+    pieces, out_ref = refs[:-1], refs[-1]
+    groups = len(pieces)
+    here = at_ref[1]
+    for turn, piece in enumerate(pieces):
+        source = (here + groups - turn) % groups
+        slot = ring_place(source, groups) - ring_place(here, groups) + groups
+        out_ref[slot % groups] = piece[...]
+
+
+def bundle(pieces, place):
+    part, rows = pieces[0].shape
+    vmem = pl.BlockSpec(memory_space=pltpu.VMEM)
+    return pl.pallas_call(
+        bundle_kernel,
+        in_specs=[pl.BlockSpec(memory_space=pltpu.SMEM)] + [vmem] * len(pieces),
+        out_specs=vmem,
+        out_shape=jax.ShapeDtypeStruct((len(pieces), part, rows), jnp.bfloat16),
+        compiler_params=with_vmem(8),
+        cost_estimate=pl.CostEstimate(
+            flops=0, bytes_accessed=4 * len(pieces) * part * rows, transcendentals=0
+        ),
+        name="bundle",
+    )(place, *pieces)
+
+
+def collect_kernel(*refs):
+    pieces, out_ref = refs[:-1], refs[-1]
+    low = 0
+    for piece in pieces:
+        out_ref[low : low + piece.shape[0]] = piece[...]
+        low += piece.shape[0]
+
+
+def collect(pieces):
+    tokens = sum(piece.shape[0] for piece in pieces)
+    width = pieces[0].shape[1]
+    vmem = pl.BlockSpec(memory_space=pltpu.VMEM)
+    block = column_chunk(width, 4)
+    return pl.pallas_call(
+        collect_kernel,
+        grid=(width // block,),
+        in_specs=[pl.BlockSpec((piece.shape[0], block), lambda i: (0, i)) for piece in pieces],
+        out_specs=pl.BlockSpec((tokens, block), lambda i: (0, i)),
+        out_shape=jax.ShapeDtypeStruct((tokens, width), jnp.bfloat16),
+        compiler_params=with_vmem(48),
+        cost_estimate=pl.CostEstimate(
+            flops=0, bytes_accessed=4 * tokens * width, transcendentals=0
+        ),
+        name="collect",
+    )(*pieces)
+
+
+def gather_ring(array, axis):
+    groups = lax.axis_size(axis)
+    order = ring_order(groups)
+    onward = list(zip(order, order[1:] + order[:1]))
+    back = [(to, at) for at, to in onward]
+    behind, ahead = [array], [array]
+    for _ in range((groups - 1) // 2):
+        behind.append(lax.ppermute(behind[-1], axis, onward))
+        ahead.append(lax.ppermute(ahead[-1], axis, back))
+    middle = []
+    if groups % 2 == 0:
+        half = array.shape[0] // 2
+        middle.append(lax.ppermute(behind[-1][:half], axis, onward))
+        middle.append(lax.ppermute(ahead[-1][half:], axis, back))
+    return collect([array, *ahead[1:], *middle, *behind[:0:-1]])
 
 
 def unpack_kernel(count, at_ref, *refs):
@@ -125,19 +230,15 @@
         for lane in range(0, strip, 128):
             piece = step[:, lane : lane + 128]
             power += piece * piece
-    power = jnp.sum(power.T, axis=0, keepdims=True)
-    if len(refs) > 4:
-        power += refs[0][...]
-    power_ref[...] = power
-
-
-def adam_pass(cotangent, inputs, state, chunk, made):
+    power_ref[...] = jnp.sum(power.T, axis=0, keepdims=True)
+
+
+def adam_pass(cotangent, inputs, state, low, made):
     rows, tokens = cotangent.shape
-    width = inputs.shape[1]
-    whole = state[0].shape[1]
-    block = row_block(rows)
-    tile = pl.BlockSpec((block, width), lambda i: (i, chunk))
-    power = pl.BlockSpec((1, block), lambda i: (0, i))
+    total, width = state[0].shape
+    block = row_block(total)
+    shift = low // block
+    tile = pl.BlockSpec((block, width), lambda i: (i + shift, 0))
     return pl.pallas_call(
         functools.partial(adam_kernel, strip_of(width)),
         grid=(rows // block,),
@@ -148,15 +249,20 @@
             tile,
             tile,
         ]
-        + ([power] + [pl.BlockSpec(memory_space=pl.ANY)] * 3 if made else []),
-        out_specs=[power, tile, tile, tile],
+        + [pl.BlockSpec(memory_space=pl.ANY)] * len(made),
+        out_specs=[
+            pl.BlockSpec((1, block), lambda i: (0, i)),
+            pl.BlockSpec((block, width), lambda i: (i, 0)),
+            tile,
+            tile,
+        ],
         out_shape=[
             jax.ShapeDtypeStruct((1, rows), jnp.float32),
-            jax.ShapeDtypeStruct((rows, whole), jnp.float32),
-            jax.ShapeDtypeStruct((rows, whole), jnp.bfloat16),
-            jax.ShapeDtypeStruct((rows, whole), jnp.bfloat16),
+            jax.ShapeDtypeStruct((rows, width), jnp.float32),
+            jax.ShapeDtypeStruct((total, width), jnp.bfloat16),
+            jax.ShapeDtypeStruct((total, width), jnp.bfloat16),
         ],
-        input_output_aliases={5 + at: at for at in range(len(made))},
+        input_output_aliases={5 + at: 2 + at for at in range(len(made))},
         compiler_params=with_vmem(48),
         cost_estimate=pl.CostEstimate(
             flops=2 * tokens * rows * width,
@@ -179,22 +285,25 @@
         out_ref[:, at] = (step_ref[:, at] * scale).astype(jnp.bfloat16)
 
 
-def finish_rows(step, powers, whole_width):
+def finish_rows(step, powers, whole_width, total, low, made):
     rows, width = step.shape
-    block = row_block(rows)
-    tile = pl.BlockSpec((block, width), lambda i: (i, 0))
+    block = row_block(total)
+    shift = low // block
     return pl.pallas_call(
         functools.partial(finish_kernel, len(powers), whole_width),
         grid=(rows // block,),
-        in_specs=[tile] + [pl.BlockSpec((1, block), lambda i: (0, i))] * len(powers),
-        out_specs=tile,
-        out_shape=jax.ShapeDtypeStruct((rows, width), jnp.bfloat16),
+        in_specs=[pl.BlockSpec((block, width), lambda i: (i, 0))]
+        + [pl.BlockSpec((1, block), lambda i: (0, i))] * len(powers)
+        + [pl.BlockSpec(memory_space=pl.ANY)] * len(made),
+        out_specs=[pl.BlockSpec((block, width), lambda i: (i + shift, 0))],
+        out_shape=[jax.ShapeDtypeStruct((total, width), jnp.bfloat16)],
+        input_output_aliases={1 + len(powers) + at: at for at in range(len(made))},
         compiler_params=with_vmem(24),
         cost_estimate=pl.CostEstimate(
             flops=rows * width, bytes_accessed=6 * rows * width, transcendentals=0
         ),
         name="finish",
-    )(step, *powers)
+    )(step, *powers, *made)
 
 
 def from_others(array, axis):
@@ -206,6 +315,14 @@
             got[turn ^ bit] = lax.ppermute(got[turn], axis, [(at, at ^ bit) for at in range(size)])
         bit //= 2
     return [got[turn] for turn in range(size)]
+
+
+def exchange(arrays, axis):
+    size = lax.axis_size(axis)
+    return [
+        lax.ppermute(array, axis, [(at, (at + turn) % size) for at in range(size)])
+        for turn, array in enumerate(arrays, 1)
+    ]
 
 
 def per_device(
@@ -232,27 +349,29 @@
         (key_weight, moment_key, second_key),
         (up_weight, moment_up, second_up),
     )
-    counts = [state[0].shape[0] for state in states]
-    place = lax.axis_index("col").astype(jnp.int32).reshape(1)
-    packed = pack((query_cotangent, key_cotangent, up_cotangent), groups, part, place)
-    owned = lax.all_to_all(packed, "dp", split_axis=0, concat_axis=0, tiled=True)
-    layer_input, owned = lax.optimization_barrier((layer_input, owned))
-    chunk = column_chunk(layer_input.shape[1], 2)
-    gathered = [
-        lax.all_gather(layer_input[:, low : low + chunk], "dp", axis=0, tiled=True)
-        for low in range(0, layer_input.shape[1], chunk)
-    ]
-    every = unpack(from_others(owned, "col"), counts, place)
-    made = [(), (), ()]
-    for at, inputs in enumerate(gathered):
-        for which in (2, 0, 1):
-            made[which] = adam_pass(every[which], inputs, states[which], at, made[which])
-    updated = [None] * 3
-    for which in (2, 0, 1):
-        updated[which] = finish_rows(
-            made[which][1], from_others(made[which][0], "col"), whole_width
-        )
-    return (*updated, *(done[2] for done in made), *(done[3] for done in made))
+    plan = chunk_plan([state[0].shape[0] for state in states])
+    place = jnp.stack([lax.axis_index("col"), lax.axis_index("dp")]).astype(jnp.int32)
+    packed = pack((query_cotangent, key_cotangent, up_cotangent), plan, groups, part, place)
+    gathered = gather_ring(layer_input, "dp")
+    moments = [[], [], []]
+    updated = [[], [], []]
+    for chunk, pieces in enumerate(plan):
+        sent = packed[chunk * groups : (chunk + 1) * groups]
+        owned = bundle([sent[0], *exchange(sent[1:], "dp")], place)
+        every = unpack(from_others(owned, "col"), [high - low for _, low, high in pieces], place)
+        for (which, low, high), cotangent in zip(pieces, every):
+            power, step, *moments[which] = adam_pass(
+                cotangent, gathered, states[which], low, moments[which]
+            )
+            powers = from_others(power, "col")
+            updated[which] = finish_rows(
+                step, powers, whole_width, states[which][0].shape[0], low, updated[which]
+            )
+    return (
+        *(made[0] for made in updated),
+        *(made[0] for made in moments),
+        *(made[1] for made in moments),
+    )
 
 
 def solution(mesh):

time: 211 us -> 187 us (0.89)
  starting transfers between devices: 5.19 us -> 43.6 us
  blocking collectives: 37.3 us -> 0 us
  between operations: 14.2 us -> 0.92 us
  local copies, waits for them, and re-layouts: 19.3 us -> 7.05 us
  Pallas kernels: 52.3 us -> 63.5 us
  waiting for transfers between devices: 81.8 us -> 70.8 us
    ppermute x0 -> x29, waiting for transfers between devices: none -> 57.6 us  [the longest x21 40.9 us: exchange(): lax.ppermute(array, axis, [(at, (at + turn) % size) for at in range(size)])]
    all_gather x2 -> x0, waiting for transfers between devices: 45.7 us -> none  [per_device(): lax.all_gather(layer_input[:, low:low + chunk], 'dp', axis=0, tiled=True)]
    all_to_all x1 -> x0, blocking collectives: 37.3 us -> none  [per_device(): lax.all_to_all(packed, 'dp', split_axis=0, concat_axis=0, tiled=True)]
    ppermute x0 -> x29, starting transfers between devices: none -> 33.7 us  [the longest x21 25.9 us: exchange(): lax.ppermute(array, axis, [(at, (at + turn) % size) for at in range(size)])]
    ppermute x12 -> x21, waiting for transfers between devices: 35.3 us -> 13.2 us  [from_others(): lax.ppermute(got[turn], axis, [(at, at ^ bit) for at in range(size)])]
    unnamed x34 -> x38, local copies, waits for them, and re-layouts: 18.5 us -> 7.01 us
    pallas_call x1 -> x5, Pallas kernels: 0.09 us -> 7.89 us  [the longest x1 3.19 us: pack(): pl.pallas_call(functools.partial(pack_kernel, plan, groups), grid_spec=pl...]
    ppermute x12 -> x21, starting transfers between devices: 5.11 us -> 9.88 us  [from_others(): lax.ppermute(got[turn], axis, [(at, at ^ bit) for at in range(size)])]
  transfers between devices with their start and end apart: 14 -> 50, of which waited for: 8 -> 23; matrix products, arithmetic and copies ran while one was open for 0% -> 0% of each run, Pallas kernels for 16% -> 29%
where the time goes in v3:
time: 187 us
  waiting for transfers between devices  70.8 us (38%)
  Pallas kernels  63.5 us (34%)
  starting transfers between devices  43.6 us (23%)
  local copies, waits for them, and re-layouts  7.05 us (4%)
    pallas_call x4, Pallas kernels, adam_pass(): pl.pallas_call(functools.partial(adam_kernel, strip_of(width)), grid=(row...  44.4 us
    ppermute x21, waiting for transfers between devices, exchange(): lax.ppermute(array, axis, [(at, (at + turn) % size) for at in range(size)])  40.9 us
    ppermute x21, starting transfers between devices, exchange(): lax.ppermute(array, axis, [(at, (at + turn) % size) for at in range(size)])  25.9 us
    ppermute x21, waiting for transfers between devices, from_others(): lax.ppermute(got[turn], axis, [(at, at ^ bit) for at in range(size)])  13.2 us
    ppermute x3, waiting for transfers between devices, gather_ring(): behind.append(lax.ppermute(behind[-1], axis, onward))  12.1 us
    ppermute x21, starting transfers between devices, from_others(): lax.ppermute(got[turn], axis, [(at, at ^ bit) for at in range(size)])  9.88 us
    pallas_call x4, Pallas kernels, finish_rows(): pl.pallas_call(functools.partial(finish_kernel, len(powers), whole_width)...  7.82 us
    unnamed x38, local copies, waits for them, and re-layouts  7.01 us
  transfers between devices with their start and end apart: 50, of which 23 were waited for; matrix products, arithmetic and copies ran while one was open for 0% of the time, Pallas kernels for 29%

profile of v3, /device:TPU:0, one launch (start us, length us, event | category | flops | bytes accessed | tf_op | source)
XLA Modules:
  0.0 186.5 jit_solution(13423315899141590157)
XLA Ops:
  0.6 3.1 %collective-permute-start.13 = (bf16[128,2048]{1,0:T(8,128)(2,1)}, bf16[128,2048]{1,0:T(8,128)(2,1)S(1)}, u32[]{:S(2)}, u32[]{:S(2)}) collective-permute-start(bf16[128,2048]{1,0:T(8,128)(2,1)} %refs_0_.3), channel_id=1, source_target_pairs={{0,2},{2,4},{4,6},{6,7},{7,5},{5,3},{3,1},{1,0},{8,10},{10,12},{12... | collective-permute-start | bytes 1572872 | tf_op jit(solution)/shard_map/ppermute | solution.py:168
  3.7 12.1 %collective-permute-done.13.refs_8_ = bf16[128,2048]{1,0:T(8,128)(2,1)S(1)} collective-permute-done((bf16[128,2048]{1,0:T(8,128)(2,1)}, bf16[128,2048]{1,0:T(8,128)(2,1)S(1)}, u32[]{:S(2)}, u32[]{:S(2)}) %collective-permute-start.13) | collective-permute-done | bytes 524320 | tf_op jit(solution)/shard_map/ppermute | solution.py:168
  15.8 1.8 collective-permute-start.14
  18.2 3.2 %pack.1 = (bf16[32,640]{1,0:T(8,128)(2,1)}, bf16[32,640]{1,0:T(8,128)(2,1)}, bf16[32,640]{1,0:T(8,128)(2,1)}, bf16[32,640]{1,0:T(8,128)(2,1)}, bf16[32,640]{1,0:...) custom-call(s32[2]{0:T(128)} %pad_add_fusion.at_ref, ...), custom_call_target="tpu_custom_call" | custom-call | bytes 2490368 | tf_op jit(solution)/shard_map/pack/pallas_call | solution.py:87
  21.7 1.7 collective-permute-start.1
  23.5 3.6 %collective-permute-start.2 = (bf16[32,640]{1,0:T(8,128)(2,1)}, bf16[32,640]{1,0:T(8,128)(2,1)S(1)}, u32[]{:S(2)}, u32[]{:S(2)}) collective-permute-start(bf16[32,640]{1,0:T(8,128)(2,1)} %get-tuple-element.54), channel_id=1, source_target_pairs={{0,3},{1,4},{2,5},{3,6},{4,7},{5,0},{6,1},{7,2},{8,11},{9,12},{10,... | collective-permute-start | bytes 122888 | tf_op jit(solution)/shard_map/ppermute | solution.py:323
  27.5 6.2 %collective-permute-done.refs_1_ = bf16[32,640]{1,0:T(8,128)(2,1)S(1)} collective-permute-done((bf16[32,640]{1,0:T(8,128)(2,1)}, bf16[32,640]{1,0:T(8,128)(2,1)S(1)}, u32[]{:S(2)}, u32[]{:S(2)}) %collective-permute-start) | collective-permute-done | bytes 40992 | tf_op jit(solution)/shard_map/ppermute | solution.py:323
  33.7 1.6 collective-permute-done.2.refs_3_
  35.3 2.3 %collective-permute-start.5 = (bf16[32,640]{1,0:T(8,128)(2,1)}, bf16[32,640]{1,0:T(8,128)(2,1)S(1)}, u32[]{:S(2)}, u32[]{:S(2)}) collective-permute-start(bf16[32,640]{1,0:T(8,128)(2,1)} %get-tuple-element.57), channel_id=1, source_target_pairs={{0,6},{1,7},{2,0},{3,1},{4,2},{5,3},{6,4},{7,5},{8,14},{9,15},{10,... | collective-permute-start | bytes 122888 | tf_op jit(solution)/shard_map/ppermute | solution.py:323
  37.6 6.0 %collective-permute-done.3.refs_4_ = bf16[32,640]{1,0:T(8,128)(2,1)S(1)} collective-permute-done((bf16[32,640]{1,0:T(8,128)(2,1)}, bf16[32,640]{1,0:T(8,128)(2,1)S(1)}, u32[]{:S(2)}, u32[]{:S(2)}) %collective-permute-start.3) | collective-permute-done | bytes 40992 | tf_op jit(solution)/shard_map/ppermute | solution.py:323
  43.7 2.9 %collective-permute-start.6 = (bf16[32,640]{1,0:T(8,128)(2,1)}, bf16[32,640]{1,0:T(8,128)(2,1)S(1)}, u32[]{:S(2)}, u32[]{:S(2)}) collective-permute-start(bf16[32,640]{1,0:T(8,128)(2,1)} %get-tuple-element.58), channel_id=1, source_target_pairs={{0,7},{1,0},{2,1},{3,2},{4,3},{5,4},{6,5},{7,6},{8,15},{9,8},{10,9... | collective-permute-start | bytes 122888 | tf_op jit(solution)/shard_map/ppermute | solution.py:323
  46.6 1.9 %collective-permute-done.6.refs_7_ = bf16[32,640]{1,0:T(8,128)(2,1)S(1)} collective-permute-done((bf16[32,640]{1,0:T(8,128)(2,1)}, bf16[32,640]{1,0:T(8,128)(2,1)S(1)}, u32[]{:S(2)}, u32[]{:S(2)}) %collective-permute-start.6) | collective-permute-done | bytes 40992 | tf_op jit(solution)/shard_map/ppermute | solution.py:323
  49.0 4.6 %collective-permute-done.24.refs_1_ = bf16[32,768]{1,0:T(8,128)(2,1)S(1)} collective-permute-done((bf16[32,768]{1,0:T(8,128)(2,1)}, bf16[32,768]{1,0:T(8,128)(2,1)S(1)}, u32[]{:S(2)}, u32[]{:S(2)}) %collective-permute-start.24) | collective-permute-done | bytes 49184 | tf_op jit(solution)/shard_map/ppermute | solution.py:323
  56.9 1.5 collective-permute-start.8
  58.4 1.1 collective-permute-done.27.refs_4_
  59.5 1.3 collective-permute-done.34.refs_1_
  60.8 1.8 collective-permute-start.36
  62.6 3.7 %collective-permute-done.35.refs_2_ = bf16[32,1024]{1,0:T(8,128)(2,1)S(1)} collective-permute-done((bf16[32,1024]{1,0:T(8,128)(2,1)}, bf16[32,1024]{1,0:T(8,128)(2,1)S(1)}, u32[]{:S(2)}, u32[]{:S(2)}) %collective-permute-start.35) | collective-permute-done | bytes 65568 | tf_op jit(solution)/shard_map/ppermute | solution.py:323
  66.3 2.3 %collective-permute-done.36.refs_3_ = bf16[32,1024]{1,0:T(8,128)(2,1)S(1)} collective-permute-done((bf16[32,1024]{1,0:T(8,128)(2,1)}, bf16[32,1024]{1,0:T(8,128)(2,1)S(1)}, u32[]{:S(2)}, u32[]{:S(2)}) %collective-permute-start.36) | collective-permute-done | bytes 65568 | tf_op jit(solution)/shard_map/ppermute | solution.py:323
  68.6 2.4 %collective-permute-start.38 = (bf16[32,1024]{1,0:T(8,128)(2,1)}, bf16[32,1024]{1,0:T(8,128)(2,1)S(1)}, u32[]{:S(2)}, u32[]{:S(2)}) collective-permute-start(bf16[32,1024]{1,0:T(8,128)(2,1)} %get-tuple-element.78), channel_id=1, source_target_pairs={{0,5},{1,6},{2,7},{3,0},{4,1},{5,2},{6,3},{7,4},{8,13},{9,14},{10,... | collective-permute-start | bytes 196616 | tf_op jit(solution)/shard_map/ppermute | solution.py:323
  71.8 2.6 %collective-permute-done.38.refs_5_ = bf16[32,1024]{1,0:T(8,128)(2,1)S(1)} collective-permute-done((bf16[32,1024]{1,0:T(8,128)(2,1)}, bf16[32,1024]{1,0:T(8,128)(2,1)S(1)}, u32[]{:S(2)}, u32[]{:S(2)}) %collective-permute-start.38) | collective-permute-done | bytes 65568 | tf_op jit(solution)/shard_map/ppermute | solution.py:323
  74.3 2.2 %collective-permute-start.40 = (bf16[32,1024]{1,0:T(8,128)(2,1)}, bf16[32,1024]{1,0:T(8,128)(2,1)S(1)}, u32[]{:S(2)}, u32[]{:S(2)}) collective-permute-start(bf16[32,1024]{1,0:T(8,128)(2,1)} %get-tuple-element.80), channel_id=1, source_target_pairs={{0,7},{1,0},{2,1},{3,2},{4,3},{5,4},{6,5},{7,6},{8,15},{9,8},{10,9... | collective-permute-start | bytes 196616 | tf_op jit(solution)/shard_map/ppermute | solution.py:323
  78.2 1.8 collective-permute-done.40.refs_7_
  80.1 2.5 %collective-permute-start.29 = (bf16[32,768]{1,0:T(8,128)(2,1)}, bf16[32,768]{1,0:T(8,128)(2,1)S(1)}, u32[]{:S(2)}, u32[]{:S(2)}) collective-permute-start(bf16[32,768]{1,0:T(8,128)(2,1)} %get-tuple-element.71), channel_id=1, source_target_pairs={{0,6},{1,7},{2,0},{3,1},{4,2},{5,3},{6,4},{7,5},{8,14},{9,15},{10,... | collective-permute-start | bytes 147464 | tf_op jit(solution)/shard_map/ppermute | solution.py:323
  84.1 1.4 collective-permute-start.42
  85.9 4.0 %collective-permute-start.30 = (bf16[32,768]{1,0:T(8,128)(2,1)}, bf16[32,768]{1,0:T(8,128)(2,1)S(1)}, u32[]{:S(2)}, u32[]{:S(2)}) collective-permute-start(bf16[32,768]{1,0:T(8,128)(2,1)} %get-tuple-element.72), channel_id=1, source_target_pairs={{0,7},{1,0},{2,1},{3,2},{4,3},{5,4},{6,5},{7,6},{8,15},{9,8},{10,9... | collective-permute-start | bytes 147464 | tf_op jit(solution)/shard_map/ppermute | solution.py:323
  89.9 5.7 %collective-permute-done.30.refs_7_ = bf16[32,768]{1,0:T(8,128)(2,1)S(1)} collective-permute-done((bf16[32,768]{1,0:T(8,128)(2,1)}, bf16[32,768]{1,0:T(8,128)(2,1)S(1)}, u32[]{:S(2)}, u32[]{:S(2)}) %collective-permute-start.30) | collective-permute-done | bytes 49184 | tf_op jit(solution)/shard_map/ppermute | solution.py:323
  97.9 10.9 %collective-permute-done.32.refs_2_ = bf16[8,32,768]{2,1,0:T(8,128)(2,1)S(1)} collective-permute-done((bf16[8,32,768]{2,1,0:T(8,128)(2,1)S(1)}, bf16[8,32,768]{2,1,0:T(8,128)(2,1)S(1)}, u32[]{:S(2)}, u32[]{:S(2)}) %collective-permute-start.32) | collective-permute-done | bytes 393248 | tf_op jit(solution)/shard_map/ppermute | solution.py:315
  109.3 2.3 %collective-permute-done.12.refs_3_ = bf16[128,2048]{1,0:T(8,128)(2,1)S(1)} collective-permute-done((bf16[128,2048]{1,0:T(8,128)(2,1)S(1)}, bf16[128,2048]{1,0:T(8,128)(2,1)S(1)}, u32[]{:S(2)}, u32[]{:S(2)}) %collective-permute-start.12) | collective-permute-done | bytes 524320 | tf_op jit(solution)/shard_map/ppermute | solution.py:169
  111.8 2.0 %collective-permute-start.17 = (bf16[64,2048]{1,0:T(8,128)(2,1)S(1)}, bf16[64,2048]{1,0:T(8,128)(2,1)S(1)}, u32[]{:S(2)}, u32[]{:S(2)}) collective-permute-start(bf16[64,2048]{1,0:T(8,128)(2,1)S(1)} %slice.9), channel_id=1, source_target_pairs={{2,0},{4,2},{6,4},{7,6},{5,7},{3,5},{1,3},{0,1},{10,8},{12,10},{14... | collective-permute-start | bytes 786440 | tf_op jit(solution)/shard_map/ppermute | solution.py:174
  113.8 1.0 unpack.3
  114.8 1.0 copy-done.4
  115.8 1.1 unpack.4.c_ref
  117.0 1.3 unpack.5.c_ref
  118.2 2.2 %collective-permute-done.16.refs_4_ = bf16[64,2048]{1,0:T(8,128)(2,1)S(1)} collective-permute-done((bf16[64,2048]{1,0:T(8,128)(2,1)S(1)}, bf16[64,2048]{1,0:T(8,128)(2,1)S(1)}, u32[]{:S(2)}, u32[]{:S(2)}) %collective-permute-start.16) | collective-permute-done | bytes 262176 | tf_op jit(solution)/shard_map/ppermute | solution.py:173
  120.5 2.7 %collect.1.x_ref = bf16[1024,2048]{1,0:T(8,128)(2,1)} custom-call(bf16[128,2048]{1,0:T(8,128)(2,1)S(1)} %copy-done.6, bf16[128,2048]{1,0:T(8,128)(2,1)S(1)} %collective-permute-done.10.refs_1_, bf16[128,2048]{1,0:T(8,128)(2,1)S(1)} %collective-permute-done.11.refs_2_, bf16[128,2048]{1,0:T(8,128)(2,1)S(1)} %collective-permute-done.12.refs_3_, ...), custom_call_target="tpu_custom_call" | custom-call | bytes 8388608 | tf_op jit(solution)/shard_map/collect/pallas_call | solution.py:147
  123.2 4.4 %adam.5 = (f32[1,128]{1,0:T(1,128)S(1)}, f32[128,2048]{1,0:T(8,128)S(1)}, bf16[128,2048]{1,0:T(8,128)(2,1)}, bf16[128,2048]{1,0:T(8,128)(2,1)}) custom-call(bf16[128,1024]{1,0:T(8,128)(2,1)S(1)} %get-tuple-element.62.c_ref, bf16[1024,2048]{1,0:T(8,128)(2,1)} %collect.1.x_ref, bf16[128,2048]{1,0:T(8,128)(2,1)S(1)} %copy-done.7, ...), custom_call_target="tpu_custom_call" | custom-call | flops 536870912 | bytes 8126464 | tf_op jit(solution)/shard_map/adam/pallas_call | solution.py:242
  127.7 1.7 collective-permute-start.22
  129.3 17.2 %adam.6 = (f32[1,1024]{1,0:T(1,128)S(1)}, f32[1024,2048]{1,0:T(8,128)}, bf16[1792,2048]{1,0:T(8,128)(2,1)}, bf16[1792,2048]{1,0:T(8,128)(2,1)}) custom-call(bf16[1024,1024]{1,0:T(8,128)(2,1)S(1)} %unpack.5.c_ref, bf16[1024,2048]{1,0:T(8,128)(2,1)} %collect.1.x_ref, bf16[1792,2048]{1,0:T(8,128)(2,1)} %w_ref.7, bf16[1792,2048]{1,0:T(8,128)(2,1)} %m_ref.7, ...), custom_call_target="tpu_custom_call" | custom-call | flops 4294967296 | bytes 35651584 | tf_op jit(solution)/shard_map/adam/pallas_call | solution.py:242
  147.0 12.6 %adam.7 = (f32[1,768]{1,0:T(1,128)S(1)}, f32[768,2048]{1,0:T(8,128)}, bf16[1792,2048]{1,0:T(8,128)(2,1)}, bf16[1792,2048]{1,0:T(8,128)(2,1)}) custom-call(bf16[768,1024]{1,0:T(8,128)(2,1)S(1)} %unpack.4.c_ref, bf16[1024,2048]{1,0:T(8,128)(2,1)S(1)} %copy-done, bf16[1792,2048]{1,0:T(8,128)(2,1)} %w_ref.7, ...), custom_call_target="tpu_custom_call", output_to_operand_aliasing={{2}: (5, {}), {3}: (6, {})} | custom-call | flops 3221225472 | bytes 27787264 | tf_op jit(solution)/shard_map/adam/pallas_call | solution.py:242
  159.6 1.7 collective-permute-start.45
  161.2 10.2 %adam.4 = (f32[1,512]{1,0:T(1,128)S(1)}, f32[512,2048]{1,0:T(8,128)}, bf16[512,2048]{1,0:T(8,128)(2,1)}, bf16[512,2048]{1,0:T(8,128)(2,1)}) custom-call(bf16[512,1024]{1,0:T(8,128)(2,1)S(1)} %copy-done.5, bf16[1024,2048]{1,0:T(8,128)(2,1)} %collect.1.x_ref, bf16[512,2048]{1,0:T(8,128)(2,1)S(1)} %copy-done.2, bf16[512,2048]{1,0:T(8,128)(2,1)S(1)} %copy-done.3, ...), custom_call_target="tpu_custom_call" | custom-call | flops 2147483648 | bytes 19922944 | tf_op jit(solution)/shard_map/adam/pallas_call | solution.py:242
  173.4 1.6 collective-permute-done.19.refs_2_
  175.6 1.0 finish.5
  176.7 2.2 %copy-done.1 = f32[512,2048]{1,0:T(8,128)S(1)} copy-done((f32[512,2048]{1,0:T(8,128)S(1)}, f32[512,2048]{1,0:T(8,128)}, u32[]{:S(2)}) %copy-start.1) | copy-done | bytes 4194328
  178.9 1.6 finish.4
  180.5 2.8 %finish.6.refs_4_ = bf16[1792,2048]{1,0:T(8,128)(2,1)} custom-call(f32[1024,2048]{1,0:T(8,128)S(1)} %bitcast.3, f32[1,1024]{1,0:T(1,128)S(1)} %get-tuple-element.86.refs_0_, f32[1,1024]{1,0:T(1,128)S(1)} %collective-permute-done.47.refs_1_, f32[1,1024]{1,0:T(1,128)S(1)} %collective-permute-done.48.refs_2_, f32[1,1024]{1,0:T(1,128)S(1)} %collective-permute-done.49.refs_3_), custom_call_target="tpu_custom_call" | custom-call | flops 2097152 | bytes 12582912 | tf_op jit(solution)/shard_map/finish/pallas_call | solution.py:292
  184.1 2.5 %finish.7 = bf16[1792,2048]{1,0:T(8,128)(2,1)} custom-call(f32[768,2048]{1,0:T(8,128)S(1)} %bitcast.5, f32[1,768]{1,0:T(1,128)S(1)} %get-tuple-element.84.refs_0_, f32[1,768]{1,0:T(1,128)S(1)} %collective-permute-done.44.refs_1_, f32[1,768]{1,0:T(1,128)S(1)} %collective-permute-done.45.refs_2_, ...), custom_call_target="tpu_custom_call", output_to_operand_aliasing={{}: (5, {})} | custom-call | flops 1572864 | bytes 9437184 | tf_op jit(solution)/shard_map/finish/pallas_call | solution.py:292
  (111 shorter events, 16.4 us)
Async XLA Ops:
  0.6 15.2 %collective-permute-start.13 = (bf16[128,2048]{1,0:T(8,128)(2,1)}, bf16[128,2048]{1,0:T(8,128)(2,1)S(1)}, u32[]{:S(2)}, u32[]{:S(2)}) collective-permute-start(bf16[128,2048]{1,0:T(8,128)(2,1)} %refs_0_.3), channel_id=1, source_target_pairs={{0,2},{2,4},{4,6},{6,7},{7,5},{5,3},{3,1},{1,0},{8,10},{10,12},{12... | collective-permute-start | bytes 1572872 | tf_op jit(solution)/shard_map/ppermute | solution.py:168
  3.7 23.4 %collective-permute-start.10 = (bf16[128,2048]{1,0:T(8,128)(2,1)}, bf16[128,2048]{1,0:T(8,128)(2,1)S(1)}, u32[]{:S(2)}, u32[]{:S(2)}) collective-permute-start(bf16[128,2048]{1,0:T(8,128)(2,1)} %refs_0_.3), channel_id=1, source_target_pairs={{2,0},{4,2},{6,4},{7,6},{5,7},{3,5},{1,3},{0,1},{10,8},{12,10},{14... | collective-permute-start | bytes 1572872 | tf_op jit(solution)/shard_map/ppermute | solution.py:169
  15.8 69.6 %collective-permute-start.14 = (bf16[128,2048]{1,0:T(8,128)(2,1)S(1)}, bf16[128,2048]{1,0:T(8,128)(2,1)S(1)}, u32[]{:S(2)}, u32[]{:S(2)}) collective-permute-start(bf16[128,2048]{1,0:T(8,128)(2,1)S(1)} %collective-permute-done.13.refs_8_), channel_id=1, source_target_pairs={{0,2},{2,4},{4,6},{6,7},{7,5},{5,3},{3,1},{1,0},{8,10},{10,12},{12... | collective-permute-start | bytes 1572872 | tf_op jit(solution)/shard_map/ppermute | solution.py:168
  21.4 12.3 %collective-permute-start = (bf16[32,640]{1,0:T(8,128)(2,1)}, bf16[32,640]{1,0:T(8,128)(2,1)S(1)}, u32[]{:S(2)}, u32[]{:S(2)}) collective-permute-start(bf16[32,640]{1,0:T(8,128)(2,1)} %get-tuple-element.52), channel_id=1, source_target_pairs={{0,1},{1,2},{2,3},{3,4},{4,5},{5,6},{6,7},{7,0},{8,9},{9,10},{10,1... | collective-permute-start | bytes 122888 | tf_op jit(solution)/shard_map/ppermute | solution.py:323
  21.7 12.0 %collective-permute-start.1 = (bf16[32,640]{1,0:T(8,128)(2,1)}, bf16[32,640]{1,0:T(8,128)(2,1)S(1)}, u32[]{:S(2)}, u32[]{:S(2)}) collective-permute-start(bf16[32,640]{1,0:T(8,128)(2,1)} %get-tuple-element.53), channel_id=1, source_target_pairs={{0,2},{1,3},{2,4},{3,5},{4,6},{5,7},{6,0},{7,1},{8,10},{9,11},{10,... | collective-permute-start | bytes 122888 | tf_op jit(solution)/shard_map/ppermute | solution.py:323
  23.5 11.8 %collective-permute-start.2 = (bf16[32,640]{1,0:T(8,128)(2,1)}, bf16[32,640]{1,0:T(8,128)(2,1)S(1)}, u32[]{:S(2)}, u32[]{:S(2)}) collective-permute-start(bf16[32,640]{1,0:T(8,128)(2,1)} %get-tuple-element.54), channel_id=1, source_target_pairs={{0,3},{1,4},{2,5},{3,6},{4,7},{5,0},{6,1},{7,2},{8,11},{9,12},{10,... | collective-permute-start | bytes 122888 | tf_op jit(solution)/shard_map/ppermute | solution.py:323
  27.1 70.5 %collective-permute-start.11 = (bf16[128,2048]{1,0:T(8,128)(2,1)S(1)}, bf16[128,2048]{1,0:T(8,128)(2,1)S(1)}, u32[]{:S(2)}, u32[]{:S(2)}) collective-permute-start(bf16[128,2048]{1,0:T(8,128)(2,1)S(1)} %collective-permute-done.10.refs_1_), channel_id=1, source_target_pairs={{2,0},{4,2},{6,4},{7,6},{5,7},{3,5},{1,3},{0,1},{10,8},{12,10},{14... | collective-permute-start | bytes 1572872 | tf_op jit(solution)/shard_map/ppermute | solution.py:169
  33.7 9.9 %collective-permute-start.3 = (bf16[32,640]{1,0:T(8,128)(2,1)}, bf16[32,640]{1,0:T(8,128)(2,1)S(1)}, u32[]{:S(2)}, u32[]{:S(2)}) collective-permute-start(bf16[32,640]{1,0:T(8,128)(2,1)} %get-tuple-element.55), channel_id=1, source_target_pairs={{0,4},{1,5},{2,6},{3,7},{4,0},{5,1},{6,2},{7,3},{8,12},{9,13},{10,... | collective-permute-start | bytes 122888 | tf_op jit(solution)/shard_map/ppermute | solution.py:323
  33.7 12.8 %collective-permute-start.4 = (bf16[32,640]{1,0:T(8,128)(2,1)}, bf16[32,640]{1,0:T(8,128)(2,1)S(1)}, u32[]{:S(2)}, u32[]{:S(2)}) collective-permute-start(bf16[32,640]{1,0:T(8,128)(2,1)} %get-tuple-element.56), channel_id=1, source_target_pairs={{0,5},{1,6},{2,7},{3,0},{4,1},{5,2},{6,3},{7,4},{8,13},{9,14},{10,... | collective-permute-start | bytes 122888 | tf_op jit(solution)/shard_map/ppermute | solution.py:323
  35.3 11.2 %collective-permute-start.5 = (bf16[32,640]{1,0:T(8,128)(2,1)}, bf16[32,640]{1,0:T(8,128)(2,1)S(1)}, u32[]{:S(2)}, u32[]{:S(2)}) collective-permute-start(bf16[32,640]{1,0:T(8,128)(2,1)} %get-tuple-element.57), channel_id=1, source_target_pairs={{0,6},{1,7},{2,0},{3,1},{4,2},{5,3},{6,4},{7,5},{8,14},{9,15},{10,... | collective-permute-start | bytes 122888 | tf_op jit(solution)/shard_map/ppermute | solution.py:323
  43.7 4.9 %collective-permute-start.6 = (bf16[32,640]{1,0:T(8,128)(2,1)}, bf16[32,640]{1,0:T(8,128)(2,1)S(1)}, u32[]{:S(2)}, u32[]{:S(2)}) collective-permute-start(bf16[32,640]{1,0:T(8,128)(2,1)} %get-tuple-element.58), channel_id=1, source_target_pairs={{0,7},{1,0},{2,1},{3,2},{4,3},{5,4},{6,5},{7,6},{8,15},{9,8},{10,9... | collective-permute-start | bytes 122888 | tf_op jit(solution)/shard_map/ppermute | solution.py:323
  46.5 7.0 %collective-permute-start.24 = (bf16[32,768]{1,0:T(8,128)(2,1)}, bf16[32,768]{1,0:T(8,128)(2,1)S(1)}, u32[]{:S(2)}, u32[]{:S(2)}) collective-permute-start(bf16[32,768]{1,0:T(8,128)(2,1)} %get-tuple-element.66), channel_id=1, source_target_pairs={{0,1},{1,2},{2,3},{3,4},{4,5},{5,6},{6,7},{7,0},{8,9},{9,10},{10,1... | collective-permute-start | bytes 147464 | tf_op jit(solution)/shard_map/ppermute | solution.py:323
  46.5 7.0 %collective-permute-start.25 = (bf16[32,768]{1,0:T(8,128)(2,1)}, bf16[32,768]{1,0:T(8,128)(2,1)S(1)}, u32[]{:S(2)}, u32[]{:S(2)}) collective-permute-start(bf16[32,768]{1,0:T(8,128)(2,1)} %get-tuple-element.67), channel_id=1, source_target_pairs={{0,2},{1,3},{2,4},{3,5},{4,6},{5,7},{6,0},{7,1},{8,10},{9,11},{10,... | collective-permute-start | bytes 147464 | tf_op jit(solution)/shard_map/ppermute | solution.py:323
  48.5 8.3 %collective-permute-start.26 = (bf16[32,768]{1,0:T(8,128)(2,1)}, bf16[32,768]{1,0:T(8,128)(2,1)S(1)}, u32[]{:S(2)}, u32[]{:S(2)}) collective-permute-start(bf16[32,768]{1,0:T(8,128)(2,1)} %get-tuple-element.68), channel_id=1, source_target_pairs={{0,3},{1,4},{2,5},{3,6},{4,7},{5,0},{6,1},{7,2},{8,11},{9,12},{10,... | collective-permute-start | bytes 147464 | tf_op jit(solution)/shard_map/ppermute | solution.py:323
  53.6 7.2 %collective-permute-start.34 = (bf16[32,1024]{1,0:T(8,128)(2,1)}, bf16[32,1024]{1,0:T(8,128)(2,1)S(1)}, u32[]{:S(2)}, u32[]{:S(2)}) collective-permute-start(bf16[32,1024]{1,0:T(8,128)(2,1)} %get-tuple-element.74), channel_id=1, source_target_pairs={{0,1},{1,2},{2,3},{3,4},{4,5},{5,6},{6,7},{7,0},{8,9},{9,10},{10,1... | collective-permute-start | bytes 196616 | tf_op jit(solution)/shard_map/ppermute | solution.py:323
  53.6 5.9 %collective-permute-start.27 = (bf16[32,768]{1,0:T(8,128)(2,1)}, bf16[32,768]{1,0:T(8,128)(2,1)S(1)}, u32[]{:S(2)}, u32[]{:S(2)}) collective-permute-start(bf16[32,768]{1,0:T(8,128)(2,1)} %get-tuple-element.69), channel_id=1, source_target_pairs={{0,4},{1,5},{2,6},{3,7},{4,0},{5,1},{6,2},{7,3},{8,12},{9,13},{10,... | collective-permute-start | bytes 147464 | tf_op jit(solution)/shard_map/ppermute | solution.py:323
  56.9 40.3 %collective-permute-start.8 = (bf16[8,32,640]{2,1,0:T(8,128)(2,1)S(1)}, bf16[8,32,640]{2,1,0:T(8,128)(2,1)S(1)}, u32[]{:S(2)}, u32[]{:S(2)}) collective-permute-start(bf16[8,32,640]{2,1,0:T(8,128)(2,1)S(1)} %bundle.3.refs_0_), channel_id=1, source_target_pairs={{0,16},{8,24},{16,0},{24,8},{1,17},{9,25},{17,1},{25,9},{2,18},{10... | collective-permute-start | bytes 983048 | tf_op jit(solution)/shard_map/ppermute | solution.py:315
  59.5 6.8 %collective-permute-start.35 = (bf16[32,1024]{1,0:T(8,128)(2,1)}, bf16[32,1024]{1,0:T(8,128)(2,1)S(1)}, u32[]{:S(2)}, u32[]{:S(2)}) collective-permute-start(bf16[32,1024]{1,0:T(8,128)(2,1)} %get-tuple-element.75), channel_id=1, source_target_pairs={{0,2},{1,3},{2,4},{3,5},{4,6},{5,7},{6,0},{7,1},{8,10},{9,11},{10,... | collective-permute-start | bytes 196616 | tf_op jit(solution)/shard_map/ppermute | solution.py:323
  60.8 7.8 %collective-permute-start.36 = (bf16[32,1024]{1,0:T(8,128)(2,1)}, bf16[32,1024]{1,0:T(8,128)(2,1)S(1)}, u32[]{:S(2)}, u32[]{:S(2)}) collective-permute-start(bf16[32,1024]{1,0:T(8,128)(2,1)} %get-tuple-element.76), channel_id=1, source_target_pairs={{0,3},{1,4},{2,5},{3,6},{4,7},{5,0},{6,1},{7,2},{8,11},{9,12},{10,... | collective-permute-start | bytes 196616 | tf_op jit(solution)/shard_map/ppermute | solution.py:323
  66.3 5.5 %collective-permute-start.37 = (bf16[32,1024]{1,0:T(8,128)(2,1)}, bf16[32,1024]{1,0:T(8,128)(2,1)S(1)}, u32[]{:S(2)}, u32[]{:S(2)}) collective-permute-start(bf16[32,1024]{1,0:T(8,128)(2,1)} %get-tuple-element.77), channel_id=1, source_target_pairs={{0,4},{1,5},{2,6},{3,7},{4,0},{5,1},{6,2},{7,3},{8,12},{9,13},{10,... | collective-permute-start | bytes 196616 | tf_op jit(solution)/shard_map/ppermute | solution.py:323
  68.6 5.7 %collective-permute-start.38 = (bf16[32,1024]{1,0:T(8,128)(2,1)}, bf16[32,1024]{1,0:T(8,128)(2,1)S(1)}, u32[]{:S(2)}, u32[]{:S(2)}) collective-permute-start(bf16[32,1024]{1,0:T(8,128)(2,1)} %get-tuple-element.78), channel_id=1, source_target_pairs={{0,5},{1,6},{2,7},{3,0},{4,1},{5,2},{6,3},{7,4},{8,13},{9,14},{10,... | collective-permute-start | bytes 196616 | tf_op jit(solution)/shard_map/ppermute | solution.py:323
  71.8 5.5 %collective-permute-start.39 = (bf16[32,1024]{1,0:T(8,128)(2,1)}, bf16[32,1024]{1,0:T(8,128)(2,1)S(1)}, u32[]{:S(2)}, u32[]{:S(2)}) collective-permute-start(bf16[32,1024]{1,0:T(8,128)(2,1)} %get-tuple-element.79), channel_id=1, source_target_pairs={{0,6},{1,7},{2,0},{3,1},{4,2},{5,3},{6,4},{7,5},{8,14},{9,15},{10,... | collective-permute-start | bytes 196616 | tf_op jit(solution)/shard_map/ppermute | solution.py:323
  74.3 5.7 %collective-permute-start.40 = (bf16[32,1024]{1,0:T(8,128)(2,1)}, bf16[32,1024]{1,0:T(8,128)(2,1)S(1)}, u32[]{:S(2)}, u32[]{:S(2)}) collective-permute-start(bf16[32,1024]{1,0:T(8,128)(2,1)} %get-tuple-element.80), channel_id=1, source_target_pairs={{0,7},{1,0},{2,1},{3,2},{4,3},{5,4},{6,5},{7,6},{8,15},{9,8},{10,9... | collective-permute-start | bytes 196616 | tf_op jit(solution)/shard_map/ppermute | solution.py:323
  77.3 6.8 %collective-permute-start.28 = (bf16[32,768]{1,0:T(8,128)(2,1)}, bf16[32,768]{1,0:T(8,128)(2,1)S(1)}, u32[]{:S(2)}, u32[]{:S(2)}) collective-permute-start(bf16[32,768]{1,0:T(8,128)(2,1)} %get-tuple-element.70), channel_id=1, source_target_pairs={{0,5},{1,6},{2,7},{3,0},{4,1},{5,2},{6,3},{7,4},{8,13},{9,14},{10,... | collective-permute-start | bytes 147464 | tf_op jit(solution)/shard_map/ppermute | solution.py:323
  80.1 5.8 %collective-permute-start.29 = (bf16[32,768]{1,0:T(8,128)(2,1)}, bf16[32,768]{1,0:T(8,128)(2,1)S(1)}, u32[]{:S(2)}, u32[]{:S(2)}) collective-permute-start(bf16[32,768]{1,0:T(8,128)(2,1)} %get-tuple-element.71), channel_id=1, source_target_pairs={{0,6},{1,7},{2,0},{3,1},{4,2},{5,3},{6,4},{7,5},{8,14},{9,15},{10,... | collective-permute-start | bytes 147464 | tf_op jit(solution)/shard_map/ppermute | solution.py:323
  84.1 24.7 %collective-permute-start.42 = (bf16[8,32,1024]{2,1,0:T(8,128)(2,1)S(1)}, bf16[8,32,1024]{2,1,0:T(8,128)(2,1)S(1)}, u32[]{:S(2)}, u32[]{:S(2)}) collective-permute-start(bf16[8,32,1024]{2,1,0:T(8,128)(2,1)S(1)} %bundle.5.refs_0_), channel_id=1, source_target_pairs={{0,16},{8,24},{16,0},{24,8},{1,17},{9,25},{17,1},{25,9},{2,18},{10... | collective-permute-start | bytes 1572872 | tf_op jit(solution)/shard_map/ppermute | solution.py:315
  85.4 23.8 %collective-permute-start.15 = (bf16[128,2048]{1,0:T(8,128)(2,1)S(1)}, bf16[128,2048]{1,0:T(8,128)(2,1)S(1)}, u32[]{:S(2)}, u32[]{:S(2)}) collective-permute-start(bf16[128,2048]{1,0:T(8,128)(2,1)S(1)} %collective-permute-done.14.refs_7_), channel_id=1, source_target_pairs={{0,2},{2,4},{4,6},{6,7},{7,5},{5,3},{3,1},{1,0},{8,10},{10,12},{12... | collective-permute-start | bytes 1572872 | tf_op jit(solution)/shard_map/ppermute | solution.py:168
  85.9 9.8 %collective-permute-start.30 = (bf16[32,768]{1,0:T(8,128)(2,1)}, bf16[32,768]{1,0:T(8,128)(2,1)S(1)}, u32[]{:S(2)}, u32[]{:S(2)}) collective-permute-start(bf16[32,768]{1,0:T(8,128)(2,1)} %get-tuple-element.72), channel_id=1, source_target_pairs={{0,7},{1,0},{2,1},{3,2},{4,3},{5,4},{6,5},{7,6},{8,15},{9,8},{10,9... | collective-permute-start | bytes 147464 | tf_op jit(solution)/shard_map/ppermute | solution.py:323
  95.7 1.9 %collective-permute-start.7 = (bf16[8,32,640]{2,1,0:T(8,128)(2,1)S(1)}, bf16[8,32,640]{2,1,0:T(8,128)(2,1)S(1)}, u32[]{:S(2)}, u32[]{:S(2)}) collective-permute-start(bf16[8,32,640]{2,1,0:T(8,128)(2,1)S(1)} %bundle.3.refs_0_), channel_id=1, source_target_pairs={{0,8},{8,0},{16,24},{24,16},{1,9},{9,1},{17,25},{25,17},{2,10},{10... | collective-permute-start | bytes 983048 | tf_op jit(solution)/shard_map/ppermute | solution.py:315
  97.1 11.6 %collective-permute-start.32 = (bf16[8,32,768]{2,1,0:T(8,128)(2,1)S(1)}, bf16[8,32,768]{2,1,0:T(8,128)(2,1)S(1)}, u32[]{:S(2)}, u32[]{:S(2)}) collective-permute-start(bf16[8,32,768]{2,1,0:T(8,128)(2,1)S(1)} %bundle.4.refs_0_), channel_id=1, source_target_pairs={{0,16},{8,24},{16,0},{24,8},{1,17},{9,25},{17,1},{25,9},{2,18},{10... | collective-permute-start | bytes 1179656 | tf_op jit(solution)/shard_map/ppermute | solution.py:315
  97.6 14.1 %collective-permute-start.12 = (bf16[128,2048]{1,0:T(8,128)(2,1)S(1)}, bf16[128,2048]{1,0:T(8,128)(2,1)S(1)}, u32[]{:S(2)}, u32[]{:S(2)}) collective-permute-start(bf16[128,2048]{1,0:T(8,128)(2,1)S(1)} %collective-permute-done.11.refs_2_), channel_id=1, source_target_pairs={{2,0},{4,2},{6,4},{7,6},{5,7},{3,5},{1,3},{0,1},{10,8},{12,10},{14... | collective-permute-start | bytes 1572872 | tf_op jit(solution)/shard_map/ppermute | solution.py:169
  97.6 14.1 %collective-permute-start.31 = (bf16[8,32,768]{2,1,0:T(8,128)(2,1)S(1)}, bf16[8,32,768]{2,1,0:T(8,128)(2,1)S(1)}, u32[]{:S(2)}, u32[]{:S(2)}) collective-permute-start(bf16[8,32,768]{2,1,0:T(8,128)(2,1)S(1)} %bundle.4.refs_0_), channel_id=1, source_target_pairs={{0,8},{8,0},{16,24},{24,16},{1,9},{9,1},{17,25},{25,17},{2,10},{10... | collective-permute-start | bytes 1179656 | tf_op jit(solution)/shard_map/ppermute | solution.py:315
  108.7 3.0 %collective-permute-start.9 = (bf16[8,32,640]{2,1,0:T(8,128)(2,1)S(1)}, bf16[8,32,640]{2,1,0:T(8,128)(2,1)S(1)}, u32[]{:S(2)}, u32[]{:S(2)}) collective-permute-start(bf16[8,32,640]{2,1,0:T(8,128)(2,1)S(1)} %collective-permute-done.8.refs_2_), channel_id=1, source_target_pairs={{0,8},{8,0},{16,24},{24,16},{1,9},{9,1},{17,25},{25,17},{2,10},{10... | collective-permute-start | bytes 983048 | tf_op jit(solution)/shard_map/ppermute | solution.py:315
  108.7 8.2 %collective-permute-start.41 = (bf16[8,32,1024]{2,1,0:T(8,128)(2,1)S(1)}, bf16[8,32,1024]{2,1,0:T(8,128)(2,1)S(1)}, u32[]{:S(2)}, u32[]{:S(2)}) collective-permute-start(bf16[8,32,1024]{2,1,0:T(8,128)(2,1)S(1)} %bundle.5.refs_0_), channel_id=1, source_target_pairs={{0,8},{8,0},{16,24},{24,16},{1,9},{9,1},{17,25},{25,17},{2,10},{10... | collective-permute-start | bytes 1572872 | tf_op jit(solution)/shard_map/ppermute | solution.py:315
  109.3 7.7 %collective-permute-start.43 = (bf16[8,32,1024]{2,1,0:T(8,128)(2,1)S(1)}, bf16[8,32,1024]{2,1,0:T(8,128)(2,1)S(1)}, u32[]{:S(2)}, u32[]{:S(2)}) collective-permute-start(bf16[8,32,1024]{2,1,0:T(8,128)(2,1)S(1)} %collective-permute-done.42.refs_2_), channel_id=1, source_target_pairs={{0,8},{8,0},{16,24},{24,16},{1,9},{9,1},{17,25},{25,17},{2,10},{10... | collective-permute-start | bytes 1572872 | tf_op jit(solution)/shard_map/ppermute | solution.py:315
  111.6 4.2 %collective-permute-start.33 = (bf16[8,32,768]{2,1,0:T(8,128)(2,1)S(1)}, bf16[8,32,768]{2,1,0:T(8,128)(2,1)S(1)}, u32[]{:S(2)}, u32[]{:S(2)}) collective-permute-start(bf16[8,32,768]{2,1,0:T(8,128)(2,1)S(1)} %collective-permute-done.32.refs_2_), channel_id=1, source_target_pairs={{0,8},{8,0},{16,24},{24,16},{1,9},{9,1},{17,25},{25,17},{2,10},{10... | collective-permute-start | bytes 1179656 | tf_op jit(solution)/shard_map/ppermute | solution.py:315
  111.7 8.8 %collective-permute-start.16 = (bf16[64,2048]{1,0:T(8,128)(2,1)S(1)}, bf16[64,2048]{1,0:T(8,128)(2,1)S(1)}, u32[]{:S(2)}, u32[]{:S(2)}) collective-permute-start(bf16[64,2048]{1,0:T(8,128)(2,1)S(1)} %slice.8), channel_id=1, source_target_pairs={{0,2},{2,4},{4,6},{6,7},{7,5},{5,3},{3,1},{1,0},{8,10},{10,12},{12... | collective-permute-start | bytes 786440 | tf_op jit(solution)/shard_map/ppermute | solution.py:173
  111.8 8.8 %collective-permute-start.17 = (bf16[64,2048]{1,0:T(8,128)(2,1)S(1)}, bf16[64,2048]{1,0:T(8,128)(2,1)S(1)}, u32[]{:S(2)}, u32[]{:S(2)}) collective-permute-start(bf16[64,2048]{1,0:T(8,128)(2,1)S(1)} %slice.9), channel_id=1, source_target_pairs={{2,0},{4,2},{6,4},{7,6},{5,7},{3,5},{1,3},{0,1},{10,8},{12,10},{14... | collective-permute-start | bytes 786440 | tf_op jit(solution)/shard_map/ppermute | solution.py:174
  127.7 44.1 %collective-permute-start.22 = (f32[1,128]{1,0:T(1,128)S(1)}, f32[1,128]{1,0:T(1,128)S(1)}, u32[]{:S(2)}, u32[]{:S(2)}) collective-permute-start(f32[1,128]{1,0:T(1,128)S(1)} %get-tuple-element.64.refs_0_), channel_id=1, source_target_pairs={{0,16},{8,24},{16,0},{24,8},{1,17},{9,25},{17,1},{25,9},{2,18},{10... | collective-permute-start | bytes 1544 | tf_op jit(solution)/shard_map/ppermute | solution.py:315
  129.3 42.5 %collective-permute-start.21 = (f32[1,128]{1,0:T(1,128)S(1)}, f32[1,128]{1,0:T(1,128)S(1)}, u32[]{:S(2)}, u32[]{:S(2)}) collective-permute-start(f32[1,128]{1,0:T(1,128)S(1)} %get-tuple-element.64.refs_0_), channel_id=1, source_target_pairs={{0,8},{8,0},{16,24},{24,16},{1,9},{9,1},{17,25},{25,17},{2,10},{10... | collective-permute-start | bytes 1544 | tf_op jit(solution)/shard_map/ppermute | solution.py:315
  146.5 26.6 %collective-permute-start.48 = (f32[1,1024]{1,0:T(1,128)S(1)}, f32[1,1024]{1,0:T(1,128)S(1)}, u32[]{:S(2)}, u32[]{:S(2)}) collective-permute-start(f32[1,1024]{1,0:T(1,128)S(1)} %get-tuple-element.86.refs_0_), channel_id=1, source_target_pairs={{0,16},{8,24},{16,0},{24,8},{1,17},{9,25},{17,1},{25,9},{2,18},{10... | collective-permute-start | bytes 12296 | tf_op jit(solution)/shard_map/ppermute | solution.py:315
  159.6 15.5 %collective-permute-start.45 = (f32[1,768]{1,0:T(1,128)S(1)}, f32[1,768]{1,0:T(1,128)S(1)}, u32[]{:S(2)}, u32[]{:S(2)}) collective-permute-start(f32[1,768]{1,0:T(1,128)S(1)} %get-tuple-element.84.refs_0_), channel_id=1, source_target_pairs={{0,16},{8,24},{16,0},{24,8},{1,17},{9,25},{17,1},{25,9},{2,18},{10... | collective-permute-start | bytes 9224 | tf_op jit(solution)/shard_map/ppermute | solution.py:315
  171.4 3.6 %collective-permute-start.19 = (f32[1,512]{1,0:T(1,128)S(1)}, f32[1,512]{1,0:T(1,128)S(1)}, u32[]{:S(2)}, u32[]{:S(2)}) collective-permute-start(f32[1,512]{1,0:T(1,128)S(1)} %get-tuple-element.61.refs_0_), channel_id=1, source_target_pairs={{0,16},{8,24},{16,0},{24,8},{1,17},{9,25},{17,1},{25,9},{2,18},{10... | collective-permute-start | bytes 6152 | tf_op jit(solution)/shard_map/ppermute | solution.py:315
  171.8 3.7 %collective-permute-start.18 = (f32[1,512]{1,0:T(1,128)S(1)}, f32[1,512]{1,0:T(1,128)S(1)}, u32[]{:S(2)}, u32[]{:S(2)}) collective-permute-start(f32[1,512]{1,0:T(1,128)S(1)} %get-tuple-element.61.refs_0_), channel_id=1, source_target_pairs={{0,8},{8,0},{16,24},{24,16},{1,9},{9,1},{17,25},{25,17},{2,10},{10... | collective-permute-start | bytes 6152 | tf_op jit(solution)/shard_map/ppermute | solution.py:315
  172.9 7.5 %collective-permute-start.47 = (f32[1,1024]{1,0:T(1,128)S(1)}, f32[1,1024]{1,0:T(1,128)S(1)}, u32[]{:S(2)}, u32[]{:S(2)}) collective-permute-start(f32[1,1024]{1,0:T(1,128)S(1)} %get-tuple-element.86.refs_0_), channel_id=1, source_target_pairs={{0,8},{8,0},{16,24},{24,16},{1,9},{9,1},{17,25},{25,17},{2,10},{10... | collective-permute-start | bytes 12296 | tf_op jit(solution)/shard_map/ppermute | solution.py:315
  173.1 7.3 %collective-permute-start.49 = (f32[1,1024]{1,0:T(1,128)S(1)}, f32[1,1024]{1,0:T(1,128)S(1)}, u32[]{:S(2)}, u32[]{:S(2)}) collective-permute-start(f32[1,1024]{1,0:T(1,128)S(1)} %collective-permute-done.48.refs_2_), channel_id=1, source_target_pairs={{0,8},{8,0},{16,24},{24,16},{1,9},{9,1},{17,25},{25,17},{2,10},{10... | collective-permute-start | bytes 12296 | tf_op jit(solution)/shard_map/ppermute | solution.py:315
  175.0 8.3 %collective-permute-start.44 = (f32[1,768]{1,0:T(1,128)S(1)}, f32[1,768]{1,0:T(1,128)S(1)}, u32[]{:S(2)}, u32[]{:S(2)}) collective-permute-start(f32[1,768]{1,0:T(1,128)S(1)} %get-tuple-element.84.refs_0_), channel_id=1, source_target_pairs={{0,8},{8,0},{16,24},{24,16},{1,9},{9,1},{17,25},{25,17},{2,10},{10... | collective-permute-start | bytes 9224 | tf_op jit(solution)/shard_map/ppermute | solution.py:315
  175.0 8.3 %collective-permute-start.46 = (f32[1,768]{1,0:T(1,128)S(1)}, f32[1,768]{1,0:T(1,128)S(1)}, u32[]{:S(2)}, u32[]{:S(2)}) collective-permute-start(f32[1,768]{1,0:T(1,128)S(1)} %collective-permute-done.45.refs_2_), channel_id=1, source_target_pairs={{0,8},{8,0},{16,24},{24,16},{1,9},{9,1},{17,25},{25,17},{2,10},{10... | collective-permute-start | bytes 9224 | tf_op jit(solution)/shard_map/ppermute | solution.py:315
  (21 other events, 330.7 us)

commit v4 on v3

--- a/solution.py
+++ b/solution.py
@@ -29,9 +29,10 @@
     first = [(which, 0, total) for which, total in enumerate(totals[:-1])]
     up = len(totals) - 1
     block = row_block(totals[up])
-    blocks = totals[up] // block
-    edges = sorted({0, block * (-(-blocks // 2)), totals[up]})
-    return [first] + [[(up, low, high)] for low, high in zip(edges, edges[1:])]
+    blocks = max(0, (sum(totals) // 2 - sum(totals[:-1])) // block)
+    if blocks:
+        first.append((up, 0, blocks * block))
+    return [first, [(up, blocks * block, totals[up])]]
 
 
 def column_chunk(width, count):
@@ -56,33 +57,25 @@
 
 
 def pack_kernel(plan, groups, at_ref, *refs):
-    count = len(plan) * groups
-    inputs, outputs, whole = refs[: -count - 1], refs[-count - 1 : -1], refs[-1]
-    edges = [0]
-    for ref in inputs:
-        rows = ref.shape[1] // groups
-        low = edges[-1]
-        for group in range(groups):
-            whole[group, :, low : low + rows] = ref[:, group * rows : (group + 1) * rows]
-        edges.append(low + rows)
-    for chunk, pieces in enumerate(plan):
-        for turn in range(groups):
-            to = (at_ref[1] + turn) % groups
-            out_ref = outputs[chunk * groups + turn]
-            start = 0
-            for which, low, high in pieces:
-                out_ref[:, start : start + high - low] = whole[
-                    to, :, edges[which] + low : edges[which] + high
+    inputs, outputs = refs[: -len(plan)], refs[-len(plan) :]
+    for pieces, out_ref in zip(plan, outputs):
+        start = 0
+        for which, low, high in pieces:
+            ref = inputs[which]
+            rows = ref.shape[1] // groups
+            for group in range(groups):
+                out_ref[group, :, start : start + high - low] = ref[
+                    :, group * rows + low : group * rows + high
                 ]
-                start += high - low
+            start += high - low
 
 
 def pack(cotangents, plan, groups, part, place):
-    rows = sum(array.shape[1] for array in cotangents) // groups
     outs = [
-        jax.ShapeDtypeStruct((part, sum(high - low for _, low, high in pieces)), jnp.bfloat16)
+        jax.ShapeDtypeStruct(
+            (groups, part, sum(high - low for _, low, high in pieces)), jnp.bfloat16
+        )
         for pieces in plan
-        for _ in range(groups)
     ]
     return pl.pallas_call(
         functools.partial(pack_kernel, plan, groups),
@@ -93,42 +86,17 @@
                 pl.BlockSpec((part, array.shape[1]), lambda i, at: (at[0], 0))
                 for array in cotangents
             ],
-            out_specs=[pl.BlockSpec(out.shape, lambda i, at: (0, 0)) for out in outs],
-            scratch_shapes=[pltpu.VMEM((groups, part, rows), jnp.bfloat16)],
+            out_specs=[pl.BlockSpec(out.shape, lambda i, at: (0, 0, 0)) for out in outs],
         ),
         out_shape=outs,
         compiler_params=with_vmem(56),
         cost_estimate=pl.CostEstimate(
-            flops=0, bytes_accessed=4 * groups * part * rows, transcendentals=0
+            flops=0,
+            bytes_accessed=4 * part * sum(array.shape[1] for array in cotangents),
+            transcendentals=0,
         ),
         name="pack",
     )(place, *cotangents)
-
-
-def bundle_kernel(at_ref, *refs):
-    pieces, out_ref = refs[:-1], refs[-1]
-    groups = len(pieces)
-    here = at_ref[1]
-    for turn, piece in enumerate(pieces):
-        source = (here + groups - turn) % groups
-        slot = ring_place(source, groups) - ring_place(here, groups) + groups
-        out_ref[slot % groups] = piece[...]
-
-
-def bundle(pieces, place):
-    part, rows = pieces[0].shape
-    vmem = pl.BlockSpec(memory_space=pltpu.VMEM)
-    return pl.pallas_call(
-        bundle_kernel,
-        in_specs=[pl.BlockSpec(memory_space=pltpu.SMEM)] + [vmem] * len(pieces),
-        out_specs=vmem,
-        out_shape=jax.ShapeDtypeStruct((len(pieces), part, rows), jnp.bfloat16),
-        compiler_params=with_vmem(8),
-        cost_estimate=pl.CostEstimate(
-            flops=0, bytes_accessed=4 * len(pieces) * part * rows, transcendentals=0
-        ),
-        name="bundle",
-    )(place, *pieces)
 
 
 def collect_kernel(*refs):
@@ -158,29 +126,39 @@
     )(*pieces)
 
 
-def gather_ring(array, axis):
+def ring_steps(array, axis):
     groups = lax.axis_size(axis)
     order = ring_order(groups)
     onward = list(zip(order, order[1:] + order[:1]))
     back = [(to, at) for at, to in onward]
-    behind, ahead = [array], [array]
-    for _ in range((groups - 1) // 2):
-        behind.append(lax.ppermute(behind[-1], axis, onward))
-        ahead.append(lax.ppermute(ahead[-1], axis, back))
-    middle = []
-    if groups % 2 == 0:
-        half = array.shape[0] // 2
-        middle.append(lax.ppermute(behind[-1][:half], axis, onward))
-        middle.append(lax.ppermute(ahead[-1][half:], axis, back))
-    return collect([array, *ahead[1:], *middle, *behind[:0:-1]])
+    behind, ahead, middle = [array], [array], []
+
+    def step(after):
+        one, two = behind[-1], ahead[-1]
+        if after is not None:
+            one, two, after = lax.optimization_barrier((one, two, after))
+        if len(behind) <= (groups - 1) // 2:
+            behind.append(lax.ppermute(one, axis, onward))
+            ahead.append(lax.ppermute(two, axis, back))
+        elif groups % 2 == 0 and not middle:
+            half = array.shape[0] // 2
+            middle.append(lax.ppermute(one[:half], axis, onward))
+            middle.append(lax.ppermute(two[half:], axis, back))
+        return after
+
+    def done():
+        return [array, *ahead[1:], *middle, *behind[:0:-1]]
+
+    return step, done
 
 
 def unpack_kernel(count, at_ref, *refs):
     pieces, outputs, order = refs[:count], refs[count:-1], refs[-1]
     groups, part, _ = pieces[0].shape
-    for turn, piece in enumerate(pieces):
-        for group in range(groups):
-            order[group * count + (at_ref[0] ^ turn)] = piece[group]
+    for group in range(groups):
+        slot = ring_place(group, groups) - ring_place(at_ref[1], groups) + groups
+        for turn, piece in enumerate(pieces):
+            order[slot % groups * count + (at_ref[0] ^ turn)] = piece[group]
     low = 0
     for out_ref in outputs:
         rows = out_ref.shape[0]
@@ -315,14 +293,6 @@
             got[turn ^ bit] = lax.ppermute(got[turn], axis, [(at, at ^ bit) for at in range(size)])
         bit //= 2
     return [got[turn] for turn in range(size)]
-
-
-def exchange(arrays, axis):
-    size = lax.axis_size(axis)
-    return [
-        lax.ppermute(array, axis, [(at, (at + turn) % size) for at in range(size)])
-        for turn, array in enumerate(arrays, 1)
-    ]
 
 
 def per_device(
@@ -352,20 +322,28 @@
     plan = chunk_plan([state[0].shape[0] for state in states])
     place = jnp.stack([lax.axis_index("col"), lax.axis_index("dp")]).astype(jnp.int32)
     packed = pack((query_cotangent, key_cotangent, up_cotangent), plan, groups, part, place)
-    gathered = gather_ring(layer_input, "dp")
+    step, ring = ring_steps(layer_input, "dp")
+    step(None)
+    owned = []
+    for array in packed:
+        if owned:
+            array, owned[-1] = lax.optimization_barrier((array, owned[-1]))
+        owned.append(lax.all_to_all(array, "dp", split_axis=0, concat_axis=0, tiled=True))
+        owned[-1] = step(owned[-1])
+    for _ in range(groups):
+        step(None)
+    gathered = collect(ring())
     moments = [[], [], []]
     updated = [[], [], []]
-    for chunk, pieces in enumerate(plan):
-        sent = packed[chunk * groups : (chunk + 1) * groups]
-        owned = bundle([sent[0], *exchange(sent[1:], "dp")], place)
-        every = unpack(from_others(owned, "col"), [high - low for _, low, high in pieces], place)
+    for array, pieces in zip(owned, plan):
+        every = unpack(from_others(array, "col"), [high - low for _, low, high in pieces], place)
         for (which, low, high), cotangent in zip(pieces, every):
-            power, step, *moments[which] = adam_pass(
+            power, new, *moments[which] = adam_pass(
                 cotangent, gathered, states[which], low, moments[which]
             )
             powers = from_others(power, "col")
             updated[which] = finish_rows(
-                step, powers, whole_width, states[which][0].shape[0], low, updated[which]
+                new, powers, whole_width, states[which][0].shape[0], low, updated[which]
             )
     return (
         *(made[0] for made in updated),

time: 187 us -> 171 us (0.914)
  starting transfers between devices: 43.6 us -> 34.4 us
  waiting for transfers between devices: 70.8 us -> 64.8 us
    ppermute x29 -> x8, starting transfers between devices: 33.7 us -> 11.2 us  [the longest x3 5.42 us: step(): behind.append(lax.ppermute(one, axis, onward))]
    all_to_all x0 -> x2, starting transfers between devices: none -> 14.1 us  [per_device(): lax.all_to_all(array, 'dp', split_axis=0, concat_axis=0, tiled=True)]
    ppermute x21 -> x18, waiting for transfers between devices: 13.2 us -> 3.45 us  [from_others(): lax.ppermute(got[turn], axis, [(at, at ^ bit) for at in range(size)])]
    ppermute x29 -> x8, waiting for transfers between devices: 57.6 us -> 61.3 us  [the longest x3 33.4 us: step(): ahead.append(lax.ppermute(two, axis, back))]
    pallas_call x3 -> x0, Pallas kernels: 2 us -> none  [bundle(): pl.pallas_call(bundle_kernel, in_specs=[pl.BlockSpec(memory_space=pltpu.S...]
    unnamed x38 -> x32, local copies, waits for them, and re-layouts: 7.01 us -> 6.17 us
    ppermute x21 -> x18, starting transfers between devices: 9.88 us -> 9.11 us  [from_others(): lax.ppermute(got[turn], axis, [(at, at ^ bit) for at in range(size)])]
  transfers between devices with their start and end apart: 50 -> 28, of which waited for: 23 -> 9; matrix products, arithmetic and copies ran while one was open for 0% -> 0% of each run, Pallas kernels for 29% -> 20%
where the time goes in v4:
time: 171 us
  waiting for transfers between devices  64.8 us (38%)
  Pallas kernels  63.8 us (37%)
  starting transfers between devices  34.4 us (20%)
  local copies, waits for them, and re-layouts  6.2 us (4%)
    pallas_call x4, Pallas kernels, adam_pass(): pl.pallas_call(functools.partial(adam_kernel, strip_of(width)), grid=(row...  45.9 us
    ppermute x3, waiting for transfers between devices, step(): ahead.append(lax.ppermute(two, axis, back))  33.4 us
    ppermute x3, waiting for transfers between devices, step(): behind.append(lax.ppermute(one, axis, onward))  22 us
    all_to_all x2, starting transfers between devices, per_device(): lax.all_to_all(array, 'dp', split_axis=0, concat_axis=0, tiled=True)  14.1 us
    ppermute x18, starting transfers between devices, from_others(): lax.ppermute(got[turn], axis, [(at, at ^ bit) for at in range(size)])  9.11 us
    pallas_call x4, Pallas kernels, finish_rows(): pl.pallas_call(functools.partial(finish_kernel, len(powers), whole_width)...  7.82 us
    unnamed x32, local copies, waits for them, and re-layouts  6.17 us
    ppermute x3, starting transfers between devices, step(): behind.append(lax.ppermute(one, axis, onward))  5.42 us
  transfers between devices with their start and end apart: 28, of which 9 were waited for; matrix products, arithmetic and copies ran while one was open for 0% of the time, Pallas kernels for 20%

profile of v4, /device:TPU:0, one launch (start us, length us, event | category | flops | bytes accessed | tf_op | source)
XLA Modules:
  0.0 170.5 jit_solution(14524489680017999489)
XLA Ops:
  0.7 0.6 pad_add_fusion.at_ref
  1.2 3.2 %pack.1 = (bf16[8,32,1152]{2,1,0:T(8,128)(2,1)}, bf16[8,32,1280]{2,1,0:T(8,128)(2,1)}) custom-call(s32[2]{0:T(128)} %pad_add_fusion.at_ref, bf16[128,4096]{1,0:T(8,128)(2,1)} %refs_0_.2, bf16[128,1024]{1,0:T(8,128)(2,1)} %refs_1_.1, bf16[128,14336]{1,0:T(8,128)(2,1)} %refs_2_.1), custom_call_target="tpu_custom_call" | custom-call | bytes 2490368 | tf_op jit(solution)/shard_map/pack/pallas_call | solution.py:80
  4.4 7.3 %all-to-all-start = ((bf16[8,32,1152]{2,1,0:T(8,128)(2,1)}), bf16[8,32,1152]{2,1,0:T(8,128)(2,1)S(1)}, u32[]{:S(2)}, u32[]{:S(2)}) async-start(bf16[8,32,1152]{2,1,0:T(8,128)(2,1)} %get-tuple-element.39), calls=%async_computation | async-start | bytes 1179648 | tf_op jit(solution)/shard_map/all_to_all | solution.py:331
  11.7 2.0 %collective-permute-start = (bf16[128,2048]{1,0:T(8,128)(2,1)S(1)}, bf16[128,2048]{1,0:T(8,128)(2,1)S(1)}, u32[]{:S(2)}, u32[]{:S(2)}) collective-permute-start(bf16[128,2048]{1,0:T(8,128)(2,1)S(1)} %copy-done.3), channel_id=1, source_target_pairs={{0,2},{2,4},{4,6},{6,7},{7,5},{5,3},{3,1},{1,0},{8,10},{10,12},{12... | collective-permute-start | bytes 1572872 | tf_op jit(solution)/shard_map/ppermute | solution.py:141
  13.8 18.8 %collective-permute-done.refs_8_ = bf16[128,2048]{1,0:T(8,128)(2,1)S(1)} collective-permute-done((bf16[128,2048]{1,0:T(8,128)(2,1)S(1)}, bf16[128,2048]{1,0:T(8,128)(2,1)S(1)}, u32[]{:S(2)}, u32[]{:S(2)}) %collective-permute-start) | collective-permute-done | bytes 524320 | tf_op jit(solution)/shard_map/ppermute | solution.py:141
  32.6 2.2 %collective-permute-done.1.refs_1_ = bf16[128,2048]{1,0:T(8,128)(2,1)S(1)} collective-permute-done((bf16[128,2048]{1,0:T(8,128)(2,1)S(1)}, bf16[128,2048]{1,0:T(8,128)(2,1)S(1)}, u32[]{:S(2)}, u32[]{:S(2)}) %collective-permute-start.1) | collective-permute-done | bytes 524320 | tf_op jit(solution)/shard_map/ppermute | solution.py:142
  34.8 6.8 %all-to-all-start.1 = ((bf16[8,32,1280]{2,1,0:T(8,128)(2,1)}), bf16[8,32,1280]{2,1,0:T(8,128)(2,1)S(1)}, u32[]{:S(2)}, u32[]{:S(2)}) async-start(bf16[8,32,1280]{2,1,0:T(8,128)(2,1)} %get-tuple-element.45), calls=%async_computation.1 | async-start | bytes 1310720 | tf_op jit(solution)/shard_map/all_to_all | solution.py:331
  41.6 2.0 %collective-permute-start.5 = (bf16[128,2048]{1,0:T(8,128)(2,1)S(1)}, bf16[128,2048]{1,0:T(8,128)(2,1)S(1)}, u32[]{:S(2)}, u32[]{:S(2)}) collective-permute-start(bf16[128,2048]{1,0:T(8,128)(2,1)S(1)} %collective-permute-done.1.refs_1_), channel_id=1, source_target_pairs={{2,0},{4,2},{6,4},{7,6},{5,7},{3,5},{1,3},{0,1},{10,8},{12,10},{14... | collective-permute-start | bytes 1572872 | tf_op jit(solution)/shard_map/ppermute | solution.py:142
  43.7 1.5 collective-permute-start.3
  45.2 20.8 %collective-permute-done.5.refs_2_ = bf16[128,2048]{1,0:T(8,128)(2,1)S(1)} collective-permute-done((bf16[128,2048]{1,0:T(8,128)(2,1)S(1)}, bf16[128,2048]{1,0:T(8,128)(2,1)S(1)}, u32[]{:S(2)}, u32[]{:S(2)}) %collective-permute-start.5) | collective-permute-done | bytes 524320 | tf_op jit(solution)/shard_map/ppermute | solution.py:142
  65.9 1.5 collective-permute-start.18
  67.4 1.6 collective-permute-start.7
  69.0 3.4 %collective-permute-start.8 = (bf16[128,2048]{1,0:T(8,128)(2,1)}, bf16[128,2048]{1,0:T(8,128)(2,1)S(1)}, u32[]{:S(2)}, u32[]{:S(2)}) collective-permute-start(bf16[128,2048]{1,0:T(8,128)(2,1)} %collective-permute-done.6.refs_7_), channel_id=1, source_target_pairs={{0,2},{2,4},{4,6},{6,7},{7,5},{5,3},{3,1},{1,0},{8,10},{10,12},{12... | collective-permute-start | bytes 1572872 | tf_op jit(solution)/shard_map/ppermute | solution.py:141
  72.4 0.2 collective-permute-start.4
  72.6 10.4 %collective-permute-done.7.refs_3_ = bf16[128,2048]{1,0:T(8,128)(2,1)S(1)} collective-permute-done((bf16[128,2048]{1,0:T(8,128)(2,1)S(1)}, bf16[128,2048]{1,0:T(8,128)(2,1)S(1)}, u32[]{:S(2)}, u32[]{:S(2)}) %collective-permute-start.7) | collective-permute-done | bytes 524320 | tf_op jit(solution)/shard_map/ppermute | solution.py:142
  83.0 0.5 collective-permute-start.19
  83.6 3.2 %collective-permute-done.8.refs_6_ = bf16[128,2048]{1,0:T(8,128)(2,1)S(1)} collective-permute-done((bf16[128,2048]{1,0:T(8,128)(2,1)}, bf16[128,2048]{1,0:T(8,128)(2,1)S(1)}, u32[]{:S(2)}, u32[]{:S(2)}) %collective-permute-start.8) | collective-permute-done | bytes 524320 | tf_op jit(solution)/shard_map/ppermute | solution.py:141
  86.8 1.7 %collective-permute-start.10 = (bf16[64,2048]{1,0:T(8,128)(2,1)S(1)}, bf16[64,2048]{1,0:T(8,128)(2,1)S(1)}, u32[]{:S(2)}, u32[]{:S(2)}) collective-permute-start(bf16[64,2048]{1,0:T(8,128)(2,1)S(1)} %slice.9), channel_id=1, source_target_pairs={{2,0},{4,2},{6,4},{7,6},{5,7},{3,5},{1,3},{0,1},{10,8},{12,10},{14... | collective-permute-start | bytes 786440 | tf_op jit(solution)/shard_map/ppermute | solution.py:146
  88.5 0.3 collective-permute-start.9
  88.9 1.4 unpack.2
  90.3 4.6 %collective-permute-done.10.refs_5_ = bf16[64,2048]{1,0:T(8,128)(2,1)S(1)} collective-permute-done((bf16[64,2048]{1,0:T(8,128)(2,1)S(1)}, bf16[64,2048]{1,0:T(8,128)(2,1)S(1)}, u32[]{:S(2)}, u32[]{:S(2)}) %collective-permute-start.10) | collective-permute-done | bytes 262176 | tf_op jit(solution)/shard_map/ppermute | solution.py:146
  94.9 1.3 collective-permute-done.9.refs_4_
  96.2 1.0 copy-done.4
  97.3 1.0 copy-done.9
  98.3 1.0 copy-done.11
  99.4 4.0 %collect.1.x_ref = bf16[1024,2048]{1,0:T(8,128)(2,1)} custom-call(bf16[128,2048]{1,0:T(8,128)(2,1)S(1)} %copy-done.4, bf16[128,2048]{1,0:T(8,128)(2,1)S(1)} %copy-done.11, bf16[128,2048]{1,0:T(8,128)(2,1)S(1)} %collective-permute-done.5.refs_2_, bf16[128,2048]{1,0:T(8,128)(2,1)S(1)} %collective-permute-done.7.refs_3_, ...), custom_call_target="tpu_custom_call" | custom-call | bytes 8388608 | tf_op jit(solution)/shard_map/collect/pallas_call | solution.py:115
  103.4 10.3 %adam.6 = (f32[1,512]{1,0:T(1,128)S(1)}, f32[512,2048]{1,0:T(8,128)S(1)}, bf16[1792,2048]{1,0:T(8,128)(2,1)}, bf16[1792,2048]{1,0:T(8,128)(2,1)}) custom-call(bf16[512,1024]{1,0:T(8,128)(2,1)S(1)} %get-tuple-element.54.c_ref, bf16[1024,2048]{1,0:T(8,128)(2,1)} %collect.1.x_ref, bf16[1792,2048]{1,0:T(8,128)(2,1)} %w_ref.7, bf16[1792,2048]{1,0:T(8,128)(2,1)} %m_ref.7, ...), custom_call_target="tpu_custom_call" | custom-call | flops 2147483648 | bytes 19922944 | tf_op jit(solution)/shard_map/adam/pallas_call | solution.py:220
  113.8 1.5 unpack.3.c_ref
  115.3 20.7 %adam.7 = (f32[1,1280]{1,0:T(1,128)S(1)}, f32[1280,2048]{1,0:T(8,128)}, bf16[1792,2048]{1,0:T(8,128)(2,1)}, bf16[1792,2048]{1,0:T(8,128)(2,1)}) custom-call(bf16[1280,1024]{1,0:T(8,128)(2,1)S(1)} %unpack.3.c_ref, bf16[1024,2048]{1,0:T(8,128)(2,1)} %collect.1.x_ref, bf16[1792,2048]{1,0:T(8,128)(2,1)} %w_ref.7, ...), custom_call_target="tpu_custom_call", output_to_operand_aliasing={{2}: (5, {}), {3}: (6, {})} | custom-call | flops 5368709120 | bytes 43515904 | tf_op jit(solution)/shard_map/adam/pallas_call | solution.py:220
  136.0 0.6 collective-permute-start.21
  136.6 4.8 %adam.5 = (f32[1,128]{1,0:T(1,128)S(1)}, f32[128,2048]{1,0:T(8,128)S(1)}, bf16[128,2048]{1,0:T(8,128)(2,1)}, bf16[128,2048]{1,0:T(8,128)(2,1)}) custom-call(bf16[128,1024]{1,0:T(8,128)(2,1)S(1)} %get-tuple-element.50.c_ref, bf16[1024,2048]{1,0:T(8,128)(2,1)} %collect.1.x_ref, bf16[128,2048]{1,0:T(8,128)(2,1)S(1)} %copy-done.5, ...), custom_call_target="tpu_custom_call" | custom-call | flops 536870912 | bytes 8126464 | tf_op jit(solution)/shard_map/adam/pallas_call | solution.py:220
  141.4 1.2 collective-permute-start.15
  142.5 0.8 collective-permute-start.24
  143.4 1.5 collective-permute-done.15.refs_2_
  144.9 0.5 collective-permute-start.20
  145.4 10.1 %adam.4 = (f32[1,512]{1,0:T(1,128)S(1)}, f32[512,2048]{1,0:T(8,128)}, bf16[512,2048]{1,0:T(8,128)(2,1)}, bf16[512,2048]{1,0:T(8,128)(2,1)}) custom-call(bf16[512,1024]{1,0:T(8,128)(2,1)S(1)} %get-tuple-element.42.c_ref, bf16[1024,2048]{1,0:T(8,128)(2,1)} %collect.1.x_ref, bf16[512,2048]{1,0:T(8,128)(2,1)S(1)} %copy-done.1, bf16[512,2048]{1,0:T(8,128)(2,1)S(1)} %copy-done.2, ...), custom_call_target="tpu_custom_call" | custom-call | flops 2147483648 | bytes 19922944 | tf_op jit(solution)/shard_map/adam/pallas_call | solution.py:220
  155.5 0.6 collective-permute-start.23
  156.1 1.2 collective-permute-start.12
  157.3 0.5 collective-permute-start.11
  157.8 1.9 %collective-permute-done.12.refs_2_ = f32[1,512]{1,0:T(1,128)S(1)} collective-permute-done((f32[1,512]{1,0:T(1,128)S(1)}, f32[1,512]{1,0:T(1,128)S(1)}, u32[]{:S(2)}, u32[]{:S(2)}) %collective-permute-start.12) | collective-permute-done | bytes 2080 | tf_op jit(solution)/shard_map/ppermute | solution.py:293
  159.7 1.0 finish.5
  160.7 1.6 finish.6.refs_4_
  162.3 0.2 copy-done
  162.5 1.6 finish.4
  164.1 0.8 slice-done
  164.9 1.4 slice-done.1
  166.3 0.6 slice-done.2
  166.9 3.7 %finish.7 = bf16[1792,2048]{1,0:T(8,128)(2,1)} custom-call(f32[1280,2048]{1,0:T(8,128)S(1)} %bitcast.3, f32[1,1280]{1,0:T(1,128)S(1)} %get-tuple-element.58.refs_0_, f32[1,1280]{1,0:T(1,128)S(1)} %collective-permute-done.20.refs_1_, f32[1,1280]{1,0:T(1,128)S(1)} %collective-permute-done.21.refs_2_, ...), custom_call_target="tpu_custom_call", output_to_operand_aliasing={{}: (5, {})} | custom-call | flops 2621440 | bytes 15728640 | tf_op jit(solution)/shard_map/finish/pallas_call | solution.py:270
  (56 shorter events, 0.3 us)
Async XLA Ops:
  0.6 11.1 %copy-start.3 = (bf16[128,2048]{1,0:T(8,128)(2,1)S(1)}, bf16[128,2048]{1,0:T(8,128)(2,1)}, u32[]{:S(2)}) copy-start(bf16[128,2048]{1,0:T(8,128)(2,1)} %refs_0_.3) | copy-start | bytes 1572868
  1.2 87.6 %copy-start.12 = (s32[2]{0:T(128)S(1)}, s32[2]{0:T(128)}, u32[]{:S(2)}) copy-start(s32[2]{0:T(128)} %pad_add_fusion.at_ref) | copy-start | bytes 28
  4.4 30.4 %all-to-all-start = ((bf16[8,32,1152]{2,1,0:T(8,128)(2,1)}), bf16[8,32,1152]{2,1,0:T(8,128)(2,1)S(1)}, u32[]{:S(2)}, u32[]{:S(2)}) async-start(bf16[8,32,1152]{2,1,0:T(8,128)(2,1)} %get-tuple-element.39), calls=%async_computation | async-start | bytes 1179648 | tf_op jit(solution)/shard_map/all_to_all | solution.py:331
  11.7 20.9 %collective-permute-start = (bf16[128,2048]{1,0:T(8,128)(2,1)S(1)}, bf16[128,2048]{1,0:T(8,128)(2,1)S(1)}, u32[]{:S(2)}, u32[]{:S(2)}) collective-permute-start(bf16[128,2048]{1,0:T(8,128)(2,1)S(1)} %copy-done.3), channel_id=1, source_target_pairs={{0,2},{2,4},{4,6},{6,7},{7,5},{5,3},{3,1},{1,0},{8,10},{10,12},{12... | collective-permute-start | bytes 1572872 | tf_op jit(solution)/shard_map/ppermute | solution.py:141
  13.7 21.0 %collective-permute-start.1 = (bf16[128,2048]{1,0:T(8,128)(2,1)S(1)}, bf16[128,2048]{1,0:T(8,128)(2,1)S(1)}, u32[]{:S(2)}, u32[]{:S(2)}) collective-permute-start(bf16[128,2048]{1,0:T(8,128)(2,1)S(1)} %copy-done.3), channel_id=1, source_target_pairs={{2,0},{4,2},{6,4},{7,6},{5,7},{3,5},{1,3},{0,1},{10,8},{12,10},{14... | collective-permute-start | bytes 1572872 | tf_op jit(solution)/shard_map/ppermute | solution.py:142
  32.6 40.1 %copy-start.8 = (bf16[128,2048]{1,0:T(8,128)(2,1)}, bf16[128,2048]{1,0:T(8,128)(2,1)S(1)}, u32[]{:S(2)}) copy-start(bf16[128,2048]{1,0:T(8,128)(2,1)S(1)} %collective-permute-done.refs_8_) | copy-start | bytes 1572868
  34.8 37.9 %copy-start.10 = (bf16[128,2048]{1,0:T(8,128)(2,1)}, bf16[128,2048]{1,0:T(8,128)(2,1)S(1)}, u32[]{:S(2)}) copy-start(bf16[128,2048]{1,0:T(8,128)(2,1)S(1)} %collective-permute-done.1.refs_1_) | copy-start | bytes 1572868
  34.8 31.2 %all-to-all-start.1 = ((bf16[8,32,1280]{2,1,0:T(8,128)(2,1)}), bf16[8,32,1280]{2,1,0:T(8,128)(2,1)S(1)}, u32[]{:S(2)}, u32[]{:S(2)}) async-start(bf16[8,32,1280]{2,1,0:T(8,128)(2,1)} %get-tuple-element.45), calls=%async_computation.1 | async-start | bytes 1310720 | tf_op jit(solution)/shard_map/all_to_all | solution.py:331
  41.6 24.3 %collective-permute-start.5 = (bf16[128,2048]{1,0:T(8,128)(2,1)S(1)}, bf16[128,2048]{1,0:T(8,128)(2,1)S(1)}, u32[]{:S(2)}, u32[]{:S(2)}) collective-permute-start(bf16[128,2048]{1,0:T(8,128)(2,1)S(1)} %collective-permute-done.1.refs_1_), channel_id=1, source_target_pairs={{2,0},{4,2},{6,4},{7,6},{5,7},{3,5},{1,3},{0,1},{10,8},{12,10},{14... | collective-permute-start | bytes 1572872 | tf_op jit(solution)/shard_map/ppermute | solution.py:142
  43.6 22.3 %collective-permute-start.6 = (bf16[128,2048]{1,0:T(8,128)(2,1)S(1)}, bf16[128,2048]{1,0:T(8,128)(2,1)}, u32[]{:S(2)}, u32[]{:S(2)}) collective-permute-start(bf16[128,2048]{1,0:T(8,128)(2,1)S(1)} %collective-permute-done.refs_8_), channel_id=1, source_target_pairs={{0,2},{2,4},{4,6},{6,7},{7,5},{5,3},{3,1},{1,0},{8,10},{10,12},{12... | collective-permute-start | bytes 1572872 | tf_op jit(solution)/shard_map/ppermute | solution.py:141
  43.7 28.7 %collective-permute-start.3 = (bf16[8,32,1152]{2,1,0:T(8,128)(2,1)S(1)}, bf16[8,32,1152]{2,1,0:T(8,128)(2,1)S(1)}, u32[]{:S(2)}, u32[]{:S(2)}) collective-permute-start(bf16[8,32,1152]{2,1,0:T(8,128)(2,1)S(1)} %all-to-all-done.refs_0_), channel_id=1, source_target_pairs={{0,16},{8,24},{16,0},{24,8},{1,17},{9,25},{17,1},{25,9},{2,18},{10... | collective-permute-start | bytes 1769480 | tf_op jit(solution)/shard_map/ppermute | solution.py:293
  65.9 17.1 %collective-permute-start.18 = (bf16[8,32,1280]{2,1,0:T(8,128)(2,1)S(1)}, bf16[8,32,1280]{2,1,0:T(8,128)(2,1)S(1)}, u32[]{:S(2)}, u32[]{:S(2)}) collective-permute-start(bf16[8,32,1280]{2,1,0:T(8,128)(2,1)S(1)} %all-to-all-done.1.refs_0_), channel_id=1, source_target_pairs={{0,16},{8,24},{16,0},{24,8},{1,17},{9,25},{17,1},{25,9},{2,18},{10... | collective-permute-start | bytes 1966088 | tf_op jit(solution)/shard_map/ppermute | solution.py:293
  67.4 15.6 %collective-permute-start.7 = (bf16[128,2048]{1,0:T(8,128)(2,1)S(1)}, bf16[128,2048]{1,0:T(8,128)(2,1)S(1)}, u32[]{:S(2)}, u32[]{:S(2)}) collective-permute-start(bf16[128,2048]{1,0:T(8,128)(2,1)S(1)} %collective-permute-done.5.refs_2_), channel_id=1, source_target_pairs={{2,0},{4,2},{6,4},{7,6},{5,7},{3,5},{1,3},{0,1},{10,8},{12,10},{14... | collective-permute-start | bytes 1572872 | tf_op jit(solution)/shard_map/ppermute | solution.py:142
  69.0 19.5 %collective-permute-start.2 = (bf16[8,32,1152]{2,1,0:T(8,128)(2,1)S(1)}, bf16[8,32,1152]{2,1,0:T(8,128)(2,1)S(1)}, u32[]{:S(2)}, u32[]{:S(2)}) collective-permute-start(bf16[8,32,1152]{2,1,0:T(8,128)(2,1)S(1)} %all-to-all-done.refs_0_), channel_id=1, source_target_pairs={{0,8},{8,0},{16,24},{24,16},{1,9},{9,1},{17,25},{25,17},{2,10},{10... | collective-permute-start | bytes 1769480 | tf_op jit(solution)/shard_map/ppermute | solution.py:293
  69.0 17.7 %collective-permute-start.8 = (bf16[128,2048]{1,0:T(8,128)(2,1)}, bf16[128,2048]{1,0:T(8,128)(2,1)S(1)}, u32[]{:S(2)}, u32[]{:S(2)}) collective-permute-start(bf16[128,2048]{1,0:T(8,128)(2,1)} %collective-permute-done.6.refs_7_), channel_id=1, source_target_pairs={{0,2},{2,4},{4,6},{6,7},{7,5},{5,3},{3,1},{1,0},{8,10},{10,12},{12... | collective-permute-start | bytes 1572872 | tf_op jit(solution)/shard_map/ppermute | solution.py:141
  72.4 16.5 %collective-permute-start.4 = (bf16[8,32,1152]{2,1,0:T(8,128)(2,1)S(1)}, bf16[8,32,1152]{2,1,0:T(8,128)(2,1)S(1)}, u32[]{:S(2)}, u32[]{:S(2)}) collective-permute-start(bf16[8,32,1152]{2,1,0:T(8,128)(2,1)S(1)} %collective-permute-done.3.refs_2_), channel_id=1, source_target_pairs={{0,8},{8,0},{16,24},{24,16},{1,9},{9,1},{17,25},{25,17},{2,10},{10... | collective-permute-start | bytes 1769480 | tf_op jit(solution)/shard_map/ppermute | solution.py:293
  83.0 30.7 %collective-permute-start.17 = (bf16[8,32,1280]{2,1,0:T(8,128)(2,1)S(1)}, bf16[8,32,1280]{2,1,0:T(8,128)(2,1)S(1)}, u32[]{:S(2)}, u32[]{:S(2)}) collective-permute-start(bf16[8,32,1280]{2,1,0:T(8,128)(2,1)S(1)} %all-to-all-done.1.refs_0_), channel_id=1, source_target_pairs={{0,8},{8,0},{16,24},{24,16},{1,9},{9,1},{17,25},{25,17},{2,10},{10... | collective-permute-start | bytes 1966088 | tf_op jit(solution)/shard_map/ppermute | solution.py:293
  83.0 30.7 %collective-permute-start.19 = (bf16[8,32,1280]{2,1,0:T(8,128)(2,1)S(1)}, bf16[8,32,1280]{2,1,0:T(8,128)(2,1)S(1)}, u32[]{:S(2)}, u32[]{:S(2)}) collective-permute-start(bf16[8,32,1280]{2,1,0:T(8,128)(2,1)S(1)} %collective-permute-done.18.refs_2_), channel_id=1, source_target_pairs={{0,8},{8,0},{16,24},{24,16},{1,9},{9,1},{17,25},{25,17},{2,10},{10... | collective-permute-start | bytes 1966088 | tf_op jit(solution)/shard_map/ppermute | solution.py:293
  86.8 8.1 %collective-permute-start.10 = (bf16[64,2048]{1,0:T(8,128)(2,1)S(1)}, bf16[64,2048]{1,0:T(8,128)(2,1)S(1)}, u32[]{:S(2)}, u32[]{:S(2)}) collective-permute-start(bf16[64,2048]{1,0:T(8,128)(2,1)S(1)} %slice.9), channel_id=1, source_target_pairs={{2,0},{4,2},{6,4},{7,6},{5,7},{3,5},{1,3},{0,1},{10,8},{12,10},{14... | collective-permute-start | bytes 786440 | tf_op jit(solution)/shard_map/ppermute | solution.py:146
  88.5 7.7 %collective-permute-start.9 = (bf16[64,2048]{1,0:T(8,128)(2,1)S(1)}, bf16[64,2048]{1,0:T(8,128)(2,1)S(1)}, u32[]{:S(2)}, u32[]{:S(2)}) collective-permute-start(bf16[64,2048]{1,0:T(8,128)(2,1)S(1)} %slice.8), channel_id=1, source_target_pairs={{0,2},{2,4},{4,6},{6,7},{7,5},{5,3},{3,1},{1,0},{8,10},{10,12},{12... | collective-permute-start | bytes 786440 | tf_op jit(solution)/shard_map/ppermute | solution.py:145
  96.2 1.0 copy-start.4
  97.3 1.0 copy-start.9
  98.3 1.0 copy-start.11
  115.2 21.4 %copy-start.5 = (bf16[128,2048]{1,0:T(8,128)(2,1)S(1)}, bf16[128,2048]{1,0:T(8,128)(2,1)}, u32[]{:S(2)}) copy-start(bf16[128,2048]{1,0:T(8,128)(2,1)} %w_ref.5) | copy-start | bytes 1572868
  115.2 21.4 %copy-start.6 = (bf16[128,2048]{1,0:T(8,128)(2,1)S(1)}, bf16[128,2048]{1,0:T(8,128)(2,1)}, u32[]{:S(2)}) copy-start(bf16[128,2048]{1,0:T(8,128)(2,1)} %m_ref.5) | copy-start | bytes 1572868
  115.3 21.3 %copy-start.7 = (bf16[128,2048]{1,0:T(8,128)(2,1)S(1)}, bf16[128,2048]{1,0:T(8,128)(2,1)}, u32[]{:S(2)}) copy-start(bf16[128,2048]{1,0:T(8,128)(2,1)} %v_ref.5) | copy-start | bytes 1572868
  136.0 9.5 %copy-start.1 = (bf16[512,2048]{1,0:T(8,128)(2,1)S(1)}, bf16[512,2048]{1,0:T(8,128)(2,1)}, u32[]{:S(2)}) copy-start(bf16[512,2048]{1,0:T(8,128)(2,1)} %w_ref.4) | copy-start | bytes 6291460
  136.0 9.5 %copy-start.2 = (bf16[512,2048]{1,0:T(8,128)(2,1)S(1)}, bf16[512,2048]{1,0:T(8,128)(2,1)}, u32[]{:S(2)}) copy-start(bf16[512,2048]{1,0:T(8,128)(2,1)} %m_ref.4) | copy-start | bytes 6291460
  136.0 9.4 %collective-permute-start.21 = (f32[1,1280]{1,0:T(1,128)S(1)}, f32[1,1280]{1,0:T(1,128)S(1)}, u32[]{:S(2)}, u32[]{:S(2)}) collective-permute-start(f32[1,1280]{1,0:T(1,128)S(1)} %get-tuple-element.58.refs_0_), channel_id=1, source_target_pairs={{0,16},{8,24},{16,0},{24,8},{1,17},{9,25},{17,1},{25,9},{2,18},{10... | collective-permute-start | bytes 15368 | tf_op jit(solution)/shard_map/ppermute | solution.py:293
  141.4 3.5 %collective-permute-start.15 = (f32[1,128]{1,0:T(1,128)S(1)}, f32[1,128]{1,0:T(1,128)S(1)}, u32[]{:S(2)}, u32[]{:S(2)}) collective-permute-start(f32[1,128]{1,0:T(1,128)S(1)} %get-tuple-element.52.refs_0_), channel_id=1, source_target_pairs={{0,16},{8,24},{16,0},{24,8},{1,17},{9,25},{17,1},{25,9},{2,18},{10... | collective-permute-start | bytes 1544 | tf_op jit(solution)/shard_map/ppermute | solution.py:293
  142.5 13.0 %collective-permute-start.14 = (f32[1,128]{1,0:T(1,128)S(1)}, f32[1,128]{1,0:T(1,128)S(1)}, u32[]{:S(2)}, u32[]{:S(2)}) collective-permute-start(f32[1,128]{1,0:T(1,128)S(1)} %get-tuple-element.52.refs_0_), channel_id=1, source_target_pairs={{0,8},{8,0},{16,24},{24,16},{1,9},{9,1},{17,25},{25,17},{2,10},{10... | collective-permute-start | bytes 1544 | tf_op jit(solution)/shard_map/ppermute | solution.py:293
  142.5 14.7 %collective-permute-start.24 = (f32[1,512]{1,0:T(1,128)S(1)}, f32[1,512]{1,0:T(1,128)S(1)}, u32[]{:S(2)}, u32[]{:S(2)}) collective-permute-start(f32[1,512]{1,0:T(1,128)S(1)} %get-tuple-element.60.refs_0_), channel_id=1, source_target_pairs={{0,16},{8,24},{16,0},{24,8},{1,17},{9,25},{17,1},{25,9},{2,18},{10... | collective-permute-start | bytes 6152 | tf_op jit(solution)/shard_map/ppermute | solution.py:293
  144.9 11.2 %collective-permute-start.16 = (f32[1,128]{1,0:T(1,128)S(1)}, f32[1,128]{1,0:T(1,128)S(1)}, u32[]{:S(2)}, u32[]{:S(2)}) collective-permute-start(f32[1,128]{1,0:T(1,128)S(1)} %collective-permute-done.15.refs_2_), channel_id=1, source_target_pairs={{0,8},{8,0},{16,24},{24,16},{1,9},{9,1},{17,25},{25,17},{2,10},{10... | collective-permute-start | bytes 1544 | tf_op jit(solution)/shard_map/ppermute | solution.py:293
  144.9 19.2 %collective-permute-start.20 = (f32[1,1280]{1,0:T(1,128)S(1)}, f32[1,1280]{1,0:T(1,128)S(1)}, u32[]{:S(2)}, u32[]{:S(2)}) collective-permute-start(f32[1,1280]{1,0:T(1,128)S(1)} %get-tuple-element.58.refs_0_), channel_id=1, source_target_pairs={{0,8},{8,0},{16,24},{24,16},{1,9},{9,1},{17,25},{25,17},{2,10},{10... | collective-permute-start | bytes 15368 | tf_op jit(solution)/shard_map/ppermute | solution.py:293
  145.4 18.7 %collective-permute-start.22 = (f32[1,1280]{1,0:T(1,128)S(1)}, f32[1,1280]{1,0:T(1,128)S(1)}, u32[]{:S(2)}, u32[]{:S(2)}) collective-permute-start(f32[1,1280]{1,0:T(1,128)S(1)} %collective-permute-done.21.refs_2_), channel_id=1, source_target_pairs={{0,8},{8,0},{16,24},{24,16},{1,9},{9,1},{17,25},{25,17},{2,10},{10... | collective-permute-start | bytes 15368 | tf_op jit(solution)/shard_map/ppermute | solution.py:293
  155.5 1.7 %collective-permute-start.23 = (f32[1,512]{1,0:T(1,128)S(1)}, f32[1,512]{1,0:T(1,128)S(1)}, u32[]{:S(2)}, u32[]{:S(2)}) collective-permute-start(f32[1,512]{1,0:T(1,128)S(1)} %get-tuple-element.60.refs_0_), channel_id=1, source_target_pairs={{0,8},{8,0},{16,24},{24,16},{1,9},{9,1},{17,25},{25,17},{2,10},{10... | collective-permute-start | bytes 6152 | tf_op jit(solution)/shard_map/ppermute | solution.py:293
  156.1 3.6 %collective-permute-start.12 = (f32[1,512]{1,0:T(1,128)S(1)}, f32[1,512]{1,0:T(1,128)S(1)}, u32[]{:S(2)}, u32[]{:S(2)}) collective-permute-start(f32[1,512]{1,0:T(1,128)S(1)} %get-tuple-element.49.refs_0_), channel_id=1, source_target_pairs={{0,16},{8,24},{16,0},{24,8},{1,17},{9,25},{17,1},{25,9},{2,18},{10... | collective-permute-start | bytes 6152 | tf_op jit(solution)/shard_map/ppermute | solution.py:293
  157.3 3.4 %collective-permute-start.25 = (f32[1,512]{1,0:T(1,128)S(1)}, f32[1,512]{1,0:T(1,128)S(1)}, u32[]{:S(2)}, u32[]{:S(2)}) collective-permute-start(f32[1,512]{1,0:T(1,128)S(1)} %collective-permute-done.24.refs_2_), channel_id=1, source_target_pairs={{0,8},{8,0},{16,24},{24,16},{1,9},{9,1},{17,25},{25,17},{2,10},{10... | collective-permute-start | bytes 6152 | tf_op jit(solution)/shard_map/ppermute | solution.py:293
  157.3 5.0 %collective-permute-start.11 = (f32[1,512]{1,0:T(1,128)S(1)}, f32[1,512]{1,0:T(1,128)S(1)}, u32[]{:S(2)}, u32[]{:S(2)}) collective-permute-start(f32[1,512]{1,0:T(1,128)S(1)} %get-tuple-element.49.refs_0_), channel_id=1, source_target_pairs={{0,8},{8,0},{16,24},{24,16},{1,9},{9,1},{17,25},{25,17},{2,10},{10... | collective-permute-start | bytes 6152 | tf_op jit(solution)/shard_map/ppermute | solution.py:293
  159.7 2.6 %collective-permute-start.13 = (f32[1,512]{1,0:T(1,128)S(1)}, f32[1,512]{1,0:T(1,128)S(1)}, u32[]{:S(2)}, u32[]{:S(2)}) collective-permute-start(f32[1,512]{1,0:T(1,128)S(1)} %collective-permute-done.12.refs_2_), channel_id=1, source_target_pairs={{0,8},{8,0},{16,24},{24,16},{1,9},{9,1},{17,25},{25,17},{2,10},{10... | collective-permute-start | bytes 6152 | tf_op jit(solution)/shard_map/ppermute | solution.py:293
  159.7 2.8 %copy-start = (f32[512,2048]{1,0:T(8,128)S(1)}, f32[512,2048]{1,0:T(8,128)}, u32[]{:S(2)}) copy-start(f32[512,2048]{1,0:T(8,128)} %get-tuple-element.48.step_ref) | copy-start | bytes 12582916
  159.7 5.2 %slice-start = ((s8[10485760]{0:T(1024)(128)(4,1)}), s8[4194304]{0:T(1024)(128)(4,1)S(1)}, s32[]{:S(2)}) async-start(s8[10485760]{0:T(1024)(128)(4,1)} %bitcast.2), calls=%async_computation.2 | async-start | bytes 8388608
  160.7 5.6 %slice-start.1 = ((s8[10485760]{0:T(1024)(128)(4,1)}), s8[4194304]{0:T(1024)(128)(4,1)S(1)}, s32[]{:S(2)}) async-start(s8[10485760]{0:T(1024)(128)(4,1)} %bitcast.2), calls=%async_computation.3 | async-start | bytes 8388608
  160.7 6.2 %slice-start.2 = ((s8[10485760]{0:T(1024)(128)(4,1)}), s8[2097152]{0:T(1024)(128)(4,1)S(1)}, s32[]{:S(2)}) async-start(s8[10485760]{0:T(1024)(128)(4,1)} %bitcast.2), calls=%async_computation.4 | async-start | bytes 4194304

commit v5 on v4

v5 whole, which is shorter than its diff:
```python
import functools

import jax
import jax.numpy as jnp
from jax import lax
from jax.experimental import pallas as pl
from jax.experimental.pallas import tpu as pltpu
from jax.sharding import PartitionSpec as P

beta_one = 0.9
beta_two = 0.95
rate = 0.1
eps_adam = 1e-08
eps_norm = 1e-06


def with_vmem(mebibytes):
    return pltpu.CompilerParams(vmem_limit_bytes=mebibytes * 1024 * 1024)


def row_block(rows, largest=256):
    for block in range(largest, 0, -128):
        if rows % block == 0:
            return block
    return rows


def chunk_plan(totals):
    first = [(which, 0, total) for which, total in enumerate(totals[:-1])]
    up = len(totals) - 1
    block = row_block(totals[up])
    blocks = max(0, (sum(totals) // 2 - sum(totals[:-1])) // block)
    if blocks:
        first.append((up, 0, blocks * block))
    return [first, [(up, blocks * block, totals[up])]]


def ring_order(groups):
    return [*range(0, groups, 2), *range(groups - 1 - groups % 2, 0, -2)]


def ring_place(at, groups):
    return jnp.where(at % 2 == 0, at // 2, groups - 1 - at // 2)


def pack_kernel(plan, groups, at_ref, *refs):
    inputs, outputs = refs[: -len(plan)], refs[-len(plan) :]
    for pieces, out_ref in zip(plan, outputs):
        start = 0
        for which, low, high in pieces:
            ref = inputs[which]
            rows = ref.shape[1] // groups
            for group in range(groups):
                out_ref[group, :, start : start + high - low] = ref[
                    :, group * rows + low : group * rows + high
                ]
            start += high - low


def pack(cotangents, plan, groups, part, place):
    outs = [
        jax.ShapeDtypeStruct(
            (groups, part, sum(high - low for _, low, high in pieces)), jnp.bfloat16
        )
        for pieces in plan
    ]
    return pl.pallas_call(
        functools.partial(pack_kernel, plan, groups),
        grid_spec=pltpu.PrefetchScalarGridSpec(
            num_scalar_prefetch=1,
            grid=(1,),
            in_specs=[
                pl.BlockSpec((part, array.shape[1]), lambda i, at: (at[0], 0))
                for array in cotangents
            ],
            out_specs=[pl.BlockSpec(out.shape, lambda i, at: (0, 0, 0)) for out in outs],
        ),
        out_shape=outs,
        compiler_params=with_vmem(16),
        cost_estimate=pl.CostEstimate(
            flops=0,
            bytes_accessed=4 * part * sum(array.shape[1] for array in cotangents),
            transcendentals=0,
        ),
        name="pack",
    )(place, *(pltpu.with_memory_space_constraint(array, pltpu.HBM) for array in cotangents))


def ring_steps(array, axis):
    groups = lax.axis_size(axis)
    order = ring_order(groups)
    onward = list(zip(order, order[1:] + order[:1]))
    back = [(to, at) for at, to in onward]
    behind, ahead, middle = [array], [array], []

    def step(after):
        one, two = behind[-1], ahead[-1]
        if after is not None:
            one, two, after = lax.optimization_barrier((one, two, after))
        if len(behind) <= (groups - 1) // 2:
            behind.append(lax.ppermute(one, axis, onward))
            ahead.append(lax.ppermute(two, axis, back))
        elif groups % 2 == 0 and not middle:
            half = array.shape[0] // 2
            middle.append(lax.ppermute(one[:half], axis, onward))
            middle.append(lax.ppermute(two[half:], axis, back))
        return after

    def done():
        return [array, *ahead[1:], *middle, *behind[:0:-1]]

    return step, done


def unpack_kernel(count, at_ref, *refs):
    pieces, outputs, order = refs[:count], refs[count:-1], refs[-1]
    groups, part, _ = pieces[0].shape
    for group in range(groups):
        slot = ring_place(group, groups) - ring_place(at_ref[1], groups) + groups
        for turn, piece in enumerate(pieces):
            order[slot % groups * count + (at_ref[0] ^ turn)] = piece[group]
    low = 0
    for out_ref in outputs:
        rows = out_ref.shape[0]
        for start in range(0, rows, 128):
            high = min(start + 128, rows)
            tokens = order[:, :, low + start : low + high].reshape(-1, high - start)
            out_ref[start:high] = tokens.T
        low += rows


def unpack(pieces, row_counts, place):
    groups, part, rows = pieces[0].shape
    tokens = groups * part * len(pieces)
    vmem = pl.BlockSpec(memory_space=pltpu.VMEM)
    return pl.pallas_call(
        functools.partial(unpack_kernel, len(pieces)),
        in_specs=[pl.BlockSpec(memory_space=pltpu.SMEM)] + [vmem] * len(pieces),
        out_specs=[vmem] * len(row_counts),
        out_shape=[pltpu.VMEM((count, tokens), jnp.bfloat16) for count in row_counts],
        scratch_shapes=[pltpu.VMEM((groups * len(pieces), part, rows), jnp.bfloat16)],
        compiler_params=with_vmem(12),
        cost_estimate=pl.CostEstimate(
            flops=0, bytes_accessed=4 * tokens * rows, transcendentals=0
        ),
        name="unpack",
    )(place, *pieces)


def preload_kernel(*refs):
    count = (len(refs) - 3) // 2
    token, sems = refs[-2:]
    outputs = refs[count + 1 :]
    copies = [pltpu.make_async_copy(refs[at], outputs[at], sems.at[at]) for at in range(count)]
    token[...] = jnp.zeros_like(token)
    for copy in copies:
        copy.start()
    for copy in copies:
        copy.wait()


def preload(arrays, after):
    return pl.pallas_call(
        preload_kernel,
        in_specs=[pl.BlockSpec(memory_space=pl.ANY)] * (len(arrays) + 1),
        out_specs=[pl.BlockSpec(memory_space=pltpu.VMEM)] * (len(arrays) + 1),
        out_shape=[pltpu.VMEM(array.shape, array.dtype) for array in arrays]
        + [jax.ShapeDtypeStruct((8, 128), jnp.float32)],
        scratch_shapes=[pltpu.SemaphoreType.DMA((len(arrays),))],
        compiler_params=with_vmem(4),
        cost_estimate=pl.CostEstimate(
            flops=0, bytes_accessed=sum(2 * array.size for array in arrays), transcendentals=0
        ),
        name="preload",
    )(*(pltpu.with_memory_space_constraint(array, pltpu.HBM) for array in arrays), after)


def write_back(buffers, outputs, sems, slot, at):
    return [
        pltpu.make_async_copy(buffer.at[slot, : at.size], out.at[at], sems.at[slot, which])
        for which, (buffer, out) in enumerate(zip(buffers, outputs))
    ]


def over_blocks(count, body):
    if count == 1:
        body(0)
    else:
        pl.loop(0, count)(body)


def update_tile(grad, weight, moment, second):
    first = beta_one * moment.astype(jnp.float32) + (1.0 - beta_one) * grad
    square = beta_two * second.astype(jnp.float32) + (1.0 - beta_two) * grad * grad
    root = square * lax.rsqrt(square) + eps_adam
    inverse = pl.reciprocal(root, approx=True)
    inverse = inverse * (2.0 - root * inverse)
    return first, square, weight.astype(jnp.float32) - rate * first * inverse


def adam_kernel(strip, count_x, cuts, *refs):
    refs = list(refs)
    take = lambda count: [refs.pop(0) for _ in range(count)]
    x_refs = take(count_x)
    ins = [(take(len(cut)), *take(3)) for cut in cuts]
    power_ref = refs.pop(0)
    outs = [take(4) for _ in cuts]
    grads, buffers, power_sum, sems = (refs[0], refs[1]), (refs[2], refs[3]), refs[4], refs[5]
    width = x_refs[0].shape[1]
    strips = width // strip
    base = 0
    for cut, (c_refs, w_ref, m_ref, v_ref), (hi_ref, lo_ref, *moments) in zip(cuts, ins, outs):
        low = 0
        for c_ref, rows in zip(c_refs, cut):
            block = row_block(rows)
            count = rows // block

            def multiply(at, which, c_ref=c_ref, block=block):
                lhs = c_ref[pl.ds(at * block, block), :]
                columns = slice(which * strip, (which + 1) * strip)
                rhs = jnp.concatenate([x_ref[:, columns] for x_ref in x_refs], axis=0)
                grads[which % 2][:block] = jnp.dot(lhs, rhs, preferred_element_type=jnp.float32)

            def one_block(at, low=low, base=base, count=count, block=block, multiply=multiply):
                slot = at % 2
                place = pl.ds(low + at * block, block)
                if count > 2:

                    @pl.when(at >= 2)
                    def _():
                        for copy in write_back(buffers, moments, sems, slot, place):
                            copy.wait()

                for which in range(strips):
                    if which + 1 < strips:
                        multiply(at, which + 1)
                    elif count > 1:
                        multiply(jnp.minimum(at + 1, count - 1), 0)
                    columns = slice(which * strip, (which + 1) * strip)
                    for row in range(0, block, 16):
                        inside = slice(row, row + 16)
                        tile = pl.ds(low + at * block + row, 16)
                        first, square, step = update_tile(
                            grads[which % 2][inside],
                            w_ref[tile, columns],
                            m_ref[tile, columns],
                            v_ref[tile, columns],
                        )
                        buffers[0][slot, inside, columns] = first.astype(jnp.bfloat16)
                        buffers[1][slot, inside, columns] = square.astype(jnp.bfloat16)
                        hi = step.astype(jnp.bfloat16)
                        hi_ref[tile, columns] = hi
                        lo_ref[tile, columns] = (step - hi.astype(jnp.float32)).astype(
                            jnp.bfloat16
                        )
                        power = step[:, :128] * step[:, :128]
                        for lane in range(128, strip, 128):
                            power += step[:, lane : lane + 128] * step[:, lane : lane + 128]
                        if which:
                            power += power_sum[inside]
                        power_sum[inside] = power
                power_ref[:, pl.ds(base + low + at * block, block)] = jnp.sum(
                    power_sum[:block].T, axis=0, keepdims=True
                )
                for copy in write_back(buffers, moments, sems, slot, place):
                    copy.start()

            multiply(0, 0)
            over_blocks(count, one_block)
            for at in range(max(0, count - 2), count):
                place = pl.ds(low + at * block, block)
                for copy in write_back(buffers, moments, sems, at % 2, place):
                    copy.wait()
            low += rows
        base += low


def strip_of(width, largest=512):
    for strip in range(largest, 0, -128):
        if width % (2 * strip) == 0:
            return strip


def adam_pass(x_pieces, cotangents, states):
    width = x_pieces[0].shape[1]
    tokens = cotangents[0][0].shape[1]
    strip = strip_of(width)
    cuts = [[piece.shape[0] for piece in pieces] for pieces in cotangents]
    rows = sum(sum(cut) for cut in cuts)
    block = max(row_block(count) for cut in cuts for count in cut)
    args, aliases, outs = list(x_pieces), {}, []
    for pieces, state in zip(cotangents, states):
        args += pieces
        aliases[len(args)] = len(outs) + 1
        aliases[len(args) + 1] = len(outs) + 2
        args += state
        shape = state[0].shape
        outs += [pltpu.VMEM(shape, jnp.bfloat16)] * 2
        outs += [jax.ShapeDtypeStruct(shape, jnp.bfloat16)] * 2
    vmem = pl.BlockSpec(memory_space=pltpu.VMEM)
    hbm = pl.BlockSpec(memory_space=pl.ANY)
    done = pl.pallas_call(
        functools.partial(adam_kernel, strip, len(x_pieces), cuts),
        in_specs=[vmem] * len(args),
        out_specs=[vmem] + [vmem, vmem, hbm, hbm] * len(states),
        out_shape=[jax.ShapeDtypeStruct((1, rows), jnp.float32), *outs],
        input_output_aliases=aliases,
        scratch_shapes=[
            pltpu.VMEM((block, strip), jnp.float32),
            pltpu.VMEM((block, strip), jnp.float32),
            pltpu.VMEM((2, block, width), jnp.bfloat16),
            pltpu.VMEM((2, block, width), jnp.bfloat16),
            pltpu.VMEM((block, 128), jnp.float32),
            pltpu.SemaphoreType.DMA((2, 2)),
        ],
        compiler_params=with_vmem(12),
        cost_estimate=pl.CostEstimate(
            flops=2 * tokens * rows * width, bytes_accessed=4 * rows * width, transcendentals=0
        ),
        name="adam",
    )(*(pltpu.with_memory_space_constraint(array, pltpu.VMEM) for array in args))
    return done[0], [done[at : at + 4] for at in range(1, len(done), 4)]


def finish_kernel(count, whole_width, matrices, *refs):
    powers, refs = refs[:count], refs[count:]
    parts, outputs, (buffer, sems) = refs[: 2 * matrices], refs[2 * matrices : -2], refs[-2:]
    base = 0
    for which, out_ref in enumerate(outputs):
        hi_ref, lo_ref = parts[2 * which : 2 * which + 2]
        rows, width = hi_ref.shape
        block = row_block(rows)
        total = rows // block

        def one_block(at, base=base, block=block, total=total):
            slot = at % 2
            place = pl.ds(at * block, block)
            if total > 2:

                @pl.when(at >= 2)
                def _():
                    for copy in write_back([buffer], [out_ref], sems, slot, place):
                        copy.wait()

            lanes = pl.ds(base + at * block, block)
            power = powers[0][:, lanes]
            for other in powers[1:]:
                power = power + other[:, lanes]
            scale = 1.0 / jnp.sqrt(power / whole_width + eps_norm)
            scale = jnp.broadcast_to(scale, (128, block)).T
            for row in range(0, block, 16):
                inside = slice(row, row + 16)
                tile = pl.ds(at * block + row, 16)
                for lane in range(0, width, 128):
                    columns = slice(lane, lane + 128)
                    step = hi_ref[tile, columns].astype(jnp.float32)
                    step = step + lo_ref[tile, columns].astype(jnp.float32)
                    buffer[slot, inside, columns] = (step * scale[inside]).astype(jnp.bfloat16)
            for copy in write_back([buffer], [out_ref], sems, slot, place):
                copy.start()

        over_blocks(total, one_block)
        for at in range(max(0, total - 2), total):
            place = pl.ds(at * block, block)
            for copy in write_back([buffer], [out_ref], sems, at % 2, place):
                copy.wait()
        base += rows


def finish_rows(parts, powers, whole_width):
    shapes = [array.shape for array in parts[::2]]
    width = shapes[0][1]
    block = max(row_block(shape[0]) for shape in shapes)
    vmem = pl.BlockSpec(memory_space=pltpu.VMEM)
    return pl.pallas_call(
        functools.partial(finish_kernel, len(powers), whole_width, len(shapes)),
        in_specs=[vmem] * (len(powers) + len(parts)),
        out_specs=[pl.BlockSpec(memory_space=pl.ANY)] * len(shapes),
        out_shape=[jax.ShapeDtypeStruct(shape, jnp.bfloat16) for shape in shapes],
        scratch_shapes=[
            pltpu.VMEM((2, block, width), jnp.bfloat16),
            pltpu.SemaphoreType.DMA((2, 1)),
        ],
        compiler_params=with_vmem(8),
        cost_estimate=pl.CostEstimate(
            flops=sum(2 * rows * width for rows, _ in shapes),
            bytes_accessed=sum(2 * rows * width for rows, _ in shapes),
            transcendentals=0,
        ),
        name="finish",
    )(*powers, *(pltpu.with_memory_space_constraint(array, pltpu.VMEM) for array in parts))


def from_others(array, axis):
    size = lax.axis_size(axis)
    bit = size // 2
    got = {0: array}
    while bit:
        for turn in list(got):
            got[turn ^ bit] = lax.ppermute(got[turn], axis, [(at, at ^ bit) for at in range(size)])
        bit //= 2
    return [got[turn] for turn in range(size)]


def per_device(
    layer_input,
    query_cotangent,
    key_cotangent,
    up_cotangent,
    query_weight,
    key_weight,
    up_weight,
    moment_query,
    moment_key,
    moment_up,
    second_query,
    second_key,
    second_up,
):
    groups = lax.axis_size("dp")
    cols = lax.axis_size("col")
    part = layer_input.shape[0] // cols
    whole_width = layer_input.shape[1] * cols
    states = (
        (query_weight, moment_query, second_query),
        (key_weight, moment_key, second_key),
        (up_weight, moment_up, second_up),
    )
    plan = chunk_plan([state[0].shape[0] for state in states])
    place = jnp.stack([lax.axis_index("col"), lax.axis_index("dp")]).astype(jnp.int32)
    packed = pack((query_cotangent, key_cotangent, up_cotangent), plan, groups, part, place)
    *held, loaded = preload([array for state in states for array in state], packed[0])
    held = [held[at : at + 3] for at in range(0, len(held), 3)]
    step, ring = ring_steps(layer_input, "dp")
    step(None)
    owned = []
    for array in packed:
        if owned:
            array, owned[-1] = lax.optimization_barrier((array, owned[-1]))
        owned.append(lax.all_to_all(array, "dp", split_axis=0, concat_axis=0, tiled=True))
        owned[-1], loaded = step((owned[-1], loaded))
    for _ in range(groups):
        step(None)
    cotangents = [[], [], []]
    for array, pieces in zip(owned, plan):
        every = unpack(from_others(array, "col"), [high - low for _, low, high in pieces], place)
        for (which, _, _), cotangent in zip(pieces, every):
            cotangents[which].append(cotangent)
    updated = [None] * 3
    moments = [None] * 3
    passes = []
    for group in ((2,), (0, 1)):
        power, made = adam_pass(
            ring(), [cotangents[which] for which in group], [held[which] for which in group]
        )
        passes.append((group, from_others(power, "col"), made))
    for group, powers, made in passes:
        parts = [array for done in made for array in done[:2]]
        for which, done, array in zip(group, made, finish_rows(parts, powers, whole_width)):
            updated[which] = array
            moments[which] = done[2:]
    return (*updated, *(done[0] for done in moments), *(done[1] for done in moments))


def solution(mesh):
    tokens_split = P("dp", None)
    split = P("dp", "col")
    return jax.shard_map(
        per_device,
        mesh=mesh,
        in_specs=(split, *(tokens_split,) * 3, *(split,) * 9),
        out_specs=(split,) * 9,
        check_vma=False,
    )
```

time: 171 us -> 164 us (0.959)
  local copies, waits for them, and re-layouts: 6.2 us -> 0.04 us
  waiting for transfers between devices: 64.8 us -> 69.6 us
  Pallas kernels: 63.8 us -> 59.2 us
    ppermute x18 -> x12, waiting for transfers between devices: 3.45 us -> 26.3 us  [from_others(): lax.ppermute(got[turn], axis, [(at, at ^ bit) for at in range(size)])]
    ppermute x3, waiting for transfers between devices: 22 us -> 0.01 us  [step(): behind.append(lax.ppermute(one, axis, onward))]
    ppermute x3, waiting for transfers between devices: 33.4 us -> 43.2 us  [step(): ahead.append(lax.ppermute(two, axis, back))]
    unnamed x32 -> x2, local copies, waits for them, and re-layouts: 6.17 us -> 0.01 us
    ppermute x1, starting transfers between devices: 0.33 us -> 5.03 us  [step(): middle.append(lax.ppermute(one[:half], axis, onward))]
    ppermute x1, waiting for transfers between devices: 4.62 us -> 0.01 us  [step(): middle.append(lax.ppermute(two[half:], axis, back))]
    pallas_call x9 -> x5, Pallas kernels: 57.8 us -> 53.4 us  [the longest x2 35.1 us: adam_pass(): pl.pallas_call(functools.partial(adam_kernel, strip, len(x_pieces), cuts)...]
    ppermute x18 -> x12, starting transfers between devices: 9.11 us -> 5.95 us  [from_others(): lax.ppermute(got[turn], axis, [(at, at ^ bit) for at in range(size)])]
  transfers between devices with their start and end apart: 28 -> 22, of which waited for: 9 -> 6; matrix products, arithmetic and copies ran while one was open for 0% -> 0% of each run, Pallas kernels for 20% -> 16%
where the time goes in v5:
time: 164 us
  waiting for transfers between devices  69.6 us (42%)
  Pallas kernels  59.2 us (36%)
  starting transfers between devices  34.3 us (21%)
    ppermute x3, waiting for transfers between devices, step(): ahead.append(lax.ppermute(two, axis, back))  43.2 us
    pallas_call x2, Pallas kernels, adam_pass(): pl.pallas_call(functools.partial(adam_kernel, strip, len(x_pieces), cuts)...  35.1 us
    ppermute x12, waiting for transfers between devices, from_others(): lax.ppermute(got[turn], axis, [(at, at ^ bit) for at in range(size)])  26.3 us
    all_to_all x2, starting transfers between devices, per_device(): lax.all_to_all(array, 'dp', split_axis=0, concat_axis=0, tiled=True)  14.1 us
    pallas_call x1, Pallas kernels, preload(): pl.pallas_call(preload_kernel, in_specs=[pl.BlockSpec(memory_space=pl.ANY...  10.3 us
    pallas_call x2, Pallas kernels, finish_rows(): pl.pallas_call(functools.partial(finish_kernel, len(powers), whole_width,...  8.09 us
    ppermute x12, starting transfers between devices, from_others(): lax.ppermute(got[turn], axis, [(at, at ^ bit) for at in range(size)])  5.95 us
    ppermute x3, starting transfers between devices, step(): behind.append(lax.ppermute(one, axis, onward))  5.06 us
  transfers between devices with their start and end apart: 22, of which 6 were waited for; matrix products, arithmetic and copies ran while one was open for 0% of the time, Pallas kernels for 16%

profile of v5, /device:TPU:0, one launch (start us, length us, event | category | flops | bytes accessed | tf_op | source)
XLA Modules:
  0.0 164.1 jit_solution(216125890728650747)
XLA Ops:
  0.7 0.1 pad_add_fusion.at_ref
  0.7 2.9 %pack.1 = (bf16[8,32,1152]{2,1,0:T(8,128)(2,1)}, bf16[8,32,1280]{2,1,0:T(8,128)(2,1)}) custom-call(s32[2]{0:T(128)S(1)} %pad_add_fusion.at_ref, bf16[128,4096]{1,0:T(8,128)(2,1)} %refs_0_.4, bf16[128,1024]{1,0:T(8,128)(2,1)} %refs_1_.2, bf16[128,14336]{1,0:T(8,128)(2,1)} %refs_2_.2), custom_call_target="tpu_custom_call" | custom-call | bytes 2490368 | tf_op jit(solution)/shard_map/pack/pallas_call | solution.py:67
  3.6 7.3 %all-to-all-start = ((bf16[8,32,1152]{2,1,0:T(8,128)(2,1)}), bf16[8,32,1152]{2,1,0:T(8,128)(2,1)S(1)}, u32[]{:S(2)}, u32[]{:S(2)}) async-start(bf16[8,32,1152]{2,1,0:T(8,128)(2,1)} %get-tuple-element.47.refs_9_), calls=%async_computation | async-start | bytes 1179648 | tf_op jit(solution)/shard_map/all_to_all | solution.py:440
  10.9 2.0 %collective-permute-start = (bf16[128,2048]{1,0:T(8,128)(2,1)S(1)}, bf16[128,2048]{1,0:T(8,128)(2,1)S(1)}, u32[]{:S(2)}, u32[]{:S(2)}) collective-permute-start(bf16[128,2048]{1,0:T(8,128)(2,1)S(1)} %copy-done), channel_id=1, source_target_pairs={{2,0},{4,2},{6,4},{7,6},{5,7},{3,5},{1,3},{0,1},{10,8},{12,10},{14... | collective-permute-start | bytes 1572872 | tf_op jit(solution)/shard_map/ppermute | solution.py:102
  13.0 0.1 collective-permute-start.1
  13.0 21.0 %collective-permute-done.refs_1_ = bf16[128,2048]{1,0:T(8,128)(2,1)S(1)} collective-permute-done((bf16[128,2048]{1,0:T(8,128)(2,1)S(1)}, bf16[128,2048]{1,0:T(8,128)(2,1)S(1)}, u32[]{:S(2)}, u32[]{:S(2)}) %collective-permute-start) | collective-permute-done | bytes 524320 | tf_op jit(solution)/shard_map/ppermute | solution.py:102
  34.0 0.0 collective-permute-done.1.refs_8_
  34.0 0.0 all-to-all-done.refs_0_
  34.0 6.8 %all-to-all-start.1 = ((bf16[8,32,1280]{2,1,0:T(8,128)(2,1)}), bf16[8,32,1280]{2,1,0:T(8,128)(2,1)S(1)}, u32[]{:S(2)}, u32[]{:S(2)}) async-start(bf16[8,32,1280]{2,1,0:T(8,128)(2,1)} %get-tuple-element.52), calls=%async_computation.1 | async-start | bytes 1310720 | tf_op jit(solution)/shard_map/all_to_all | solution.py:440
  40.8 2.0 %collective-permute-start.2 = (bf16[128,2048]{1,0:T(8,128)(2,1)S(1)}, bf16[128,2048]{1,0:T(8,128)(2,1)S(1)}, u32[]{:S(2)}, u32[]{:S(2)}) collective-permute-start(bf16[128,2048]{1,0:T(8,128)(2,1)S(1)} %collective-permute-done.refs_1_), channel_id=1, source_target_pairs={{2,0},{4,2},{6,4},{7,6},{5,7},{3,5},{1,3},{0,1},{10,8},{12,10},{14... | collective-permute-start | bytes 1572872 | tf_op jit(solution)/shard_map/ppermute | solution.py:102
  42.9 0.0 collective-permute-start.3
  42.9 22.2 %collective-permute-done.2.refs_2_ = bf16[128,2048]{1,0:T(8,128)(2,1)S(1)} collective-permute-done((bf16[128,2048]{1,0:T(8,128)(2,1)S(1)}, bf16[128,2048]{1,0:T(8,128)(2,1)S(1)}, u32[]{:S(2)}, u32[]{:S(2)}) %collective-permute-start.2) | collective-permute-done | bytes 524320 | tf_op jit(solution)/shard_map/ppermute | solution.py:102
  65.1 0.0 collective-permute-done.3.refs_7_
  65.2 0.0 all-to-all-done.1.refs_0_
  65.2 1.5 collective-permute-start.15
  66.6 0.5 collective-permute-start.9
  67.2 5.0 %collective-permute-start.5 = (bf16[128,2048]{1,0:T(8,128)(2,1)}, bf16[128,2048]{1,0:T(8,128)(2,1)S(1)}, u32[]{:S(2)}, u32[]{:S(2)}) collective-permute-start(bf16[128,2048]{1,0:T(8,128)(2,1)} %collective-permute-done.3.refs_7_), channel_id=1, source_target_pairs={{0,2},{2,4},{4,6},{6,7},{7,5},{5,3},{3,1},{1,0},{8,10},{10,12},{12... | collective-permute-start | bytes 1572872 | tf_op jit(solution)/shard_map/ppermute | solution.py:101
  72.2 0.0 collective-permute-start.8
  72.2 0.0 collective-permute-start.4
  72.2 21.1 %collective-permute-done.9.refs_2_ = bf16[8,32,1152]{2,1,0:T(8,128)(2,1)S(1)} collective-permute-done((bf16[8,32,1152]{2,1,0:T(8,128)(2,1)S(1)}, bf16[8,32,1152]{2,1,0:T(8,128)(2,1)S(1)}, u32[]{:S(2)}, u32[]{:S(2)}) %collective-permute-start.9) | collective-permute-done | bytes 589856 | tf_op jit(solution)/shard_map/ppermute | solution.py:400
  93.3 0.0 collective-permute-start.14
  93.3 0.0 collective-permute-done.15.refs_2_
  93.3 0.5 collective-permute-start.16
  93.8 0.0 collective-permute-done.5.refs_6_
  93.8 0.1 collective-permute-start.10
  93.9 0.0 collective-permute-done.4.refs_3_
  93.9 5.0 %collective-permute-start.6 = (bf16[64,2048]{1,0:T(8,128)(2,1)S(1)}, bf16[64,2048]{1,0:T(8,128)(2,1)S(1)}, u32[]{:S(2)}, u32[]{:S(2)}) collective-permute-start(bf16[64,2048]{1,0:T(8,128)(2,1)S(1)} %slice.8), channel_id=1, source_target_pairs={{0,2},{2,4},{4,6},{6,7},{7,5},{5,3},{3,1},{1,0},{8,10},{10,12},{12... | collective-permute-start | bytes 786440 | tf_op jit(solution)/shard_map/ppermute | solution.py:105
  99.0 0.1 collective-permute-start.7
  99.0 10.3 %preload.1 = (bf16[512,2048]{1,0:T(8,128)(2,1)S(1)}, bf16[512,2048]{1,0:T(8,128)(2,1)S(1)}, bf16[512,2048]{1,0:T(8,128)(2,1)S(1)}, bf16[128,2048]{1,0:T(8,128)(2...) custom-call(bf16[512,2048]{1,0:T(8,128)(2,1)} %refs_0_.5, ...), custom_call_target="tpu_custom_call" | custom-call | bytes 29884416 | tf_op jit(solution)/shard_map/preload/pallas_call | solution.py:163
  109.3 0.0 collective-permute-done.10.refs_3_
  109.3 1.4 unpack.2
  110.7 1.5 unpack.3.refs_10_
  112.2 0.0 collective-permute-done.6.refs_4_
  112.2 0.0 collective-permute-done.7.refs_5_
  112.2 24.3 %adam.3 = (f32[1,1792]{1,0:T(1,128)S(1)}, bf16[1792,2048]{1,0:T(8,128)(2,1)S(1)}, bf16[1792,2048]{1,0:T(8,128)(2,1)S(1)}, bf16[1792,2048]{1,0:T(8,128)(2,1)}, bf16[1792,2048]{1,0:T(8,128)(2,1)}) custom-call(bf16[128,2048]{1,0:T(8,128)(2,1)S(1)} %copy-done, ...), custom_call_target="tpu_custom_call", output_to_operand_aliasing={{1}: (11, {}), {2}: (12, {})} | custom-call | flops 7516192768 | bytes 14680064 | tf_op jit(solution)/shard_map/adam/pallas_call | solution.py:302
  136.5 1.6 collective-permute-start.18
  138.1 2.1 %collective-permute-done.18.refs_2_ = f32[1,1792]{1,0:T(1,128)S(1)} collective-permute-done((f32[1,1792]{1,0:T(1,128)S(1)}, f32[1,1792]{1,0:T(1,128)S(1)}, u32[]{:S(2)}, u32[]{:S(2)}) %collective-permute-start.18) | collective-permute-done | bytes 7200 | tf_op jit(solution)/shard_map/ppermute | solution.py:400
  140.2 0.0 collective-permute-start.19
  140.2 10.8 %adam.2 = (f32[1,640]{1,0:T(1,128)S(1)}, bf16[512,2048]{1,0:T(8,128)(2,1)S(1)}, bf16[512,2048]{1,0:T(8,128)(2,1)S(1)}, bf16[512,2048]{1,0:T(8,128)(2,1)}, bf16[5...) custom-call(bf16[128,2048]{1,0:T(8,128)(2,1)S(1)} %copy-done, ...), custom_call_target="tpu_custom_call", output_to_operand_aliasing={{1}: (10, {}), {2}: (11, {}), {5}: (14, {}), {6}: (15, {})} | custom-call | flops 2684354560 | bytes 5242880 | tf_op jit(solution)/shard_map/adam/pallas_call | solution.py:302
  151.0 1.6 collective-permute-start.12
  152.6 0.2 collective-permute-start.11
  152.8 1.9 %collective-permute-done.12.refs_2_ = f32[1,640]{1,0:T(1,128)S(1)} collective-permute-done((f32[1,640]{1,0:T(1,128)S(1)}, f32[1,640]{1,0:T(1,128)S(1)}, u32[]{:S(2)}, u32[]{:S(2)}) %collective-permute-start.12) | collective-permute-done | bytes 2592 | tf_op jit(solution)/shard_map/ppermute | solution.py:400
  154.7 0.0 collective-permute-start.13
  154.7 0.0 collective-permute-done.11.refs_1_
  154.7 1.2 collective-permute-done.13.refs_3_
  155.8 2.7 %finish.2 = (bf16[512,2048]{1,0:T(8,128)(2,1)}, bf16[128,2048]{1,0:T(8,128)(2,1)}) custom-call(f32[1,640]{1,0:T(1,128)S(1)} %get-tuple-element.64.refs_0_, f32[1,640]{1,0:T(1,128)S(1)} %collective-permute-done.11.refs_1_, f32[1,640]{1,0:T(1,128)S(1)} %collective-permute-done.12.refs_2_, f32[1,640]{1,0:T(1,128)S(1)} %collective-permute-done.13.refs_3_, ...), custom_call_target="tpu_custom_call" | custom-call | flops 2621440 | bytes 2621440 | tf_op jit(solution)/shard_map/finish/pallas_call | solution.py:375
  158.6 0.0 collective-permute-done.19.refs_3_
  158.6 5.4 %finish.3 = bf16[1792,2048]{1,0:T(8,128)(2,1)} custom-call(f32[1,1792]{1,0:T(1,128)S(1)} %get-tuple-element.76.refs_0_, f32[1,1792]{1,0:T(1,128)S(1)} %collective-permute-done.17.refs_1_, f32[1,1792]{1,0:T(1,128)S(1)} %collective-permute-done.18.refs_2_, f32[1,1792]{1,0:T(1,128)S(1)} %collective-permute-done.19.refs_3_, ...), custom_call_target="tpu_custom_call" | custom-call | flops 7340032 | bytes 7340032 | tf_op jit(solution)/shard_map/finish/pallas_call | solution.py:375
  (9 shorter events, 0.1 us)
Async XLA Ops:
  0.6 10.3 %copy-start = (bf16[128,2048]{1,0:T(8,128)(2,1)S(1)}, bf16[128,2048]{1,0:T(8,128)(2,1)}, u32[]{:S(2)}) copy-start(bf16[128,2048]{1,0:T(8,128)(2,1)} %refs_0_.7) | copy-start | bytes 1572868
  3.6 30.4 %all-to-all-start = ((bf16[8,32,1152]{2,1,0:T(8,128)(2,1)}), bf16[8,32,1152]{2,1,0:T(8,128)(2,1)S(1)}, u32[]{:S(2)}, u32[]{:S(2)}) async-start(bf16[8,32,1152]{2,1,0:T(8,128)(2,1)} %get-tuple-element.47.refs_9_), calls=%async_computation | async-start | bytes 1179648 | tf_op jit(solution)/shard_map/all_to_all | solution.py:440
  10.9 23.1 %collective-permute-start = (bf16[128,2048]{1,0:T(8,128)(2,1)S(1)}, bf16[128,2048]{1,0:T(8,128)(2,1)S(1)}, u32[]{:S(2)}, u32[]{:S(2)}) collective-permute-start(bf16[128,2048]{1,0:T(8,128)(2,1)S(1)} %copy-done), channel_id=1, source_target_pairs={{2,0},{4,2},{6,4},{7,6},{5,7},{3,5},{1,3},{0,1},{10,8},{12,10},{14... | collective-permute-start | bytes 1572872 | tf_op jit(solution)/shard_map/ppermute | solution.py:102
  13.0 21.0 %collective-permute-start.1 = (bf16[128,2048]{1,0:T(8,128)(2,1)S(1)}, bf16[128,2048]{1,0:T(8,128)(2,1)S(1)}, u32[]{:S(2)}, u32[]{:S(2)}) collective-permute-start(bf16[128,2048]{1,0:T(8,128)(2,1)S(1)} %copy-done), channel_id=1, source_target_pairs={{0,2},{2,4},{4,6},{6,7},{7,5},{5,3},{3,1},{1,0},{8,10},{10,12},{12... | collective-permute-start | bytes 1572872 | tf_op jit(solution)/shard_map/ppermute | solution.py:101
  34.0 31.2 %all-to-all-start.1 = ((bf16[8,32,1280]{2,1,0:T(8,128)(2,1)}), bf16[8,32,1280]{2,1,0:T(8,128)(2,1)S(1)}, u32[]{:S(2)}, u32[]{:S(2)}) async-start(bf16[8,32,1280]{2,1,0:T(8,128)(2,1)} %get-tuple-element.52), calls=%async_computation.1 | async-start | bytes 1310720 | tf_op jit(solution)/shard_map/all_to_all | solution.py:440
  40.8 24.3 %collective-permute-start.2 = (bf16[128,2048]{1,0:T(8,128)(2,1)S(1)}, bf16[128,2048]{1,0:T(8,128)(2,1)S(1)}, u32[]{:S(2)}, u32[]{:S(2)}) collective-permute-start(bf16[128,2048]{1,0:T(8,128)(2,1)S(1)} %collective-permute-done.refs_1_), channel_id=1, source_target_pairs={{2,0},{4,2},{6,4},{7,6},{5,7},{3,5},{1,3},{0,1},{10,8},{12,10},{14... | collective-permute-start | bytes 1572872 | tf_op jit(solution)/shard_map/ppermute | solution.py:102
  42.9 22.3 %collective-permute-start.3 = (bf16[128,2048]{1,0:T(8,128)(2,1)S(1)}, bf16[128,2048]{1,0:T(8,128)(2,1)}, u32[]{:S(2)}, u32[]{:S(2)}) collective-permute-start(bf16[128,2048]{1,0:T(8,128)(2,1)S(1)} %collective-permute-done.1.refs_8_), channel_id=1, source_target_pairs={{0,2},{2,4},{4,6},{6,7},{7,5},{5,3},{3,1},{1,0},{8,10},{10,12},{12... | collective-permute-start | bytes 1572872 | tf_op jit(solution)/shard_map/ppermute | solution.py:101
  65.2 28.1 %collective-permute-start.15 = (bf16[8,32,1280]{2,1,0:T(8,128)(2,1)S(1)}, bf16[8,32,1280]{2,1,0:T(8,128)(2,1)S(1)}, u32[]{:S(2)}, u32[]{:S(2)}) collective-permute-start(bf16[8,32,1280]{2,1,0:T(8,128)(2,1)S(1)} %all-to-all-done.1.refs_0_), channel_id=1, source_target_pairs={{0,16},{8,24},{16,0},{24,8},{1,17},{9,25},{17,1},{25,9},{2,18},{10... | collective-permute-start | bytes 1966088 | tf_op jit(solution)/shard_map/ppermute | solution.py:400
  66.6 26.6 %collective-permute-start.9 = (bf16[8,32,1152]{2,1,0:T(8,128)(2,1)S(1)}, bf16[8,32,1152]{2,1,0:T(8,128)(2,1)S(1)}, u32[]{:S(2)}, u32[]{:S(2)}) collective-permute-start(bf16[8,32,1152]{2,1,0:T(8,128)(2,1)S(1)} %all-to-all-done.refs_0_), channel_id=1, source_target_pairs={{0,16},{8,24},{16,0},{24,8},{1,17},{9,25},{17,1},{25,9},{2,18},{10... | collective-permute-start | bytes 1769480 | tf_op jit(solution)/shard_map/ppermute | solution.py:400
  67.2 26.6 %collective-permute-start.5 = (bf16[128,2048]{1,0:T(8,128)(2,1)}, bf16[128,2048]{1,0:T(8,128)(2,1)S(1)}, u32[]{:S(2)}, u32[]{:S(2)}) collective-permute-start(bf16[128,2048]{1,0:T(8,128)(2,1)} %collective-permute-done.3.refs_7_), channel_id=1, source_target_pairs={{0,2},{2,4},{4,6},{6,7},{7,5},{5,3},{3,1},{1,0},{8,10},{10,12},{12... | collective-permute-start | bytes 1572872 | tf_op jit(solution)/shard_map/ppermute | solution.py:101
  72.2 26.8 %collective-permute-start.8 = (bf16[8,32,1152]{2,1,0:T(8,128)(2,1)S(1)}, bf16[8,32,1152]{2,1,0:T(8,128)(2,1)S(1)}, u32[]{:S(2)}, u32[]{:S(2)}) collective-permute-start(bf16[8,32,1152]{2,1,0:T(8,128)(2,1)S(1)} %all-to-all-done.refs_0_), channel_id=1, source_target_pairs={{0,8},{8,0},{16,24},{24,16},{1,9},{9,1},{17,25},{25,17},{2,10},{10... | collective-permute-start | bytes 1769480 | tf_op jit(solution)/shard_map/ppermute | solution.py:400
  72.2 21.7 %collective-permute-start.4 = (bf16[128,2048]{1,0:T(8,128)(2,1)S(1)}, bf16[128,2048]{1,0:T(8,128)(2,1)S(1)}, u32[]{:S(2)}, u32[]{:S(2)}) collective-permute-start(bf16[128,2048]{1,0:T(8,128)(2,1)S(1)} %collective-permute-done.2.refs_2_), channel_id=1, source_target_pairs={{2,0},{4,2},{6,4},{7,6},{5,7},{3,5},{1,3},{0,1},{10,8},{12,10},{14... | collective-permute-start | bytes 1572872 | tf_op jit(solution)/shard_map/ppermute | solution.py:102
  93.3 17.4 %collective-permute-start.14 = (bf16[8,32,1280]{2,1,0:T(8,128)(2,1)S(1)}, bf16[8,32,1280]{2,1,0:T(8,128)(2,1)S(1)}, u32[]{:S(2)}, u32[]{:S(2)}) collective-permute-start(bf16[8,32,1280]{2,1,0:T(8,128)(2,1)S(1)} %all-to-all-done.1.refs_0_), channel_id=1, source_target_pairs={{0,8},{8,0},{16,24},{24,16},{1,9},{9,1},{17,25},{25,17},{2,10},{10... | collective-permute-start | bytes 1966088 | tf_op jit(solution)/shard_map/ppermute | solution.py:400
  93.3 17.4 %collective-permute-start.16 = (bf16[8,32,1280]{2,1,0:T(8,128)(2,1)S(1)}, bf16[8,32,1280]{2,1,0:T(8,128)(2,1)S(1)}, u32[]{:S(2)}, u32[]{:S(2)}) collective-permute-start(bf16[8,32,1280]{2,1,0:T(8,128)(2,1)S(1)} %collective-permute-done.15.refs_2_), channel_id=1, source_target_pairs={{0,8},{8,0},{16,24},{24,16},{1,9},{9,1},{17,25},{25,17},{2,10},{10... | collective-permute-start | bytes 1966088 | tf_op jit(solution)/shard_map/ppermute | solution.py:400
  93.8 15.5 %collective-permute-start.10 = (bf16[8,32,1152]{2,1,0:T(8,128)(2,1)S(1)}, bf16[8,32,1152]{2,1,0:T(8,128)(2,1)S(1)}, u32[]{:S(2)}, u32[]{:S(2)}) collective-permute-start(bf16[8,32,1152]{2,1,0:T(8,128)(2,1)S(1)} %collective-permute-done.9.refs_2_), channel_id=1, source_target_pairs={{0,8},{8,0},{16,24},{24,16},{1,9},{9,1},{17,25},{25,17},{2,10},{10... | collective-permute-start | bytes 1769480 | tf_op jit(solution)/shard_map/ppermute | solution.py:400
  93.9 18.3 %collective-permute-start.6 = (bf16[64,2048]{1,0:T(8,128)(2,1)S(1)}, bf16[64,2048]{1,0:T(8,128)(2,1)S(1)}, u32[]{:S(2)}, u32[]{:S(2)}) collective-permute-start(bf16[64,2048]{1,0:T(8,128)(2,1)S(1)} %slice.8), channel_id=1, source_target_pairs={{0,2},{2,4},{4,6},{6,7},{7,5},{5,3},{3,1},{1,0},{8,10},{10,12},{12... | collective-permute-start | bytes 786440 | tf_op jit(solution)/shard_map/ppermute | solution.py:105
  99.0 13.2 %collective-permute-start.7 = (bf16[64,2048]{1,0:T(8,128)(2,1)S(1)}, bf16[64,2048]{1,0:T(8,128)(2,1)S(1)}, u32[]{:S(2)}, u32[]{:S(2)}) collective-permute-start(bf16[64,2048]{1,0:T(8,128)(2,1)S(1)} %slice.9), channel_id=1, source_target_pairs={{2,0},{4,2},{6,4},{7,6},{5,7},{3,5},{1,3},{0,1},{10,8},{12,10},{14... | collective-permute-start | bytes 786440 | tf_op jit(solution)/shard_map/ppermute | solution.py:106
  136.5 3.7 %collective-permute-start.18 = (f32[1,1792]{1,0:T(1,128)S(1)}, f32[1,1792]{1,0:T(1,128)S(1)}, u32[]{:S(2)}, u32[]{:S(2)}) collective-permute-start(f32[1,1792]{1,0:T(1,128)S(1)} %get-tuple-element.76.refs_0_), channel_id=1, source_target_pairs={{0,16},{8,24},{16,0},{24,8},{1,17},{9,25},{17,1},{25,9},{2,18},{10... | collective-permute-start | bytes 21512 | tf_op jit(solution)/shard_map/ppermute | solution.py:400
  138.1 20.5 %collective-permute-start.17 = (f32[1,1792]{1,0:T(1,128)S(1)}, f32[1,1792]{1,0:T(1,128)S(1)}, u32[]{:S(2)}, u32[]{:S(2)}) collective-permute-start(f32[1,1792]{1,0:T(1,128)S(1)} %get-tuple-element.76.refs_0_), channel_id=1, source_target_pairs={{0,8},{8,0},{16,24},{24,16},{1,9},{9,1},{17,25},{25,17},{2,10},{10... | collective-permute-start | bytes 21512 | tf_op jit(solution)/shard_map/ppermute | solution.py:400
  140.2 18.3 %collective-permute-start.19 = (f32[1,1792]{1,0:T(1,128)S(1)}, f32[1,1792]{1,0:T(1,128)S(1)}, u32[]{:S(2)}, u32[]{:S(2)}) collective-permute-start(f32[1,1792]{1,0:T(1,128)S(1)} %collective-permute-done.18.refs_2_), channel_id=1, source_target_pairs={{0,8},{8,0},{16,24},{24,16},{1,9},{9,1},{17,25},{25,17},{2,10},{10... | collective-permute-start | bytes 21512 | tf_op jit(solution)/shard_map/ppermute | solution.py:400
  151.0 3.7 %collective-permute-start.12 = (f32[1,640]{1,0:T(1,128)S(1)}, f32[1,640]{1,0:T(1,128)S(1)}, u32[]{:S(2)}, u32[]{:S(2)}) collective-permute-start(f32[1,640]{1,0:T(1,128)S(1)} %get-tuple-element.64.refs_0_), channel_id=1, source_target_pairs={{0,16},{8,24},{16,0},{24,8},{1,17},{9,25},{17,1},{25,9},{2,18},{10... | collective-permute-start | bytes 7688 | tf_op jit(solution)/shard_map/ppermute | solution.py:400
  152.6 2.1 %collective-permute-start.11 = (f32[1,640]{1,0:T(1,128)S(1)}, f32[1,640]{1,0:T(1,128)S(1)}, u32[]{:S(2)}, u32[]{:S(2)}) collective-permute-start(f32[1,640]{1,0:T(1,128)S(1)} %get-tuple-element.64.refs_0_), channel_id=1, source_target_pairs={{0,8},{8,0},{16,24},{24,16},{1,9},{9,1},{17,25},{25,17},{2,10},{10... | collective-permute-start | bytes 7688 | tf_op jit(solution)/shard_map/ppermute | solution.py:400
  154.7 1.2 collective-permute-start.13

commit v6 on v5

--- a/solution.py
+++ b/solution.py
@@ -93,10 +93,11 @@
     back = [(to, at) for at, to in onward]
     behind, ahead, middle = [array], [array], []
 
-    def step(after):
+    def step(after=()):
         one, two = behind[-1], ahead[-1]
-        if after is not None:
-            one, two, after = lax.optimization_barrier((one, two, after))
+        if after:
+            one, two = join((one, two), after)
+            behind[-1], ahead[-1] = one, two
         if len(behind) <= (groups - 1) // 2:
             behind.append(lax.ppermute(one, axis, onward))
             ahead.append(lax.ppermute(two, axis, back))
@@ -104,7 +105,7 @@
             half = array.shape[0] // 2
             middle.append(lax.ppermute(one[:half], axis, onward))
             middle.append(lax.ppermute(two[half:], axis, back))
-        return after
+        return behind[-1], ahead[-1]
 
     def done():
         return [array, *ahead[1:], *middle, *behind[:0:-1]]
@@ -147,10 +148,28 @@
     )(place, *pieces)
 
 
+def join_kernel(*refs):
+    pass
+
+
+def join(arrays, after):
+    count = len(arrays)
+    hbm = pl.BlockSpec(memory_space=pl.ANY)
+    return pl.pallas_call(
+        join_kernel,
+        in_specs=[hbm] * (count + len(after)),
+        out_specs=[hbm] * count,
+        out_shape=[jax.ShapeDtypeStruct(array.shape, array.dtype) for array in arrays],
+        input_output_aliases={at: at for at in range(count)},
+        compiler_params=with_vmem(1),
+        name="join",
+    )(*arrays, *after)
+
+
 def preload_kernel(*refs):
-    count = (len(refs) - 3) // 2
+    count = (len(refs) - 2) // 2
     token, sems = refs[-2:]
-    outputs = refs[count + 1 :]
+    outputs = refs[count:]
     copies = [pltpu.make_async_copy(refs[at], outputs[at], sems.at[at]) for at in range(count)]
     token[...] = jnp.zeros_like(token)
     for copy in copies:
@@ -159,10 +178,10 @@
         copy.wait()
 
 
-def preload(arrays, after):
+def preload(arrays):
     return pl.pallas_call(
         preload_kernel,
-        in_specs=[pl.BlockSpec(memory_space=pl.ANY)] * (len(arrays) + 1),
+        in_specs=[pl.BlockSpec(memory_space=pl.ANY)] * len(arrays),
         out_specs=[pl.BlockSpec(memory_space=pltpu.VMEM)] * (len(arrays) + 1),
         out_shape=[pltpu.VMEM(array.shape, array.dtype) for array in arrays]
         + [jax.ShapeDtypeStruct((8, 128), jnp.float32)],
@@ -172,7 +191,7 @@
             flops=0, bytes_accessed=sum(2 * array.size for array in arrays), transcendentals=0
         ),
         name="preload",
-    )(*(pltpu.with_memory_space_constraint(array, pltpu.HBM) for array in arrays), after)
+    )(*(pltpu.with_memory_space_constraint(array, pltpu.HBM) for array in arrays))
 
 
 def write_back(buffers, outputs, sems, slot, at):
@@ -192,8 +211,8 @@
 def update_tile(grad, weight, moment, second):
     first = beta_one * moment.astype(jnp.float32) + (1.0 - beta_one) * grad
     square = beta_two * second.astype(jnp.float32) + (1.0 - beta_two) * grad * grad
-    root = square * lax.rsqrt(square) + eps_adam
-    inverse = pl.reciprocal(root, approx=True)
+    inverse = lax.rsqrt(square)
+    root = square * inverse + eps_adam
     inverse = inverse * (2.0 - root * inverse)
     return first, square, weight.astype(jnp.float32) - rate * first * inverse
 
@@ -275,7 +294,7 @@
         base += low
 
 
-def strip_of(width, largest=512):
+def strip_of(width, largest=256):
     for strip in range(largest, 0, -128):
         if width % (2 * strip) == 0:
             return strip
@@ -325,19 +344,20 @@
 def finish_kernel(count, whole_width, matrices, *refs):
     powers, refs = refs[:count], refs[count:]
     parts, outputs, (buffer, sems) = refs[: 2 * matrices], refs[2 * matrices : -2], refs[-2:]
+    slots = buffer.shape[0]
     base = 0
     for which, out_ref in enumerate(outputs):
         hi_ref, lo_ref = parts[2 * which : 2 * which + 2]
         rows, width = hi_ref.shape
-        block = row_block(rows)
+        block = row_block(rows, 128)
         total = rows // block
 
         def one_block(at, base=base, block=block, total=total):
-            slot = at % 2
+            slot = at % slots
             place = pl.ds(at * block, block)
-            if total > 2:
-
-                @pl.when(at >= 2)
+            if total > slots:
+
+                @pl.when(at >= slots)
                 def _():
                     for copy in write_back([buffer], [out_ref], sems, slot, place):
                         copy.wait()
@@ -360,9 +380,9 @@
                 copy.start()
 
         over_blocks(total, one_block)
-        for at in range(max(0, total - 2), total):
+        for at in range(max(0, total - slots), total):
             place = pl.ds(at * block, block)
-            for copy in write_back([buffer], [out_ref], sems, at % 2, place):
+            for copy in write_back([buffer], [out_ref], sems, at % slots, place):
                 copy.wait()
         base += rows
 
@@ -370,7 +390,7 @@
 def finish_rows(parts, powers, whole_width):
     shapes = [array.shape for array in parts[::2]]
     width = shapes[0][1]
-    block = max(row_block(shape[0]) for shape in shapes)
+    block = max(row_block(shape[0], 128) for shape in shapes)
     vmem = pl.BlockSpec(memory_space=pltpu.VMEM)
     return pl.pallas_call(
         functools.partial(finish_kernel, len(powers), whole_width, len(shapes)),
@@ -378,8 +398,8 @@
         out_specs=[pl.BlockSpec(memory_space=pl.ANY)] * len(shapes),
         out_shape=[jax.ShapeDtypeStruct(shape, jnp.bfloat16) for shape in shapes],
         scratch_shapes=[
-            pltpu.VMEM((2, block, width), jnp.bfloat16),
-            pltpu.SemaphoreType.DMA((2, 1)),
+            pltpu.VMEM((4, block, width), jnp.bfloat16),
+            pltpu.SemaphoreType.DMA((4, 1)),
         ],
         compiler_params=with_vmem(8),
         cost_estimate=pl.CostEstimate(
@@ -400,6 +420,14 @@
             got[turn ^ bit] = lax.ppermute(got[turn], axis, [(at, at ^ bit) for at in range(size)])
         bit //= 2
     return [got[turn] for turn in range(size)]
+
+
+def straight_from_others(array, axis):
+    size = lax.axis_size(axis)
+    return [array] + [
+        lax.ppermute(array, axis, [(at, at ^ turn) for at in range(size)])
+        for turn in range(1, size)
+    ]
 
 
 def per_device(
@@ -429,18 +457,18 @@
     plan = chunk_plan([state[0].shape[0] for state in states])
     place = jnp.stack([lax.axis_index("col"), lax.axis_index("dp")]).astype(jnp.int32)
     packed = pack((query_cotangent, key_cotangent, up_cotangent), plan, groups, part, place)
-    *held, loaded = preload([array for state in states for array in state], packed[0])
+    step, ring = ring_steps(layer_input, "dp")
+    arrived = step()
+    *held, loaded = preload([array for state in states for array in state])
     held = [held[at : at + 3] for at in range(0, len(held), 3)]
-    step, ring = ring_steps(layer_input, "dp")
-    step(None)
-    owned = []
-    for array in packed:
-        if owned:
-            array, owned[-1] = lax.optimization_barrier((array, owned[-1]))
-        owned.append(lax.all_to_all(array, "dp", split_axis=0, concat_axis=0, tiled=True))
-        owned[-1], loaded = step((owned[-1], loaded))
+    packed = join(packed, (*arrived, loaded))
+    step()
+    owned = [
+        lax.all_to_all(array, "dp", split_axis=0, concat_axis=0, tiled=True) for array in packed
+    ]
+    step(owned)
     for _ in range(groups):
-        step(None)
+        step()
     cotangents = [[], [], []]
     for array, pieces in zip(owned, plan):
         every = unpack(from_others(array, "col"), [high - low for _, low, high in pieces], place)
@@ -453,7 +481,7 @@
         power, made = adam_pass(
             ring(), [cotangents[which] for which in group], [held[which] for which in group]
         )
-        passes.append((group, from_others(power, "col"), made))
+        passes.append((group, straight_from_others(power, "col"), made))
     for group, powers, made in passes:
         parts = [array for done in made for array in done[:2]]
         for which, done, array in zip(group, made, finish_rows(parts, powers, whole_width)):

time: 164 us -> 166 us (1.012)
  waiting for transfers between devices: 69.6 us -> 34.7 us
  local copies, waits for them, and re-layouts: 0.04 us -> 25.1 us
  blocking collectives: 0 us -> 23.5 us
  starting transfers between devices: 34.3 us -> 24.2 us
  Pallas kernels: 59.2 us -> 57.2 us
    ppermute x3, waiting for transfers between devices: 43.2 us -> 6.86 us  [step(): ahead.append(lax.ppermute(two, axis, back))]
    unnamed x2 -> x56, local copies, waits for them, and re-layouts: 0.01 us -> 25 us
    all_to_all x0 -> x1, blocking collectives: none -> 23.5 us  [per_device(): lax.all_to_all(array, 'dp', split_axis=0, concat_axis=0, tiled=True)]
    ppermute x12 -> x6, waiting for transfers between devices: 26.3 us -> 2.83 us  [from_others(): lax.ppermute(got[turn], axis, [(at, at ^ bit) for at in range(size)])]
    all_to_all x2 -> x1, waiting for transfers between devices: 0.01 us -> 13 us  [per_device(): lax.all_to_all(array, 'dp', split_axis=0, concat_axis=0, tiled=True)]
    all_to_all x2 -> x1, starting transfers between devices: 14.1 us -> 4.2 us  [per_device(): lax.all_to_all(array, 'dp', split_axis=0, concat_axis=0, tiled=True)]
    ppermute x3, waiting for transfers between devices: 0.01 us -> 8 us  [step(): behind.append(lax.ppermute(one, axis, onward))]
    ppermute x1, starting transfers between devices: 5.03 us -> 0.27 us  [step(): middle.append(lax.ppermute(one[:half], axis, onward))]
  transfers between devices with their start and end apart: 22 -> 21, of which waited for: 6 -> 10; matrix products, arithmetic and copies ran while one was open for 0% -> 0% of each run, Pallas kernels for 16% -> 18%
where the time goes in v6:
time: 166 us
  Pallas kernels  57.2 us (34%)
  waiting for transfers between devices  34.7 us (21%)
  local copies, waits for them, and re-layouts  25.1 us (15%)
  starting transfers between devices  24.2 us (15%)
  blocking collectives  23.5 us (14%)
    pallas_call x2, Pallas kernels, adam_pass(): pl.pallas_call(functools.partial(adam_kernel, strip, len(x_pieces), cuts)...  34.5 us
    unnamed x56, local copies, waits for them, and re-layouts  25 us
    all_to_all x1, blocking collectives, per_device(): lax.all_to_all(array, 'dp', split_axis=0, concat_axis=0, tiled=True)  23.5 us
    all_to_all x1, waiting for transfers between devices, per_device(): lax.all_to_all(array, 'dp', split_axis=0, concat_axis=0, tiled=True)  13 us
    pallas_call x1, Pallas kernels, preload(): pl.pallas_call(preload_kernel, in_specs=[pl.BlockSpec(memory_space=pl.ANY...  9.68 us
    ppermute x3, waiting for transfers between devices, step(): behind.append(lax.ppermute(one, axis, onward))  8 us
    pallas_call x2, Pallas kernels, finish_rows(): pl.pallas_call(functools.partial(finish_kernel, len(powers), whole_width,...  6.91 us
    ppermute x3, waiting for transfers between devices, step(): ahead.append(lax.ppermute(two, axis, back))  6.86 us
  transfers between devices with their start and end apart: 21, of which 10 were waited for; matrix products, arithmetic and copies ran while one was open for 0% of the time, Pallas kernels for 18%

profile of v6, /device:TPU:0, one launch (start us, length us, event | category | flops | bytes accessed | tf_op | source)
XLA Modules:
  0.0 165.8 jit_solution(8558758613069759679)
XLA Ops:
  0.6 3.0 %collective-permute-start = (bf16[128,2048]{1,0:T(8,128)(2,1)}, bf16[128,2048]{1,0:T(8,128)(2,1)S(1)}, u32[]{:S(2)}, u32[]{:S(2)}) collective-permute-start(bf16[128,2048]{1,0:T(8,128)(2,1)} %refs_0_.7), channel_id=1, source_target_pairs={{2,0},{4,2},{6,4},{7,6},{5,7},{3,5},{1,3},{0,1},{10,8},{12,10},{14... | collective-permute-start | bytes 1572872 | tf_op jit(solution)/shard_map/ppermute | solution.py:103
  3.9 1.9 %pack.1 = (bf16[8,32,1152]{2,1,0:T(8,128)(2,1)S(1)}, bf16[8,32,1280]{2,1,0:T(8,128)(2,1)S(1)}) custom-call(s32[2]{0:T(128)S(1)} %pad_add_fusion.at_ref, bf16[128,4096]{1,0:T(8,128)(2,1)} %refs_0_.4, bf16[128,1024]{1,0:T(8,128)(2,1)} %refs_1_.2, bf16[128,14336]{1,0:T(8,128)(2,1)} %refs_2_.2), custom_call_target="tpu_custom_call" | custom-call | bytes 2490368 | tf_op jit(solution)/shard_map/pack/pallas_call | solution.py:67
  5.8 9.7 %preload.1 = (bf16[512,2048]{1,0:T(8,128)(2,1)S(1)}, bf16[512,2048]{1,0:T(8,128)(2,1)S(1)}, bf16[512,2048]{1,0:T(8,128)(2,1)S(1)}, bf16[128,2048]{1,0:T(8,128)(2...) custom-call(bf16[512,2048]{1,0:T(8,128)(2,1)} %refs_0_.5, ...), custom_call_target="tpu_custom_call" | custom-call | bytes 29884416 | tf_op jit(solution)/shard_map/preload/pallas_call | solution.py:182
  15.5 3.0 %copy-done = bf16[1792,2048]{1,0:T(8,128)(2,1)} copy-done((bf16[1792,2048]{1,0:T(8,128)(2,1)}, bf16[1792,2048]{1,0:T(8,128)(2,1)S(1)}, u32[]{:S(2)}) %copy-start) | copy-done | bytes 7340056
  18.5 3.0 %copy-done.1 = bf16[1792,2048]{1,0:T(8,128)(2,1)} copy-done((bf16[1792,2048]{1,0:T(8,128)(2,1)}, bf16[1792,2048]{1,0:T(8,128)(2,1)S(1)}, u32[]{:S(2)}) %copy-start.1) | copy-done | bytes 7340056
  21.6 1.3 copy-done.6
  22.9 3.0 %copy-done.8 = bf16[1792,2048]{1,0:T(8,128)(2,1)} copy-done((bf16[1792,2048]{1,0:T(8,128)(2,1)}, bf16[1792,2048]{1,0:T(8,128)(2,1)S(1)}, u32[]{:S(2)}) %copy-start.8) | copy-done | bytes 7340056
  25.9 1.3 copy-done.16
  27.3 0.8 copy-done.18
  28.1 0.8 copy-done.20
  28.8 0.8 copy-done.22
  29.7 1.3 copy-done.4
  30.9 0.2 copy-done.10
  31.1 0.2 copy-done.12
  31.3 23.5 %all_to_all.10.refs_3_.refs_0_ = bf16[8,32,1280]{2,1,0:T(8,128)(2,1)} all-to-all(bf16[8,32,1280]{2,1,0:T(8,128)(2,1)S(1)} %get-tuple-element.48), channel_id=1, replica_groups=mesh['col'=4,'dp'=8] {'dp'}, dimensions={0} | all-to-all | bytes 1310720 | tf_op jit(solution)/shard_map/all_to_all | solution.py:467
  54.8 4.2 %all-to-all-start = ((bf16[8,32,1152]{2,1,0:T(8,128)(2,1)}), bf16[8,32,1152]{2,1,0:T(8,128)(2,1)}, u32[]{:S(2)}, u32[]{:S(2)}) async-start(bf16[8,32,1152]{2,1,0:T(8,128)(2,1)} %copy-done.14), calls=%async_computation | async-start | bytes 1179648 | tf_op jit(solution)/shard_map/all_to_all | solution.py:467
  59.0 1.9 %collective-permute-start.2 = (bf16[128,2048]{1,0:T(8,128)(2,1)}, bf16[128,2048]{1,0:T(8,128)(2,1)}, u32[]{:S(2)}, u32[]{:S(2)}) collective-permute-start(bf16[128,2048]{1,0:T(8,128)(2,1)} %copy-done.12), channel_id=1, source_target_pairs={{0,2},{2,4},{4,6},{6,7},{7,5},{5,3},{3,1},{1,0},{8,10},{10,12},{12... | collective-permute-start | bytes 1572872 | tf_op jit(solution)/shard_map/ppermute | solution.py:102
  60.9 0.2 collective-permute-start.3
  61.1 1.5 collective-permute-start.15
  62.6 13.0 %all-to-all-done.refs_2_.refs_0_ = bf16[8,32,1152]{2,1,0:T(8,128)(2,1)} async-done(((bf16[8,32,1152]{2,1,0:T(8,128)(2,1)}), bf16[8,32,1152]{2,1,0:T(8,128)(2,1)}, u32[]{:S(2)}, u32[]{:S(2)}) %all-to-all-start) | async-done | bytes 589856 | tf_op jit(solution)/shard_map/all_to_all | solution.py:467
  75.6 1.5 collective-permute-start.9
  77.1 1.5 collective-permute-done.2.refs_0_
  78.6 2.2 %collective-permute-done.3.refs_1_ = bf16[128,2048]{1,0:T(8,128)(2,1)} collective-permute-done((bf16[128,2048]{1,0:T(8,128)(2,1)}, bf16[128,2048]{1,0:T(8,128)(2,1)}, u32[]{:S(2)}, u32[]{:S(2)}) %collective-permute-start.3) | collective-permute-done | bytes 524320 | tf_op jit(solution)/shard_map/ppermute | solution.py:103
  80.8 4.7 %collective-permute-start.5 = (bf16[128,2048]{1,0:T(8,128)(2,1)}, bf16[128,2048]{1,0:T(8,128)(2,1)S(1)}, u32[]{:S(2)}, u32[]{:S(2)}) collective-permute-start(bf16[128,2048]{1,0:T(8,128)(2,1)} %get-tuple-element.50.refs_7_), channel_id=1, source_target_pairs={{0,2},{2,4},{4,6},{6,7},{7,5},{5,3},{3,1},{1,0},{8,10},{10,12},{12... | collective-permute-start | bytes 1572872 | tf_op jit(solution)/shard_map/ppermute | solution.py:102
  85.4 2.8 %collective-permute-done.9.refs_2_ = bf16[8,32,1152]{2,1,0:T(8,128)(2,1)S(1)} collective-permute-done((bf16[8,32,1152]{2,1,0:T(8,128)(2,1)}, bf16[8,32,1152]{2,1,0:T(8,128)(2,1)S(1)}, u32[]{:S(2)}, u32[]{:S(2)}) %collective-permute-start.9) | collective-permute-done | bytes 589856 | tf_op jit(solution)/shard_map/ppermute | solution.py:420
  88.3 0.5 collective-permute-start.16
  88.8 6.5 %collective-permute-done.5.refs_6_ = bf16[128,2048]{1,0:T(8,128)(2,1)S(1)} collective-permute-done((bf16[128,2048]{1,0:T(8,128)(2,1)}, bf16[128,2048]{1,0:T(8,128)(2,1)S(1)}, u32[]{:S(2)}, u32[]{:S(2)}) %collective-permute-start.5) | collective-permute-done | bytes 524320 | tf_op jit(solution)/shard_map/ppermute | solution.py:102
  95.3 4.7 %collective-permute-done.4.refs_3_ = bf16[128,2048]{1,0:T(8,128)(2,1)S(1)} collective-permute-done((bf16[128,2048]{1,0:T(8,128)(2,1)}, bf16[128,2048]{1,0:T(8,128)(2,1)S(1)}, u32[]{:S(2)}, u32[]{:S(2)}) %collective-permute-start.4) | collective-permute-done | bytes 524320 | tf_op jit(solution)/shard_map/ppermute | solution.py:103
  100.0 0.3 collective-permute-start.6
  100.3 1.8 %collective-permute-start.7 = (bf16[64,2048]{1,0:T(8,128)(2,1)S(1)}, bf16[64,2048]{1,0:T(8,128)(2,1)S(1)}, u32[]{:S(2)}, u32[]{:S(2)}) collective-permute-start(bf16[64,2048]{1,0:T(8,128)(2,1)S(1)} %slice.9), channel_id=1, source_target_pairs={{2,0},{4,2},{6,4},{7,6},{5,7},{3,5},{1,3},{0,1},{10,8},{12,10},{14... | collective-permute-start | bytes 786440 | tf_op jit(solution)/shard_map/ppermute | solution.py:107
  102.2 1.9 %unpack.2 = (bf16[512,1024]{1,0:T(8,128)(2,1)S(1)}, bf16[128,1024]{1,0:T(8,128)(2,1)S(1)}, bf16[512,1024]{1,0:T(8,128)(2,1)S(1)}) custom-call(s32[2]{0:T(128)S(1)} %pad_add_fusion.at_ref, bf16[8,32,1152]{2,1,0:T(8,128)(2,1)} %all-to-all-done.refs_2_.refs_0_, bf16[8,32,1152]{2,1,0:T(8,128)(2,1)S(1)} %collective-permute-done.8.refs_1_, ...), custom_call_target="tpu_custom_call" | custom-call | bytes 4718592 | tf_op jit(solution)/shard_map/unpack/pallas_call | solution.py:137
  104.1 2.2 %unpack.3.refs_10_ = bf16[1280,1024]{1,0:T(8,128)(2,1)S(1)} custom-call(s32[2]{0:T(128)S(1)} %pad_add_fusion.at_ref, bf16[8,32,1280]{2,1,0:T(8,128)(2,1)} %all_to_all.10.refs_3_.refs_0_, bf16[8,32,1280]{2,1,0:T(8,128)(2,1)S(1)} %collective-permute-done.14.refs_1_, bf16[8,32,1280]{2,1,0:T(8,128)(2,1)} %collective-permute-done.15.refs_2_, ...), custom_call_target="tpu_custom_call" | custom-call | bytes 5242880 | tf_op jit(solution)/shard_map/unpack/pallas_call | solution.py:137
  106.3 1.6 collective-permute-done.6.refs_4_
  107.9 0.1 collective-permute-done.7.refs_5_
  108.1 3.1 %copy-done.2 = bf16[1792,2048]{1,0:T(8,128)(2,1)S(1)} copy-done((bf16[1792,2048]{1,0:T(8,128)(2,1)S(1)}, bf16[1792,2048]{1,0:T(8,128)(2,1)}, u32[]{:S(2)}) %copy-start.2) | copy-done | bytes 7340056
  111.2 3.1 %copy-done.9 = bf16[1792,2048]{1,0:T(8,128)(2,1)S(1)} copy-done((bf16[1792,2048]{1,0:T(8,128)(2,1)S(1)}, bf16[1792,2048]{1,0:T(8,128)(2,1)}, u32[]{:S(2)}) %copy-start.9) | copy-done | bytes 7340056
  114.3 23.8 %adam.3 = (f32[1,1792]{1,0:T(1,128)S(1)}, bf16[1792,2048]{1,0:T(8,128)(2,1)S(1)}, bf16[1792,2048]{1,0:T(8,128)(2,1)S(1)}, bf16[1792,2048]{1,0:T(8,128)(2,1)}, bf16[1792,2048]{1,0:T(8,128)(2,1)}) custom-call(bf16[128,2048]{1,0:T(8,128)(2,1)S(1)} %copy-done.15, bf16[128,2048]{1,0:T(8,128)(2,1)S(1)} %copy-done.11, ...), custom_call_target="tpu_custom_call", output_to_operand_aliasing={{1}: (11, {}), {2}: (12, {})} | custom-call | flops 7516192768 | bytes 14680064 | tf_op jit(solution)/shard_map/adam/pallas_call | solution.py:321
  138.1 3.0 %copy-done.3 = bf16[1792,2048]{1,0:T(8,128)(2,1)} copy-done((bf16[1792,2048]{1,0:T(8,128)(2,1)}, bf16[1792,2048]{1,0:T(8,128)(2,1)S(1)}, u32[]{:S(2)}) %copy-start.3) | copy-done | bytes 7340056
  141.1 1.5 collective-permute-start.18
  142.6 0.4 collective-permute-start.19
  143.0 10.7 %adam.2 = (f32[1,640]{1,0:T(1,128)S(1)}, bf16[512,2048]{1,0:T(8,128)(2,1)S(1)}, bf16[512,2048]{1,0:T(8,128)(2,1)S(1)}, bf16[512,2048]{1,0:T(8,128)(2,1)}, bf16[5...) custom-call(bf16[128,2048]{1,0:T(8,128)(2,1)S(1)} %copy-done.15, ...), custom_call_target="tpu_custom_call", output_to_operand_aliasing={{1}: (10, {}), {2}: (11, {}), {5}: (14, {}), {6}: (15, {})} | custom-call | flops 2684354560 | bytes 5242880 | tf_op jit(solution)/shard_map/adam/pallas_call | solution.py:321
  153.8 0.3 collective-permute-start.11
  154.1 1.5 collective-permute-start.12
  155.6 0.8 collective-permute-start.13
  156.4 1.3 collective-permute-done.12.refs_2_
  157.7 0.9 collective-permute-done.13.refs_3_
  158.7 2.6 %finish.2 = (bf16[512,2048]{1,0:T(8,128)(2,1)}, bf16[128,2048]{1,0:T(8,128)(2,1)}) custom-call(f32[1,640]{1,0:T(1,128)S(1)} %get-tuple-element.59.refs_0_, f32[1,640]{1,0:T(1,128)S(1)} %collective-permute-done.11.refs_1_, f32[1,640]{1,0:T(1,128)S(1)} %collective-permute-done.12.refs_2_, f32[1,640]{1,0:T(1,128)S(1)} %collective-permute-done.13.refs_3_, ...), custom_call_target="tpu_custom_call" | custom-call | flops 2621440 | bytes 2621440 | tf_op jit(solution)/shard_map/finish/pallas_call | solution.py:395
  161.4 4.3 %finish.3 = bf16[1792,2048]{1,0:T(8,128)(2,1)} custom-call(f32[1,1792]{1,0:T(1,128)S(1)} %get-tuple-element.70.refs_0_, f32[1,1792]{1,0:T(1,128)S(1)} %collective-permute-done.17.refs_1_, f32[1,1792]{1,0:T(1,128)S(1)} %collective-permute-done.18.refs_2_, f32[1,1792]{1,0:T(1,128)S(1)} %collective-permute-done.19.refs_3_, ...), custom_call_target="tpu_custom_call" | custom-call | flops 7340032 | bytes 7340032 | tf_op jit(solution)/shard_map/finish/pallas_call | solution.py:395
  (66 shorter events, 0.4 us)
Async XLA Ops:
  0.6 29.0 %collective-permute-start = (bf16[128,2048]{1,0:T(8,128)(2,1)}, bf16[128,2048]{1,0:T(8,128)(2,1)S(1)}, u32[]{:S(2)}, u32[]{:S(2)}) collective-permute-start(bf16[128,2048]{1,0:T(8,128)(2,1)} %refs_0_.7), channel_id=1, source_target_pairs={{2,0},{4,2},{6,4},{7,6},{5,7},{3,5},{1,3},{0,1},{10,8},{12,10},{14... | collective-permute-start | bytes 1572872 | tf_op jit(solution)/shard_map/ppermute | solution.py:103
  3.7 26.0 %collective-permute-start.1 = (bf16[128,2048]{1,0:T(8,128)(2,1)}, bf16[128,2048]{1,0:T(8,128)(2,1)S(1)}, u32[]{:S(2)}, u32[]{:S(2)}) collective-permute-start(bf16[128,2048]{1,0:T(8,128)(2,1)} %refs_0_.7), channel_id=1, source_target_pairs={{0,2},{2,4},{4,6},{6,7},{7,5},{5,3},{3,1},{1,0},{8,10},{10,12},{12... | collective-permute-start | bytes 1572872 | tf_op jit(solution)/shard_map/ppermute | solution.py:102
  15.5 3.1 %copy-start = (bf16[1792,2048]{1,0:T(8,128)(2,1)}, bf16[1792,2048]{1,0:T(8,128)(2,1)S(1)}, u32[]{:S(2)}) copy-start(bf16[1792,2048]{1,0:T(8,128)(2,1)S(1)} %get-tuple-element.67.refs_11_) | copy-start | bytes 22020100
  18.5 3.0 %copy-start.1 = (bf16[1792,2048]{1,0:T(8,128)(2,1)}, bf16[1792,2048]{1,0:T(8,128)(2,1)S(1)}, u32[]{:S(2)}) copy-start(bf16[1792,2048]{1,0:T(8,128)(2,1)S(1)} %get-tuple-element.68.refs_12_) | copy-start | bytes 22020100
  21.6 1.3 copy-start.6
  22.9 3.0 %copy-start.8 = (bf16[1792,2048]{1,0:T(8,128)(2,1)}, bf16[1792,2048]{1,0:T(8,128)(2,1)S(1)}, u32[]{:S(2)}) copy-start(bf16[1792,2048]{1,0:T(8,128)(2,1)S(1)} %get-tuple-element.69.refs_13_) | copy-start | bytes 22020100
  25.9 1.3 copy-start.16
  27.3 0.8 copy-start.18
  28.8 0.8 copy-start.22
  29.6 1.3 copy-start.4
  29.6 1.5 copy-start.10
  29.6 1.6 copy-start.12
  31.3 23.5 %copy-start.14 = (bf16[8,32,1152]{2,1,0:T(8,128)(2,1)}, bf16[8,32,1152]{2,1,0:T(8,128)(2,1)S(1)}, u32[]{:S(2)}) copy-start(bf16[8,32,1152]{2,1,0:T(8,128)(2,1)S(1)} %get-tuple-element.47) | copy-start | bytes 1769476
  31.3 76.8 %slice-start = ((s8[7340032]{0:T(1024)(128)(4,1)}), s8[3145728]{0:T(1024)(128)(4,1)S(1)}, s32[]{:S(2)}) async-start(s8[7340032]{0:T(1024)(128)(4,1)} %bitcast.2), calls=%async_computation.2 | async-start | bytes 6291456
  54.8 20.8 %all-to-all-start = ((bf16[8,32,1152]{2,1,0:T(8,128)(2,1)}), bf16[8,32,1152]{2,1,0:T(8,128)(2,1)}, u32[]{:S(2)}, u32[]{:S(2)}) async-start(bf16[8,32,1152]{2,1,0:T(8,128)(2,1)} %copy-done.14), calls=%async_computation | async-start | bytes 1179648 | tf_op jit(solution)/shard_map/all_to_all | solution.py:467
  59.0 19.6 %collective-permute-start.2 = (bf16[128,2048]{1,0:T(8,128)(2,1)}, bf16[128,2048]{1,0:T(8,128)(2,1)}, u32[]{:S(2)}, u32[]{:S(2)}) collective-permute-start(bf16[128,2048]{1,0:T(8,128)(2,1)} %copy-done.12), channel_id=1, source_target_pairs={{0,2},{2,4},{4,6},{6,7},{7,5},{5,3},{3,1},{1,0},{8,10},{10,12},{12... | collective-permute-start | bytes 1572872 | tf_op jit(solution)/shard_map/ppermute | solution.py:102
  60.9 19.8 %collective-permute-start.3 = (bf16[128,2048]{1,0:T(8,128)(2,1)}, bf16[128,2048]{1,0:T(8,128)(2,1)}, u32[]{:S(2)}, u32[]{:S(2)}) collective-permute-start(bf16[128,2048]{1,0:T(8,128)(2,1)} %copy-done.10), channel_id=1, source_target_pairs={{2,0},{4,2},{6,4},{7,6},{5,7},{3,5},{1,3},{0,1},{10,8},{12,10},{14... | collective-permute-start | bytes 1572872 | tf_op jit(solution)/shard_map/ppermute | solution.py:103
  61.1 27.2 %collective-permute-start.15 = (bf16[8,32,1280]{2,1,0:T(8,128)(2,1)}, bf16[8,32,1280]{2,1,0:T(8,128)(2,1)}, u32[]{:S(2)}, u32[]{:S(2)}) collective-permute-start(bf16[8,32,1280]{2,1,0:T(8,128)(2,1)} %all_to_all.10.refs_3_.refs_0_), channel_id=1, source_target_pairs={{0,16},{8,24},{16,0},{24,8},{1,17},{9,25},{17,1},{25,9},{2,18},{10... | collective-permute-start | bytes 1966088 | tf_op jit(solution)/shard_map/ppermute | solution.py:420
  75.6 12.7 %collective-permute-start.9 = (bf16[8,32,1152]{2,1,0:T(8,128)(2,1)}, bf16[8,32,1152]{2,1,0:T(8,128)(2,1)S(1)}, u32[]{:S(2)}, u32[]{:S(2)}) collective-permute-start(bf16[8,32,1152]{2,1,0:T(8,128)(2,1)} %all-to-all-done.refs_2_.refs_0_), channel_id=1, source_target_pairs={{0,16},{8,24},{16,0},{24,8},{1,17},{9,25},{17,1},{25,9},{2,18},{10... | collective-permute-start | bytes 1769480 | tf_op jit(solution)/shard_map/ppermute | solution.py:420
  80.8 14.5 %collective-permute-start.5 = (bf16[128,2048]{1,0:T(8,128)(2,1)}, bf16[128,2048]{1,0:T(8,128)(2,1)S(1)}, u32[]{:S(2)}, u32[]{:S(2)}) collective-permute-start(bf16[128,2048]{1,0:T(8,128)(2,1)} %get-tuple-element.50.refs_7_), channel_id=1, source_target_pairs={{0,2},{2,4},{4,6},{6,7},{7,5},{5,3},{3,1},{1,0},{8,10},{10,12},{12... | collective-permute-start | bytes 1572872 | tf_op jit(solution)/shard_map/ppermute | solution.py:102
  85.4 14.9 %collective-permute-start.8 = (bf16[8,32,1152]{2,1,0:T(8,128)(2,1)}, bf16[8,32,1152]{2,1,0:T(8,128)(2,1)S(1)}, u32[]{:S(2)}, u32[]{:S(2)}) collective-permute-start(bf16[8,32,1152]{2,1,0:T(8,128)(2,1)} %all-to-all-done.refs_2_.refs_0_), channel_id=1, source_target_pairs={{0,8},{8,0},{16,24},{24,16},{1,9},{9,1},{17,25},{25,17},{2,10},{10... | collective-permute-start | bytes 1769480 | tf_op jit(solution)/shard_map/ppermute | solution.py:420
  85.4 14.5 %collective-permute-start.4 = (bf16[128,2048]{1,0:T(8,128)(2,1)}, bf16[128,2048]{1,0:T(8,128)(2,1)S(1)}, u32[]{:S(2)}, u32[]{:S(2)}) collective-permute-start(bf16[128,2048]{1,0:T(8,128)(2,1)} %get-tuple-element.49.refs_2_), channel_id=1, source_target_pairs={{2,0},{4,2},{6,4},{7,6},{5,7},{3,5},{1,3},{0,1},{10,8},{12,10},{14... | collective-permute-start | bytes 1572872 | tf_op jit(solution)/shard_map/ppermute | solution.py:103
  88.3 15.8 %collective-permute-start.14 = (bf16[8,32,1280]{2,1,0:T(8,128)(2,1)}, bf16[8,32,1280]{2,1,0:T(8,128)(2,1)S(1)}, u32[]{:S(2)}, u32[]{:S(2)}) collective-permute-start(bf16[8,32,1280]{2,1,0:T(8,128)(2,1)} %all_to_all.10.refs_3_.refs_0_), channel_id=1, source_target_pairs={{0,8},{8,0},{16,24},{24,16},{1,9},{9,1},{17,25},{25,17},{2,10},{10... | collective-permute-start | bytes 1966088 | tf_op jit(solution)/shard_map/ppermute | solution.py:420
  88.3 15.8 %collective-permute-start.16 = (bf16[8,32,1280]{2,1,0:T(8,128)(2,1)}, bf16[8,32,1280]{2,1,0:T(8,128)(2,1)S(1)}, u32[]{:S(2)}, u32[]{:S(2)}) collective-permute-start(bf16[8,32,1280]{2,1,0:T(8,128)(2,1)} %collective-permute-done.15.refs_2_), channel_id=1, source_target_pairs={{0,8},{8,0},{16,24},{24,16},{1,9},{9,1},{17,25},{25,17},{2,10},{10... | collective-permute-start | bytes 1966088 | tf_op jit(solution)/shard_map/ppermute | solution.py:420
  95.3 6.9 %collective-permute-start.10 = (bf16[8,32,1152]{2,1,0:T(8,128)(2,1)S(1)}, bf16[8,32,1152]{2,1,0:T(8,128)(2,1)S(1)}, u32[]{:S(2)}, u32[]{:S(2)}) collective-permute-start(bf16[8,32,1152]{2,1,0:T(8,128)(2,1)S(1)} %collective-permute-done.9.refs_2_), channel_id=1, source_target_pairs={{0,8},{8,0},{16,24},{24,16},{1,9},{9,1},{17,25},{25,17},{2,10},{10... | collective-permute-start | bytes 1769480 | tf_op jit(solution)/shard_map/ppermute | solution.py:420
  100.0 7.9 %collective-permute-start.6 = (bf16[64,2048]{1,0:T(8,128)(2,1)S(1)}, bf16[64,2048]{1,0:T(8,128)(2,1)S(1)}, u32[]{:S(2)}, u32[]{:S(2)}) collective-permute-start(bf16[64,2048]{1,0:T(8,128)(2,1)S(1)} %slice.8), channel_id=1, source_target_pairs={{0,2},{2,4},{4,6},{6,7},{7,5},{5,3},{3,1},{1,0},{8,10},{10,12},{12... | collective-permute-start | bytes 786440 | tf_op jit(solution)/shard_map/ppermute | solution.py:106
  100.3 7.8 %slice-start.1 = ((s8[7340032]{0:T(1024)(128)(4,1)}), s8[4194304]{0:T(1024)(128)(4,1)S(1)}, s32[]{:S(2)}) async-start(s8[7340032]{0:T(1024)(128)(4,1)} %bitcast.2), calls=%async_computation.3 | async-start | bytes 8388608
  100.3 7.8 %copy-start.11 = (bf16[128,2048]{1,0:T(8,128)(2,1)S(1)}, bf16[128,2048]{1,0:T(8,128)(2,1)}, u32[]{:S(2)}) copy-start(bf16[128,2048]{1,0:T(8,128)(2,1)} %copy-done.10) | copy-start | bytes 1572868
  100.3 7.8 %copy-start.13 = (bf16[128,2048]{1,0:T(8,128)(2,1)S(1)}, bf16[128,2048]{1,0:T(8,128)(2,1)}, u32[]{:S(2)}) copy-start(bf16[128,2048]{1,0:T(8,128)(2,1)} %copy-done.12) | copy-start | bytes 1572868
  100.3 7.8 %copy-start.15 = (bf16[128,2048]{1,0:T(8,128)(2,1)S(1)}, bf16[128,2048]{1,0:T(8,128)(2,1)}, u32[]{:S(2)}) copy-start(bf16[128,2048]{1,0:T(8,128)(2,1)} %refs_0_.7) | copy-start | bytes 1572868
  100.3 7.7 %collective-permute-start.7 = (bf16[64,2048]{1,0:T(8,128)(2,1)S(1)}, bf16[64,2048]{1,0:T(8,128)(2,1)S(1)}, u32[]{:S(2)}, u32[]{:S(2)}) collective-permute-start(bf16[64,2048]{1,0:T(8,128)(2,1)S(1)} %slice.9), channel_id=1, source_target_pairs={{2,0},{4,2},{6,4},{7,6},{5,7},{3,5},{1,3},{0,1},{10,8},{12,10},{14... | collective-permute-start | bytes 786440 | tf_op jit(solution)/shard_map/ppermute | solution.py:107
  108.1 3.1 %copy-start.2 = (bf16[1792,2048]{1,0:T(8,128)(2,1)S(1)}, bf16[1792,2048]{1,0:T(8,128)(2,1)}, u32[]{:S(2)}) copy-start(bf16[1792,2048]{1,0:T(8,128)(2,1)} %copy-done.1) | copy-start | bytes 22020100
  111.2 3.1 %copy-start.9 = (bf16[1792,2048]{1,0:T(8,128)(2,1)S(1)}, bf16[1792,2048]{1,0:T(8,128)(2,1)}, u32[]{:S(2)}) copy-start(bf16[1792,2048]{1,0:T(8,128)(2,1)} %copy-done.8) | copy-start | bytes 22020100
  114.3 28.7 %copy-start.5 = (bf16[512,2048]{1,0:T(8,128)(2,1)S(1)}, bf16[512,2048]{1,0:T(8,128)(2,1)}, u32[]{:S(2)}) copy-start(bf16[512,2048]{1,0:T(8,128)(2,1)} %copy-done.4) | copy-start | bytes 6291460
  114.3 28.7 %copy-start.7 = (bf16[512,2048]{1,0:T(8,128)(2,1)S(1)}, bf16[512,2048]{1,0:T(8,128)(2,1)}, u32[]{:S(2)}) copy-start(bf16[512,2048]{1,0:T(8,128)(2,1)} %copy-done.6) | copy-start | bytes 6291460
  114.3 28.7 %copy-start.17 = (bf16[512,2048]{1,0:T(8,128)(2,1)S(1)}, bf16[512,2048]{1,0:T(8,128)(2,1)}, u32[]{:S(2)}) copy-start(bf16[512,2048]{1,0:T(8,128)(2,1)} %copy-done.16) | copy-start | bytes 6291460
  114.3 28.7 %copy-start.19 = (bf16[128,2048]{1,0:T(8,128)(2,1)S(1)}, bf16[128,2048]{1,0:T(8,128)(2,1)}, u32[]{:S(2)}) copy-start(bf16[128,2048]{1,0:T(8,128)(2,1)} %copy-done.18) | copy-start | bytes 1572868
  114.3 28.7 %copy-start.21 = (bf16[128,2048]{1,0:T(8,128)(2,1)S(1)}, bf16[128,2048]{1,0:T(8,128)(2,1)}, u32[]{:S(2)}) copy-start(bf16[128,2048]{1,0:T(8,128)(2,1)} %copy-done.20) | copy-start | bytes 1572868
  114.3 28.7 %copy-start.23 = (bf16[128,2048]{1,0:T(8,128)(2,1)S(1)}, bf16[128,2048]{1,0:T(8,128)(2,1)}, u32[]{:S(2)}) copy-start(bf16[128,2048]{1,0:T(8,128)(2,1)} %copy-done.22) | copy-start | bytes 1572868
  138.1 3.1 %copy-start.3 = (bf16[1792,2048]{1,0:T(8,128)(2,1)}, bf16[1792,2048]{1,0:T(8,128)(2,1)S(1)}, u32[]{:S(2)}) copy-start(bf16[1792,2048]{1,0:T(8,128)(2,1)S(1)} %get-tuple-element.72.refs_5_) | copy-start | bytes 22020100
  141.1 20.2 %collective-permute-start.17 = (f32[1,1792]{1,0:T(1,128)S(1)}, f32[1,1792]{1,0:T(1,128)S(1)}, u32[]{:S(2)}, u32[]{:S(2)}) collective-permute-start(f32[1,1792]{1,0:T(1,128)S(1)} %get-tuple-element.70.refs_0_), channel_id=1, source_target_pairs={{0,8},{8,0},{16,24},{24,16},{1,9},{9,1},{17,25},{25,17},{2,10},{10... | collective-permute-start | bytes 21512 | tf_op jit(solution)/shard_map/ppermute | solution.py:428
  141.1 20.2 %collective-permute-start.18 = (f32[1,1792]{1,0:T(1,128)S(1)}, f32[1,1792]{1,0:T(1,128)S(1)}, u32[]{:S(2)}, u32[]{:S(2)}) collective-permute-start(f32[1,1792]{1,0:T(1,128)S(1)} %get-tuple-element.70.refs_0_), channel_id=1, source_target_pairs={{0,16},{8,24},{16,0},{24,8},{1,17},{9,25},{17,1},{25,9},{2,18},{10... | collective-permute-start | bytes 21512 | tf_op jit(solution)/shard_map/ppermute | solution.py:428
  142.6 18.7 %collective-permute-start.19 = (f32[1,1792]{1,0:T(1,128)S(1)}, f32[1,1792]{1,0:T(1,128)S(1)}, u32[]{:S(2)}, u32[]{:S(2)}) collective-permute-start(f32[1,1792]{1,0:T(1,128)S(1)} %get-tuple-element.70.refs_0_), channel_id=1, source_target_pairs={{0,24},{8,16},{16,8},{24,0},{1,25},{9,17},{17,9},{25,1},{2,26},{10... | collective-permute-start | bytes 21512 | tf_op jit(solution)/shard_map/ppermute | solution.py:428
  143.0 18.3 %slice-start.2 = ((s8[7340032]{0:T(1024)(128)(4,1)}), s8[4194304]{0:T(1024)(128)(4,1)S(1)}, s32[]{:S(2)}) async-start(s8[7340032]{0:T(1024)(128)(4,1)} %bitcast.4), calls=%async_computation.4 | async-start | bytes 8388608
  143.0 18.3 %slice-start.3 = ((s8[7340032]{0:T(1024)(128)(4,1)}), s8[3145728]{0:T(1024)(128)(4,1)S(1)}, s32[]{:S(2)}) async-start(s8[7340032]{0:T(1024)(128)(4,1)} %bitcast.4), calls=%async_computation.5 | async-start | bytes 6291456
  153.8 1.9 %collective-permute-start.11 = (f32[1,640]{1,0:T(1,128)S(1)}, f32[1,640]{1,0:T(1,128)S(1)}, u32[]{:S(2)}, u32[]{:S(2)}) collective-permute-start(f32[1,640]{1,0:T(1,128)S(1)} %get-tuple-element.59.refs_0_), channel_id=1, source_target_pairs={{0,8},{8,0},{16,24},{24,16},{1,9},{9,1},{17,25},{25,17},{2,10},{10... | collective-permute-start | bytes 7688 | tf_op jit(solution)/shard_map/ppermute | solution.py:428
  154.1 3.6 %collective-permute-start.12 = (f32[1,640]{1,0:T(1,128)S(1)}, f32[1,640]{1,0:T(1,128)S(1)}, u32[]{:S(2)}, u32[]{:S(2)}) collective-permute-start(f32[1,640]{1,0:T(1,128)S(1)} %get-tuple-element.59.refs_0_), channel_id=1, source_target_pairs={{0,16},{8,24},{16,0},{24,8},{1,17},{9,25},{17,1},{25,9},{2,18},{10... | collective-permute-start | bytes 7688 | tf_op jit(solution)/shard_map/ppermute | solution.py:428
  155.6 3.0 %collective-permute-start.13 = (f32[1,640]{1,0:T(1,128)S(1)}, f32[1,640]{1,0:T(1,128)S(1)}, u32[]{:S(2)}, u32[]{:S(2)}) collective-permute-start(f32[1,640]{1,0:T(1,128)S(1)} %get-tuple-element.59.refs_0_), channel_id=1, source_target_pairs={{0,24},{8,16},{16,8},{24,0},{1,25},{9,17},{17,9},{25,1},{2,26},{10... | collective-permute-start | bytes 7688 | tf_op jit(solution)/shard_map/ppermute | solution.py:428
  (1 other events, 0.8 us)

commit v7 on v6

--- a/solution.py
+++ b/solution.py
@@ -23,6 +23,14 @@
         if rows % block == 0:
             return block
     return rows
+
+
+def ring_order(groups):
+    return [*range(0, groups, 2), *range(groups - 1 - groups % 2, 0, -2)]
+
+
+def ring_place(at, groups):
+    return jnp.where(at % 2 == 0, at // 2, groups - 1 - at // 2)
 
 
 def chunk_plan(totals):
@@ -33,14 +41,6 @@
     if blocks:
         first.append((up, 0, blocks * block))
     return [first, [(up, blocks * block, totals[up])]]
-
-
-def ring_order(groups):
-    return [*range(0, groups, 2), *range(groups - 1 - groups % 2, 0, -2)]
-
-
-def ring_place(at, groups):
-    return jnp.where(at % 2 == 0, at // 2, groups - 1 - at // 2)
 
 
 def pack_kernel(plan, groups, at_ref, *refs):
@@ -86,47 +86,56 @@
     )(place, *(pltpu.with_memory_space_constraint(array, pltpu.HBM) for array in cotangents))
 
 
-def ring_steps(array, axis):
-    groups = lax.axis_size(axis)
+def halves_kernel(one_ref, two_ref, first_ref, last_ref):
+    half = first_ref.shape[0]
+    first_ref[...] = one_ref[:half]
+    last_ref[...] = two_ref[half:]
+
+
+def halves(one, two):
+    half = jax.ShapeDtypeStruct((one.shape[0] // 2, one.shape[1]), one.dtype)
+    vmem = pl.BlockSpec(memory_space=pltpu.VMEM)
+    return pl.pallas_call(
+        halves_kernel,
+        in_specs=[vmem] * 2,
+        out_specs=[vmem] * 2,
+        out_shape=[half] * 2,
+        compiler_params=with_vmem(4),
+        cost_estimate=pl.CostEstimate(
+            flops=0, bytes_accessed=4 * one.size, transcendentals=0
+        ),
+        name="halves",
+    )(one, two)
+
+
+def ring_paths(groups):
     order = ring_order(groups)
     onward = list(zip(order, order[1:] + order[:1]))
-    back = [(to, at) for at, to in onward]
-    behind, ahead, middle = [array], [array], []
-
-    def step(after=()):
-        one, two = behind[-1], ahead[-1]
-        if after:
-            one, two = join((one, two), after)
-            behind[-1], ahead[-1] = one, two
-        if len(behind) <= (groups - 1) // 2:
-            behind.append(lax.ppermute(one, axis, onward))
-            ahead.append(lax.ppermute(two, axis, back))
-        elif groups % 2 == 0 and not middle:
-            half = array.shape[0] // 2
-            middle.append(lax.ppermute(one[:half], axis, onward))
-            middle.append(lax.ppermute(two[half:], axis, back))
-        return behind[-1], ahead[-1]
-
-    def done():
-        return [array, *ahead[1:], *middle, *behind[:0:-1]]
-
-    return step, done
+    return onward, [(to, at) for at, to in onward]
+
+
+def ring_step(one, two, axis):
+    onward, back = ring_paths(lax.axis_size(axis))
+    return lax.ppermute(one, axis, onward), lax.ppermute(two, axis, back)
 
 
 def unpack_kernel(count, at_ref, *refs):
-    pieces, outputs, order = refs[:count], refs[count:-1], refs[-1]
-    groups, part, _ = pieces[0].shape
-    for group in range(groups):
-        slot = ring_place(group, groups) - ring_place(at_ref[1], groups) + groups
-        for turn, piece in enumerate(pieces):
-            order[slot % groups * count + (at_ref[0] ^ turn)] = piece[group]
+    pieces, outputs, orders = refs[:count], refs[count:-2], refs[-2:]
+    groups = pieces[0].shape[0]
+    here = ring_place(at_ref[1], groups)
+    slots = [(ring_place(group, groups) - here + groups) % groups for group in range(groups)]
     low = 0
     for out_ref in outputs:
         rows = out_ref.shape[0]
         for start in range(0, rows, 128):
             high = min(start + 128, rows)
-            tokens = order[:, :, low + start : low + high].reshape(-1, high - start)
-            out_ref[start:high] = tokens.T
+            order = orders[start // 128 % 2]
+            for group, slot in enumerate(slots):
+                for turn, piece in enumerate(pieces):
+                    order[slot * count + (at_ref[0] ^ turn), :, : high - start] = piece[
+                        group, :, low + start : low + high
+                    ]
+            out_ref[start:high] = order[...].reshape(-1, 128).T[: high - start]
         low += rows
 
 
@@ -134,13 +143,14 @@
     groups, part, rows = pieces[0].shape
     tokens = groups * part * len(pieces)
     vmem = pl.BlockSpec(memory_space=pltpu.VMEM)
+    order = pltpu.VMEM((groups * len(pieces), part, 128), jnp.bfloat16)
     return pl.pallas_call(
         functools.partial(unpack_kernel, len(pieces)),
         in_specs=[pl.BlockSpec(memory_space=pltpu.SMEM)] + [vmem] * len(pieces),
         out_specs=[vmem] * len(row_counts),
         out_shape=[pltpu.VMEM((count, tokens), jnp.bfloat16) for count in row_counts],
-        scratch_shapes=[pltpu.VMEM((groups * len(pieces), part, rows), jnp.bfloat16)],
-        compiler_params=with_vmem(12),
+        scratch_shapes=[order, order],
+        compiler_params=with_vmem(4 + 6 * tokens * 256 // 2**20),
         cost_estimate=pl.CostEstimate(
             flops=0, bytes_accessed=4 * tokens * rows, transcendentals=0
         ),
@@ -152,7 +162,7 @@
     pass
 
 
-def join(arrays, after):
+def join(arrays, after=()):
     count = len(arrays)
     hbm = pl.BlockSpec(memory_space=pl.ANY)
     return pl.pallas_call(
@@ -167,9 +177,9 @@
 
 
 def preload_kernel(*refs):
-    count = (len(refs) - 2) // 2
+    count = (len(refs) - 3) // 2
     token, sems = refs[-2:]
-    outputs = refs[count:]
+    outputs = refs[count + 1 :]
     copies = [pltpu.make_async_copy(refs[at], outputs[at], sems.at[at]) for at in range(count)]
     token[...] = jnp.zeros_like(token)
     for copy in copies:
@@ -178,10 +188,10 @@
         copy.wait()
 
 
-def preload(arrays):
+def preload(arrays, after):
     return pl.pallas_call(
         preload_kernel,
-        in_specs=[pl.BlockSpec(memory_space=pl.ANY)] * len(arrays),
+        in_specs=[pl.BlockSpec(memory_space=pl.ANY)] * (len(arrays) + 1),
         out_specs=[pl.BlockSpec(memory_space=pltpu.VMEM)] * (len(arrays) + 1),
         out_shape=[pltpu.VMEM(array.shape, array.dtype) for array in arrays]
         + [jax.ShapeDtypeStruct((8, 128), jnp.float32)],
@@ -191,12 +201,16 @@
             flops=0, bytes_accessed=sum(2 * array.size for array in arrays), transcendentals=0
         ),
         name="preload",
-    )(*(pltpu.with_memory_space_constraint(array, pltpu.HBM) for array in arrays))
-
-
-def write_back(buffers, outputs, sems, slot, at):
+    )(*(pltpu.with_memory_space_constraint(array, pltpu.HBM) for array in arrays), after)
+
+
+def write_back(buffers, outputs, sems, slot, rows, columns):
     return [
-        pltpu.make_async_copy(buffer.at[slot, : at.size], out.at[at], sems.at[slot, which])
+        pltpu.make_async_copy(
+            buffer.at[slot, : rows.size, : columns.size],
+            out.at[rows, columns],
+            sems.at[slot, which],
+        )
         for which, (buffer, out) in enumerate(zip(buffers, outputs))
     ]
 
@@ -225,73 +239,77 @@
     power_ref = refs.pop(0)
     outs = [take(4) for _ in cuts]
     grads, buffers, power_sum, sems = (refs[0], refs[1]), (refs[2], refs[3]), refs[4], refs[5]
-    width = x_refs[0].shape[1]
-    strips = width // strip
+    pairs = x_refs[0].shape[1] // (2 * strip)
     base = 0
     for cut, (c_refs, w_ref, m_ref, v_ref), (hi_ref, lo_ref, *moments) in zip(cuts, ins, outs):
-        low = 0
-        for c_ref, rows in zip(c_refs, cut):
-            block = row_block(rows)
-            count = rows // block
-
-            def multiply(at, which, c_ref=c_ref, block=block):
-                lhs = c_ref[pl.ds(at * block, block), :]
-                columns = slice(which * strip, (which + 1) * strip)
+        for c_ref, low, rows in cut_rows(c_refs, cut):
+            place = pl.ds(low, rows)
+
+            def columns_of(pair, side):
+                return pl.ds(pl.multiple_of((2 * pair + side) * strip, strip), strip)
+
+            def multiply(pair, side, c_ref=c_ref, rows=rows):
+                columns = columns_of(pair, side)
                 rhs = jnp.concatenate([x_ref[:, columns] for x_ref in x_refs], axis=0)
-                grads[which % 2][:block] = jnp.dot(lhs, rhs, preferred_element_type=jnp.float32)
-
-            def one_block(at, low=low, base=base, count=count, block=block, multiply=multiply):
-                slot = at % 2
-                place = pl.ds(low + at * block, block)
-                if count > 2:
-
-                    @pl.when(at >= 2)
-                    def _():
-                        for copy in write_back(buffers, moments, sems, slot, place):
-                            copy.wait()
-
-                for which in range(strips):
-                    if which + 1 < strips:
-                        multiply(at, which + 1)
-                    elif count > 1:
-                        multiply(jnp.minimum(at + 1, count - 1), 0)
-                    columns = slice(which * strip, (which + 1) * strip)
-                    for row in range(0, block, 16):
+                grads[side][:rows] = jnp.dot(c_ref[...], rhs, preferred_element_type=jnp.float32)
+
+            def one_pair(pair, low=low, rows=rows, place=place, multiply=multiply):
+                for side in range(2):
+                    if side == 0:
+                        multiply(pair, 1)
+                    elif pairs > 1:
+                        multiply(jnp.minimum(pair + 1, pairs - 1), 0)
+                    columns = columns_of(pair, side)
+                    if pairs > 1:
+
+                        @pl.when(pair > 0)
+                        def _():
+                            for copy in write_back(buffers, moments, sems, side, place, columns):
+                                copy.wait()
+
+                    for row in range(0, rows, 16):
                         inside = slice(row, row + 16)
-                        tile = pl.ds(low + at * block + row, 16)
+                        tile = slice(low + row, low + row + 16)
                         first, square, step = update_tile(
-                            grads[which % 2][inside],
+                            grads[side][inside],
                             w_ref[tile, columns],
                             m_ref[tile, columns],
                             v_ref[tile, columns],
                         )
-                        buffers[0][slot, inside, columns] = first.astype(jnp.bfloat16)
-                        buffers[1][slot, inside, columns] = square.astype(jnp.bfloat16)
+                        buffers[0][side, inside] = first.astype(jnp.bfloat16)
+                        buffers[1][side, inside] = square.astype(jnp.bfloat16)
                         hi = step.astype(jnp.bfloat16)
                         hi_ref[tile, columns] = hi
                         lo_ref[tile, columns] = (step - hi.astype(jnp.float32)).astype(
                             jnp.bfloat16
                         )
-                        power = step[:, :128] * step[:, :128]
-                        for lane in range(128, strip, 128):
+                        power = power_sum[inside]
+                        for lane in range(0, strip, 128):
                             power += step[:, lane : lane + 128] * step[:, lane : lane + 128]
-                        if which:
-                            power += power_sum[inside]
                         power_sum[inside] = power
-                power_ref[:, pl.ds(base + low + at * block, block)] = jnp.sum(
-                    power_sum[:block].T, axis=0, keepdims=True
-                )
-                for copy in write_back(buffers, moments, sems, slot, place):
-                    copy.start()
-
+                    for copy in write_back(buffers, moments, sems, side, place, columns):
+                        copy.start()
+
+            power_sum[:rows] = jnp.zeros((rows, 128), jnp.float32)
             multiply(0, 0)
-            over_blocks(count, one_block)
-            for at in range(max(0, count - 2), count):
-                place = pl.ds(low + at * block, block)
-                for copy in write_back(buffers, moments, sems, at % 2, place):
+            over_blocks(pairs, one_pair)
+            start = base + low
+            power_ref[:, start : start + rows] = jnp.sum(
+                power_sum[:rows].T, axis=0, keepdims=True
+            )
+            for side in range(2):
+                for copy in write_back(buffers, moments, sems, side, place, columns_of(0, side)):
                     copy.wait()
-            low += rows
-        base += low
+        base += sum(cut)
+
+
+def cut_rows(c_refs, cut, largest=896):
+    start = 0
+    for c_ref, rows in zip(c_refs, cut):
+        block = row_block(rows, largest)
+        for low in range(0, rows, block):
+            yield c_ref.at[low : low + block], start + low, block
+        start += rows
 
 
 def strip_of(width, largest=256):
@@ -306,7 +324,7 @@
     strip = strip_of(width)
     cuts = [[piece.shape[0] for piece in pieces] for pieces in cotangents]
     rows = sum(sum(cut) for cut in cuts)
-    block = max(row_block(count) for cut in cuts for count in cut)
+    block = max(row_block(count, 896) for cut in cuts for count in cut)
     args, aliases, outs = list(x_pieces), {}, []
     for pieces, state in zip(cotangents, states):
         args += pieces
@@ -327,12 +345,12 @@
         scratch_shapes=[
             pltpu.VMEM((block, strip), jnp.float32),
             pltpu.VMEM((block, strip), jnp.float32),
-            pltpu.VMEM((2, block, width), jnp.bfloat16),
-            pltpu.VMEM((2, block, width), jnp.bfloat16),
+            pltpu.VMEM((2, block, strip), jnp.bfloat16),
+            pltpu.VMEM((2, block, strip), jnp.bfloat16),
             pltpu.VMEM((block, 128), jnp.float32),
             pltpu.SemaphoreType.DMA((2, 2)),
         ],
-        compiler_params=with_vmem(12),
+        compiler_params=with_vmem(8 + (18 * block + 4 * tokens) * strip // 2**20),
         cost_estimate=pl.CostEstimate(
             flops=2 * tokens * rows * width, bytes_accessed=4 * rows * width, transcendentals=0
         ),
@@ -351,15 +369,16 @@
         rows, width = hi_ref.shape
         block = row_block(rows, 128)
         total = rows // block
-
-        def one_block(at, base=base, block=block, total=total):
+        every = pl.ds(0, width)
+
+        def one_block(at, base=base, block=block, total=total, every=every):
             slot = at % slots
             place = pl.ds(at * block, block)
             if total > slots:
 
                 @pl.when(at >= slots)
                 def _():
-                    for copy in write_back([buffer], [out_ref], sems, slot, place):
+                    for copy in write_back([buffer], [out_ref], sems, slot, place, every):
                         copy.wait()
 
             lanes = pl.ds(base + at * block, block)
@@ -376,13 +395,13 @@
                     step = hi_ref[tile, columns].astype(jnp.float32)
                     step = step + lo_ref[tile, columns].astype(jnp.float32)
                     buffer[slot, inside, columns] = (step * scale[inside]).astype(jnp.bfloat16)
-            for copy in write_back([buffer], [out_ref], sems, slot, place):
+            for copy in write_back([buffer], [out_ref], sems, slot, place, every):
                 copy.start()
 
         over_blocks(total, one_block)
         for at in range(max(0, total - slots), total):
             place = pl.ds(at * block, block)
-            for copy in write_back([buffer], [out_ref], sems, at % slots, place):
+            for copy in write_back([buffer], [out_ref], sems, at % slots, place, every):
                 copy.wait()
         base += rows
 
@@ -411,15 +430,18 @@
     )(*powers, *(pltpu.with_memory_space_constraint(array, pltpu.VMEM) for array in parts))
 
 
-def from_others(array, axis):
-    size = lax.axis_size(axis)
-    bit = size // 2
-    got = {0: array}
-    while bit:
+def swap(array, axis, bit):
+    return lax.ppermute(array, axis, [(at, at ^ bit) for at in range(lax.axis_size(axis))])
+
+
+def from_others(pair, axis):
+    bit = lax.axis_size(axis) // 2
+    got = {0: pair[0], bit: pair[1]}
+    while bit > 1:
+        bit //= 2
         for turn in list(got):
-            got[turn ^ bit] = lax.ppermute(got[turn], axis, [(at, at ^ bit) for at in range(size)])
-        bit //= 2
-    return [got[turn] for turn in range(size)]
+            got[turn ^ bit] = swap(got[turn], axis, bit)
+    return [got[turn] for turn in range(len(got))]
 
 
 def straight_from_others(array, axis):
@@ -454,24 +476,42 @@
         (key_weight, moment_key, second_key),
         (up_weight, moment_up, second_up),
     )
+    place = jnp.stack([lax.axis_index("col"), lax.axis_index("dp")]).astype(jnp.int32)
     plan = chunk_plan([state[0].shape[0] for state in states])
-    place = jnp.stack([lax.axis_index("col"), lax.axis_index("dp")]).astype(jnp.int32)
-    packed = pack((query_cotangent, key_cotangent, up_cotangent), plan, groups, part, place)
-    step, ring = ring_steps(layer_input, "dp")
-    arrived = step()
-    *held, loaded = preload([array for state in states for array in state])
+    packed = [*pack((query_cotangent, key_cotangent, up_cotangent), plan, groups, part, place)]
+    behind, ahead = [layer_input], [layer_input]
+    swaps = [[], []]
+    for chunk in range(2):
+        one, two = ring_step(behind[-1], ahead[-1], "dp")
+        owned = lax.all_to_all(packed[chunk], "dp", split_axis=0, concat_axis=0, tiled=True)
+        if chunk == 0:
+            owned, one, two, packed[1] = join((owned, one, two, packed[1]))
+            swaps[0] = [owned, swap(owned, "col", cols // 2)]
+        else:
+            owned, one, two, swaps[0][1] = join((owned, one, two, swaps[0][1]))
+            swaps[1] = [owned, swap(owned, "col", cols // 2)]
+        behind.append(one)
+        ahead.append(two)
+    *held, loaded = preload([array for state in states for array in state], owned)
     held = [held[at : at + 3] for at in range(0, len(held), 3)]
-    packed = join(packed, (*arrived, loaded))
-    step()
-    owned = [
-        lax.all_to_all(array, "dp", split_axis=0, concat_axis=0, tiled=True) for array in packed
-    ]
-    step(owned)
-    for _ in range(groups):
-        step()
+    middle = []
+    while 2 * len(behind) <= groups:
+        if 2 * len(behind) < groups:
+            one, two = ring_step(behind[-1], ahead[-1], "dp")
+            if loaded is not None:
+                one, two, swaps[1][1] = join((one, two, swaps[1][1]), (loaded,))
+                loaded = None
+            behind.append(one)
+            ahead.append(two)
+        else:
+            middle = list(ring_step(*halves(behind[-1], ahead[-1]), "dp"))
+            break
+    x_pieces = [layer_input, *ahead[1:], *middle, *behind[:0:-1]]
     cotangents = [[], [], []]
-    for array, pieces in zip(owned, plan):
-        every = unpack(from_others(array, "col"), [high - low for _, low, high in pieces], place)
+    for got, pieces in zip(swaps, plan):
+        every = unpack(
+            from_others(got, "col"), [high - low for _, low, high in pieces], place
+        )
         for (which, _, _), cotangent in zip(pieces, every):
             cotangents[which].append(cotangent)
     updated = [None] * 3
@@ -479,7 +519,7 @@
     passes = []
     for group in ((2,), (0, 1)):
         power, made = adam_pass(
-            ring(), [cotangents[which] for which in group], [held[which] for which in group]
+            x_pieces, [cotangents[which] for which in group], [held[which] for which in group]
         )
         passes.append((group, straight_from_others(power, "col"), made))
     for group, powers, made in passes:

time: 166 us -> 155 us (0.934)
  blocking collectives: 23.5 us -> 0 us
  local copies, waits for them, and re-layouts: 25.1 us -> 3.54 us
  waiting for transfers between devices: 34.7 us -> 51 us
  starting transfers between devices: 24.2 us -> 33.9 us
  Pallas kernels: 57.2 us -> 65.6 us
    ppermute x14, waiting for transfers between devices: 19.4 us -> 48.7 us  [the longest x8 48.4 us: ring_step(): return (lax.ppermute(one, axis, onward), lax.ppermute(two, axis, back))]
    all_to_all x1 -> x0, blocking collectives: 23.5 us -> none  [per_device(): lax.all_to_all(array, 'dp', split_axis=0, concat_axis=0, tiled=True)]
    unnamed x56 -> x14, local copies, waits for them, and re-layouts: 25 us -> 3.54 us
    all_to_all x1 -> x2, waiting for transfers between devices: 13 us -> 0.01 us  [per_device(): lax.all_to_all(packed[chunk], 'dp', split_axis=0, concat_axis=0, tiled=True)]
    all_to_all x1 -> x2, starting transfers between devices: 4.2 us -> 14.1 us  [per_device(): lax.all_to_all(packed[chunk], 'dp', split_axis=0, concat_axis=0, tiled=True)]
    pallas_call x2, Pallas kernels: 34.5 us -> 43.6 us  [adam_pass(): pl.pallas_call(functools.partial(adam_kernel, strip, len(x_pieces), cuts)...]
  transfers between devices with their start and end apart: 21 -> 22, of which waited for: 10 -> 10; matrix products, arithmetic and copies ran while one was open for 0% -> 0% of each run, Pallas kernels for 18% -> 18%
where the time goes in v7:
time: 155 us
  Pallas kernels  65.6 us (42%)
  waiting for transfers between devices  51 us (33%)
  starting transfers between devices  33.9 us (22%)
  local copies, waits for them, and re-layouts  3.54 us (2%)
    ppermute x8, waiting for transfers between devices, ring_step(): return (lax.ppermute(one, axis, onward), lax.ppermute(two, axis, back))  48.4 us
    pallas_call x2, Pallas kernels, adam_pass(): pl.pallas_call(functools.partial(adam_kernel, strip, len(x_pieces), cuts)...  43.6 us
    all_to_all x2, starting transfers between devices, per_device(): lax.all_to_all(packed[chunk], 'dp', split_axis=0, concat_axis=0, tiled=True)  14.1 us
    ppermute x8, starting transfers between devices, ring_step(): return (lax.ppermute(one, axis, onward), lax.ppermute(two, axis, back))  11.2 us
    pallas_call x1, Pallas kernels, preload(): pl.pallas_call(preload_kernel, in_specs=[pl.BlockSpec(memory_space=pl.ANY...  9.66 us
    pallas_call x2, Pallas kernels, finish_rows(): pl.pallas_call(functools.partial(finish_kernel, len(powers), whole_width,...  6.85 us
    ppermute x6, starting transfers between devices, straight_from_others(): lax.ppermute(array, axis, [(at, at ^ turn) for at in range(size)])  4.6 us
    ppermute x6, starting transfers between devices, swap(): lax.ppermute(array, axis, [(at, at ^ bit) for at in range(lax.axis_size(a...  4 us
  transfers between devices with their start and end apart: 22, of which 10 were waited for; matrix products, arithmetic and copies ran while one was open for 0% of the time, Pallas kernels for 18%

profile of v7, /device:TPU:0, one launch (start us, length us, event | category | flops | bytes accessed | tf_op | source)
XLA Modules:
  0.0 155.0 jit_solution(10880166137345034742)
XLA Ops:
  0.6 0.0 copy-start.5
  0.7 0.1 pad_add_fusion.at_ref
  0.7 2.7 %pack.1 = (bf16[8,32,1152]{2,1,0:T(8,128)(2,1)}, bf16[8,32,1280]{2,1,0:T(8,128)(2,1)S(1)}) custom-call(s32[2]{0:T(128)S(1)} %pad_add_fusion.at_ref, bf16[128,4096]{1,0:T(8,128)(2,1)} %refs_0_.4, bf16[128,1024]{1,0:T(8,128)(2,1)} %refs_1_.2, bf16[128,14336]{1,0:T(8,128)(2,1)} %refs_2_.2), custom_call_target="tpu_custom_call" | custom-call | bytes 2490368 | tf_op jit(solution)/shard_map/pack/pallas_call | solution.py:67
  3.4 7.3 %all-to-all-start = ((bf16[8,32,1152]{2,1,0:T(8,128)(2,1)}), bf16[8,32,1152]{2,1,0:T(8,128)(2,1)S(1)}, u32[]{:S(2)}, u32[]{:S(2)}) async-start(bf16[8,32,1152]{2,1,0:T(8,128)(2,1)} %get-tuple-element.53), calls=%async_computation | async-start | bytes 1179648 | tf_op jit(solution)/shard_map/all_to_all | solution.py:486
  10.7 2.0 %collective-permute-start = (bf16[128,2048]{1,0:T(8,128)(2,1)S(1)}, bf16[128,2048]{1,0:T(8,128)(2,1)S(1)}, u32[]{:S(2)}, u32[]{:S(2)}) collective-permute-start(bf16[128,2048]{1,0:T(8,128)(2,1)S(1)} %copy-done.5), channel_id=1, source_target_pairs={{0,2},{2,4},{4,6},{6,7},{7,5},{5,3},{3,1},{1,0},{8,10},{10,12},{12... | collective-permute-start | bytes 1572872 | tf_op jit(solution)/shard_map/ppermute | solution.py:119
  12.7 0.1 collective-permute-start.1
  12.8 18.8 %collective-permute-done.refs_1_ = bf16[128,2048]{1,0:T(8,128)(2,1)S(1)} collective-permute-done((bf16[128,2048]{1,0:T(8,128)(2,1)S(1)}, bf16[128,2048]{1,0:T(8,128)(2,1)S(1)}, u32[]{:S(2)}, u32[]{:S(2)}) %collective-permute-start) | collective-permute-done | bytes 524320 | tf_op jit(solution)/shard_map/ppermute | solution.py:119
  31.6 2.2 %collective-permute-done.1.refs_2_ = bf16[128,2048]{1,0:T(8,128)(2,1)S(1)} collective-permute-done((bf16[128,2048]{1,0:T(8,128)(2,1)S(1)}, bf16[128,2048]{1,0:T(8,128)(2,1)S(1)}, u32[]{:S(2)}, u32[]{:S(2)}) %collective-permute-start.1) | collective-permute-done | bytes 524320 | tf_op jit(solution)/shard_map/ppermute | solution.py:119
  33.8 0.8 copy-done
  34.6 6.8 %all-to-all-start.1 = ((bf16[8,32,1280]{2,1,0:T(8,128)(2,1)}), bf16[8,32,1280]{2,1,0:T(8,128)(2,1)S(1)}, u32[]{:S(2)}, u32[]{:S(2)}) async-start(bf16[8,32,1280]{2,1,0:T(8,128)(2,1)} %copy-done), calls=%async_computation.1 | async-start | bytes 1310720 | tf_op jit(solution)/shard_map/all_to_all | solution.py:486
  41.5 1.5 collective-permute-start.4
  43.0 2.0 %collective-permute-start.2 = (bf16[128,2048]{1,0:T(8,128)(2,1)S(1)}, bf16[128,2048]{1,0:T(8,128)(2,1)S(1)}, u32[]{:S(2)}, u32[]{:S(2)}) collective-permute-start(bf16[128,2048]{1,0:T(8,128)(2,1)S(1)} %get-tuple-element.57.refs_8_), channel_id=1, source_target_pairs={{0,2},{2,4},{4,6},{6,7},{7,5},{5,3},{3,1},{1,0},{8,10},{10,12},{12... | collective-permute-start | bytes 1572872 | tf_op jit(solution)/shard_map/ppermute | solution.py:119
  45.0 0.0 collective-permute-start.3
  45.0 18.6 %collective-permute-done.2.refs_1_ = bf16[128,2048]{1,0:T(8,128)(2,1)S(1)} collective-permute-done((bf16[128,2048]{1,0:T(8,128)(2,1)S(1)}, bf16[128,2048]{1,0:T(8,128)(2,1)S(1)}, u32[]{:S(2)}, u32[]{:S(2)}) %collective-permute-start.2) | collective-permute-done | bytes 524320 | tf_op jit(solution)/shard_map/ppermute | solution.py:119
  63.6 2.2 %collective-permute-done.3.refs_2_ = bf16[128,2048]{1,0:T(8,128)(2,1)S(1)} collective-permute-done((bf16[128,2048]{1,0:T(8,128)(2,1)S(1)}, bf16[128,2048]{1,0:T(8,128)(2,1)S(1)}, u32[]{:S(2)}, u32[]{:S(2)}) %collective-permute-start.3) | collective-permute-done | bytes 524320 | tf_op jit(solution)/shard_map/ppermute | solution.py:119
  65.8 0.8 copy-done.1
  66.6 0.0 all-to-all-done.1.refs_0_
  66.6 1.1 copy-done.2
  67.7 0.8 copy-done.3
  68.5 1.5 collective-permute-start.7
  70.0 5.0 %collective-permute-start.5 = (bf16[128,2048]{1,0:T(8,128)(2,1)S(1)}, bf16[128,2048]{1,0:T(8,128)(2,1)S(1)}, u32[]{:S(2)}, u32[]{:S(2)}) collective-permute-start(bf16[128,2048]{1,0:T(8,128)(2,1)S(1)} %get-tuple-element.60.refs_7_), channel_id=1, source_target_pairs={{0,2},{2,4},{4,6},{6,7},{7,5},{5,3},{3,1},{1,0},{8,10},{10,12},{12... | collective-permute-start | bytes 1572872 | tf_op jit(solution)/shard_map/ppermute | solution.py:119
  74.9 0.0 collective-permute-start.10
  75.0 0.5 collective-permute-start.15
  75.5 9.7 %preload.1 = (bf16[512,2048]{1,0:T(8,128)(2,1)S(1)}, bf16[512,2048]{1,0:T(8,128)(2,1)S(1)}, bf16[512,2048]{1,0:T(8,128)(2,1)S(1)}, bf16[128,2048]{1,0:T(8,128)(2...) custom-call(bf16[512,2048]{1,0:T(8,128)(2,1)} %refs_0_.5, ...), custom_call_target="tpu_custom_call" | custom-call | bytes 29884416 | tf_op jit(solution)/shard_map/preload/pallas_call | solution.py:192
  85.1 0.0 collective-permute-done.5.refs_0_
  85.1 1.9 %collective-permute-done.6.refs_1_ = bf16[128,2048]{1,0:T(8,128)(2,1)S(1)} collective-permute-done((bf16[128,2048]{1,0:T(8,128)(2,1)S(1)}, bf16[128,2048]{1,0:T(8,128)(2,1)S(1)}, u32[]{:S(2)}, u32[]{:S(2)}) %collective-permute-start.6) | collective-permute-done | bytes 524320 | tf_op jit(solution)/shard_map/ppermute | solution.py:119
  87.1 0.0 collective-permute-done.7.refs_2_
  87.1 0.5 collective-permute-start.11
  87.6 1.9 %collective-permute-start.8 = (bf16[64,2048]{1,0:T(8,128)(2,1)S(1)}, bf16[64,2048]{1,0:T(8,128)(2,1)S(1)}, u32[]{:S(2)}, u32[]{:S(2)}) collective-permute-start(bf16[64,2048]{1,0:T(8,128)(2,1)S(1)} %get-tuple-element.65), channel_id=1, source_target_pairs={{0,2},{2,4},{4,6},{6,7},{7,5},{5,3},{3,1},{1,0},{8,10},{10,12},{12... | collective-permute-start | bytes 786440 | tf_op jit(solution)/shard_map/ppermute | solution.py:119
  89.5 0.0 collective-permute-done.10.refs_1_
  89.5 0.2 collective-permute-start.9
  89.7 0.3 collective-permute-done.11.refs_3_
  90.0 1.4 unpack.2
  91.4 1.4 unpack.3.refs_10_
  92.8 3.2 %collective-permute-done.8.refs_4_ = bf16[64,2048]{1,0:T(8,128)(2,1)S(1)} collective-permute-done((bf16[64,2048]{1,0:T(8,128)(2,1)S(1)}, bf16[64,2048]{1,0:T(8,128)(2,1)S(1)}, u32[]{:S(2)}, u32[]{:S(2)}) %collective-permute-start.8) | collective-permute-done | bytes 262176 | tf_op jit(solution)/shard_map/ppermute | solution.py:119
  96.0 1.5 collective-permute-done.9.refs_5_
  97.5 30.4 %adam.3 = (f32[1,1792]{1,0:T(1,128)S(1)}, bf16[1792,2048]{1,0:T(8,128)(2,1)S(1)}, bf16[1792,2048]{1,0:T(8,128)(2,1)S(1)}, bf16[1792,2048]{1,0:T(8,128)(2,1)}, bf16[1792,2048]{1,0:T(8,128)(2,1)}) custom-call(bf16[128,2048]{1,0:T(8,128)(2,1)S(1)} %copy-done.6, ...), custom_call_target="tpu_custom_call", output_to_operand_aliasing={{1}: (11, {}), {2}: (12, {})} | custom-call | flops 7516192768 | bytes 14680064 | tf_op jit(solution)/shard_map/adam/pallas_call | solution.py:339
  127.9 0.1 collective-permute-start.17
  128.0 1.6 %collective-permute-start.18 = (f32[1,1792]{1,0:T(1,128)S(1)}, f32[1,1792]{1,0:T(1,128)S(1)}, u32[]{:S(2)}, u32[]{:S(2)}) collective-permute-start(f32[1,1792]{1,0:T(1,128)S(1)} %get-tuple-element.88.refs_0_), channel_id=1, source_target_pairs={{0,16},{8,24},{16,0},{24,8},{1,17},{9,25},{17,1},{25,9},{2,18},{10... | collective-permute-start | bytes 21512 | tf_op jit(solution)/shard_map/ppermute | solution.py:450
  129.5 0.3 collective-permute-start.19
  129.9 13.2 %adam.2 = (f32[1,640]{1,0:T(1,128)S(1)}, bf16[512,2048]{1,0:T(8,128)(2,1)S(1)}, bf16[512,2048]{1,0:T(8,128)(2,1)S(1)}, bf16[512,2048]{1,0:T(8,128)(2,1)}, bf16[5...) custom-call(bf16[128,2048]{1,0:T(8,128)(2,1)S(1)} %copy-done.6, ...), custom_call_target="tpu_custom_call", output_to_operand_aliasing={{1}: (10, {}), {2}: (11, {}), {5}: (14, {}), {6}: (15, {})} | custom-call | flops 2684354560 | bytes 5242880 | tf_op jit(solution)/shard_map/adam/pallas_call | solution.py:339
  143.1 0.4 collective-permute-start.12
  143.5 1.5 collective-permute-start.13
  145.0 0.8 collective-permute-start.14
  145.7 1.3 collective-permute-done.13.refs_2_
  147.1 0.9 collective-permute-done.14.refs_3_
  148.0 2.6 %finish.2 = (bf16[512,2048]{1,0:T(8,128)(2,1)}, bf16[128,2048]{1,0:T(8,128)(2,1)}) custom-call(f32[1,640]{1,0:T(1,128)S(1)} %get-tuple-element.76.refs_0_, f32[1,640]{1,0:T(1,128)S(1)} %collective-permute-done.12.refs_1_, f32[1,640]{1,0:T(1,128)S(1)} %collective-permute-done.13.refs_2_, f32[1,640]{1,0:T(1,128)S(1)} %collective-permute-done.14.refs_3_, ...), custom_call_target="tpu_custom_call" | custom-call | flops 2621440 | bytes 2621440 | tf_op jit(solution)/shard_map/finish/pallas_call | solution.py:414
  150.7 4.2 %finish.3 = bf16[1792,2048]{1,0:T(8,128)(2,1)} custom-call(f32[1,1792]{1,0:T(1,128)S(1)} %get-tuple-element.88.refs_0_, f32[1,1792]{1,0:T(1,128)S(1)} %collective-permute-done.17.refs_1_, f32[1,1792]{1,0:T(1,128)S(1)} %collective-permute-done.18.refs_2_, f32[1,1792]{1,0:T(1,128)S(1)} %collective-permute-done.19.refs_3_, ...), custom_call_target="tpu_custom_call" | custom-call | flops 7340032 | bytes 7340032 | tf_op jit(solution)/shard_map/finish/pallas_call | solution.py:414
  (23 shorter events, 0.1 us)
Async XLA Ops:
  0.6 10.1 %copy-start.5 = (bf16[128,2048]{1,0:T(8,128)(2,1)S(1)}, bf16[128,2048]{1,0:T(8,128)(2,1)}, u32[]{:S(2)}) copy-start(bf16[128,2048]{1,0:T(8,128)(2,1)} %refs_0_.7) | copy-start | bytes 1572868
  3.4 30.4 %all-to-all-start = ((bf16[8,32,1152]{2,1,0:T(8,128)(2,1)}), bf16[8,32,1152]{2,1,0:T(8,128)(2,1)S(1)}, u32[]{:S(2)}, u32[]{:S(2)}) async-start(bf16[8,32,1152]{2,1,0:T(8,128)(2,1)} %get-tuple-element.53), calls=%async_computation | async-start | bytes 1179648 | tf_op jit(solution)/shard_map/all_to_all | solution.py:486
  10.7 20.9 %collective-permute-start = (bf16[128,2048]{1,0:T(8,128)(2,1)S(1)}, bf16[128,2048]{1,0:T(8,128)(2,1)S(1)}, u32[]{:S(2)}, u32[]{:S(2)}) collective-permute-start(bf16[128,2048]{1,0:T(8,128)(2,1)S(1)} %copy-done.5), channel_id=1, source_target_pairs={{0,2},{2,4},{4,6},{6,7},{7,5},{5,3},{3,1},{1,0},{8,10},{10,12},{12... | collective-permute-start | bytes 1572872 | tf_op jit(solution)/shard_map/ppermute | solution.py:119
  12.7 21.0 %collective-permute-start.1 = (bf16[128,2048]{1,0:T(8,128)(2,1)S(1)}, bf16[128,2048]{1,0:T(8,128)(2,1)S(1)}, u32[]{:S(2)}, u32[]{:S(2)}) collective-permute-start(bf16[128,2048]{1,0:T(8,128)(2,1)S(1)} %copy-done.5), channel_id=1, source_target_pairs={{2,0},{4,2},{6,4},{7,6},{5,7},{3,5},{1,3},{0,1},{10,8},{12,10},{14... | collective-permute-start | bytes 1572872 | tf_op jit(solution)/shard_map/ppermute | solution.py:119
  33.8 0.8 copy-start
  34.6 32.0 %all-to-all-start.1 = ((bf16[8,32,1280]{2,1,0:T(8,128)(2,1)}), bf16[8,32,1280]{2,1,0:T(8,128)(2,1)S(1)}, u32[]{:S(2)}, u32[]{:S(2)}) async-start(bf16[8,32,1280]{2,1,0:T(8,128)(2,1)} %copy-done), calls=%async_computation.1 | async-start | bytes 1310720 | tf_op jit(solution)/shard_map/all_to_all | solution.py:486
  41.5 24.3 %collective-permute-start.4 = (bf16[8,32,1152]{2,1,0:T(8,128)(2,1)S(1)}, bf16[8,32,1152]{2,1,0:T(8,128)(2,1)S(1)}, u32[]{:S(2)}, u32[]{:S(2)}) collective-permute-start(bf16[8,32,1152]{2,1,0:T(8,128)(2,1)S(1)} %get-tuple-element.58.refs_0_), channel_id=1, source_target_pairs={{0,16},{8,24},{16,0},{24,8},{1,17},{9,25},{17,1},{25,9},{2,18},{10... | collective-permute-start | bytes 1769480 | tf_op jit(solution)/shard_map/ppermute | solution.py:434
  43.0 20.6 %collective-permute-start.2 = (bf16[128,2048]{1,0:T(8,128)(2,1)S(1)}, bf16[128,2048]{1,0:T(8,128)(2,1)S(1)}, u32[]{:S(2)}, u32[]{:S(2)}) collective-permute-start(bf16[128,2048]{1,0:T(8,128)(2,1)S(1)} %get-tuple-element.57.refs_8_), channel_id=1, source_target_pairs={{0,2},{2,4},{4,6},{6,7},{7,5},{5,3},{3,1},{1,0},{8,10},{10,12},{12... | collective-permute-start | bytes 1572872 | tf_op jit(solution)/shard_map/ppermute | solution.py:119
  45.0 20.8 %collective-permute-start.3 = (bf16[128,2048]{1,0:T(8,128)(2,1)S(1)}, bf16[128,2048]{1,0:T(8,128)(2,1)S(1)}, u32[]{:S(2)}, u32[]{:S(2)}) collective-permute-start(bf16[128,2048]{1,0:T(8,128)(2,1)S(1)} %get-tuple-element.55.refs_1_), channel_id=1, source_target_pairs={{2,0},{4,2},{6,4},{7,6},{5,7},{3,5},{1,3},{0,1},{10,8},{12,10},{14... | collective-permute-start | bytes 1572872 | tf_op jit(solution)/shard_map/ppermute | solution.py:119
  65.8 0.8 copy-start.1
  66.6 1.1 copy-start.2
  67.7 0.8 copy-start.3
  68.5 18.6 %collective-permute-start.7 = (bf16[8,32,1280]{2,1,0:T(8,128)(2,1)S(1)}, bf16[8,32,1280]{2,1,0:T(8,128)(2,1)S(1)}, u32[]{:S(2)}, u32[]{:S(2)}) collective-permute-start(bf16[8,32,1280]{2,1,0:T(8,128)(2,1)S(1)} %get-tuple-element.61.refs_9_.refs_0_), channel_id=1, source_target_pairs={{0,16},{8,24},{16,0},{24,8},{1,17},{9,25},{17,1},{25,9},{2,18},{10... | collective-permute-start | bytes 1966088 | tf_op jit(solution)/shard_map/ppermute | solution.py:434
  70.0 15.2 %collective-permute-start.5 = (bf16[128,2048]{1,0:T(8,128)(2,1)S(1)}, bf16[128,2048]{1,0:T(8,128)(2,1)S(1)}, u32[]{:S(2)}, u32[]{:S(2)}) collective-permute-start(bf16[128,2048]{1,0:T(8,128)(2,1)S(1)} %get-tuple-element.60.refs_7_), channel_id=1, source_target_pairs={{0,2},{2,4},{4,6},{6,7},{7,5},{5,3},{3,1},{1,0},{8,10},{10,12},{12... | collective-permute-start | bytes 1572872 | tf_op jit(solution)/shard_map/ppermute | solution.py:119
  74.9 12.1 %copy-start.4 = (bf16[8,32,1152]{2,1,0:T(8,128)(2,1)S(1)}, bf16[8,32,1152]{2,1,0:T(8,128)(2,1)}, u32[]{:S(2)}) copy-start(bf16[8,32,1152]{2,1,0:T(8,128)(2,1)} %copy-done.3) | copy-start | bytes 1769476
  74.9 12.1 %collective-permute-start.6 = (bf16[128,2048]{1,0:T(8,128)(2,1)S(1)}, bf16[128,2048]{1,0:T(8,128)(2,1)S(1)}, u32[]{:S(2)}, u32[]{:S(2)}) collective-permute-start(bf16[128,2048]{1,0:T(8,128)(2,1)S(1)} %get-tuple-element.59.refs_2_), channel_id=1, source_target_pairs={{2,0},{4,2},{6,4},{7,6},{5,7},{3,5},{1,3},{0,1},{10,8},{12,10},{14... | collective-permute-start | bytes 1572872 | tf_op jit(solution)/shard_map/ppermute | solution.py:119
  74.9 14.6 %collective-permute-start.10 = (bf16[8,32,1152]{2,1,0:T(8,128)(2,1)S(1)}, bf16[8,32,1152]{2,1,0:T(8,128)(2,1)S(1)}, u32[]{:S(2)}, u32[]{:S(2)}) collective-permute-start(bf16[8,32,1152]{2,1,0:T(8,128)(2,1)S(1)} %get-tuple-element.58.refs_0_), channel_id=1, source_target_pairs={{0,8},{8,0},{16,24},{24,16},{1,9},{9,1},{17,25},{25,17},{2,10},{10... | collective-permute-start | bytes 1769480 | tf_op jit(solution)/shard_map/ppermute | solution.py:434
  75.0 16.4 %collective-permute-start.15 = (bf16[8,32,1280]{2,1,0:T(8,128)(2,1)S(1)}, bf16[8,32,1280]{2,1,0:T(8,128)(2,1)S(1)}, u32[]{:S(2)}, u32[]{:S(2)}) collective-permute-start(bf16[8,32,1280]{2,1,0:T(8,128)(2,1)S(1)} %get-tuple-element.61.refs_9_.refs_0_), channel_id=1, source_target_pairs={{0,8},{8,0},{16,24},{24,16},{1,9},{9,1},{17,25},{25,17},{2,10},{10... | collective-permute-start | bytes 1966088 | tf_op jit(solution)/shard_map/ppermute | solution.py:434
  87.1 4.3 %collective-permute-start.16 = (bf16[8,32,1280]{2,1,0:T(8,128)(2,1)S(1)}, bf16[8,32,1280]{2,1,0:T(8,128)(2,1)S(1)}, u32[]{:S(2)}, u32[]{:S(2)}) collective-permute-start(bf16[8,32,1280]{2,1,0:T(8,128)(2,1)S(1)} %get-tuple-element.84.refs_2_), channel_id=1, source_target_pairs={{0,8},{8,0},{16,24},{24,16},{1,9},{9,1},{17,25},{25,17},{2,10},{10... | collective-permute-start | bytes 1966088 | tf_op jit(solution)/shard_map/ppermute | solution.py:434
  87.1 2.9 %collective-permute-start.11 = (bf16[8,32,1152]{2,1,0:T(8,128)(2,1)S(1)}, bf16[8,32,1152]{2,1,0:T(8,128)(2,1)S(1)}, u32[]{:S(2)}, u32[]{:S(2)}) collective-permute-start(bf16[8,32,1152]{2,1,0:T(8,128)(2,1)S(1)} %copy-done.4), channel_id=1, source_target_pairs={{0,8},{8,0},{16,24},{24,16},{1,9},{9,1},{17,25},{25,17},{2,10},{10... | collective-permute-start | bytes 1769480 | tf_op jit(solution)/shard_map/ppermute | solution.py:434
  87.6 8.3 %collective-permute-start.8 = (bf16[64,2048]{1,0:T(8,128)(2,1)S(1)}, bf16[64,2048]{1,0:T(8,128)(2,1)S(1)}, u32[]{:S(2)}, u32[]{:S(2)}) collective-permute-start(bf16[64,2048]{1,0:T(8,128)(2,1)S(1)} %get-tuple-element.65), channel_id=1, source_target_pairs={{0,2},{2,4},{4,6},{6,7},{7,5},{5,3},{3,1},{1,0},{8,10},{10,12},{12... | collective-permute-start | bytes 786440 | tf_op jit(solution)/shard_map/ppermute | solution.py:119
  89.5 7.9 %copy-start.6 = (bf16[128,2048]{1,0:T(8,128)(2,1)S(1)}, bf16[128,2048]{1,0:T(8,128)(2,1)}, u32[]{:S(2)}) copy-start(bf16[128,2048]{1,0:T(8,128)(2,1)} %refs_0_.7) | copy-start | bytes 1572868
  89.5 7.9 %collective-permute-start.9 = (bf16[64,2048]{1,0:T(8,128)(2,1)S(1)}, bf16[64,2048]{1,0:T(8,128)(2,1)S(1)}, u32[]{:S(2)}, u32[]{:S(2)}) collective-permute-start(bf16[64,2048]{1,0:T(8,128)(2,1)S(1)} %get-tuple-element.66), channel_id=1, source_target_pairs={{2,0},{4,2},{6,4},{7,6},{5,7},{3,5},{1,3},{0,1},{10,8},{12,10},{14... | collective-permute-start | bytes 786440 | tf_op jit(solution)/shard_map/ppermute | solution.py:119
  127.9 22.7 %collective-permute-start.17 = (f32[1,1792]{1,0:T(1,128)S(1)}, f32[1,1792]{1,0:T(1,128)S(1)}, u32[]{:S(2)}, u32[]{:S(2)}) collective-permute-start(f32[1,1792]{1,0:T(1,128)S(1)} %get-tuple-element.88.refs_0_), channel_id=1, source_target_pairs={{0,8},{8,0},{16,24},{24,16},{1,9},{9,1},{17,25},{25,17},{2,10},{10... | collective-permute-start | bytes 21512 | tf_op jit(solution)/shard_map/ppermute | solution.py:450
  128.0 22.6 %collective-permute-start.18 = (f32[1,1792]{1,0:T(1,128)S(1)}, f32[1,1792]{1,0:T(1,128)S(1)}, u32[]{:S(2)}, u32[]{:S(2)}) collective-permute-start(f32[1,1792]{1,0:T(1,128)S(1)} %get-tuple-element.88.refs_0_), channel_id=1, source_target_pairs={{0,16},{8,24},{16,0},{24,8},{1,17},{9,25},{17,1},{25,9},{2,18},{10... | collective-permute-start | bytes 21512 | tf_op jit(solution)/shard_map/ppermute | solution.py:450
  129.5 21.1 %collective-permute-start.19 = (f32[1,1792]{1,0:T(1,128)S(1)}, f32[1,1792]{1,0:T(1,128)S(1)}, u32[]{:S(2)}, u32[]{:S(2)}) collective-permute-start(f32[1,1792]{1,0:T(1,128)S(1)} %get-tuple-element.88.refs_0_), channel_id=1, source_target_pairs={{0,24},{8,16},{16,8},{24,0},{1,25},{9,17},{17,9},{25,1},{2,26},{10... | collective-permute-start | bytes 21512 | tf_op jit(solution)/shard_map/ppermute | solution.py:450
  143.1 1.9 %collective-permute-start.12 = (f32[1,640]{1,0:T(1,128)S(1)}, f32[1,640]{1,0:T(1,128)S(1)}, u32[]{:S(2)}, u32[]{:S(2)}) collective-permute-start(f32[1,640]{1,0:T(1,128)S(1)} %get-tuple-element.76.refs_0_), channel_id=1, source_target_pairs={{0,8},{8,0},{16,24},{24,16},{1,9},{9,1},{17,25},{25,17},{2,10},{10... | collective-permute-start | bytes 7688 | tf_op jit(solution)/shard_map/ppermute | solution.py:450
  143.5 3.6 %collective-permute-start.13 = (f32[1,640]{1,0:T(1,128)S(1)}, f32[1,640]{1,0:T(1,128)S(1)}, u32[]{:S(2)}, u32[]{:S(2)}) collective-permute-start(f32[1,640]{1,0:T(1,128)S(1)} %get-tuple-element.76.refs_0_), channel_id=1, source_target_pairs={{0,16},{8,24},{16,0},{24,8},{1,17},{9,25},{17,1},{25,9},{2,18},{10... | collective-permute-start | bytes 7688 | tf_op jit(solution)/shard_map/ppermute | solution.py:450
  145.0 3.0 %collective-permute-start.14 = (f32[1,640]{1,0:T(1,128)S(1)}, f32[1,640]{1,0:T(1,128)S(1)}, u32[]{:S(2)}, u32[]{:S(2)}) collective-permute-start(f32[1,640]{1,0:T(1,128)S(1)} %get-tuple-element.76.refs_0_), channel_id=1, source_target_pairs={{0,24},{8,16},{16,8},{24,0},{1,25},{9,17},{17,9},{25,1},{2,26},{10... | collective-permute-start | bytes 7688 | tf_op jit(solution)/shard_map/ppermute | solution.py:450

commit v8 on v6

--- a/solution.py
+++ b/solution.py
@@ -23,16 +23,6 @@
         if rows % block == 0:
             return block
     return rows
-
-
-def chunk_plan(totals):
-    first = [(which, 0, total) for which, total in enumerate(totals[:-1])]
-    up = len(totals) - 1
-    block = row_block(totals[up])
-    blocks = max(0, (sum(totals) // 2 - sum(totals[:-1])) // block)
-    if blocks:
-        first.append((up, 0, blocks * block))
-    return [first, [(up, blocks * block, totals[up])]]
 
 
 def ring_order(groups):
@@ -86,47 +76,56 @@
     )(place, *(pltpu.with_memory_space_constraint(array, pltpu.HBM) for array in cotangents))
 
 
-def ring_steps(array, axis):
-    groups = lax.axis_size(axis)
+def halves_kernel(one_ref, two_ref, first_ref, last_ref):
+    half = first_ref.shape[0]
+    first_ref[...] = one_ref[:half]
+    last_ref[...] = two_ref[half:]
+
+
+def halves(one, two):
+    half = jax.ShapeDtypeStruct((one.shape[0] // 2, one.shape[1]), one.dtype)
+    vmem = pl.BlockSpec(memory_space=pltpu.VMEM)
+    return pl.pallas_call(
+        halves_kernel,
+        in_specs=[vmem] * 2,
+        out_specs=[vmem] * 2,
+        out_shape=[half] * 2,
+        compiler_params=with_vmem(4),
+        cost_estimate=pl.CostEstimate(
+            flops=0, bytes_accessed=4 * one.size, transcendentals=0
+        ),
+        name="halves",
+    )(one, two)
+
+
+def ring_paths(groups):
     order = ring_order(groups)
     onward = list(zip(order, order[1:] + order[:1]))
-    back = [(to, at) for at, to in onward]
-    behind, ahead, middle = [array], [array], []
-
-    def step(after=()):
-        one, two = behind[-1], ahead[-1]
-        if after:
-            one, two = join((one, two), after)
-            behind[-1], ahead[-1] = one, two
-        if len(behind) <= (groups - 1) // 2:
-            behind.append(lax.ppermute(one, axis, onward))
-            ahead.append(lax.ppermute(two, axis, back))
-        elif groups % 2 == 0 and not middle:
-            half = array.shape[0] // 2
-            middle.append(lax.ppermute(one[:half], axis, onward))
-            middle.append(lax.ppermute(two[half:], axis, back))
-        return behind[-1], ahead[-1]
-
-    def done():
-        return [array, *ahead[1:], *middle, *behind[:0:-1]]
-
-    return step, done
+    return onward, [(to, at) for at, to in onward]
+
+
+def ring_step(one, two, axis):
+    onward, back = ring_paths(lax.axis_size(axis))
+    return lax.ppermute(one, axis, onward), lax.ppermute(two, axis, back)
 
 
 def unpack_kernel(count, at_ref, *refs):
-    pieces, outputs, order = refs[:count], refs[count:-1], refs[-1]
-    groups, part, _ = pieces[0].shape
-    for group in range(groups):
-        slot = ring_place(group, groups) - ring_place(at_ref[1], groups) + groups
-        for turn, piece in enumerate(pieces):
-            order[slot % groups * count + (at_ref[0] ^ turn)] = piece[group]
+    pieces, outputs, orders = refs[:count], refs[count:-2], refs[-2:]
+    groups = pieces[0].shape[0]
+    here = ring_place(at_ref[1], groups)
+    slots = [(ring_place(group, groups) - here + groups) % groups for group in range(groups)]
     low = 0
     for out_ref in outputs:
         rows = out_ref.shape[0]
         for start in range(0, rows, 128):
             high = min(start + 128, rows)
-            tokens = order[:, :, low + start : low + high].reshape(-1, high - start)
-            out_ref[start:high] = tokens.T
+            order = orders[start // 128 % 2]
+            for group, slot in enumerate(slots):
+                for turn, piece in enumerate(pieces):
+                    order[slot * count + (at_ref[0] ^ turn), :, : high - start] = piece[
+                        group, :, low + start : low + high
+                    ]
+            out_ref[start:high] = order[...].reshape(-1, 128).T[: high - start]
         low += rows
 
 
@@ -134,13 +133,14 @@
     groups, part, rows = pieces[0].shape
     tokens = groups * part * len(pieces)
     vmem = pl.BlockSpec(memory_space=pltpu.VMEM)
+    order = pltpu.VMEM((groups * len(pieces), part, 128), jnp.bfloat16)
     return pl.pallas_call(
         functools.partial(unpack_kernel, len(pieces)),
         in_specs=[pl.BlockSpec(memory_space=pltpu.SMEM)] + [vmem] * len(pieces),
         out_specs=[vmem] * len(row_counts),
         out_shape=[pltpu.VMEM((count, tokens), jnp.bfloat16) for count in row_counts],
-        scratch_shapes=[pltpu.VMEM((groups * len(pieces), part, rows), jnp.bfloat16)],
-        compiler_params=with_vmem(12),
+        scratch_shapes=[order, order],
+        compiler_params=with_vmem(4 + 6 * tokens * 256 // 2**20),
         cost_estimate=pl.CostEstimate(
             flops=0, bytes_accessed=4 * tokens * rows, transcendentals=0
         ),
@@ -152,7 +152,7 @@
     pass
 
 
-def join(arrays, after):
+def join(arrays, after=()):
     count = len(arrays)
     hbm = pl.BlockSpec(memory_space=pl.ANY)
     return pl.pallas_call(
@@ -167,9 +167,9 @@
 
 
 def preload_kernel(*refs):
-    count = (len(refs) - 2) // 2
+    count = (len(refs) - 3) // 2
     token, sems = refs[-2:]
-    outputs = refs[count:]
+    outputs = refs[count + 1 :]
     copies = [pltpu.make_async_copy(refs[at], outputs[at], sems.at[at]) for at in range(count)]
     token[...] = jnp.zeros_like(token)
     for copy in copies:
@@ -178,10 +178,10 @@
         copy.wait()
 
 
-def preload(arrays):
+def preload(arrays, after):
     return pl.pallas_call(
         preload_kernel,
-        in_specs=[pl.BlockSpec(memory_space=pl.ANY)] * len(arrays),
+        in_specs=[pl.BlockSpec(memory_space=pl.ANY)] * (len(arrays) + 1),
         out_specs=[pl.BlockSpec(memory_space=pltpu.VMEM)] * (len(arrays) + 1),
         out_shape=[pltpu.VMEM(array.shape, array.dtype) for array in arrays]
         + [jax.ShapeDtypeStruct((8, 128), jnp.float32)],
@@ -191,7 +191,7 @@
             flops=0, bytes_accessed=sum(2 * array.size for array in arrays), transcendentals=0
         ),
         name="preload",
-    )(*(pltpu.with_memory_space_constraint(array, pltpu.HBM) for array in arrays))
+    )(*(pltpu.with_memory_space_constraint(array, pltpu.HBM) for array in arrays), after)
 
 
 def write_back(buffers, outputs, sems, slot, at):
@@ -343,7 +343,7 @@
 
 def finish_kernel(count, whole_width, matrices, *refs):
     powers, refs = refs[:count], refs[count:]
-    parts, outputs, (buffer, sems) = refs[: 2 * matrices], refs[2 * matrices : -2], refs[-2:]
+    parts, outputs, (buffer, sems) = refs[: 2 * matrices], refs[-2 - matrices : -2], refs[-2:]
     slots = buffer.shape[0]
     base = 0
     for which, out_ref in enumerate(outputs):
@@ -387,14 +387,15 @@
         base += rows
 
 
-def finish_rows(parts, powers, whole_width):
+def finish_rows(parts, powers, whole_width, after):
     shapes = [array.shape for array in parts[::2]]
     width = shapes[0][1]
     block = max(row_block(shape[0], 128) for shape in shapes)
     vmem = pl.BlockSpec(memory_space=pltpu.VMEM)
     return pl.pallas_call(
         functools.partial(finish_kernel, len(powers), whole_width, len(shapes)),
-        in_specs=[vmem] * (len(powers) + len(parts)),
+        in_specs=[vmem] * (len(powers) + len(parts))
+        + [pl.BlockSpec(memory_space=pl.ANY)] * len(after),
         out_specs=[pl.BlockSpec(memory_space=pl.ANY)] * len(shapes),
         out_shape=[jax.ShapeDtypeStruct(shape, jnp.bfloat16) for shape in shapes],
         scratch_shapes=[
@@ -408,18 +409,25 @@
             transcendentals=0,
         ),
         name="finish",
-    )(*powers, *(pltpu.with_memory_space_constraint(array, pltpu.VMEM) for array in parts))
-
-
-def from_others(array, axis):
-    size = lax.axis_size(axis)
-    bit = size // 2
-    got = {0: array}
-    while bit:
+    )(
+        *powers,
+        *(pltpu.with_memory_space_constraint(array, pltpu.VMEM) for array in parts),
+        *after,
+    )
+
+
+def swap(array, axis, bit):
+    return lax.ppermute(array, axis, [(at, at ^ bit) for at in range(lax.axis_size(axis))])
+
+
+def from_others(pair, axis):
+    bit = lax.axis_size(axis) // 2
+    got = {0: pair[0], bit: pair[1]}
+    while bit > 1:
+        bit //= 2
         for turn in list(got):
-            got[turn ^ bit] = lax.ppermute(got[turn], axis, [(at, at ^ bit) for at in range(size)])
-        bit //= 2
-    return [got[turn] for turn in range(size)]
+            got[turn ^ bit] = swap(got[turn], axis, bit)
+    return [got[turn] for turn in range(len(got))]
 
 
 def straight_from_others(array, axis):
@@ -454,24 +462,38 @@
         (key_weight, moment_key, second_key),
         (up_weight, moment_up, second_up),
     )
-    plan = chunk_plan([state[0].shape[0] for state in states])
     place = jnp.stack([lax.axis_index("col"), lax.axis_index("dp")]).astype(jnp.int32)
+    plan = [[(2, 0, up_weight.shape[0])]]
+    plan.append([(which, 0, states[which][0].shape[0]) for which in (0, 1)])
     packed = pack((query_cotangent, key_cotangent, up_cotangent), plan, groups, part, place)
-    step, ring = ring_steps(layer_input, "dp")
-    arrived = step()
-    *held, loaded = preload([array for state in states for array in state])
+    one, two = ring_step(layer_input, layer_input, "dp")
+    chunk, one, two = join((packed[0], one, two))
+    behind, ahead = [layer_input, one], [layer_input, two]
+    owned = lax.all_to_all(chunk, "dp", split_axis=0, concat_axis=0, tiled=True)
+    one, two = ring_step(one, two, "dp")
+    owned, one, two, chunk = join((owned, one, two, packed[1]))
+    behind.append(one)
+    ahead.append(two)
+    swaps = [(owned, swap(owned, "col", cols // 2))]
+    owned = lax.all_to_all(chunk, "dp", split_axis=0, concat_axis=0, tiled=True)
+    one, two = ring_step(one, two, "dp")
+    owned, one, two = join((owned, one, two), (swaps[0][1],))
+    behind.append(one)
+    ahead.append(two)
+    swaps.append((owned, swap(owned, "col", cols // 2)))
+    *held, _ = preload([array for state in states for array in state], owned)
     held = [held[at : at + 3] for at in range(0, len(held), 3)]
-    packed = join(packed, (*arrived, loaded))
-    step()
-    owned = [
-        lax.all_to_all(array, "dp", split_axis=0, concat_axis=0, tiled=True) for array in packed
-    ]
-    step(owned)
-    for _ in range(groups):
-        step()
+    while 2 * len(behind) < groups:
+        one, two = ring_step(one, two, "dp")
+        behind.append(one)
+        ahead.append(two)
+    middle = ring_step(*halves(one, two), "dp")
+    x_pieces = [layer_input, *ahead[1:], *middle, *behind[:0:-1]]
     cotangents = [[], [], []]
-    for array, pieces in zip(owned, plan):
-        every = unpack(from_others(array, "col"), [high - low for _, low, high in pieces], place)
+    for got, pieces in zip(swaps, plan):
+        every = unpack(
+            from_others(got, "col"), [high - low for _, low, high in pieces], place
+        )
         for (which, _, _), cotangent in zip(pieces, every):
             cotangents[which].append(cotangent)
     updated = [None] * 3
@@ -479,12 +501,14 @@
     passes = []
     for group in ((2,), (0, 1)):
         power, made = adam_pass(
-            ring(), [cotangents[which] for which in group], [held[which] for which in group]
+            x_pieces, [cotangents[which] for which in group], [held[which] for which in group]
         )
         passes.append((group, straight_from_others(power, "col"), made))
     for group, powers, made in passes:
         parts = [array for done in made for array in done[:2]]
-        for which, done, array in zip(group, made, finish_rows(parts, powers, whole_width)):
+        after = [array for array in updated if array is not None]
+        finished = finish_rows(parts, powers, whole_width, after)
+        for which, done, array in zip(group, made, finished):
             updated[which] = array
             moments[which] = done[2:]
     return (*updated, *(done[0] for done in moments), *(done[1] for done in moments))

time: 166 us -> 151 us (0.910)
  waiting for transfers between devices: 34.7 us -> 61.1 us
  blocking collectives: 23.5 us -> 0 us
  local copies, waits for them, and re-layouts: 25.1 us -> 3.1 us
  starting transfers between devices: 24.2 us -> 28.9 us
    ppermute x14, waiting for transfers between devices: 19.4 us -> 61.1 us  [the longest x8 45.3 us: ring_step(): return (lax.ppermute(one, axis, onward), lax.ppermute(two, axis, back))]
    all_to_all x1 -> x0, blocking collectives: 23.5 us -> none  [per_device(): lax.all_to_all(array, 'dp', split_axis=0, concat_axis=0, tiled=True)]
    unnamed x56 -> x8, local copies, waits for them, and re-layouts: 25 us -> 3.1 us
    all_to_all x1 -> x2, waiting for transfers between devices: 13 us -> 0.01 us  [per_device(): owned = lax.all_to_all(chunk, 'dp', split_axis=0, concat_axis=0, tiled=True)]
    all_to_all x1 -> x2, starting transfers between devices: 4.2 us -> 13.5 us  [per_device(): owned = lax.all_to_all(chunk, 'dp', split_axis=0, concat_axis=0, tiled=True)]
    ppermute x14, starting transfers between devices: 15.5 us -> 11.5 us  [the longest x8 9.44 us: ring_step(): return (lax.ppermute(one, axis, onward), lax.ppermute(two, axis, back))]
    pallas_call x2, Pallas kernels: 34.5 us -> 31.7 us  [adam_pass(): pl.pallas_call(functools.partial(adam_kernel, strip, len(x_pieces), cuts)...]
    ppermute x6, waiting for transfers between devices: 2.26 us -> 0.02 us  [straight_from_others(): lax.ppermute(array, axis, [(at, at ^ turn) for at in range(size)])]
  transfers between devices with their start and end apart: 21 -> 22, of which waited for: 10 -> 8; matrix products, arithmetic and copies ran while one was open for 0% -> 0% of each run, Pallas kernels for 18% -> 21%
where the time goes in v8:
time: 151 us; the launch traced here: 150 us
  waiting for transfers between devices  61.1 us (40%)
  Pallas kernels  55.8 us (37%)
  starting transfers between devices  28.9 us (19%)
  local copies, waits for them, and re-layouts  3.1 us (2%)
    ppermute x8, waiting for transfers between devices, ring_step(): return (lax.ppermute(one, axis, onward), lax.ppermute(two, axis, back))  45.3 us
    pallas_call x2, Pallas kernels, adam_pass(): pl.pallas_call(functools.partial(adam_kernel, strip, len(x_pieces), cuts)...  31.7 us
    ppermute x6, waiting for transfers between devices, swap(): lax.ppermute(array, axis, [(at, at ^ bit) for at in range(lax.axis_size(a...  15.8 us
    all_to_all x2, starting transfers between devices, per_device(): owned = lax.all_to_all(chunk, 'dp', split_axis=0, concat_axis=0, tiled=True)  13.5 us
    pallas_call x1, Pallas kernels, preload(): pl.pallas_call(preload_kernel, in_specs=[pl.BlockSpec(memory_space=pl.ANY...  10.3 us
    ppermute x8, starting transfers between devices, ring_step(): return (lax.ppermute(one, axis, onward), lax.ppermute(two, axis, back))  9.44 us
    pallas_call x2, Pallas kernels, finish_rows(): pl.pallas_call(functools.partial(finish_kernel, len(powers), whole_width,...  6.83 us
    pallas_call x2, Pallas kernels, unpack(): pl.pallas_call(functools.partial(unpack_kernel, len(pieces)), in_specs=[p...  4.01 us
  transfers between devices with their start and end apart: 22, of which 8 were waited for; matrix products, arithmetic and copies ran while one was open for 0% of the time, Pallas kernels for 21%

profile of v8, /device:TPU:0, one launch (start us, length us, event | category | flops | bytes accessed | tf_op | source)
XLA Modules:
  0.0 149.8 jit_solution(2338934519494622305)
XLA Ops:
  0.6 3.1 %collective-permute-start = (bf16[128,2048]{1,0:T(8,128)(2,1)}, bf16[128,2048]{1,0:T(8,128)(2,1)S(1)}, u32[]{:S(2)}, u32[]{:S(2)}) collective-permute-start(bf16[128,2048]{1,0:T(8,128)(2,1)} %refs_0_.7), channel_id=1, source_target_pairs={{0,2},{2,4},{4,6},{6,7},{7,5},{5,3},{3,1},{1,0},{8,10},{10,12},{12... | collective-permute-start | bytes 1572872 | tf_op jit(solution)/shard_map/ppermute | solution.py:109
  3.7 0.0 collective-permute-start.1
  3.7 0.1 pad_add_fusion.at_ref
  3.8 2.9 %pack.1 = (bf16[8,32,1792]{2,1,0:T(8,128)(2,1)}, bf16[8,32,640]{2,1,0:T(8,128)(2,1)}) custom-call(s32[2]{0:T(128)S(1)} %pad_add_fusion.at_ref, bf16[128,4096]{1,0:T(8,128)(2,1)} %refs_0_.4, bf16[128,1024]{1,0:T(8,128)(2,1)} %refs_1_.2, bf16[128,14336]{1,0:T(8,128)(2,1)} %refs_2_.2), custom_call_target="tpu_custom_call" | custom-call | bytes 2490368 | tf_op jit(solution)/shard_map/pack/pallas_call | solution.py:57
  6.7 9.1 %collective-permute-done.refs_1_ = bf16[128,2048]{1,0:T(8,128)(2,1)S(1)} collective-permute-done((bf16[128,2048]{1,0:T(8,128)(2,1)}, bf16[128,2048]{1,0:T(8,128)(2,1)S(1)}, u32[]{:S(2)}, u32[]{:S(2)}) %collective-permute-start) | collective-permute-done | bytes 524320 | tf_op jit(solution)/shard_map/ppermute | solution.py:109
  15.8 1.5 %collective-permute-done.1.refs_2_ = bf16[128,2048]{1,0:T(8,128)(2,1)S(1)} collective-permute-done((bf16[128,2048]{1,0:T(8,128)(2,1)}, bf16[128,2048]{1,0:T(8,128)(2,1)S(1)}, u32[]{:S(2)}, u32[]{:S(2)}) %collective-permute-start.1) | collective-permute-done | bytes 524320 | tf_op jit(solution)/shard_map/ppermute | solution.py:109
  17.3 4.8 %all-to-all-start = ((bf16[8,32,1792]{2,1,0:T(8,128)(2,1)}), bf16[8,32,1792]{2,1,0:T(8,128)(2,1)S(1)}, u32[]{:S(2)}, u32[]{:S(2)}) async-start(bf16[8,32,1792]{2,1,0:T(8,128)(2,1)} %get-tuple-element.52), calls=%async_computation | async-start | bytes 1835008 | tf_op jit(solution)/shard_map/all_to_all | solution.py:472
  22.1 2.0 %collective-permute-start.2 = (bf16[128,2048]{1,0:T(8,128)(2,1)S(1)}, bf16[128,2048]{1,0:T(8,128)(2,1)}, u32[]{:S(2)}, u32[]{:S(2)}) collective-permute-start(bf16[128,2048]{1,0:T(8,128)(2,1)S(1)} %get-tuple-element.53.refs_8_), channel_id=1, source_target_pairs={{0,2},{2,4},{4,6},{6,7},{7,5},{5,3},{3,1},{1,0},{8,10},{10,12},{12... | collective-permute-start | bytes 1572872 | tf_op jit(solution)/shard_map/ppermute | solution.py:109
  24.2 0.0 collective-permute-start.3
  24.2 23.2 %collective-permute-done.2.refs_1_ = bf16[128,2048]{1,0:T(8,128)(2,1)} collective-permute-done((bf16[128,2048]{1,0:T(8,128)(2,1)S(1)}, bf16[128,2048]{1,0:T(8,128)(2,1)}, u32[]{:S(2)}, u32[]{:S(2)}) %collective-permute-start.2) | collective-permute-done | bytes 524320 | tf_op jit(solution)/shard_map/ppermute | solution.py:109
  47.3 2.0 %collective-permute-done.3.refs_2_ = bf16[128,2048]{1,0:T(8,128)(2,1)S(1)} collective-permute-done((bf16[128,2048]{1,0:T(8,128)(2,1)S(1)}, bf16[128,2048]{1,0:T(8,128)(2,1)S(1)}, u32[]{:S(2)}, u32[]{:S(2)}) %collective-permute-start.3) | collective-permute-done | bytes 524320 | tf_op jit(solution)/shard_map/ppermute | solution.py:109
  49.3 0.0 all-to-all-done.refs_0_
  49.3 1.5 collective-permute-start.6
  50.8 8.7 %all-to-all-start.1 = ((bf16[8,32,640]{2,1,0:T(8,128)(2,1)}), bf16[8,32,640]{2,1,0:T(8,128)(2,1)S(1)}, u32[]{:S(2)}, u32[]{:S(2)}) async-start(bf16[8,32,640]{2,1,0:T(8,128)(2,1)} %get-tuple-element.56), calls=%async_computation.1 | async-start | bytes 655360 | tf_op jit(solution)/shard_map/all_to_all | solution.py:478
  59.6 2.0 %collective-permute-start.4 = (bf16[128,2048]{1,0:T(8,128)(2,1)}, bf16[128,2048]{1,0:T(8,128)(2,1)S(1)}, u32[]{:S(2)}, u32[]{:S(2)}) collective-permute-start(bf16[128,2048]{1,0:T(8,128)(2,1)} %get-tuple-element.57.refs_7_), channel_id=1, source_target_pairs={{0,2},{2,4},{4,6},{6,7},{7,5},{5,3},{3,1},{1,0},{8,10},{10,12},{12... | collective-permute-start | bytes 1572872 | tf_op jit(solution)/shard_map/ppermute | solution.py:109
  61.6 0.1 collective-permute-start.5
  61.6 0.0 collective-permute-start.15
  61.6 7.6 %collective-permute-done.6.refs_3_.refs_2_ = bf16[8,32,1792]{2,1,0:T(8,128)(2,1)} collective-permute-done((bf16[8,32,1792]{2,1,0:T(8,128)(2,1)S(1)}, bf16[8,32,1792]{2,1,0:T(8,128)(2,1)}, u32[]{:S(2)}, u32[]{:S(2)}) %collective-permute-start.6) | collective-permute-done | bytes 917536 | tf_op jit(solution)/shard_map/ppermute | solution.py:420
  69.2 0.0 collective-permute-start.16
  69.2 7.3 %collective-permute-done.4.refs_1_ = bf16[128,2048]{1,0:T(8,128)(2,1)S(1)} collective-permute-done((bf16[128,2048]{1,0:T(8,128)(2,1)}, bf16[128,2048]{1,0:T(8,128)(2,1)S(1)}, u32[]{:S(2)}, u32[]{:S(2)}) %collective-permute-start.4) | collective-permute-done | bytes 524320 | tf_op jit(solution)/shard_map/ppermute | solution.py:109
  76.5 2.4 %collective-permute-done.5.refs_2_ = bf16[128,2048]{1,0:T(8,128)(2,1)S(1)} collective-permute-done((bf16[128,2048]{1,0:T(8,128)(2,1)}, bf16[128,2048]{1,0:T(8,128)(2,1)S(1)}, u32[]{:S(2)}, u32[]{:S(2)}) %collective-permute-start.5) | collective-permute-done | bytes 524320 | tf_op jit(solution)/shard_map/ppermute | solution.py:109
  78.8 0.0 all-to-all-done.1.refs_0_
  78.8 0.5 collective-permute-start.10
  79.4 8.2 %collective-permute-done.10.refs_2_ = bf16[8,32,640]{2,1,0:T(8,128)(2,1)S(1)} collective-permute-done((bf16[8,32,640]{2,1,0:T(8,128)(2,1)S(1)}, bf16[8,32,640]{2,1,0:T(8,128)(2,1)S(1)}, u32[]{:S(2)}, u32[]{:S(2)}) %collective-permute-start.10) | collective-permute-done | bytes 327712 | tf_op jit(solution)/shard_map/ppermute | solution.py:420
  87.5 0.0 collective-permute-start.11
  87.6 2.2 %collective-permute-start.7 = (bf16[64,2048]{1,0:T(8,128)(2,1)S(1)}, bf16[64,2048]{1,0:T(8,128)(2,1)S(1)}, u32[]{:S(2)}, u32[]{:S(2)}) collective-permute-start(bf16[64,2048]{1,0:T(8,128)(2,1)S(1)} %get-tuple-element.61), channel_id=1, source_target_pairs={{0,2},{2,4},{4,6},{6,7},{7,5},{5,3},{3,1},{1,0},{8,10},{10,12},{12... | collective-permute-start | bytes 786440 | tf_op jit(solution)/shard_map/ppermute | solution.py:109
  89.8 10.3 %preload.1 = (bf16[512,2048]{1,0:T(8,128)(2,1)S(1)}, bf16[512,2048]{1,0:T(8,128)(2,1)S(1)}, bf16[512,2048]{1,0:T(8,128)(2,1)S(1)}, bf16[128,2048]{1,0:T(8,128)(2...) custom-call(bf16[512,2048]{1,0:T(8,128)(2,1)} %refs_0_.5, ...), custom_call_target="tpu_custom_call" | custom-call | bytes 29884416 | tf_op jit(solution)/shard_map/preload/pallas_call | solution.py:182
  100.1 1.1 unpack.2
  101.2 0.0 copy-start.2
  101.2 0.0 copy-start.3
  101.2 0.0 collective-permute-done.15.refs_1_
  101.2 2.9 %unpack.3.refs_9_ = bf16[1792,1024]{1,0:T(8,128)(2,1)S(1)} custom-call(s32[2]{0:T(128)S(1)} %pad_add_fusion.at_ref, bf16[8,32,1792]{2,1,0:T(8,128)(2,1)S(1)} %get-tuple-element.58.refs_0_, bf16[8,32,1792]{2,1,0:T(8,128)(2,1)} %collective-permute-done.15.refs_1_, bf16[8,32,1792]{2,1,0:T(8,128)(2,1)} %collective-permute-done.6.refs_3_.refs_2_, ...), custom_call_target="tpu_custom_call" | custom-call | bytes 7340032 | tf_op jit(solution)/shard_map/unpack/pallas_call | solution.py:137
  104.2 0.0 collective-permute-done.8.refs_5_
  104.2 21.4 %adam.3 = (f32[1,1792]{1,0:T(1,128)S(1)}, bf16[1792,2048]{1,0:T(8,128)(2,1)S(1)}, bf16[1792,2048]{1,0:T(8,128)(2,1)S(1)}, bf16[1792,2048]{1,0:T(8,128)(2,1)}, bf16[1792,2048]{1,0:T(8,128)(2,1)}) custom-call(bf16[128,2048]{1,0:T(8,128)(2,1)S(1)} %copy-done.3, ...), custom_call_target="tpu_custom_call", output_to_operand_aliasing={{1}: (10, {}), {2}: (11, {})} | custom-call | flops 7516192768 | bytes 14680064 | tf_op jit(solution)/shard_map/adam/pallas_call | solution.py:321
  125.6 0.3 collective-permute-start.17
  125.9 0.5 collective-permute-start.18
  126.5 1.1 collective-permute-start.19
  127.6 10.3 %adam.2 = (f32[1,640]{1,0:T(1,128)S(1)}, bf16[512,2048]{1,0:T(8,128)(2,1)S(1)}, bf16[512,2048]{1,0:T(8,128)(2,1)S(1)}, bf16[512,2048]{1,0:T(8,128)(2,1)}, bf16[5...) custom-call(bf16[128,2048]{1,0:T(8,128)(2,1)S(1)} %copy-done.3, ...), custom_call_target="tpu_custom_call", output_to_operand_aliasing={{1}: (10, {}), {2}: (11, {}), {5}: (14, {}), {6}: (15, {})} | custom-call | flops 2684354560 | bytes 5242880 | tf_op jit(solution)/shard_map/adam/pallas_call | solution.py:321
  137.9 0.6 collective-permute-start.12
  138.4 0.5 collective-permute-start.13
  139.0 0.0 collective-permute-done.17.refs_1_
  139.0 0.9 collective-permute-start.14
  139.9 0.0 collective-permute-done.19.refs_3_
  139.9 4.2 %finish.2.refs_8_ = bf16[1792,2048]{1,0:T(8,128)(2,1)} custom-call(f32[1,1792]{1,0:T(1,128)S(1)} %get-tuple-element.80.refs_0_, f32[1,1792]{1,0:T(1,128)S(1)} %collective-permute-done.17.refs_1_, f32[1,1792]{1,0:T(1,128)S(1)} %collective-permute-done.18.refs_2_, f32[1,1792]{1,0:T(1,128)S(1)} %collective-permute-done.19.refs_3_, ...), custom_call_target="tpu_custom_call" | custom-call | flops 7340032 | bytes 7340032 | tf_op jit(solution)/shard_map/finish/pallas_call | solution.py:395
  144.1 0.0 collective-permute-done.12.refs_1_
  144.1 0.0 copy-start
  144.1 3.1 %copy-done = bf16[1792,2048]{1,0:T(8,128)(2,1)S(1)} copy-done((bf16[1792,2048]{1,0:T(8,128)(2,1)S(1)}, bf16[1792,2048]{1,0:T(8,128)(2,1)}, u32[]{:S(2)}) %copy-start) | copy-done | bytes 7340056
  147.2 2.6 %finish.3 = (bf16[512,2048]{1,0:T(8,128)(2,1)}, bf16[128,2048]{1,0:T(8,128)(2,1)}) custom-call(f32[1,640]{1,0:T(1,128)S(1)} %get-tuple-element.72.refs_0_, f32[1,640]{1,0:T(1,128)S(1)} %collective-permute-done.12.refs_1_, f32[1,640]{1,0:T(1,128)S(1)} %collective-permute-done.13.refs_2_, f32[1,640]{1,0:T(1,128)S(1)} %collective-permute-done.14.refs_3_, ...), custom_call_target="tpu_custom_call" | custom-call | flops 2621440 | bytes 2621440 | tf_op jit(solution)/shard_map/finish/pallas_call | solution.py:395
  (17 shorter events, 0.1 us)
Async XLA Ops:
  0.6 15.2 %collective-permute-start = (bf16[128,2048]{1,0:T(8,128)(2,1)}, bf16[128,2048]{1,0:T(8,128)(2,1)S(1)}, u32[]{:S(2)}, u32[]{:S(2)}) collective-permute-start(bf16[128,2048]{1,0:T(8,128)(2,1)} %refs_0_.7), channel_id=1, source_target_pairs={{0,2},{2,4},{4,6},{6,7},{7,5},{5,3},{3,1},{1,0},{8,10},{10,12},{12... | collective-permute-start | bytes 1572872 | tf_op jit(solution)/shard_map/ppermute | solution.py:109
  3.7 13.6 %collective-permute-start.1 = (bf16[128,2048]{1,0:T(8,128)(2,1)}, bf16[128,2048]{1,0:T(8,128)(2,1)S(1)}, u32[]{:S(2)}, u32[]{:S(2)}) collective-permute-start(bf16[128,2048]{1,0:T(8,128)(2,1)} %refs_0_.7), channel_id=1, source_target_pairs={{2,0},{4,2},{6,4},{7,6},{5,7},{3,5},{1,3},{0,1},{10,8},{12,10},{14... | collective-permute-start | bytes 1572872 | tf_op jit(solution)/shard_map/ppermute | solution.py:109
  17.3 32.0 %all-to-all-start = ((bf16[8,32,1792]{2,1,0:T(8,128)(2,1)}), bf16[8,32,1792]{2,1,0:T(8,128)(2,1)S(1)}, u32[]{:S(2)}, u32[]{:S(2)}) async-start(bf16[8,32,1792]{2,1,0:T(8,128)(2,1)} %get-tuple-element.52), calls=%async_computation | async-start | bytes 1835008 | tf_op jit(solution)/shard_map/all_to_all | solution.py:472
  22.1 25.2 %collective-permute-start.2 = (bf16[128,2048]{1,0:T(8,128)(2,1)S(1)}, bf16[128,2048]{1,0:T(8,128)(2,1)}, u32[]{:S(2)}, u32[]{:S(2)}) collective-permute-start(bf16[128,2048]{1,0:T(8,128)(2,1)S(1)} %get-tuple-element.53.refs_8_), channel_id=1, source_target_pairs={{0,2},{2,4},{4,6},{6,7},{7,5},{5,3},{3,1},{1,0},{8,10},{10,12},{12... | collective-permute-start | bytes 1572872 | tf_op jit(solution)/shard_map/ppermute | solution.py:109
  24.2 25.2 %collective-permute-start.3 = (bf16[128,2048]{1,0:T(8,128)(2,1)S(1)}, bf16[128,2048]{1,0:T(8,128)(2,1)S(1)}, u32[]{:S(2)}, u32[]{:S(2)}) collective-permute-start(bf16[128,2048]{1,0:T(8,128)(2,1)S(1)} %get-tuple-element.51.refs_1_), channel_id=1, source_target_pairs={{2,0},{4,2},{6,4},{7,6},{5,7},{3,5},{1,3},{0,1},{10,8},{12,10},{14... | collective-permute-start | bytes 1572872 | tf_op jit(solution)/shard_map/ppermute | solution.py:109
  49.3 10.2 %copy-start.1 = (bf16[128,2048]{1,0:T(8,128)(2,1)}, bf16[128,2048]{1,0:T(8,128)(2,1)S(1)}, u32[]{:S(2)}) copy-start(bf16[128,2048]{1,0:T(8,128)(2,1)S(1)} %get-tuple-element.55.refs_2_) | copy-start | bytes 1572868
  49.3 19.9 %collective-permute-start.6 = (bf16[8,32,1792]{2,1,0:T(8,128)(2,1)S(1)}, bf16[8,32,1792]{2,1,0:T(8,128)(2,1)}, u32[]{:S(2)}, u32[]{:S(2)}) collective-permute-start(bf16[8,32,1792]{2,1,0:T(8,128)(2,1)S(1)} %get-tuple-element.58.refs_0_), channel_id=1, source_target_pairs={{0,16},{8,24},{16,0},{24,8},{1,17},{9,25},{17,1},{25,9},{2,18},{10... | collective-permute-start | bytes 2752520 | tf_op jit(solution)/shard_map/ppermute | solution.py:420
  50.8 28.0 %all-to-all-start.1 = ((bf16[8,32,640]{2,1,0:T(8,128)(2,1)}), bf16[8,32,640]{2,1,0:T(8,128)(2,1)S(1)}, u32[]{:S(2)}, u32[]{:S(2)}) async-start(bf16[8,32,640]{2,1,0:T(8,128)(2,1)} %get-tuple-element.56), calls=%async_computation.1 | async-start | bytes 655360 | tf_op jit(solution)/shard_map/all_to_all | solution.py:478
  59.6 16.9 %collective-permute-start.4 = (bf16[128,2048]{1,0:T(8,128)(2,1)}, bf16[128,2048]{1,0:T(8,128)(2,1)S(1)}, u32[]{:S(2)}, u32[]{:S(2)}) collective-permute-start(bf16[128,2048]{1,0:T(8,128)(2,1)} %get-tuple-element.57.refs_7_), channel_id=1, source_target_pairs={{0,2},{2,4},{4,6},{6,7},{7,5},{5,3},{3,1},{1,0},{8,10},{10,12},{12... | collective-permute-start | bytes 1572872 | tf_op jit(solution)/shard_map/ppermute | solution.py:109
  61.6 17.2 %collective-permute-start.5 = (bf16[128,2048]{1,0:T(8,128)(2,1)}, bf16[128,2048]{1,0:T(8,128)(2,1)S(1)}, u32[]{:S(2)}, u32[]{:S(2)}) collective-permute-start(bf16[128,2048]{1,0:T(8,128)(2,1)} %copy-done.1), channel_id=1, source_target_pairs={{2,0},{4,2},{6,4},{7,6},{5,7},{3,5},{1,3},{0,1},{10,8},{12,10},{14... | collective-permute-start | bytes 1572872 | tf_op jit(solution)/shard_map/ppermute | solution.py:109
  61.6 39.5 %collective-permute-start.15 = (bf16[8,32,1792]{2,1,0:T(8,128)(2,1)S(1)}, bf16[8,32,1792]{2,1,0:T(8,128)(2,1)}, u32[]{:S(2)}, u32[]{:S(2)}) collective-permute-start(bf16[8,32,1792]{2,1,0:T(8,128)(2,1)S(1)} %get-tuple-element.58.refs_0_), channel_id=1, source_target_pairs={{0,8},{8,0},{16,24},{24,16},{1,9},{9,1},{17,25},{25,17},{2,10},{10... | collective-permute-start | bytes 2752520 | tf_op jit(solution)/shard_map/ppermute | solution.py:420
  69.2 32.0 %collective-permute-start.16 = (bf16[8,32,1792]{2,1,0:T(8,128)(2,1)}, bf16[8,32,1792]{2,1,0:T(8,128)(2,1)}, u32[]{:S(2)}, u32[]{:S(2)}) collective-permute-start(bf16[8,32,1792]{2,1,0:T(8,128)(2,1)} %collective-permute-done.6.refs_3_.refs_2_), channel_id=1, source_target_pairs={{0,8},{8,0},{16,24},{24,16},{1,9},{9,1},{17,25},{25,17},{2,10},{10... | collective-permute-start | bytes 2752520 | tf_op jit(solution)/shard_map/ppermute | solution.py:420
  78.8 8.7 %collective-permute-start.10 = (bf16[8,32,640]{2,1,0:T(8,128)(2,1)S(1)}, bf16[8,32,640]{2,1,0:T(8,128)(2,1)S(1)}, u32[]{:S(2)}, u32[]{:S(2)}) collective-permute-start(bf16[8,32,640]{2,1,0:T(8,128)(2,1)S(1)} %get-tuple-element.63.refs_0_.refs_9_), channel_id=1, source_target_pairs={{0,16},{8,24},{16,0},{24,8},{1,17},{9,25},{17,1},{25,9},{2,18},{10... | collective-permute-start | bytes 983048 | tf_op jit(solution)/shard_map/ppermute | solution.py:420
  79.3 10.5 %collective-permute-start.9 = (bf16[8,32,640]{2,1,0:T(8,128)(2,1)S(1)}, bf16[8,32,640]{2,1,0:T(8,128)(2,1)S(1)}, u32[]{:S(2)}, u32[]{:S(2)}) collective-permute-start(bf16[8,32,640]{2,1,0:T(8,128)(2,1)S(1)} %get-tuple-element.63.refs_0_.refs_9_), channel_id=1, source_target_pairs={{0,8},{8,0},{16,24},{24,16},{1,9},{9,1},{17,25},{25,17},{2,10},{10... | collective-permute-start | bytes 983048 | tf_op jit(solution)/shard_map/ppermute | solution.py:420
  87.5 12.5 %collective-permute-start.11 = (bf16[8,32,640]{2,1,0:T(8,128)(2,1)S(1)}, bf16[8,32,640]{2,1,0:T(8,128)(2,1)S(1)}, u32[]{:S(2)}, u32[]{:S(2)}) collective-permute-start(bf16[8,32,640]{2,1,0:T(8,128)(2,1)S(1)} %collective-permute-done.10.refs_2_), channel_id=1, source_target_pairs={{0,8},{8,0},{16,24},{24,16},{1,9},{9,1},{17,25},{25,17},{2,10},{10... | collective-permute-start | bytes 983048 | tf_op jit(solution)/shard_map/ppermute | solution.py:420
  87.6 16.6 %collective-permute-start.7 = (bf16[64,2048]{1,0:T(8,128)(2,1)S(1)}, bf16[64,2048]{1,0:T(8,128)(2,1)S(1)}, u32[]{:S(2)}, u32[]{:S(2)}) collective-permute-start(bf16[64,2048]{1,0:T(8,128)(2,1)S(1)} %get-tuple-element.61), channel_id=1, source_target_pairs={{0,2},{2,4},{4,6},{6,7},{7,5},{5,3},{3,1},{1,0},{8,10},{10,12},{12... | collective-permute-start | bytes 786440 | tf_op jit(solution)/shard_map/ppermute | solution.py:109
  89.8 14.4 %collective-permute-start.8 = (bf16[64,2048]{1,0:T(8,128)(2,1)S(1)}, bf16[64,2048]{1,0:T(8,128)(2,1)S(1)}, u32[]{:S(2)}, u32[]{:S(2)}) collective-permute-start(bf16[64,2048]{1,0:T(8,128)(2,1)S(1)} %get-tuple-element.62), channel_id=1, source_target_pairs={{2,0},{4,2},{6,4},{7,6},{5,7},{3,5},{1,3},{0,1},{10,8},{12,10},{14... | collective-permute-start | bytes 786440 | tf_op jit(solution)/shard_map/ppermute | solution.py:109
  101.2 3.0 %copy-start.2 = (bf16[128,2048]{1,0:T(8,128)(2,1)S(1)}, bf16[128,2048]{1,0:T(8,128)(2,1)}, u32[]{:S(2)}) copy-start(bf16[128,2048]{1,0:T(8,128)(2,1)} %copy-done.1) | copy-start | bytes 1572868
  101.2 3.0 %copy-start.3 = (bf16[128,2048]{1,0:T(8,128)(2,1)S(1)}, bf16[128,2048]{1,0:T(8,128)(2,1)}, u32[]{:S(2)}) copy-start(bf16[128,2048]{1,0:T(8,128)(2,1)} %refs_0_.7) | copy-start | bytes 1572868
  125.6 13.4 %collective-permute-start.17 = (f32[1,1792]{1,0:T(1,128)S(1)}, f32[1,1792]{1,0:T(1,128)S(1)}, u32[]{:S(2)}, u32[]{:S(2)}) collective-permute-start(f32[1,1792]{1,0:T(1,128)S(1)} %get-tuple-element.80.refs_0_), channel_id=1, source_target_pairs={{0,8},{8,0},{16,24},{24,16},{1,9},{9,1},{17,25},{25,17},{2,10},{10... | collective-permute-start | bytes 21512 | tf_op jit(solution)/shard_map/ppermute | solution.py:436
  125.9 14.0 %collective-permute-start.18 = (f32[1,1792]{1,0:T(1,128)S(1)}, f32[1,1792]{1,0:T(1,128)S(1)}, u32[]{:S(2)}, u32[]{:S(2)}) collective-permute-start(f32[1,1792]{1,0:T(1,128)S(1)} %get-tuple-element.80.refs_0_), channel_id=1, source_target_pairs={{0,16},{8,24},{16,0},{24,8},{1,17},{9,25},{17,1},{25,9},{2,18},{10... | collective-permute-start | bytes 21512 | tf_op jit(solution)/shard_map/ppermute | solution.py:436
  126.5 13.4 %collective-permute-start.19 = (f32[1,1792]{1,0:T(1,128)S(1)}, f32[1,1792]{1,0:T(1,128)S(1)}, u32[]{:S(2)}, u32[]{:S(2)}) collective-permute-start(f32[1,1792]{1,0:T(1,128)S(1)} %get-tuple-element.80.refs_0_), channel_id=1, source_target_pairs={{0,24},{8,16},{16,8},{24,0},{1,25},{9,17},{17,9},{25,1},{2,26},{10... | collective-permute-start | bytes 21512 | tf_op jit(solution)/shard_map/ppermute | solution.py:436
  137.9 6.2 %collective-permute-start.12 = (f32[1,640]{1,0:T(1,128)S(1)}, f32[1,640]{1,0:T(1,128)S(1)}, u32[]{:S(2)}, u32[]{:S(2)}) collective-permute-start(f32[1,640]{1,0:T(1,128)S(1)} %get-tuple-element.72.refs_0_), channel_id=1, source_target_pairs={{0,8},{8,0},{16,24},{24,16},{1,9},{9,1},{17,25},{25,17},{2,10},{10... | collective-permute-start | bytes 7688 | tf_op jit(solution)/shard_map/ppermute | solution.py:436
  138.4 5.7 %collective-permute-start.13 = (f32[1,640]{1,0:T(1,128)S(1)}, f32[1,640]{1,0:T(1,128)S(1)}, u32[]{:S(2)}, u32[]{:S(2)}) collective-permute-start(f32[1,640]{1,0:T(1,128)S(1)} %get-tuple-element.72.refs_0_), channel_id=1, source_target_pairs={{0,16},{8,24},{16,0},{24,8},{1,17},{9,25},{17,1},{25,9},{2,18},{10... | collective-permute-start | bytes 7688 | tf_op jit(solution)/shard_map/ppermute | solution.py:436
  139.0 5.1 %collective-permute-start.14 = (f32[1,640]{1,0:T(1,128)S(1)}, f32[1,640]{1,0:T(1,128)S(1)}, u32[]{:S(2)}, u32[]{:S(2)}) collective-permute-start(f32[1,640]{1,0:T(1,128)S(1)} %get-tuple-element.72.refs_0_), channel_id=1, source_target_pairs={{0,24},{8,16},{16,8},{24,0},{1,25},{9,17},{17,9},{25,1},{2,26},{10... | collective-permute-start | bytes 7688 | tf_op jit(solution)/shard_map/ppermute | solution.py:436
  144.1 3.1 %copy-start = (bf16[1792,2048]{1,0:T(8,128)(2,1)S(1)}, bf16[1792,2048]{1,0:T(8,128)(2,1)}, u32[]{:S(2)}) copy-start(bf16[1792,2048]{1,0:T(8,128)(2,1)} %finish.2.refs_8_) | copy-start | bytes 22020100

commit v9 on v8

--- a/solution.py
+++ b/solution.py
@@ -231,7 +231,7 @@
     for cut, (c_refs, w_ref, m_ref, v_ref), (hi_ref, lo_ref, *moments) in zip(cuts, ins, outs):
         low = 0
         for c_ref, rows in zip(c_refs, cut):
-            block = row_block(rows)
+            block = row_block(rows, 128)
             count = rows // block
 
             def multiply(at, which, c_ref=c_ref, block=block):
@@ -306,7 +306,7 @@
     strip = strip_of(width)
     cuts = [[piece.shape[0] for piece in pieces] for pieces in cotangents]
     rows = sum(sum(cut) for cut in cuts)
-    block = max(row_block(count) for cut in cuts for count in cut)
+    block = max(row_block(count, 128) for cut in cuts for count in cut)
     args, aliases, outs = list(x_pieces), {}, []
     for pieces, state in zip(cotangents, states):
         args += pieces
@@ -412,7 +412,7 @@
     )(
         *powers,
         *(pltpu.with_memory_space_constraint(array, pltpu.VMEM) for array in parts),
-        *after,
+        *(pltpu.with_memory_space_constraint(array, pltpu.HBM) for array in after),
     )
 
 
@@ -481,13 +481,15 @@
     behind.append(one)
     ahead.append(two)
     swaps.append((owned, swap(owned, "col", cols // 2)))
-    *held, _ = preload([array for state in states for array in state], owned)
-    held = [held[at : at + 3] for at in range(0, len(held), 3)]
     while 2 * len(behind) < groups:
         one, two = ring_step(one, two, "dp")
         behind.append(one)
         ahead.append(two)
-    middle = ring_step(*halves(one, two), "dp")
+    one, two = halves(one, two)
+    middle = ring_step(one, two, "dp")
+    *held, loaded = preload([array for state in states for array in state], one)
+    held = [held[at : at + 3] for at in range(0, len(held), 3)]
+    swaps[1] = join(swaps[1], (loaded, *middle))
     x_pieces = [layer_input, *ahead[1:], *middle, *behind[:0:-1]]
     cotangents = [[], [], []]
     for got, pieces in zip(swaps, plan):

time: 151 us -> 141 us (0.934)
  waiting for transfers between devices: 61.1 us -> 54.5 us
  local copies, waits for them, and re-layouts: 3.1 us -> 0.02 us
    ppermute x6, waiting for transfers between devices: 15.8 us -> 9.16 us  [swap(): lax.ppermute(array, axis, [(at, at ^ bit) for at in range(lax.axis_size(a...]
    unnamed x8 -> x6, local copies, waits for them, and re-layouts: 3.1 us -> 0.02 us
  transfers between devices with their start and end apart: 22 -> 22, of which waited for: 8 -> 9; matrix products, arithmetic and copies ran while one was open for 0% -> 0% of each run, Pallas kernels for 21% -> 20%
where the time goes in v9:
time: 141 us
  Pallas kernels  55.4 us (39%)
  waiting for transfers between devices  54.5 us (39%)
  starting transfers between devices  30 us (21%)
    ppermute x8, waiting for transfers between devices, ring_step(): return (lax.ppermute(one, axis, onward), lax.ppermute(two, axis, back))  45.3 us
    pallas_call x2, Pallas kernels, adam_pass(): pl.pallas_call(functools.partial(adam_kernel, strip, len(x_pieces), cuts)...  31.9 us
    all_to_all x2, starting transfers between devices, per_device(): owned = lax.all_to_all(chunk, 'dp', split_axis=0, concat_axis=0, tiled=True)  13.5 us
    ppermute x8, starting transfers between devices, ring_step(): return (lax.ppermute(one, axis, onward), lax.ppermute(two, axis, back))  9.94 us
    pallas_call x1, Pallas kernels, preload(): pl.pallas_call(preload_kernel, in_specs=[pl.BlockSpec(memory_space=pl.ANY...  9.66 us
    ppermute x6, waiting for transfers between devices, swap(): lax.ppermute(array, axis, [(at, at ^ bit) for at in range(lax.axis_size(a...  9.16 us
    pallas_call x2, Pallas kernels, finish_rows(): pl.pallas_call(functools.partial(finish_kernel, len(powers), whole_width,...  6.85 us
    pallas_call x2, Pallas kernels, unpack(): pl.pallas_call(functools.partial(unpack_kernel, len(pieces)), in_specs=[p...  4.02 us
  transfers between devices with their start and end apart: 22, of which 9 were waited for; matrix products, arithmetic and copies ran while one was open for 0% of the time, Pallas kernels for 20%

profile of v9, /device:TPU:0, one launch (start us, length us, event | category | flops | bytes accessed | tf_op | source)
XLA Modules:
  0.0 140.8 jit_solution(11484314140851765356)
XLA Ops:
  0.6 3.1 %collective-permute-start = (bf16[128,2048]{1,0:T(8,128)(2,1)}, bf16[128,2048]{1,0:T(8,128)(2,1)S(1)}, u32[]{:S(2)}, u32[]{:S(2)}) collective-permute-start(bf16[128,2048]{1,0:T(8,128)(2,1)} %refs_0_.7), channel_id=1, source_target_pairs={{0,2},{2,4},{4,6},{6,7},{7,5},{5,3},{3,1},{1,0},{8,10},{10,12},{12... | collective-permute-start | bytes 1572872 | tf_op jit(solution)/shard_map/ppermute | solution.py:109
  3.7 0.0 collective-permute-start.1
  3.7 0.1 pad_add_fusion.at_ref
  3.8 2.9 %pack.1 = (bf16[8,32,1792]{2,1,0:T(8,128)(2,1)}, bf16[8,32,640]{2,1,0:T(8,128)(2,1)}) custom-call(s32[2]{0:T(128)S(1)} %pad_add_fusion.at_ref, bf16[128,4096]{1,0:T(8,128)(2,1)} %refs_0_.4, bf16[128,1024]{1,0:T(8,128)(2,1)} %refs_1_.2, bf16[128,14336]{1,0:T(8,128)(2,1)} %refs_2_.2), custom_call_target="tpu_custom_call" | custom-call | bytes 2490368 | tf_op jit(solution)/shard_map/pack/pallas_call | solution.py:57
  6.7 9.1 %collective-permute-done.refs_1_ = bf16[128,2048]{1,0:T(8,128)(2,1)S(1)} collective-permute-done((bf16[128,2048]{1,0:T(8,128)(2,1)}, bf16[128,2048]{1,0:T(8,128)(2,1)S(1)}, u32[]{:S(2)}, u32[]{:S(2)}) %collective-permute-start) | collective-permute-done | bytes 524320 | tf_op jit(solution)/shard_map/ppermute | solution.py:109
  15.8 1.5 %collective-permute-done.1.refs_2_ = bf16[128,2048]{1,0:T(8,128)(2,1)S(1)} collective-permute-done((bf16[128,2048]{1,0:T(8,128)(2,1)}, bf16[128,2048]{1,0:T(8,128)(2,1)S(1)}, u32[]{:S(2)}, u32[]{:S(2)}) %collective-permute-start.1) | collective-permute-done | bytes 524320 | tf_op jit(solution)/shard_map/ppermute | solution.py:109
  17.3 4.8 %all-to-all-start = ((bf16[8,32,1792]{2,1,0:T(8,128)(2,1)}), bf16[8,32,1792]{2,1,0:T(8,128)(2,1)S(1)}, u32[]{:S(2)}, u32[]{:S(2)}) async-start(bf16[8,32,1792]{2,1,0:T(8,128)(2,1)} %get-tuple-element.55), calls=%async_computation | async-start | bytes 1835008 | tf_op jit(solution)/shard_map/all_to_all | solution.py:472
  22.1 2.0 %collective-permute-start.2 = (bf16[128,2048]{1,0:T(8,128)(2,1)S(1)}, bf16[128,2048]{1,0:T(8,128)(2,1)}, u32[]{:S(2)}, u32[]{:S(2)}) collective-permute-start(bf16[128,2048]{1,0:T(8,128)(2,1)S(1)} %get-tuple-element.56.refs_8_), channel_id=1, source_target_pairs={{0,2},{2,4},{4,6},{6,7},{7,5},{5,3},{3,1},{1,0},{8,10},{10,12},{12... | collective-permute-start | bytes 1572872 | tf_op jit(solution)/shard_map/ppermute | solution.py:109
  24.2 0.0 collective-permute-start.3
  24.2 23.2 %collective-permute-done.2.refs_1_ = bf16[128,2048]{1,0:T(8,128)(2,1)} collective-permute-done((bf16[128,2048]{1,0:T(8,128)(2,1)S(1)}, bf16[128,2048]{1,0:T(8,128)(2,1)}, u32[]{:S(2)}, u32[]{:S(2)}) %collective-permute-start.2) | collective-permute-done | bytes 524320 | tf_op jit(solution)/shard_map/ppermute | solution.py:109
  47.3 2.0 %collective-permute-done.3.refs_2_ = bf16[128,2048]{1,0:T(8,128)(2,1)S(1)} collective-permute-done((bf16[128,2048]{1,0:T(8,128)(2,1)S(1)}, bf16[128,2048]{1,0:T(8,128)(2,1)S(1)}, u32[]{:S(2)}, u32[]{:S(2)}) %collective-permute-start.3) | collective-permute-done | bytes 524320 | tf_op jit(solution)/shard_map/ppermute | solution.py:109
  49.3 0.0 all-to-all-done.refs_0_
  49.3 1.5 %collective-permute-start.6 = (bf16[8,32,1792]{2,1,0:T(8,128)(2,1)S(1)}, bf16[8,32,1792]{2,1,0:T(8,128)(2,1)}, u32[]{:S(2)}, u32[]{:S(2)}) collective-permute-start(bf16[8,32,1792]{2,1,0:T(8,128)(2,1)S(1)} %get-tuple-element.61.refs_0_), channel_id=1, source_target_pairs={{0,16},{8,24},{16,0},{24,8},{1,17},{9,25},{17,1},{25,9},{2,18},{10... | collective-permute-start | bytes 2752520 | tf_op jit(solution)/shard_map/ppermute | solution.py:420
  50.8 8.7 %all-to-all-start.1 = ((bf16[8,32,640]{2,1,0:T(8,128)(2,1)}), bf16[8,32,640]{2,1,0:T(8,128)(2,1)S(1)}, u32[]{:S(2)}, u32[]{:S(2)}) async-start(bf16[8,32,640]{2,1,0:T(8,128)(2,1)} %get-tuple-element.59), calls=%async_computation.1 | async-start | bytes 655360 | tf_op jit(solution)/shard_map/all_to_all | solution.py:478
  59.6 2.0 %collective-permute-start.4 = (bf16[128,2048]{1,0:T(8,128)(2,1)}, bf16[128,2048]{1,0:T(8,128)(2,1)S(1)}, u32[]{:S(2)}, u32[]{:S(2)}) collective-permute-start(bf16[128,2048]{1,0:T(8,128)(2,1)} %get-tuple-element.60.refs_7_), channel_id=1, source_target_pairs={{0,2},{2,4},{4,6},{6,7},{7,5},{5,3},{3,1},{1,0},{8,10},{10,12},{12... | collective-permute-start | bytes 1572872 | tf_op jit(solution)/shard_map/ppermute | solution.py:109
  61.6 0.1 collective-permute-start.5
  61.6 7.6 %collective-permute-done.6.refs_3_.refs_2_ = bf16[8,32,1792]{2,1,0:T(8,128)(2,1)} collective-permute-done((bf16[8,32,1792]{2,1,0:T(8,128)(2,1)S(1)}, bf16[8,32,1792]{2,1,0:T(8,128)(2,1)}, u32[]{:S(2)}, u32[]{:S(2)}) %collective-permute-start.6) | collective-permute-done | bytes 917536 | tf_op jit(solution)/shard_map/ppermute | solution.py:420
  69.2 7.3 %collective-permute-done.4.refs_1_ = bf16[128,2048]{1,0:T(8,128)(2,1)S(1)} collective-permute-done((bf16[128,2048]{1,0:T(8,128)(2,1)}, bf16[128,2048]{1,0:T(8,128)(2,1)S(1)}, u32[]{:S(2)}, u32[]{:S(2)}) %collective-permute-start.4) | collective-permute-done | bytes 524320 | tf_op jit(solution)/shard_map/ppermute | solution.py:109
  76.5 2.4 %collective-permute-done.5.refs_2_ = bf16[128,2048]{1,0:T(8,128)(2,1)S(1)} collective-permute-done((bf16[128,2048]{1,0:T(8,128)(2,1)}, bf16[128,2048]{1,0:T(8,128)(2,1)S(1)}, u32[]{:S(2)}, u32[]{:S(2)}) %collective-permute-start.5) | collective-permute-done | bytes 524320 | tf_op jit(solution)/shard_map/ppermute | solution.py:109
  78.8 0.5 collective-permute-start.9
  79.4 2.7 %collective-permute-start.7 = (bf16[64,2048]{1,0:T(8,128)(2,1)S(1)}, bf16[64,2048]{1,0:T(8,128)(2,1)S(1)}, u32[]{:S(2)}, u32[]{:S(2)}) collective-permute-start(bf16[64,2048]{1,0:T(8,128)(2,1)S(1)} %get-tuple-element.64.refs_9_), channel_id=1, source_target_pairs={{0,2},{2,4},{4,6},{6,7},{7,5},{5,3},{3,1},{1,0},{8,10},{10,12},{12... | collective-permute-start | bytes 786440 | tf_op jit(solution)/shard_map/ppermute | solution.py:109
  82.1 0.0 collective-permute-start.8
  82.1 9.7 %preload.1 = (bf16[512,2048]{1,0:T(8,128)(2,1)S(1)}, bf16[512,2048]{1,0:T(8,128)(2,1)S(1)}, bf16[512,2048]{1,0:T(8,128)(2,1)S(1)}, bf16[128,2048]{1,0:T(8,128)(2...) custom-call(bf16[512,2048]{1,0:T(8,128)(2,1)} %refs_0_.5, ...), custom_call_target="tpu_custom_call" | custom-call | bytes 29884416 | tf_op jit(solution)/shard_map/preload/pallas_call | solution.py:182
  91.8 0.0 collective-permute-done.7.refs_3_.refs_4_
  91.8 0.0 collective-permute-done.8.refs_4_.refs_5_
  91.8 0.1 collective-permute-start.10
  91.9 0.5 collective-permute-start.11
  92.4 1.1 collective-permute-done.10.refs_1_
  93.5 0.5 collective-permute-done.11.refs_3_
  94.0 1.1 unpack.2
  95.1 0.0 copy-start.1
  95.1 0.0 copy-start.2
  95.1 0.0 collective-permute-done.15.refs_1_
  95.1 2.9 %unpack.3.refs_9_ = bf16[1792,1024]{1,0:T(8,128)(2,1)S(1)} custom-call(s32[2]{0:T(128)S(1)} %pad_add_fusion.at_ref, bf16[8,32,1792]{2,1,0:T(8,128)(2,1)S(1)} %get-tuple-element.61.refs_0_, bf16[8,32,1792]{2,1,0:T(8,128)(2,1)} %collective-permute-done.15.refs_1_, bf16[8,32,1792]{2,1,0:T(8,128)(2,1)} %collective-permute-done.6.refs_3_.refs_2_, ...), custom_call_target="tpu_custom_call" | custom-call | bytes 7340032 | tf_op jit(solution)/shard_map/unpack/pallas_call | solution.py:137
  98.1 21.3 %adam.3 = (f32[1,1792]{1,0:T(1,128)S(1)}, bf16[1792,2048]{1,0:T(8,128)(2,1)S(1)}, bf16[1792,2048]{1,0:T(8,128)(2,1)S(1)}, bf16[1792,2048]{1,0:T(8,128)(2,1)}, bf16[1792,2048]{1,0:T(8,128)(2,1)}) custom-call(bf16[128,2048]{1,0:T(8,128)(2,1)S(1)} %copy-done.2, ...), custom_call_target="tpu_custom_call", output_to_operand_aliasing={{1}: (10, {}), {2}: (11, {})} | custom-call | flops 7516192768 | bytes 14680064 | tf_op jit(solution)/shard_map/adam/pallas_call | solution.py:321
  119.4 0.2 collective-permute-start.17
  119.6 1.5 %collective-permute-start.18 = (f32[1,1792]{1,0:T(1,128)S(1)}, f32[1,1792]{1,0:T(1,128)S(1)}, u32[]{:S(2)}, u32[]{:S(2)}) collective-permute-start(f32[1,1792]{1,0:T(1,128)S(1)} %get-tuple-element.86.refs_0_), channel_id=1, source_target_pairs={{0,16},{8,24},{16,0},{24,8},{1,17},{9,25},{17,1},{25,9},{2,18},{10... | collective-permute-start | bytes 21512 | tf_op jit(solution)/shard_map/ppermute | solution.py:436
  121.1 0.2 collective-permute-start.19
  121.4 10.5 %adam.2 = (f32[1,640]{1,0:T(1,128)S(1)}, bf16[512,2048]{1,0:T(8,128)(2,1)S(1)}, bf16[512,2048]{1,0:T(8,128)(2,1)S(1)}, bf16[512,2048]{1,0:T(8,128)(2,1)}, bf16[5...) custom-call(bf16[128,2048]{1,0:T(8,128)(2,1)S(1)} %copy-done.2, ...), custom_call_target="tpu_custom_call", output_to_operand_aliasing={{1}: (10, {}), {2}: (11, {}), {5}: (14, {}), {6}: (15, {})} | custom-call | flops 2684354560 | bytes 5242880 | tf_op jit(solution)/shard_map/adam/pallas_call | solution.py:321
  131.9 0.5 collective-permute-start.12
  132.4 1.5 %collective-permute-start.13 = (f32[1,640]{1,0:T(1,128)S(1)}, f32[1,640]{1,0:T(1,128)S(1)}, u32[]{:S(2)}, u32[]{:S(2)}) collective-permute-start(f32[1,640]{1,0:T(1,128)S(1)} %get-tuple-element.78.refs_0_), channel_id=1, source_target_pairs={{0,16},{8,24},{16,0},{24,8},{1,17},{9,25},{17,1},{25,9},{2,18},{10... | collective-permute-start | bytes 7688 | tf_op jit(solution)/shard_map/ppermute | solution.py:436
  133.9 0.0 collective-permute-done.17.refs_1_
  133.9 0.0 collective-permute-start.14
  133.9 0.0 collective-permute-done.18.refs_2_
  133.9 4.2 %finish.2.refs_8_ = bf16[1792,2048]{1,0:T(8,128)(2,1)} custom-call(f32[1,1792]{1,0:T(1,128)S(1)} %get-tuple-element.86.refs_0_, f32[1,1792]{1,0:T(1,128)S(1)} %collective-permute-done.17.refs_1_, f32[1,1792]{1,0:T(1,128)S(1)} %collective-permute-done.18.refs_2_, f32[1,1792]{1,0:T(1,128)S(1)} %collective-permute-done.19.refs_3_, ...), custom_call_target="tpu_custom_call" | custom-call | flops 7340032 | bytes 7340032 | tf_op jit(solution)/shard_map/finish/pallas_call | solution.py:395
  138.2 0.0 collective-permute-done.12.refs_1_
  138.2 0.0 collective-permute-done.13.refs_2_
  138.2 2.6 %finish.3 = (bf16[512,2048]{1,0:T(8,128)(2,1)}, bf16[128,2048]{1,0:T(8,128)(2,1)}) custom-call(f32[1,640]{1,0:T(1,128)S(1)} %get-tuple-element.78.refs_0_, f32[1,640]{1,0:T(1,128)S(1)} %collective-permute-done.12.refs_1_, f32[1,640]{1,0:T(1,128)S(1)} %collective-permute-done.13.refs_2_, f32[1,640]{1,0:T(1,128)S(1)} %collective-permute-done.14.refs_3_, ...), custom_call_target="tpu_custom_call" | custom-call | flops 2621440 | bytes 2621440 | tf_op jit(solution)/shard_map/finish/pallas_call | solution.py:395
  (16 shorter events, 0.1 us)
Async XLA Ops:
  0.6 15.2 %collective-permute-start = (bf16[128,2048]{1,0:T(8,128)(2,1)}, bf16[128,2048]{1,0:T(8,128)(2,1)S(1)}, u32[]{:S(2)}, u32[]{:S(2)}) collective-permute-start(bf16[128,2048]{1,0:T(8,128)(2,1)} %refs_0_.7), channel_id=1, source_target_pairs={{0,2},{2,4},{4,6},{6,7},{7,5},{5,3},{3,1},{1,0},{8,10},{10,12},{12... | collective-permute-start | bytes 1572872 | tf_op jit(solution)/shard_map/ppermute | solution.py:109
  3.7 13.6 %collective-permute-start.1 = (bf16[128,2048]{1,0:T(8,128)(2,1)}, bf16[128,2048]{1,0:T(8,128)(2,1)S(1)}, u32[]{:S(2)}, u32[]{:S(2)}) collective-permute-start(bf16[128,2048]{1,0:T(8,128)(2,1)} %refs_0_.7), channel_id=1, source_target_pairs={{2,0},{4,2},{6,4},{7,6},{5,7},{3,5},{1,3},{0,1},{10,8},{12,10},{14... | collective-permute-start | bytes 1572872 | tf_op jit(solution)/shard_map/ppermute | solution.py:109
  17.3 32.0 %all-to-all-start = ((bf16[8,32,1792]{2,1,0:T(8,128)(2,1)}), bf16[8,32,1792]{2,1,0:T(8,128)(2,1)S(1)}, u32[]{:S(2)}, u32[]{:S(2)}) async-start(bf16[8,32,1792]{2,1,0:T(8,128)(2,1)} %get-tuple-element.55), calls=%async_computation | async-start | bytes 1835008 | tf_op jit(solution)/shard_map/all_to_all | solution.py:472
  22.1 25.2 %collective-permute-start.2 = (bf16[128,2048]{1,0:T(8,128)(2,1)S(1)}, bf16[128,2048]{1,0:T(8,128)(2,1)}, u32[]{:S(2)}, u32[]{:S(2)}) collective-permute-start(bf16[128,2048]{1,0:T(8,128)(2,1)S(1)} %get-tuple-element.56.refs_8_), channel_id=1, source_target_pairs={{0,2},{2,4},{4,6},{6,7},{7,5},{5,3},{3,1},{1,0},{8,10},{10,12},{12... | collective-permute-start | bytes 1572872 | tf_op jit(solution)/shard_map/ppermute | solution.py:109
  24.2 25.2 %collective-permute-start.3 = (bf16[128,2048]{1,0:T(8,128)(2,1)S(1)}, bf16[128,2048]{1,0:T(8,128)(2,1)S(1)}, u32[]{:S(2)}, u32[]{:S(2)}) collective-permute-start(bf16[128,2048]{1,0:T(8,128)(2,1)S(1)} %get-tuple-element.54.refs_1_), channel_id=1, source_target_pairs={{2,0},{4,2},{6,4},{7,6},{5,7},{3,5},{1,3},{0,1},{10,8},{12,10},{14... | collective-permute-start | bytes 1572872 | tf_op jit(solution)/shard_map/ppermute | solution.py:109
  49.3 10.2 %copy-start = (bf16[128,2048]{1,0:T(8,128)(2,1)}, bf16[128,2048]{1,0:T(8,128)(2,1)S(1)}, u32[]{:S(2)}) copy-start(bf16[128,2048]{1,0:T(8,128)(2,1)S(1)} %get-tuple-element.58.refs_2_) | copy-start | bytes 1572868
  49.3 19.9 %collective-permute-start.6 = (bf16[8,32,1792]{2,1,0:T(8,128)(2,1)S(1)}, bf16[8,32,1792]{2,1,0:T(8,128)(2,1)}, u32[]{:S(2)}, u32[]{:S(2)}) collective-permute-start(bf16[8,32,1792]{2,1,0:T(8,128)(2,1)S(1)} %get-tuple-element.61.refs_0_), channel_id=1, source_target_pairs={{0,16},{8,24},{16,0},{24,8},{1,17},{9,25},{17,1},{25,9},{2,18},{10... | collective-permute-start | bytes 2752520 | tf_op jit(solution)/shard_map/ppermute | solution.py:420
  50.8 28.0 %all-to-all-start.1 = ((bf16[8,32,640]{2,1,0:T(8,128)(2,1)}), bf16[8,32,640]{2,1,0:T(8,128)(2,1)S(1)}, u32[]{:S(2)}, u32[]{:S(2)}) async-start(bf16[8,32,640]{2,1,0:T(8,128)(2,1)} %get-tuple-element.59), calls=%async_computation.1 | async-start | bytes 655360 | tf_op jit(solution)/shard_map/all_to_all | solution.py:478
  59.6 16.9 %collective-permute-start.4 = (bf16[128,2048]{1,0:T(8,128)(2,1)}, bf16[128,2048]{1,0:T(8,128)(2,1)S(1)}, u32[]{:S(2)}, u32[]{:S(2)}) collective-permute-start(bf16[128,2048]{1,0:T(8,128)(2,1)} %get-tuple-element.60.refs_7_), channel_id=1, source_target_pairs={{0,2},{2,4},{4,6},{6,7},{7,5},{5,3},{3,1},{1,0},{8,10},{10,12},{12... | collective-permute-start | bytes 1572872 | tf_op jit(solution)/shard_map/ppermute | solution.py:109
  61.6 17.2 %collective-permute-start.5 = (bf16[128,2048]{1,0:T(8,128)(2,1)}, bf16[128,2048]{1,0:T(8,128)(2,1)S(1)}, u32[]{:S(2)}, u32[]{:S(2)}) collective-permute-start(bf16[128,2048]{1,0:T(8,128)(2,1)} %copy-done), channel_id=1, source_target_pairs={{2,0},{4,2},{6,4},{7,6},{5,7},{3,5},{1,3},{0,1},{10,8},{12,10},{14... | collective-permute-start | bytes 1572872 | tf_op jit(solution)/shard_map/ppermute | solution.py:109
  61.6 33.5 %collective-permute-start.15 = (bf16[8,32,1792]{2,1,0:T(8,128)(2,1)S(1)}, bf16[8,32,1792]{2,1,0:T(8,128)(2,1)}, u32[]{:S(2)}, u32[]{:S(2)}) collective-permute-start(bf16[8,32,1792]{2,1,0:T(8,128)(2,1)S(1)} %get-tuple-element.61.refs_0_), channel_id=1, source_target_pairs={{0,8},{8,0},{16,24},{24,16},{1,9},{9,1},{17,25},{25,17},{2,10},{10... | collective-permute-start | bytes 2752520 | tf_op jit(solution)/shard_map/ppermute | solution.py:420
  69.2 25.9 %collective-permute-start.16 = (bf16[8,32,1792]{2,1,0:T(8,128)(2,1)}, bf16[8,32,1792]{2,1,0:T(8,128)(2,1)}, u32[]{:S(2)}, u32[]{:S(2)}) collective-permute-start(bf16[8,32,1792]{2,1,0:T(8,128)(2,1)} %collective-permute-done.6.refs_3_.refs_2_), channel_id=1, source_target_pairs={{0,8},{8,0},{16,24},{24,16},{1,9},{9,1},{17,25},{25,17},{2,10},{10... | collective-permute-start | bytes 2752520 | tf_op jit(solution)/shard_map/ppermute | solution.py:420
  78.8 13.0 %collective-permute-start.9 = (bf16[8,32,640]{2,1,0:T(8,128)(2,1)S(1)}, bf16[8,32,640]{2,1,0:T(8,128)(2,1)S(1)}, u32[]{:S(2)}, u32[]{:S(2)}) collective-permute-start(bf16[8,32,640]{2,1,0:T(8,128)(2,1)S(1)} %get-tuple-element.66.refs_0_), channel_id=1, source_target_pairs={{0,16},{8,24},{16,0},{24,8},{1,17},{9,25},{17,1},{25,9},{2,18},{10... | collective-permute-start | bytes 983048 | tf_op jit(solution)/shard_map/ppermute | solution.py:420
  79.4 12.4 %collective-permute-start.7 = (bf16[64,2048]{1,0:T(8,128)(2,1)S(1)}, bf16[64,2048]{1,0:T(8,128)(2,1)S(1)}, u32[]{:S(2)}, u32[]{:S(2)}) collective-permute-start(bf16[64,2048]{1,0:T(8,128)(2,1)S(1)} %get-tuple-element.64.refs_9_), channel_id=1, source_target_pairs={{0,2},{2,4},{4,6},{6,7},{7,5},{5,3},{3,1},{1,0},{8,10},{10,12},{12... | collective-permute-start | bytes 786440 | tf_op jit(solution)/shard_map/ppermute | solution.py:109
  82.1 9.7 %collective-permute-start.8 = (bf16[64,2048]{1,0:T(8,128)(2,1)S(1)}, bf16[64,2048]{1,0:T(8,128)(2,1)S(1)}, u32[]{:S(2)}, u32[]{:S(2)}) collective-permute-start(bf16[64,2048]{1,0:T(8,128)(2,1)S(1)} %get-tuple-element.65), channel_id=1, source_target_pairs={{2,0},{4,2},{6,4},{7,6},{5,7},{3,5},{1,3},{0,1},{10,8},{12,10},{14... | collective-permute-start | bytes 786440 | tf_op jit(solution)/shard_map/ppermute | solution.py:109
  91.8 1.7 %collective-permute-start.10 = (bf16[8,32,640]{2,1,0:T(8,128)(2,1)S(1)}, bf16[8,32,640]{2,1,0:T(8,128)(2,1)S(1)}, u32[]{:S(2)}, u32[]{:S(2)}) collective-permute-start(bf16[8,32,640]{2,1,0:T(8,128)(2,1)S(1)} %get-tuple-element.68.refs_0_), channel_id=1, source_target_pairs={{0,8},{8,0},{16,24},{24,16},{1,9},{9,1},{17,25},{25,17},{2,10},{10... | collective-permute-start | bytes 983048 | tf_op jit(solution)/shard_map/ppermute | solution.py:420
  91.9 2.1 %collective-permute-start.11 = (bf16[8,32,640]{2,1,0:T(8,128)(2,1)S(1)}, bf16[8,32,640]{2,1,0:T(8,128)(2,1)S(1)}, u32[]{:S(2)}, u32[]{:S(2)}) collective-permute-start(bf16[8,32,640]{2,1,0:T(8,128)(2,1)S(1)} %get-tuple-element.69.refs_2_), channel_id=1, source_target_pairs={{0,8},{8,0},{16,24},{24,16},{1,9},{9,1},{17,25},{25,17},{2,10},{10... | collective-permute-start | bytes 983048 | tf_op jit(solution)/shard_map/ppermute | solution.py:420
  95.1 3.0 %copy-start.1 = (bf16[128,2048]{1,0:T(8,128)(2,1)S(1)}, bf16[128,2048]{1,0:T(8,128)(2,1)}, u32[]{:S(2)}) copy-start(bf16[128,2048]{1,0:T(8,128)(2,1)} %copy-done) | copy-start | bytes 1572868
  95.1 3.0 %copy-start.2 = (bf16[128,2048]{1,0:T(8,128)(2,1)S(1)}, bf16[128,2048]{1,0:T(8,128)(2,1)}, u32[]{:S(2)}) copy-start(bf16[128,2048]{1,0:T(8,128)(2,1)} %refs_0_.7) | copy-start | bytes 1572868
  119.4 14.5 %collective-permute-start.17 = (f32[1,1792]{1,0:T(1,128)S(1)}, f32[1,1792]{1,0:T(1,128)S(1)}, u32[]{:S(2)}, u32[]{:S(2)}) collective-permute-start(f32[1,1792]{1,0:T(1,128)S(1)} %get-tuple-element.86.refs_0_), channel_id=1, source_target_pairs={{0,8},{8,0},{16,24},{24,16},{1,9},{9,1},{17,25},{25,17},{2,10},{10... | collective-permute-start | bytes 21512 | tf_op jit(solution)/shard_map/ppermute | solution.py:436
  119.6 14.3 %collective-permute-start.18 = (f32[1,1792]{1,0:T(1,128)S(1)}, f32[1,1792]{1,0:T(1,128)S(1)}, u32[]{:S(2)}, u32[]{:S(2)}) collective-permute-start(f32[1,1792]{1,0:T(1,128)S(1)} %get-tuple-element.86.refs_0_), channel_id=1, source_target_pairs={{0,16},{8,24},{16,0},{24,8},{1,17},{9,25},{17,1},{25,9},{2,18},{10... | collective-permute-start | bytes 21512 | tf_op jit(solution)/shard_map/ppermute | solution.py:436
  121.1 12.8 %collective-permute-start.19 = (f32[1,1792]{1,0:T(1,128)S(1)}, f32[1,1792]{1,0:T(1,128)S(1)}, u32[]{:S(2)}, u32[]{:S(2)}) collective-permute-start(f32[1,1792]{1,0:T(1,128)S(1)} %get-tuple-element.86.refs_0_), channel_id=1, source_target_pairs={{0,24},{8,16},{16,8},{24,0},{1,25},{9,17},{17,9},{25,1},{2,26},{10... | collective-permute-start | bytes 21512 | tf_op jit(solution)/shard_map/ppermute | solution.py:436
  131.9 6.2 %collective-permute-start.12 = (f32[1,640]{1,0:T(1,128)S(1)}, f32[1,640]{1,0:T(1,128)S(1)}, u32[]{:S(2)}, u32[]{:S(2)}) collective-permute-start(f32[1,640]{1,0:T(1,128)S(1)} %get-tuple-element.78.refs_0_), channel_id=1, source_target_pairs={{0,8},{8,0},{16,24},{24,16},{1,9},{9,1},{17,25},{25,17},{2,10},{10... | collective-permute-start | bytes 7688 | tf_op jit(solution)/shard_map/ppermute | solution.py:436
  132.4 5.8 %collective-permute-start.13 = (f32[1,640]{1,0:T(1,128)S(1)}, f32[1,640]{1,0:T(1,128)S(1)}, u32[]{:S(2)}, u32[]{:S(2)}) collective-permute-start(f32[1,640]{1,0:T(1,128)S(1)} %get-tuple-element.78.refs_0_), channel_id=1, source_target_pairs={{0,16},{8,24},{16,0},{24,8},{1,17},{9,25},{17,1},{25,9},{2,18},{10... | collective-permute-start | bytes 7688 | tf_op jit(solution)/shard_map/ppermute | solution.py:436
  133.9 4.3 %collective-permute-start.14 = (f32[1,640]{1,0:T(1,128)S(1)}, f32[1,640]{1,0:T(1,128)S(1)}, u32[]{:S(2)}, u32[]{:S(2)}) collective-permute-start(f32[1,640]{1,0:T(1,128)S(1)} %get-tuple-element.78.refs_0_), channel_id=1, source_target_pairs={{0,24},{8,16},{16,8},{24,0},{1,25},{9,17},{17,9},{25,1},{2,26},{10... | collective-permute-start | bytes 7688 | tf_op jit(solution)/shard_map/ppermute | solution.py:436

commit v10 on v9

--- a/solution.py
+++ b/solution.py
@@ -463,17 +463,13 @@
         (up_weight, moment_up, second_up),
     )
     place = jnp.stack([lax.axis_index("col"), lax.axis_index("dp")]).astype(jnp.int32)
-    plan = [[(2, 0, up_weight.shape[0])]]
-    plan.append([(which, 0, states[which][0].shape[0]) for which in (0, 1)])
+    plan = [[(which, 0, states[which][0].shape[0]) for which in (0, 1)]]
+    plan.append([(2, 0, up_weight.shape[0])])
     packed = pack((query_cotangent, key_cotangent, up_cotangent), plan, groups, part, place)
     one, two = ring_step(layer_input, layer_input, "dp")
-    chunk, one, two = join((packed[0], one, two))
+    owned = lax.all_to_all(packed[0], "dp", split_axis=0, concat_axis=0, tiled=True)
+    owned, one, two, chunk = join((owned, one, two, packed[1]))
     behind, ahead = [layer_input, one], [layer_input, two]
-    owned = lax.all_to_all(chunk, "dp", split_axis=0, concat_axis=0, tiled=True)
-    one, two = ring_step(one, two, "dp")
-    owned, one, two, chunk = join((owned, one, two, packed[1]))
-    behind.append(one)
-    ahead.append(two)
     swaps = [(owned, swap(owned, "col", cols // 2))]
     owned = lax.all_to_all(chunk, "dp", split_axis=0, concat_axis=0, tiled=True)
     one, two = ring_step(one, two, "dp")
@@ -481,15 +477,17 @@
     behind.append(one)
     ahead.append(two)
     swaps.append((owned, swap(owned, "col", cols // 2)))
+    *held, loaded = preload([array for state in states for array in state], owned)
+    held = [held[at : at + 3] for at in range(0, len(held), 3)]
+    one, two = join(ring_step(one, two, "dp"), (loaded,))
+    behind.append(one)
+    ahead.append(two)
     while 2 * len(behind) < groups:
         one, two = ring_step(one, two, "dp")
         behind.append(one)
         ahead.append(two)
-    one, two = halves(one, two)
-    middle = ring_step(one, two, "dp")
-    *held, loaded = preload([array for state in states for array in state], one)
-    held = [held[at : at + 3] for at in range(0, len(held), 3)]
-    swaps[1] = join(swaps[1], (loaded, *middle))
+    middle = ring_step(*halves(one, two), "dp")
+    swaps[1] = join(swaps[1], middle)
     x_pieces = [layer_input, *ahead[1:], *middle, *behind[:0:-1]]
     cotangents = [[], [], []]
     for got, pieces in zip(swaps, plan):

time: 141 us -> 141 us (level)
  starting transfers between devices: 30 us -> 33 us
  Pallas kernels: 55.4 us -> 52.6 us
  waiting for transfers between devices: 54.5 us -> 52.3 us
  local copies, waits for them, and re-layouts: 0.02 us -> 1.72 us
    all_to_all x2 -> x1, starting transfers between devices: 13.5 us -> 5.02 us  [per_device(): owned = lax.all_to_all(chunk, 'dp', split_axis=0, concat_axis=0, tiled=True)]
    all_to_all x0 -> x1, starting transfers between devices: none -> 7.28 us  [per_device(): lax.all_to_all(packed[0], 'dp', split_axis=0, concat_axis=0, tiled=True)]
    ppermute x8, waiting for transfers between devices: 45.3 us -> 41.7 us  [ring_step(): return (lax.ppermute(one, axis, onward), lax.ppermute(two, axis, back))]
    ppermute x8, starting transfers between devices: 9.94 us -> 12.9 us  [ring_step(): return (lax.ppermute(one, axis, onward), lax.ppermute(two, axis, back))]
    unnamed x6 -> x10, local copies, waits for them, and re-layouts: 0.02 us -> 1.72 us
    pallas_call x2, Pallas kernels: 31.9 us -> 30.3 us  [adam_pass(): pl.pallas_call(functools.partial(adam_kernel, strip, len(x_pieces), cuts)...]
    ppermute x6, waiting for transfers between devices: 9.16 us -> 10.6 us  [swap(): lax.ppermute(array, axis, [(at, at ^ bit) for at in range(lax.axis_size(a...]
  transfers between devices with their start and end apart: 22 -> 22, of which waited for: 9 -> 10; matrix products, arithmetic and copies ran while one was open for 0% -> 0% of each run, Pallas kernels for 20% -> 17%
where the time goes in v10:
time: 141 us; the launch traced here: 140 us
  Pallas kernels  52.6 us (37%)
  waiting for transfers between devices  52.3 us (37%)
  starting transfers between devices  33 us (23%)
  local copies, waits for them, and re-layouts  1.72 us (1%)
    ppermute x8, waiting for transfers between devices, ring_step(): return (lax.ppermute(one, axis, onward), lax.ppermute(two, axis, back))  41.7 us
    pallas_call x2, Pallas kernels, adam_pass(): pl.pallas_call(functools.partial(adam_kernel, strip, len(x_pieces), cuts)...  30.3 us
    ppermute x8, starting transfers between devices, ring_step(): return (lax.ppermute(one, axis, onward), lax.ppermute(two, axis, back))  12.9 us
    ppermute x6, waiting for transfers between devices, swap(): lax.ppermute(array, axis, [(at, at ^ bit) for at in range(lax.axis_size(a...  10.6 us
    pallas_call x1, Pallas kernels, preload(): pl.pallas_call(preload_kernel, in_specs=[pl.BlockSpec(memory_space=pl.ANY...  9.66 us
    all_to_all x1, starting transfers between devices, per_device(): lax.all_to_all(packed[0], 'dp', split_axis=0, concat_axis=0, tiled=True)  7.28 us
    pallas_call x2, Pallas kernels, finish_rows(): pl.pallas_call(functools.partial(finish_kernel, len(powers), whole_width,...  6.84 us
    all_to_all x1, starting transfers between devices, per_device(): owned = lax.all_to_all(chunk, 'dp', split_axis=0, concat_axis=0, tiled=True)  5.02 us
  transfers between devices with their start and end apart: 22, of which 10 were waited for; matrix products, arithmetic and copies ran while one was open for 0% of the time, Pallas kernels for 17%

profile of v10, /device:TPU:0, one launch (start us, length us, event | category | flops | bytes accessed | tf_op | source)
XLA Modules:
  0.0 140.5 jit_solution(11447268453251522039)
XLA Ops:
  0.6 0.0 copy-start
  0.7 0.1 pad_add_fusion.at_ref
  0.7 2.9 %pack.1 = (bf16[8,32,640]{2,1,0:T(8,128)(2,1)}, bf16[8,32,1792]{2,1,0:T(8,128)(2,1)}) custom-call(s32[2]{0:T(128)S(1)} %pad_add_fusion.at_ref, bf16[128,4096]{1,0:T(8,128)(2,1)} %refs_0_.4, bf16[128,1024]{1,0:T(8,128)(2,1)} %refs_1_.2, bf16[128,14336]{1,0:T(8,128)(2,1)} %refs_2_.2), custom_call_target="tpu_custom_call" | custom-call | bytes 2490368 | tf_op jit(solution)/shard_map/pack/pallas_call | solution.py:57
  3.6 7.3 %all-to-all-start = ((bf16[8,32,640]{2,1,0:T(8,128)(2,1)}), bf16[8,32,640]{2,1,0:T(8,128)(2,1)S(1)}, u32[]{:S(2)}, u32[]{:S(2)}) async-start(bf16[8,32,640]{2,1,0:T(8,128)(2,1)} %get-tuple-element.52), calls=%async_computation | async-start | bytes 655360 | tf_op jit(solution)/shard_map/all_to_all | solution.py:470
  10.9 2.0 %collective-permute-start = (bf16[128,2048]{1,0:T(8,128)(2,1)S(1)}, bf16[128,2048]{1,0:T(8,128)(2,1)S(1)}, u32[]{:S(2)}, u32[]{:S(2)}) collective-permute-start(bf16[128,2048]{1,0:T(8,128)(2,1)S(1)} %copy-done), channel_id=1, source_target_pairs={{0,2},{2,4},{4,6},{6,7},{7,5},{5,3},{3,1},{1,0},{8,10},{10,12},{12... | collective-permute-start | bytes 1572872 | tf_op jit(solution)/shard_map/ppermute | solution.py:109
  12.9 0.1 collective-permute-start.1
  13.0 15.0 %collective-permute-done.refs_1_ = bf16[128,2048]{1,0:T(8,128)(2,1)S(1)} collective-permute-done((bf16[128,2048]{1,0:T(8,128)(2,1)S(1)}, bf16[128,2048]{1,0:T(8,128)(2,1)S(1)}, u32[]{:S(2)}, u32[]{:S(2)}) %collective-permute-start) | collective-permute-done | bytes 524320 | tf_op jit(solution)/shard_map/ppermute | solution.py:109
  28.0 2.1 %collective-permute-done.1.refs_2_ = bf16[128,2048]{1,0:T(8,128)(2,1)S(1)} collective-permute-done((bf16[128,2048]{1,0:T(8,128)(2,1)S(1)}, bf16[128,2048]{1,0:T(8,128)(2,1)S(1)}, u32[]{:S(2)}, u32[]{:S(2)}) %collective-permute-start.1) | collective-permute-done | bytes 524320 | tf_op jit(solution)/shard_map/ppermute | solution.py:109
  30.1 0.0 all-to-all-done.refs_0_
  30.2 5.0 %all-to-all-start.1 = ((bf16[8,32,1792]{2,1,0:T(8,128)(2,1)}), bf16[8,32,1792]{2,1,0:T(8,128)(2,1)S(1)}, u32[]{:S(2)}, u32[]{:S(2)}) async-start(bf16[8,32,1792]{2,1,0:T(8,128)(2,1)} %get-tuple-element.55), calls=%async_computation.1 | async-start | bytes 1835008 | tf_op jit(solution)/shard_map/all_to_all | solution.py:474
  35.2 2.0 %collective-permute-start.2 = (bf16[128,2048]{1,0:T(8,128)(2,1)S(1)}, bf16[128,2048]{1,0:T(8,128)(2,1)S(1)}, u32[]{:S(2)}, u32[]{:S(2)}) collective-permute-start(bf16[128,2048]{1,0:T(8,128)(2,1)S(1)} %get-tuple-element.56.refs_8_), channel_id=1, source_target_pairs={{0,2},{2,4},{4,6},{6,7},{7,5},{5,3},{3,1},{1,0},{8,10},{10,12},{12... | collective-permute-start | bytes 1572872 | tf_op jit(solution)/shard_map/ppermute | solution.py:109
  37.2 0.0 collective-permute-start.3
  37.2 1.5 %collective-permute-start.4 = (bf16[8,32,640]{2,1,0:T(8,128)(2,1)S(1)}, bf16[8,32,640]{2,1,0:T(8,128)(2,1)S(1)}, u32[]{:S(2)}, u32[]{:S(2)}) collective-permute-start(bf16[8,32,640]{2,1,0:T(8,128)(2,1)S(1)} %get-tuple-element.57.refs_0_), channel_id=1, source_target_pairs={{0,16},{8,24},{16,0},{24,8},{1,17},{9,25},{17,1},{25,9},{2,18},{10... | collective-permute-start | bytes 983048 | tf_op jit(solution)/shard_map/ppermute | solution.py:420
  38.7 6.9 %collective-permute-done.4.refs_3_.refs_2_ = bf16[8,32,640]{2,1,0:T(8,128)(2,1)S(1)} collective-permute-done((bf16[8,32,640]{2,1,0:T(8,128)(2,1)S(1)}, bf16[8,32,640]{2,1,0:T(8,128)(2,1)S(1)}, u32[]{:S(2)}, u32[]{:S(2)}) %collective-permute-start.4) | collective-permute-done | bytes 327712 | tf_op jit(solution)/shard_map/ppermute | solution.py:420
  45.6 0.7 copy-done.2
  46.3 14.7 %collective-permute-done.2.refs_1_ = bf16[128,2048]{1,0:T(8,128)(2,1)S(1)} collective-permute-done((bf16[128,2048]{1,0:T(8,128)(2,1)S(1)}, bf16[128,2048]{1,0:T(8,128)(2,1)S(1)}, u32[]{:S(2)}, u32[]{:S(2)}) %collective-permute-start.2) | collective-permute-done | bytes 524320 | tf_op jit(solution)/shard_map/ppermute | solution.py:109
  61.1 2.2 %collective-permute-done.3.refs_2_ = bf16[128,2048]{1,0:T(8,128)(2,1)S(1)} collective-permute-done((bf16[128,2048]{1,0:T(8,128)(2,1)S(1)}, bf16[128,2048]{1,0:T(8,128)(2,1)S(1)}, u32[]{:S(2)}, u32[]{:S(2)}) %collective-permute-start.3) | collective-permute-done | bytes 524320 | tf_op jit(solution)/shard_map/ppermute | solution.py:109
  63.3 0.0 all-to-all-done.1.refs_0_
  63.3 1.0 copy-done.3
  64.3 1.5 %collective-permute-start.14 = (bf16[8,32,1792]{2,1,0:T(8,128)(2,1)S(1)}, bf16[8,32,1792]{2,1,0:T(8,128)(2,1)S(1)}, u32[]{:S(2)}, u32[]{:S(2)}) collective-permute-start(bf16[8,32,1792]{2,1,0:T(8,128)(2,1)S(1)} %get-tuple-element.60.refs_9_.refs_0_), channel_id=1, source_target_pairs={{0,16},{8,24},{16,0},{24,8},{1,17},{9,25},{17,1},{25,9},{2,18},{10... | collective-permute-start | bytes 2752520 | tf_op jit(solution)/shard_map/ppermute | solution.py:420
  65.8 6.7 %collective-permute-start.5 = (bf16[128,2048]{1,0:T(8,128)(2,1)S(1)}, bf16[128,2048]{1,0:T(8,128)(2,1)S(1)}, u32[]{:S(2)}, u32[]{:S(2)}) collective-permute-start(bf16[128,2048]{1,0:T(8,128)(2,1)S(1)} %get-tuple-element.59.refs_7_), channel_id=1, source_target_pairs={{0,2},{2,4},{4,6},{6,7},{7,5},{5,3},{3,1},{1,0},{8,10},{10,12},{12... | collective-permute-start | bytes 1572872 | tf_op jit(solution)/shard_map/ppermute | solution.py:109
  72.4 9.7 %preload.1 = (bf16[512,2048]{1,0:T(8,128)(2,1)S(1)}, bf16[512,2048]{1,0:T(8,128)(2,1)S(1)}, bf16[512,2048]{1,0:T(8,128)(2,1)S(1)}, bf16[128,2048]{1,0:T(8,128)(2...) custom-call(bf16[512,2048]{1,0:T(8,128)(2,1)} %refs_0_.5, ...), custom_call_target="tpu_custom_call" | custom-call | bytes 29884416 | tf_op jit(solution)/shard_map/preload/pallas_call | solution.py:182
  82.1 0.0 copy-start.4
  82.1 0.0 collective-permute-done.5.refs_0_
  82.1 2.2 %collective-permute-done.6.refs_1_ = bf16[128,2048]{1,0:T(8,128)(2,1)S(1)} collective-permute-done((bf16[128,2048]{1,0:T(8,128)(2,1)S(1)}, bf16[128,2048]{1,0:T(8,128)(2,1)S(1)}, u32[]{:S(2)}, u32[]{:S(2)}) %collective-permute-start.6) | collective-permute-done | bytes 524320 | tf_op jit(solution)/shard_map/ppermute | solution.py:109
  84.4 1.1 collective-permute-start.7
  85.4 1.0 collective-permute-start.8
  86.5 4.3 %collective-permute-done.7.refs_4_.refs_2_ = bf16[64,2048]{1,0:T(8,128)(2,1)S(1)} collective-permute-done((bf16[64,2048]{1,0:T(8,128)(2,1)S(1)}, bf16[64,2048]{1,0:T(8,128)(2,1)S(1)}, u32[]{:S(2)}, u32[]{:S(2)}) %collective-permute-start.7) | collective-permute-done | bytes 262176 | tf_op jit(solution)/shard_map/ppermute | solution.py:109
  90.8 1.0 collective-permute-done.8.refs_5_.refs_3_
  91.8 0.0 collective-permute-done.14.refs_1_
  91.8 0.5 collective-permute-start.16
  92.3 0.1 collective-permute-start.9
  92.4 0.4 collective-permute-start.10
  92.8 3.2 %collective-permute-done.9.refs_1_ = bf16[8,32,640]{2,1,0:T(8,128)(2,1)S(1)} collective-permute-done((bf16[8,32,640]{2,1,0:T(8,128)(2,1)S(1)}, bf16[8,32,640]{2,1,0:T(8,128)(2,1)S(1)}, u32[]{:S(2)}, u32[]{:S(2)}) %collective-permute-start.9) | collective-permute-done | bytes 327712 | tf_op jit(solution)/shard_map/ppermute | solution.py:420
  96.1 0.5 collective-permute-done.10.refs_3_
  96.5 1.1 unpack.2
  97.6 0.0 copy-start.1
  97.6 1.7 %unpack.3.refs_9_ = bf16[1792,1024]{1,0:T(8,128)(2,1)S(1)} custom-call(s32[2]{0:T(128)S(1)} %pad_add_fusion.at_ref, bf16[8,32,1792]{2,1,0:T(8,128)(2,1)S(1)} %get-tuple-element.79.refs_0_, bf16[8,32,1792]{2,1,0:T(8,128)(2,1)S(1)} %collective-permute-done.15.refs_1_, bf16[8,32,1792]{2,1,0:T(8,128)(2,1)S(1)} %get-tuple-element.80.refs_2_, ...), custom_call_target="tpu_custom_call" | custom-call | bytes 7340032 | tf_op jit(solution)/shard_map/unpack/pallas_call | solution.py:137
  99.4 21.0 %adam.3 = (f32[1,1792]{1,0:T(1,128)S(1)}, bf16[1792,2048]{1,0:T(8,128)(2,1)S(1)}, bf16[1792,2048]{1,0:T(8,128)(2,1)S(1)}, bf16[1792,2048]{1,0:T(8,128)(2,1)}, bf16[1792,2048]{1,0:T(8,128)(2,1)}) custom-call(bf16[128,2048]{1,0:T(8,128)(2,1)S(1)} %copy-done.1, ...), custom_call_target="tpu_custom_call", output_to_operand_aliasing={{1}: (10, {}), {2}: (11, {})} | custom-call | flops 7516192768 | bytes 14680064 | tf_op jit(solution)/shard_map/adam/pallas_call | solution.py:321
  120.4 0.2 collective-permute-start.17
  120.6 0.6 collective-permute-start.18
  121.2 1.2 collective-permute-start.19
  122.3 9.3 %adam.2 = (f32[1,640]{1,0:T(1,128)S(1)}, bf16[512,2048]{1,0:T(8,128)(2,1)S(1)}, bf16[512,2048]{1,0:T(8,128)(2,1)S(1)}, bf16[512,2048]{1,0:T(8,128)(2,1)}, bf16[5...) custom-call(bf16[128,2048]{1,0:T(8,128)(2,1)S(1)} %copy-done.1, ...), custom_call_target="tpu_custom_call", output_to_operand_aliasing={{1}: (10, {}), {2}: (11, {}), {5}: (14, {}), {6}: (15, {})} | custom-call | flops 2684354560 | bytes 5242880 | tf_op jit(solution)/shard_map/adam/pallas_call | solution.py:321
  131.7 0.5 collective-permute-start.11
  132.2 0.5 collective-permute-start.12
  132.7 0.9 collective-permute-start.13
  133.6 4.2 %finish.2.refs_8_ = bf16[1792,2048]{1,0:T(8,128)(2,1)} custom-call(f32[1,1792]{1,0:T(1,128)S(1)} %get-tuple-element.84.refs_0_, f32[1,1792]{1,0:T(1,128)S(1)} %collective-permute-done.17.refs_1_, f32[1,1792]{1,0:T(1,128)S(1)} %collective-permute-done.18.refs_2_, f32[1,1792]{1,0:T(1,128)S(1)} %collective-permute-done.19.refs_3_, ...), custom_call_target="tpu_custom_call" | custom-call | flops 7340032 | bytes 7340032 | tf_op jit(solution)/shard_map/finish/pallas_call | solution.py:395
  137.8 2.6 %finish.3 = (bf16[512,2048]{1,0:T(8,128)(2,1)}, bf16[128,2048]{1,0:T(8,128)(2,1)}) custom-call(f32[1,640]{1,0:T(1,128)S(1)} %get-tuple-element.74.refs_0_, f32[1,640]{1,0:T(1,128)S(1)} %collective-permute-done.11.refs_1_, f32[1,640]{1,0:T(1,128)S(1)} %collective-permute-done.12.refs_2_, f32[1,640]{1,0:T(1,128)S(1)} %collective-permute-done.13.refs_3_, ...), custom_call_target="tpu_custom_call" | custom-call | flops 2621440 | bytes 2621440 | tf_op jit(solution)/shard_map/finish/pallas_call | solution.py:395
  (20 shorter events, 0.1 us)
Async XLA Ops:
  0.6 10.3 %copy-start = (bf16[128,2048]{1,0:T(8,128)(2,1)S(1)}, bf16[128,2048]{1,0:T(8,128)(2,1)}, u32[]{:S(2)}) copy-start(bf16[128,2048]{1,0:T(8,128)(2,1)} %refs_0_.7) | copy-start | bytes 1572868
  3.6 26.5 %all-to-all-start = ((bf16[8,32,640]{2,1,0:T(8,128)(2,1)}), bf16[8,32,640]{2,1,0:T(8,128)(2,1)S(1)}, u32[]{:S(2)}, u32[]{:S(2)}) async-start(bf16[8,32,640]{2,1,0:T(8,128)(2,1)} %get-tuple-element.52), calls=%async_computation | async-start | bytes 655360 | tf_op jit(solution)/shard_map/all_to_all | solution.py:470
  10.9 17.1 %collective-permute-start = (bf16[128,2048]{1,0:T(8,128)(2,1)S(1)}, bf16[128,2048]{1,0:T(8,128)(2,1)S(1)}, u32[]{:S(2)}, u32[]{:S(2)}) collective-permute-start(bf16[128,2048]{1,0:T(8,128)(2,1)S(1)} %copy-done), channel_id=1, source_target_pairs={{0,2},{2,4},{4,6},{6,7},{7,5},{5,3},{3,1},{1,0},{8,10},{10,12},{12... | collective-permute-start | bytes 1572872 | tf_op jit(solution)/shard_map/ppermute | solution.py:109
  12.9 17.2 %collective-permute-start.1 = (bf16[128,2048]{1,0:T(8,128)(2,1)S(1)}, bf16[128,2048]{1,0:T(8,128)(2,1)S(1)}, u32[]{:S(2)}, u32[]{:S(2)}) collective-permute-start(bf16[128,2048]{1,0:T(8,128)(2,1)S(1)} %copy-done), channel_id=1, source_target_pairs={{2,0},{4,2},{6,4},{7,6},{5,7},{3,5},{1,3},{0,1},{10,8},{12,10},{14... | collective-permute-start | bytes 1572872 | tf_op jit(solution)/shard_map/ppermute | solution.py:109
  30.2 33.1 %all-to-all-start.1 = ((bf16[8,32,1792]{2,1,0:T(8,128)(2,1)}), bf16[8,32,1792]{2,1,0:T(8,128)(2,1)S(1)}, u32[]{:S(2)}, u32[]{:S(2)}) async-start(bf16[8,32,1792]{2,1,0:T(8,128)(2,1)} %get-tuple-element.55), calls=%async_computation.1 | async-start | bytes 1835008 | tf_op jit(solution)/shard_map/all_to_all | solution.py:474
  35.2 25.9 %collective-permute-start.2 = (bf16[128,2048]{1,0:T(8,128)(2,1)S(1)}, bf16[128,2048]{1,0:T(8,128)(2,1)S(1)}, u32[]{:S(2)}, u32[]{:S(2)}) collective-permute-start(bf16[128,2048]{1,0:T(8,128)(2,1)S(1)} %get-tuple-element.56.refs_8_), channel_id=1, source_target_pairs={{0,2},{2,4},{4,6},{6,7},{7,5},{5,3},{3,1},{1,0},{8,10},{10,12},{12... | collective-permute-start | bytes 1572872 | tf_op jit(solution)/shard_map/ppermute | solution.py:109
  37.2 26.1 %collective-permute-start.3 = (bf16[128,2048]{1,0:T(8,128)(2,1)S(1)}, bf16[128,2048]{1,0:T(8,128)(2,1)S(1)}, u32[]{:S(2)}, u32[]{:S(2)}) collective-permute-start(bf16[128,2048]{1,0:T(8,128)(2,1)S(1)} %get-tuple-element.54.refs_1_), channel_id=1, source_target_pairs={{2,0},{4,2},{6,4},{7,6},{5,7},{3,5},{1,3},{0,1},{10,8},{12,10},{14... | collective-permute-start | bytes 1572872 | tf_op jit(solution)/shard_map/ppermute | solution.py:109
  37.2 8.4 %collective-permute-start.4 = (bf16[8,32,640]{2,1,0:T(8,128)(2,1)S(1)}, bf16[8,32,640]{2,1,0:T(8,128)(2,1)S(1)}, u32[]{:S(2)}, u32[]{:S(2)}) collective-permute-start(bf16[8,32,640]{2,1,0:T(8,128)(2,1)S(1)} %get-tuple-element.57.refs_0_), channel_id=1, source_target_pairs={{0,16},{8,24},{16,0},{24,8},{1,17},{9,25},{17,1},{25,9},{2,18},{10... | collective-permute-start | bytes 983048 | tf_op jit(solution)/shard_map/ppermute | solution.py:420
  45.6 0.7 copy-start.2
  63.3 1.0 copy-start.3
  64.3 27.5 %collective-permute-start.14 = (bf16[8,32,1792]{2,1,0:T(8,128)(2,1)S(1)}, bf16[8,32,1792]{2,1,0:T(8,128)(2,1)S(1)}, u32[]{:S(2)}, u32[]{:S(2)}) collective-permute-start(bf16[8,32,1792]{2,1,0:T(8,128)(2,1)S(1)} %get-tuple-element.60.refs_9_.refs_0_), channel_id=1, source_target_pairs={{0,16},{8,24},{16,0},{24,8},{1,17},{9,25},{17,1},{25,9},{2,18},{10... | collective-permute-start | bytes 2752520 | tf_op jit(solution)/shard_map/ppermute | solution.py:420
  65.8 16.4 %collective-permute-start.5 = (bf16[128,2048]{1,0:T(8,128)(2,1)S(1)}, bf16[128,2048]{1,0:T(8,128)(2,1)S(1)}, u32[]{:S(2)}, u32[]{:S(2)}) collective-permute-start(bf16[128,2048]{1,0:T(8,128)(2,1)S(1)} %get-tuple-element.59.refs_7_), channel_id=1, source_target_pairs={{0,2},{2,4},{4,6},{6,7},{7,5},{5,3},{3,1},{1,0},{8,10},{10,12},{12... | collective-permute-start | bytes 1572872 | tf_op jit(solution)/shard_map/ppermute | solution.py:109
  72.4 11.9 %collective-permute-start.6 = (bf16[128,2048]{1,0:T(8,128)(2,1)S(1)}, bf16[128,2048]{1,0:T(8,128)(2,1)S(1)}, u32[]{:S(2)}, u32[]{:S(2)}) collective-permute-start(bf16[128,2048]{1,0:T(8,128)(2,1)S(1)} %get-tuple-element.58.refs_2_), channel_id=1, source_target_pairs={{2,0},{4,2},{6,4},{7,6},{5,7},{3,5},{1,3},{0,1},{10,8},{12,10},{14... | collective-permute-start | bytes 1572872 | tf_op jit(solution)/shard_map/ppermute | solution.py:109
  82.1 10.3 %copy-start.4 = (bf16[8,32,640]{2,1,0:T(8,128)(2,1)S(1)}, bf16[8,32,640]{2,1,0:T(8,128)(2,1)}, u32[]{:S(2)}) copy-start(bf16[8,32,640]{2,1,0:T(8,128)(2,1)} %copy-done.2) | copy-start | bytes 983044
  84.4 6.4 %collective-permute-start.7 = (bf16[64,2048]{1,0:T(8,128)(2,1)S(1)}, bf16[64,2048]{1,0:T(8,128)(2,1)S(1)}, u32[]{:S(2)}, u32[]{:S(2)}) collective-permute-start(bf16[64,2048]{1,0:T(8,128)(2,1)S(1)} %get-tuple-element.64), channel_id=1, source_target_pairs={{0,2},{2,4},{4,6},{6,7},{7,5},{5,3},{3,1},{1,0},{8,10},{10,12},{12... | collective-permute-start | bytes 786440 | tf_op jit(solution)/shard_map/ppermute | solution.py:109
  85.4 6.4 %collective-permute-start.8 = (bf16[64,2048]{1,0:T(8,128)(2,1)S(1)}, bf16[64,2048]{1,0:T(8,128)(2,1)S(1)}, u32[]{:S(2)}, u32[]{:S(2)}) collective-permute-start(bf16[64,2048]{1,0:T(8,128)(2,1)S(1)} %get-tuple-element.65), channel_id=1, source_target_pairs={{2,0},{4,2},{6,4},{7,6},{5,7},{3,5},{1,3},{0,1},{10,8},{12,10},{14... | collective-permute-start | bytes 786440 | tf_op jit(solution)/shard_map/ppermute | solution.py:109
  91.8 5.8 %collective-permute-start.15 = (bf16[8,32,1792]{2,1,0:T(8,128)(2,1)S(1)}, bf16[8,32,1792]{2,1,0:T(8,128)(2,1)S(1)}, u32[]{:S(2)}, u32[]{:S(2)}) collective-permute-start(bf16[8,32,1792]{2,1,0:T(8,128)(2,1)S(1)} %get-tuple-element.79.refs_0_), channel_id=1, source_target_pairs={{0,8},{8,0},{16,24},{24,16},{1,9},{9,1},{17,25},{25,17},{2,10},{10... | collective-permute-start | bytes 2752520 | tf_op jit(solution)/shard_map/ppermute | solution.py:420
  91.8 5.8 %collective-permute-start.16 = (bf16[8,32,1792]{2,1,0:T(8,128)(2,1)S(1)}, bf16[8,32,1792]{2,1,0:T(8,128)(2,1)S(1)}, u32[]{:S(2)}, u32[]{:S(2)}) collective-permute-start(bf16[8,32,1792]{2,1,0:T(8,128)(2,1)S(1)} %get-tuple-element.80.refs_2_), channel_id=1, source_target_pairs={{0,8},{8,0},{16,24},{24,16},{1,9},{9,1},{17,25},{25,17},{2,10},{10... | collective-permute-start | bytes 2752520 | tf_op jit(solution)/shard_map/ppermute | solution.py:420
  92.3 3.7 %collective-permute-start.9 = (bf16[8,32,640]{2,1,0:T(8,128)(2,1)S(1)}, bf16[8,32,640]{2,1,0:T(8,128)(2,1)S(1)}, u32[]{:S(2)}, u32[]{:S(2)}) collective-permute-start(bf16[8,32,640]{2,1,0:T(8,128)(2,1)S(1)} %get-tuple-element.57.refs_0_), channel_id=1, source_target_pairs={{0,8},{8,0},{16,24},{24,16},{1,9},{9,1},{17,25},{25,17},{2,10},{10... | collective-permute-start | bytes 983048 | tf_op jit(solution)/shard_map/ppermute | solution.py:420
  92.4 4.1 %collective-permute-start.10 = (bf16[8,32,640]{2,1,0:T(8,128)(2,1)S(1)}, bf16[8,32,640]{2,1,0:T(8,128)(2,1)S(1)}, u32[]{:S(2)}, u32[]{:S(2)}) collective-permute-start(bf16[8,32,640]{2,1,0:T(8,128)(2,1)S(1)} %copy-done.4), channel_id=1, source_target_pairs={{0,8},{8,0},{16,24},{24,16},{1,9},{9,1},{17,25},{25,17},{2,10},{10... | collective-permute-start | bytes 983048 | tf_op jit(solution)/shard_map/ppermute | solution.py:420
  97.6 1.8 %copy-start.1 = (bf16[128,2048]{1,0:T(8,128)(2,1)S(1)}, bf16[128,2048]{1,0:T(8,128)(2,1)}, u32[]{:S(2)}) copy-start(bf16[128,2048]{1,0:T(8,128)(2,1)} %refs_0_.7) | copy-start | bytes 1572868
  120.4 12.3 %collective-permute-start.17 = (f32[1,1792]{1,0:T(1,128)S(1)}, f32[1,1792]{1,0:T(1,128)S(1)}, u32[]{:S(2)}, u32[]{:S(2)}) collective-permute-start(f32[1,1792]{1,0:T(1,128)S(1)} %get-tuple-element.84.refs_0_), channel_id=1, source_target_pairs={{0,8},{8,0},{16,24},{24,16},{1,9},{9,1},{17,25},{25,17},{2,10},{10... | collective-permute-start | bytes 21512 | tf_op jit(solution)/shard_map/ppermute | solution.py:436
  120.6 13.0 %collective-permute-start.18 = (f32[1,1792]{1,0:T(1,128)S(1)}, f32[1,1792]{1,0:T(1,128)S(1)}, u32[]{:S(2)}, u32[]{:S(2)}) collective-permute-start(f32[1,1792]{1,0:T(1,128)S(1)} %get-tuple-element.84.refs_0_), channel_id=1, source_target_pairs={{0,16},{8,24},{16,0},{24,8},{1,17},{9,25},{17,1},{25,9},{2,18},{10... | collective-permute-start | bytes 21512 | tf_op jit(solution)/shard_map/ppermute | solution.py:436
  121.2 12.4 %collective-permute-start.19 = (f32[1,1792]{1,0:T(1,128)S(1)}, f32[1,1792]{1,0:T(1,128)S(1)}, u32[]{:S(2)}, u32[]{:S(2)}) collective-permute-start(f32[1,1792]{1,0:T(1,128)S(1)} %get-tuple-element.84.refs_0_), channel_id=1, source_target_pairs={{0,24},{8,16},{16,8},{24,0},{1,25},{9,17},{17,9},{25,1},{2,26},{10... | collective-permute-start | bytes 21512 | tf_op jit(solution)/shard_map/ppermute | solution.py:436
  131.7 6.2 %collective-permute-start.11 = (f32[1,640]{1,0:T(1,128)S(1)}, f32[1,640]{1,0:T(1,128)S(1)}, u32[]{:S(2)}, u32[]{:S(2)}) collective-permute-start(f32[1,640]{1,0:T(1,128)S(1)} %get-tuple-element.74.refs_0_), channel_id=1, source_target_pairs={{0,8},{8,0},{16,24},{24,16},{1,9},{9,1},{17,25},{25,17},{2,10},{10... | collective-permute-start | bytes 7688 | tf_op jit(solution)/shard_map/ppermute | solution.py:436
  132.2 5.7 %collective-permute-start.12 = (f32[1,640]{1,0:T(1,128)S(1)}, f32[1,640]{1,0:T(1,128)S(1)}, u32[]{:S(2)}, u32[]{:S(2)}) collective-permute-start(f32[1,640]{1,0:T(1,128)S(1)} %get-tuple-element.74.refs_0_), channel_id=1, source_target_pairs={{0,16},{8,24},{16,0},{24,8},{1,17},{9,25},{17,1},{25,9},{2,18},{10... | collective-permute-start | bytes 7688 | tf_op jit(solution)/shard_map/ppermute | solution.py:436
  132.7 5.1 %collective-permute-start.13 = (f32[1,640]{1,0:T(1,128)S(1)}, f32[1,640]{1,0:T(1,128)S(1)}, u32[]{:S(2)}, u32[]{:S(2)}) collective-permute-start(f32[1,640]{1,0:T(1,128)S(1)} %get-tuple-element.74.refs_0_), channel_id=1, source_target_pairs={{0,24},{8,16},{16,8},{24,0},{1,25},{9,17},{17,9},{25,1},{2,26},{10... | collective-permute-start | bytes 7688 | tf_op jit(solution)/shard_map/ppermute | solution.py:436

commit v11 on v10

--- a/solution.py
+++ b/solution.py
@@ -436,6 +436,10 @@
         lax.ppermute(array, axis, [(at, at ^ turn) for at in range(size)])
         for turn in range(1, size)
     ]
+
+
+def unpack_chunk(pair, pieces, place):
+    return unpack(from_others(pair, "col"), [high - low for _, low, high in pieces], place)
 
 
 def per_device(
@@ -479,7 +483,8 @@
     swaps.append((owned, swap(owned, "col", cols // 2)))
     *held, loaded = preload([array for state in states for array in state], owned)
     held = [held[at : at + 3] for at in range(0, len(held), 3)]
-    one, two = join(ring_step(one, two, "dp"), (loaded,))
+    early = unpack_chunk(swaps[0], plan[0], place)
+    one, two = join(ring_step(one, two, "dp"), (loaded, *early))
     behind.append(one)
     ahead.append(two)
     while 2 * len(behind) < groups:
@@ -490,10 +495,7 @@
     swaps[1] = join(swaps[1], middle)
     x_pieces = [layer_input, *ahead[1:], *middle, *behind[:0:-1]]
     cotangents = [[], [], []]
-    for got, pieces in zip(swaps, plan):
-        every = unpack(
-            from_others(got, "col"), [high - low for _, low, high in pieces], place
-        )
+    for every, pieces in zip((early, unpack_chunk(swaps[1], plan[1], place)), plan):
         for (which, _, _), cotangent in zip(pieces, every):
             cotangents[which].append(cotangent)
     updated = [None] * 3

time: 141 us -> 144 us (1.021)
  waiting for transfers between devices: 52.3 us -> 54.3 us
  transfers between devices with their start and end apart: 22 -> 22, of which waited for: 10 -> 11; matrix products, arithmetic and copies ran while one was open for 0% -> 0% of each run, Pallas kernels for 17% -> 17%
where the time goes in v11:
time: 144 us; the launch traced here: 143 us
  waiting for transfers between devices  54.3 us (38%)
  Pallas kernels  52.8 us (37%)
  starting transfers between devices  33.1 us (23%)
  local copies, waits for them, and re-layouts  1.96 us (1%)
    ppermute x8, waiting for transfers between devices, ring_step(): return (lax.ppermute(one, axis, onward), lax.ppermute(two, axis, back))  42.3 us
    pallas_call x2, Pallas kernels, adam_pass(): pl.pallas_call(functools.partial(adam_kernel, strip, len(x_pieces), cuts)...  30.5 us
    ppermute x8, starting transfers between devices, ring_step(): return (lax.ppermute(one, axis, onward), lax.ppermute(two, axis, back))  12.9 us
    ppermute x6, waiting for transfers between devices, swap(): lax.ppermute(array, axis, [(at, at ^ bit) for at in range(lax.axis_size(a...  12 us
    pallas_call x1, Pallas kernels, preload(): pl.pallas_call(preload_kernel, in_specs=[pl.BlockSpec(memory_space=pl.ANY...  9.68 us
    all_to_all x1, starting transfers between devices, per_device(): lax.all_to_all(packed[0], 'dp', split_axis=0, concat_axis=0, tiled=True)  7.28 us
    pallas_call x2, Pallas kernels, finish_rows(): pl.pallas_call(functools.partial(finish_kernel, len(powers), whole_width,...  6.84 us
    all_to_all x1, starting transfers between devices, per_device(): owned = lax.all_to_all(chunk, 'dp', split_axis=0, concat_axis=0, tiled=True)  5.02 us
  transfers between devices with their start and end apart: 22, of which 11 were waited for; matrix products, arithmetic and copies ran while one was open for 0% of the time, Pallas kernels for 17%

profile of v11, /device:TPU:0, one launch (start us, length us, event | category | flops | bytes accessed | tf_op | source)
XLA Modules:
  0.0 143.0 jit_solution(992694220563521534)
XLA Ops:
  0.6 0.0 copy-start
  0.7 0.1 pad_add_fusion.at_ref
  0.7 2.9 %pack.1 = (bf16[8,32,640]{2,1,0:T(8,128)(2,1)}, bf16[8,32,1792]{2,1,0:T(8,128)(2,1)}) custom-call(s32[2]{0:T(128)S(1)} %pad_add_fusion.at_ref, bf16[128,4096]{1,0:T(8,128)(2,1)} %refs_0_.4, bf16[128,1024]{1,0:T(8,128)(2,1)} %refs_1_.2, bf16[128,14336]{1,0:T(8,128)(2,1)} %refs_2_.2), custom_call_target="tpu_custom_call" | custom-call | bytes 2490368 | tf_op jit(solution)/shard_map/pack/pallas_call | solution.py:57
  3.6 7.3 %all-to-all-start = ((bf16[8,32,640]{2,1,0:T(8,128)(2,1)}), bf16[8,32,640]{2,1,0:T(8,128)(2,1)S(1)}, u32[]{:S(2)}, u32[]{:S(2)}) async-start(bf16[8,32,640]{2,1,0:T(8,128)(2,1)} %get-tuple-element.52), calls=%async_computation | async-start | bytes 655360 | tf_op jit(solution)/shard_map/all_to_all | solution.py:474
  10.9 2.0 %collective-permute-start = (bf16[128,2048]{1,0:T(8,128)(2,1)S(1)}, bf16[128,2048]{1,0:T(8,128)(2,1)S(1)}, u32[]{:S(2)}, u32[]{:S(2)}) collective-permute-start(bf16[128,2048]{1,0:T(8,128)(2,1)S(1)} %copy-done), channel_id=1, source_target_pairs={{0,2},{2,4},{4,6},{6,7},{7,5},{5,3},{3,1},{1,0},{8,10},{10,12},{12... | collective-permute-start | bytes 1572872 | tf_op jit(solution)/shard_map/ppermute | solution.py:109
  12.9 0.1 collective-permute-start.1
  13.0 15.0 %collective-permute-done.refs_1_ = bf16[128,2048]{1,0:T(8,128)(2,1)S(1)} collective-permute-done((bf16[128,2048]{1,0:T(8,128)(2,1)S(1)}, bf16[128,2048]{1,0:T(8,128)(2,1)S(1)}, u32[]{:S(2)}, u32[]{:S(2)}) %collective-permute-start) | collective-permute-done | bytes 524320 | tf_op jit(solution)/shard_map/ppermute | solution.py:109
  28.0 2.1 %collective-permute-done.1.refs_2_ = bf16[128,2048]{1,0:T(8,128)(2,1)S(1)} collective-permute-done((bf16[128,2048]{1,0:T(8,128)(2,1)S(1)}, bf16[128,2048]{1,0:T(8,128)(2,1)S(1)}, u32[]{:S(2)}, u32[]{:S(2)}) %collective-permute-start.1) | collective-permute-done | bytes 524320 | tf_op jit(solution)/shard_map/ppermute | solution.py:109
  30.2 5.0 %all-to-all-start.1 = ((bf16[8,32,1792]{2,1,0:T(8,128)(2,1)}), bf16[8,32,1792]{2,1,0:T(8,128)(2,1)S(1)}, u32[]{:S(2)}, u32[]{:S(2)}) async-start(bf16[8,32,1792]{2,1,0:T(8,128)(2,1)} %get-tuple-element.55), calls=%async_computation.1 | async-start | bytes 1835008 | tf_op jit(solution)/shard_map/all_to_all | solution.py:478
  35.2 2.0 %collective-permute-start.2 = (bf16[128,2048]{1,0:T(8,128)(2,1)S(1)}, bf16[128,2048]{1,0:T(8,128)(2,1)S(1)}, u32[]{:S(2)}, u32[]{:S(2)}) collective-permute-start(bf16[128,2048]{1,0:T(8,128)(2,1)S(1)} %get-tuple-element.56.refs_8_), channel_id=1, source_target_pairs={{0,2},{2,4},{4,6},{6,7},{7,5},{5,3},{3,1},{1,0},{8,10},{10,12},{12... | collective-permute-start | bytes 1572872 | tf_op jit(solution)/shard_map/ppermute | solution.py:109
  37.2 0.0 collective-permute-start.3
  37.2 1.5 %collective-permute-start.4 = (bf16[8,32,640]{2,1,0:T(8,128)(2,1)S(1)}, bf16[8,32,640]{2,1,0:T(8,128)(2,1)S(1)}, u32[]{:S(2)}, u32[]{:S(2)}) collective-permute-start(bf16[8,32,640]{2,1,0:T(8,128)(2,1)S(1)} %get-tuple-element.57.refs_0_), channel_id=1, source_target_pairs={{0,16},{8,24},{16,0},{24,8},{1,17},{9,25},{17,1},{25,9},{2,18},{10... | collective-permute-start | bytes 983048 | tf_op jit(solution)/shard_map/ppermute | solution.py:420
  38.7 6.9 %collective-permute-done.4.refs_3_.refs_2_ = bf16[8,32,640]{2,1,0:T(8,128)(2,1)S(1)} collective-permute-done((bf16[8,32,640]{2,1,0:T(8,128)(2,1)S(1)}, bf16[8,32,640]{2,1,0:T(8,128)(2,1)S(1)}, u32[]{:S(2)}, u32[]{:S(2)}) %collective-permute-start.4) | collective-permute-done | bytes 327712 | tf_op jit(solution)/shard_map/ppermute | solution.py:420
  45.6 15.5 %collective-permute-done.2.refs_1_ = bf16[128,2048]{1,0:T(8,128)(2,1)S(1)} collective-permute-done((bf16[128,2048]{1,0:T(8,128)(2,1)S(1)}, bf16[128,2048]{1,0:T(8,128)(2,1)S(1)}, u32[]{:S(2)}, u32[]{:S(2)}) %collective-permute-start.2) | collective-permute-done | bytes 524320 | tf_op jit(solution)/shard_map/ppermute | solution.py:109
  61.1 2.2 %collective-permute-done.3.refs_2_ = bf16[128,2048]{1,0:T(8,128)(2,1)S(1)} collective-permute-done((bf16[128,2048]{1,0:T(8,128)(2,1)S(1)}, bf16[128,2048]{1,0:T(8,128)(2,1)S(1)}, u32[]{:S(2)}, u32[]{:S(2)}) %collective-permute-start.3) | collective-permute-done | bytes 524320 | tf_op jit(solution)/shard_map/ppermute | solution.py:109
  63.3 1.0 copy-done.3
  64.3 1.5 %collective-permute-start.14 = (bf16[8,32,1792]{2,1,0:T(8,128)(2,1)S(1)}, bf16[8,32,1792]{2,1,0:T(8,128)(2,1)S(1)}, u32[]{:S(2)}, u32[]{:S(2)}) collective-permute-start(bf16[8,32,1792]{2,1,0:T(8,128)(2,1)S(1)} %get-tuple-element.60.refs_9_.refs_0_), channel_id=1, source_target_pairs={{0,16},{8,24},{16,0},{24,8},{1,17},{9,25},{17,1},{25,9},{2,18},{10... | collective-permute-start | bytes 2752520 | tf_op jit(solution)/shard_map/ppermute | solution.py:420
  65.8 6.7 %collective-permute-start.5 = (bf16[128,2048]{1,0:T(8,128)(2,1)S(1)}, bf16[128,2048]{1,0:T(8,128)(2,1)S(1)}, u32[]{:S(2)}, u32[]{:S(2)}) collective-permute-start(bf16[128,2048]{1,0:T(8,128)(2,1)S(1)} %get-tuple-element.59.refs_7_), channel_id=1, source_target_pairs={{0,2},{2,4},{4,6},{6,7},{7,5},{5,3},{3,1},{1,0},{8,10},{10,12},{12... | collective-permute-start | bytes 1572872 | tf_op jit(solution)/shard_map/ppermute | solution.py:109
  72.4 0.0 collective-permute-start.6
  72.4 0.0 collective-permute-start.7
  72.4 0.5 collective-permute-start.8
  72.9 1.5 %collective-permute-done.7.refs_1_ = bf16[8,32,640]{2,1,0:T(8,128)(2,1)S(1)} collective-permute-done((bf16[8,32,640]{2,1,0:T(8,128)(2,1)S(1)}, bf16[8,32,640]{2,1,0:T(8,128)(2,1)S(1)}, u32[]{:S(2)}, u32[]{:S(2)}) %collective-permute-start.7) | collective-permute-done | bytes 327712 | tf_op jit(solution)/shard_map/ppermute | solution.py:420
  74.5 0.2 collective-permute-done.8.refs_3_
  74.7 1.0 copy-done.4
  75.7 1.1 unpack.2
  76.8 9.7 %preload.1 = (bf16[512,2048]{1,0:T(8,128)(2,1)S(1)}, bf16[512,2048]{1,0:T(8,128)(2,1)S(1)}, bf16[512,2048]{1,0:T(8,128)(2,1)S(1)}, bf16[128,2048]{1,0:T(8,128)(2...) custom-call(bf16[512,2048]{1,0:T(8,128)(2,1)} %refs_0_.5, ...), custom_call_target="tpu_custom_call" | custom-call | bytes 29884416 | tf_op jit(solution)/shard_map/preload/pallas_call | solution.py:182
  86.5 0.0 collective-permute-done.5.refs_0_
  86.5 0.0 collective-permute-done.6.refs_1_
  86.6 1.2 collective-permute-start.10
  87.8 0.9 collective-permute-start.9
  88.7 6.5 %collective-permute-done.10.refs_5_.refs_3_ = bf16[64,2048]{1,0:T(8,128)(2,1)S(1)} collective-permute-done((bf16[64,2048]{1,0:T(8,128)(2,1)S(1)}, bf16[64,2048]{1,0:T(8,128)(2,1)S(1)}, u32[]{:S(2)}, u32[]{:S(2)}) %collective-permute-start.10) | collective-permute-done | bytes 262176 | tf_op jit(solution)/shard_map/ppermute | solution.py:109
  95.2 0.9 collective-permute-done.9.refs_4_.refs_2_
  96.1 0.0 collective-permute-start.15
  96.1 0.5 collective-permute-start.16
  96.6 2.0 %collective-permute-done.15.refs_1_ = bf16[8,32,1792]{2,1,0:T(8,128)(2,1)S(1)} collective-permute-done((bf16[8,32,1792]{2,1,0:T(8,128)(2,1)S(1)}, bf16[8,32,1792]{2,1,0:T(8,128)(2,1)S(1)}, u32[]{:S(2)}, u32[]{:S(2)}) %collective-permute-start.15) | collective-permute-done | bytes 917536 | tf_op jit(solution)/shard_map/ppermute | solution.py:420
  98.6 1.3 collective-permute-done.16.refs_3_
  99.9 1.7 %unpack.3.refs_9_ = bf16[1792,1024]{1,0:T(8,128)(2,1)S(1)} custom-call(s32[2]{0:T(128)S(1)} %pad_add_fusion.at_ref, bf16[8,32,1792]{2,1,0:T(8,128)(2,1)S(1)} %get-tuple-element.79.refs_0_, bf16[8,32,1792]{2,1,0:T(8,128)(2,1)S(1)} %collective-permute-done.15.refs_1_, bf16[8,32,1792]{2,1,0:T(8,128)(2,1)S(1)} %get-tuple-element.80.refs_2_, ...), custom_call_target="tpu_custom_call" | custom-call | bytes 7340032 | tf_op jit(solution)/shard_map/unpack/pallas_call | solution.py:137
  101.7 21.0 %adam.3 = (f32[1,1792]{1,0:T(1,128)S(1)}, bf16[1792,2048]{1,0:T(8,128)(2,1)S(1)}, bf16[1792,2048]{1,0:T(8,128)(2,1)S(1)}, bf16[1792,2048]{1,0:T(8,128)(2,1)}, bf16[1792,2048]{1,0:T(8,128)(2,1)}) custom-call(bf16[128,2048]{1,0:T(8,128)(2,1)S(1)} %copy-done.1, ...), custom_call_target="tpu_custom_call", output_to_operand_aliasing={{1}: (10, {}), {2}: (11, {})} | custom-call | flops 7516192768 | bytes 14680064 | tf_op jit(solution)/shard_map/adam/pallas_call | solution.py:321
  122.7 0.2 collective-permute-start.17
  122.9 0.6 collective-permute-start.18
  123.5 1.2 collective-permute-start.19
  124.6 9.5 %adam.2 = (f32[1,640]{1,0:T(1,128)S(1)}, bf16[512,2048]{1,0:T(8,128)(2,1)S(1)}, bf16[512,2048]{1,0:T(8,128)(2,1)S(1)}, bf16[512,2048]{1,0:T(8,128)(2,1)}, bf16[5...) custom-call(bf16[128,2048]{1,0:T(8,128)(2,1)S(1)} %copy-done.1, ...), custom_call_target="tpu_custom_call", output_to_operand_aliasing={{1}: (10, {}), {2}: (11, {}), {5}: (14, {}), {6}: (15, {})} | custom-call | flops 2684354560 | bytes 5242880 | tf_op jit(solution)/shard_map/adam/pallas_call | solution.py:321
  134.1 0.5 collective-permute-start.11
  134.6 0.5 collective-permute-start.12
  135.2 0.9 collective-permute-start.13
  136.1 4.2 %finish.2.refs_8_ = bf16[1792,2048]{1,0:T(8,128)(2,1)} custom-call(f32[1,1792]{1,0:T(1,128)S(1)} %get-tuple-element.84.refs_0_, f32[1,1792]{1,0:T(1,128)S(1)} %collective-permute-done.17.refs_1_, f32[1,1792]{1,0:T(1,128)S(1)} %collective-permute-done.18.refs_2_, f32[1,1792]{1,0:T(1,128)S(1)} %collective-permute-done.19.refs_3_, ...), custom_call_target="tpu_custom_call" | custom-call | flops 7340032 | bytes 7340032 | tf_op jit(solution)/shard_map/finish/pallas_call | solution.py:395
  140.3 0.0 collective-permute-done.11.refs_1_
  140.3 2.6 %finish.3 = (bf16[512,2048]{1,0:T(8,128)(2,1)}, bf16[128,2048]{1,0:T(8,128)(2,1)}) custom-call(f32[1,640]{1,0:T(1,128)S(1)} %get-tuple-element.74.refs_0_, f32[1,640]{1,0:T(1,128)S(1)} %collective-permute-done.11.refs_1_, f32[1,640]{1,0:T(1,128)S(1)} %collective-permute-done.12.refs_2_, f32[1,640]{1,0:T(1,128)S(1)} %collective-permute-done.13.refs_3_, ...), custom_call_target="tpu_custom_call" | custom-call | flops 2621440 | bytes 2621440 | tf_op jit(solution)/shard_map/finish/pallas_call | solution.py:395
  (20 shorter events, 0.1 us)
Async XLA Ops:
  0.6 10.3 %copy-start = (bf16[128,2048]{1,0:T(8,128)(2,1)S(1)}, bf16[128,2048]{1,0:T(8,128)(2,1)}, u32[]{:S(2)}) copy-start(bf16[128,2048]{1,0:T(8,128)(2,1)} %refs_0_.7) | copy-start | bytes 1572868
  3.6 26.5 %all-to-all-start = ((bf16[8,32,640]{2,1,0:T(8,128)(2,1)}), bf16[8,32,640]{2,1,0:T(8,128)(2,1)S(1)}, u32[]{:S(2)}, u32[]{:S(2)}) async-start(bf16[8,32,640]{2,1,0:T(8,128)(2,1)} %get-tuple-element.52), calls=%async_computation | async-start | bytes 655360 | tf_op jit(solution)/shard_map/all_to_all | solution.py:474
  10.9 17.1 %collective-permute-start = (bf16[128,2048]{1,0:T(8,128)(2,1)S(1)}, bf16[128,2048]{1,0:T(8,128)(2,1)S(1)}, u32[]{:S(2)}, u32[]{:S(2)}) collective-permute-start(bf16[128,2048]{1,0:T(8,128)(2,1)S(1)} %copy-done), channel_id=1, source_target_pairs={{0,2},{2,4},{4,6},{6,7},{7,5},{5,3},{3,1},{1,0},{8,10},{10,12},{12... | collective-permute-start | bytes 1572872 | tf_op jit(solution)/shard_map/ppermute | solution.py:109
  12.9 17.2 %collective-permute-start.1 = (bf16[128,2048]{1,0:T(8,128)(2,1)S(1)}, bf16[128,2048]{1,0:T(8,128)(2,1)S(1)}, u32[]{:S(2)}, u32[]{:S(2)}) collective-permute-start(bf16[128,2048]{1,0:T(8,128)(2,1)S(1)} %copy-done), channel_id=1, source_target_pairs={{2,0},{4,2},{6,4},{7,6},{5,7},{3,5},{1,3},{0,1},{10,8},{12,10},{14... | collective-permute-start | bytes 1572872 | tf_op jit(solution)/shard_map/ppermute | solution.py:109
  30.2 33.1 %all-to-all-start.1 = ((bf16[8,32,1792]{2,1,0:T(8,128)(2,1)}), bf16[8,32,1792]{2,1,0:T(8,128)(2,1)S(1)}, u32[]{:S(2)}, u32[]{:S(2)}) async-start(bf16[8,32,1792]{2,1,0:T(8,128)(2,1)} %get-tuple-element.55), calls=%async_computation.1 | async-start | bytes 1835008 | tf_op jit(solution)/shard_map/all_to_all | solution.py:478
  35.2 25.9 %collective-permute-start.2 = (bf16[128,2048]{1,0:T(8,128)(2,1)S(1)}, bf16[128,2048]{1,0:T(8,128)(2,1)S(1)}, u32[]{:S(2)}, u32[]{:S(2)}) collective-permute-start(bf16[128,2048]{1,0:T(8,128)(2,1)S(1)} %get-tuple-element.56.refs_8_), channel_id=1, source_target_pairs={{0,2},{2,4},{4,6},{6,7},{7,5},{5,3},{3,1},{1,0},{8,10},{10,12},{12... | collective-permute-start | bytes 1572872 | tf_op jit(solution)/shard_map/ppermute | solution.py:109
  37.2 26.1 %collective-permute-start.3 = (bf16[128,2048]{1,0:T(8,128)(2,1)S(1)}, bf16[128,2048]{1,0:T(8,128)(2,1)S(1)}, u32[]{:S(2)}, u32[]{:S(2)}) collective-permute-start(bf16[128,2048]{1,0:T(8,128)(2,1)S(1)} %get-tuple-element.54.refs_1_), channel_id=1, source_target_pairs={{2,0},{4,2},{6,4},{7,6},{5,7},{3,5},{1,3},{0,1},{10,8},{12,10},{14... | collective-permute-start | bytes 1572872 | tf_op jit(solution)/shard_map/ppermute | solution.py:109
  37.2 8.4 %collective-permute-start.4 = (bf16[8,32,640]{2,1,0:T(8,128)(2,1)S(1)}, bf16[8,32,640]{2,1,0:T(8,128)(2,1)S(1)}, u32[]{:S(2)}, u32[]{:S(2)}) collective-permute-start(bf16[8,32,640]{2,1,0:T(8,128)(2,1)S(1)} %get-tuple-element.57.refs_0_), channel_id=1, source_target_pairs={{0,16},{8,24},{16,0},{24,8},{1,17},{9,25},{17,1},{25,9},{2,18},{10... | collective-permute-start | bytes 983048 | tf_op jit(solution)/shard_map/ppermute | solution.py:420
  45.6 15.5 %copy-start.2 = (bf16[8,32,640]{2,1,0:T(8,128)(2,1)}, bf16[8,32,640]{2,1,0:T(8,128)(2,1)S(1)}, u32[]{:S(2)}) copy-start(bf16[8,32,640]{2,1,0:T(8,128)(2,1)S(1)} %collective-permute-done.4.refs_3_.refs_2_) | copy-start | bytes 983044
  63.3 1.0 copy-start.3
  64.3 31.9 %collective-permute-start.14 = (bf16[8,32,1792]{2,1,0:T(8,128)(2,1)S(1)}, bf16[8,32,1792]{2,1,0:T(8,128)(2,1)S(1)}, u32[]{:S(2)}, u32[]{:S(2)}) collective-permute-start(bf16[8,32,1792]{2,1,0:T(8,128)(2,1)S(1)} %get-tuple-element.60.refs_9_.refs_0_), channel_id=1, source_target_pairs={{0,16},{8,24},{16,0},{24,8},{1,17},{9,25},{17,1},{25,9},{2,18},{10... | collective-permute-start | bytes 2752520 | tf_op jit(solution)/shard_map/ppermute | solution.py:420
  65.8 20.7 %collective-permute-start.5 = (bf16[128,2048]{1,0:T(8,128)(2,1)S(1)}, bf16[128,2048]{1,0:T(8,128)(2,1)S(1)}, u32[]{:S(2)}, u32[]{:S(2)}) collective-permute-start(bf16[128,2048]{1,0:T(8,128)(2,1)S(1)} %get-tuple-element.59.refs_7_), channel_id=1, source_target_pairs={{0,2},{2,4},{4,6},{6,7},{7,5},{5,3},{3,1},{1,0},{8,10},{10,12},{12... | collective-permute-start | bytes 1572872 | tf_op jit(solution)/shard_map/ppermute | solution.py:109
  72.4 14.1 %collective-permute-start.6 = (bf16[128,2048]{1,0:T(8,128)(2,1)S(1)}, bf16[128,2048]{1,0:T(8,128)(2,1)S(1)}, u32[]{:S(2)}, u32[]{:S(2)}) collective-permute-start(bf16[128,2048]{1,0:T(8,128)(2,1)S(1)} %get-tuple-element.58.refs_2_), channel_id=1, source_target_pairs={{2,0},{4,2},{6,4},{7,6},{5,7},{3,5},{1,3},{0,1},{10,8},{12,10},{14... | collective-permute-start | bytes 1572872 | tf_op jit(solution)/shard_map/ppermute | solution.py:109
  72.4 2.1 %collective-permute-start.7 = (bf16[8,32,640]{2,1,0:T(8,128)(2,1)S(1)}, bf16[8,32,640]{2,1,0:T(8,128)(2,1)S(1)}, u32[]{:S(2)}, u32[]{:S(2)}) collective-permute-start(bf16[8,32,640]{2,1,0:T(8,128)(2,1)S(1)} %get-tuple-element.57.refs_0_), channel_id=1, source_target_pairs={{0,8},{8,0},{16,24},{24,16},{1,9},{9,1},{17,25},{25,17},{2,10},{10... | collective-permute-start | bytes 983048 | tf_op jit(solution)/shard_map/ppermute | solution.py:420
  72.4 2.3 %collective-permute-start.8 = (bf16[8,32,640]{2,1,0:T(8,128)(2,1)}, bf16[8,32,640]{2,1,0:T(8,128)(2,1)S(1)}, u32[]{:S(2)}, u32[]{:S(2)}) collective-permute-start(bf16[8,32,640]{2,1,0:T(8,128)(2,1)} %copy-done.2), channel_id=1, source_target_pairs={{0,8},{8,0},{16,24},{24,16},{1,9},{9,1},{17,25},{25,17},{2,10},{10... | collective-permute-start | bytes 983048 | tf_op jit(solution)/shard_map/ppermute | solution.py:420
  74.7 1.0 copy-start.4
  86.6 8.7 %collective-permute-start.10 = (bf16[64,2048]{1,0:T(8,128)(2,1)S(1)}, bf16[64,2048]{1,0:T(8,128)(2,1)S(1)}, u32[]{:S(2)}, u32[]{:S(2)}) collective-permute-start(bf16[64,2048]{1,0:T(8,128)(2,1)S(1)} %get-tuple-element.67), channel_id=1, source_target_pairs={{2,0},{4,2},{6,4},{7,6},{5,7},{3,5},{1,3},{0,1},{10,8},{12,10},{14... | collective-permute-start | bytes 786440 | tf_op jit(solution)/shard_map/ppermute | solution.py:109
  87.8 8.3 %collective-permute-start.9 = (bf16[64,2048]{1,0:T(8,128)(2,1)S(1)}, bf16[64,2048]{1,0:T(8,128)(2,1)S(1)}, u32[]{:S(2)}, u32[]{:S(2)}) collective-permute-start(bf16[64,2048]{1,0:T(8,128)(2,1)S(1)} %get-tuple-element.66), channel_id=1, source_target_pairs={{0,2},{2,4},{4,6},{6,7},{7,5},{5,3},{3,1},{1,0},{8,10},{10,12},{12... | collective-permute-start | bytes 786440 | tf_op jit(solution)/shard_map/ppermute | solution.py:109
  96.1 2.5 %collective-permute-start.15 = (bf16[8,32,1792]{2,1,0:T(8,128)(2,1)S(1)}, bf16[8,32,1792]{2,1,0:T(8,128)(2,1)S(1)}, u32[]{:S(2)}, u32[]{:S(2)}) collective-permute-start(bf16[8,32,1792]{2,1,0:T(8,128)(2,1)S(1)} %get-tuple-element.79.refs_0_), channel_id=1, source_target_pairs={{0,8},{8,0},{16,24},{24,16},{1,9},{9,1},{17,25},{25,17},{2,10},{10... | collective-permute-start | bytes 2752520 | tf_op jit(solution)/shard_map/ppermute | solution.py:420
  96.1 5.5 %copy-start.1 = (bf16[128,2048]{1,0:T(8,128)(2,1)S(1)}, bf16[128,2048]{1,0:T(8,128)(2,1)}, u32[]{:S(2)}) copy-start(bf16[128,2048]{1,0:T(8,128)(2,1)} %refs_0_.7) | copy-start | bytes 1572868
  96.1 3.8 %collective-permute-start.16 = (bf16[8,32,1792]{2,1,0:T(8,128)(2,1)S(1)}, bf16[8,32,1792]{2,1,0:T(8,128)(2,1)S(1)}, u32[]{:S(2)}, u32[]{:S(2)}) collective-permute-start(bf16[8,32,1792]{2,1,0:T(8,128)(2,1)S(1)} %get-tuple-element.80.refs_2_), channel_id=1, source_target_pairs={{0,8},{8,0},{16,24},{24,16},{1,9},{9,1},{17,25},{25,17},{2,10},{10... | collective-permute-start | bytes 2752520 | tf_op jit(solution)/shard_map/ppermute | solution.py:420
  122.7 12.5 %collective-permute-start.17 = (f32[1,1792]{1,0:T(1,128)S(1)}, f32[1,1792]{1,0:T(1,128)S(1)}, u32[]{:S(2)}, u32[]{:S(2)}) collective-permute-start(f32[1,1792]{1,0:T(1,128)S(1)} %get-tuple-element.84.refs_0_), channel_id=1, source_target_pairs={{0,8},{8,0},{16,24},{24,16},{1,9},{9,1},{17,25},{25,17},{2,10},{10... | collective-permute-start | bytes 21512 | tf_op jit(solution)/shard_map/ppermute | solution.py:436
  122.9 13.2 %collective-permute-start.18 = (f32[1,1792]{1,0:T(1,128)S(1)}, f32[1,1792]{1,0:T(1,128)S(1)}, u32[]{:S(2)}, u32[]{:S(2)}) collective-permute-start(f32[1,1792]{1,0:T(1,128)S(1)} %get-tuple-element.84.refs_0_), channel_id=1, source_target_pairs={{0,16},{8,24},{16,0},{24,8},{1,17},{9,25},{17,1},{25,9},{2,18},{10... | collective-permute-start | bytes 21512 | tf_op jit(solution)/shard_map/ppermute | solution.py:436
  123.5 12.6 %collective-permute-start.19 = (f32[1,1792]{1,0:T(1,128)S(1)}, f32[1,1792]{1,0:T(1,128)S(1)}, u32[]{:S(2)}, u32[]{:S(2)}) collective-permute-start(f32[1,1792]{1,0:T(1,128)S(1)} %get-tuple-element.84.refs_0_), channel_id=1, source_target_pairs={{0,24},{8,16},{16,8},{24,0},{1,25},{9,17},{17,9},{25,1},{2,26},{10... | collective-permute-start | bytes 21512 | tf_op jit(solution)/shard_map/ppermute | solution.py:436
  134.1 6.2 %collective-permute-start.11 = (f32[1,640]{1,0:T(1,128)S(1)}, f32[1,640]{1,0:T(1,128)S(1)}, u32[]{:S(2)}, u32[]{:S(2)}) collective-permute-start(f32[1,640]{1,0:T(1,128)S(1)} %get-tuple-element.74.refs_0_), channel_id=1, source_target_pairs={{0,8},{8,0},{16,24},{24,16},{1,9},{9,1},{17,25},{25,17},{2,10},{10... | collective-permute-start | bytes 7688 | tf_op jit(solution)/shard_map/ppermute | solution.py:436
  134.6 5.7 %collective-permute-start.12 = (f32[1,640]{1,0:T(1,128)S(1)}, f32[1,640]{1,0:T(1,128)S(1)}, u32[]{:S(2)}, u32[]{:S(2)}) collective-permute-start(f32[1,640]{1,0:T(1,128)S(1)} %get-tuple-element.74.refs_0_), channel_id=1, source_target_pairs={{0,16},{8,24},{16,0},{24,8},{1,17},{9,25},{17,1},{25,9},{2,18},{10... | collective-permute-start | bytes 7688 | tf_op jit(solution)/shard_map/ppermute | solution.py:436
  135.2 5.1 %collective-permute-start.13 = (f32[1,640]{1,0:T(1,128)S(1)}, f32[1,640]{1,0:T(1,128)S(1)}, u32[]{:S(2)}, u32[]{:S(2)}) collective-permute-start(f32[1,640]{1,0:T(1,128)S(1)} %get-tuple-element.74.refs_0_), channel_id=1, source_target_pairs={{0,24},{8,16},{16,8},{24,0},{1,25},{9,17},{17,9},{25,1},{2,26},{10... | collective-permute-start | bytes 7688 | tf_op jit(solution)/shard_map/ppermute | solution.py:436
